TPU v7x, 256 devices: a whole 4x4x8 slice. The times are simulated.
256 devices in a mesh: ctx: 8 (over y_lo, x), head: 32 (over z, y_hi, core).
Axes of the slice: x: 4, y: 4 (y_hi: 2, y_lo: 2; y = y_hi * 2 + y_lo), z: 8, core: 2. Of those that a mesh axis runs over, the one named last changes fastest.
Arguments:
- tokens: bfloat16 [4096, 2304], P('ctx'), may hold values from -6 to 6
- w_qkv: bfloat16 [2304, 3, 4096], P(None, None, 'head'), may hold values from -0.125 to 0.125
- conv_weight: float32 [4, 3, 4096], P(None, None, 'head'), may hold values from -3 to 3
- f_down: bfloat16 [2304, 128], replicated, may hold values from -0.125 to 0.125
- f_up: bfloat16 [128, 4096], P(None, 'head'), may hold values from -0.5 to 0.5
- dt_bias: float32 [4096], P('head'), may hold values from -9 to -3
- a_log: float32 [32], P('head'), may hold values from -1 to 0.5
- w_beta: bfloat16 [2304, 32], P(None, 'head'), may hold values from -0.125 to 0.125
- o_down: bfloat16 [2304, 128], replicated, may hold values from -0.125 to 0.125
- o_up: bfloat16 [128, 4096], P(None, 'head'), may hold values from -0.5 to 0.5
- norm_gain: float32 [128], replicated, may hold values from 0.5 to 1.5
- w_out: bfloat16 [4096, 2304], P('head'), may hold values from -0.09375 to 0.09375
Outputs:
- layer_out: bfloat16 [4096, 2304], P(('ctx', 'head'))
All inputs are finite; a program needn't handle non-finite values.
Results may differ from a plain program's by a relative error of at most 0.023.
Values may be sent and summed in bfloat16 or wider, within the bound.
No kernel may reach another device: no remote copies, remote signals or barrier semaphores. Data moves between devices by JAX's collectives and lax.ppermute only.
A program may use at most 128 MiB of HBM per device.

v0:
```python
import jax
import jax.numpy as jnp
from jax import lax
from jax.sharding import PartitionSpec as P

BLOCK = 64


HIGHEST = lax.Precision.HIGHEST


def from_behind(value, axis, steps):
    count = lax.axis_size(axis)
    first, last = (max(0, -steps), min(count, count - steps))
    return lax.ppermute(value, axis, [(source, source + steps) for source in range(first, last)])


def product(left, right):
    return jnp.dot(left, right, precision=HIGHEST)


def advance(carry, item):
    before, offset = carry
    moving, adding = item
    return ((product(moving, before), product(moving, offset) + adding), (before, offset))


def on_device(
    tokens, w_qkv, conv_weight, f_down, f_up, dt_bias, a_log, w_beta, o_down, o_up, norm_gain, w_out
):
    tok_rows, model_width = tokens.shape
    head_size = f_up.shape[1]
    conv_taps = conv_weight.shape[0]
    block_count = tok_rows // BLOCK
    raw = jnp.dot(
        tokens, w_qkv.reshape(model_width, 3 * head_size), preferred_element_type=jnp.float32
    ).astype(jnp.bfloat16)
    rim_rows = from_behind(raw[tok_rows - (conv_taps - 1) :], "ctx", 1)
    padded = lax.optimization_barrier(jnp.concatenate([rim_rows, raw], axis=0)).astype(jnp.float32)
    kernel = conv_weight.reshape(conv_taps, 3 * head_size)
    mixed = padded[0:tok_rows] * kernel[0]
    for tap_index in range(1, conv_taps):
        mixed = mixed + padded[tap_index : tap_index + tok_rows] * kernel[tap_index]
    active = jax.nn.silu(mixed)
    query_raw = active[:, 0:head_size]
    key_raw = active[:, head_size : 2 * head_size]
    queries = (
        query_raw
        * lax.rsqrt(jnp.sum(query_raw * query_raw, axis=-1, keepdims=True) + 1e-06)
        * head_size ** (-0.5)
    )
    keyset = key_raw * lax.rsqrt(jnp.sum(key_raw * key_raw, axis=-1, keepdims=True) + 1e-06)
    rounded = lax.optimization_barrier(
        (
            queries.astype(jnp.bfloat16),
            keyset.astype(jnp.bfloat16),
            active[:, 2 * head_size :].astype(jnp.bfloat16),
        )
    )
    queries = rounded[0].astype(jnp.float32).reshape(block_count, BLOCK, head_size)
    keyset = rounded[1].astype(jnp.float32).reshape(block_count, BLOCK, head_size)
    values = rounded[2].astype(jnp.float32).reshape(block_count, BLOCK, head_size)
    gate_low = jnp.dot(tokens, f_down, preferred_element_type=jnp.float32).astype(jnp.bfloat16)
    gate_logit = jnp.dot(gate_low, f_up, preferred_element_type=jnp.float32) + dt_bias
    decays = -jnp.exp(a_log[0]) * jax.nn.softplus(gate_logit)
    beta_rate = jax.nn.sigmoid(jnp.dot(tokens, w_beta, preferred_element_type=jnp.float32)).reshape(
        block_count, BLOCK
    )
    cumulative = jnp.cumsum(decays.reshape(block_count, BLOCK, head_size), axis=1)
    rising = jnp.exp(cumulative)
    falling = jnp.exp(-cumulative)
    key_rise = keyset * rising
    key_fall = keyset * falling
    query_rise = queries * rising
    strict_mask = jnp.tri(BLOCK, k=-1, dtype=jnp.float32)
    causal_mask = jnp.tri(BLOCK, dtype=jnp.float32)
    inner = jnp.einsum("btc,bsc->bts", key_rise, key_fall, precision=HIGHEST)
    scores = jnp.einsum("btc,bsc->bts", query_rise, key_fall, precision=HIGHEST) * causal_mask
    system = jnp.eye(BLOCK, dtype=jnp.float32) + beta_rate[:, :, None] * inner * strict_mask
    target = beta_rate[:, :, None] * jnp.concatenate([values, key_rise], axis=-1)
    solved = lax.linalg.triangular_solve(
        system, target, left_side=True, lower=True, unit_diagonal=True
    )
    value_part = solved[:, :, 0:head_size]
    key_part = solved[:, :, head_size:]
    tail_keys = keyset * jnp.exp(cumulative[:, -1:, :] - cumulative)
    identity = jnp.eye(head_size, dtype=jnp.float32)
    transitions = jnp.exp(cumulative[:, -1, :])[:, :, None] * identity
    transitions = transitions - jnp.einsum("btc,btd->bcd", tail_keys, key_part, precision=HIGHEST)
    additions = jnp.einsum("btc,btv->bcv", tail_keys, value_part, precision=HIGHEST)
    zero_state = jnp.zeros((head_size, head_size), jnp.float32)
    totals, prefixes = lax.scan(advance, (identity, zero_state), (transitions, additions))
    incoming = zero_state
    for step_index in range(lax.axis_size("ctx") - 1):
        leaving = product(totals[0], incoming) + totals[1]
        incoming = from_behind(leaving.astype(jnp.bfloat16), "ctx", 1).astype(leaving.dtype)
    starts = jnp.einsum("bcd,dv->bcv", prefixes[0], incoming, precision=HIGHEST) + prefixes[1]
    updates = value_part - jnp.einsum("btc,bcv->btv", key_part, starts, precision=HIGHEST)
    core = jnp.einsum("btc,bcv->btv", query_rise, starts, precision=HIGHEST)
    core = core + jnp.einsum("bts,bsv->btv", scores, updates, precision=HIGHEST)
    core = core.reshape(tok_rows, head_size)
    out_low = jnp.dot(tokens, o_down, preferred_element_type=jnp.float32).astype(jnp.bfloat16)
    out_gate = jax.nn.sigmoid(jnp.dot(out_low, o_up, preferred_element_type=jnp.float32))
    scale = lax.rsqrt(jnp.mean(core * core, axis=-1, keepdims=True) + 1e-05)
    gated = (core * scale * norm_gain * out_gate).astype(jnp.bfloat16)
    return lax.psum_scatter(
        jnp.dot(gated, w_out, preferred_element_type=jnp.float32).astype(jnp.bfloat16),
        "head",
        scatter_dimension=0,
        tiled=True,
    )


def solution(mesh):
    in_specs = (
        P("ctx", None),
        P(None, None, "head"),
        P(None, None, "head"),
        P(),
        P(None, "head"),
        P("head"),
        P("head"),
        P(None, "head"),
        P(),
        P(None, "head"),
        P(),
        P("head", None),
    )
    out_specs = P(("ctx", "head"), None)
    return jax.shard_map(
        on_device, mesh=mesh, in_specs=in_specs, out_specs=out_specs, check_vma=False
    )
```

profile of v0, /device:TPU:1, one launch (start us, length us, event | category | flops | bytes accessed | tf_op | source)
XLA Modules:
  0.0 277.8 jit_solution(7633016532142212593)
XLA Ops:
  6.5 4.0 %copy.27 = bf16[2304,3,128]{0,2,1:T(8,128)(2,1)} copy(bf16[2304,3,128]{2,0,1:T(8,128)(2,1)} %param.15) | data formatting | bytes 3538944 | tf_op args[1]
  10.5 2.9 %convolution_convert_fusion.1 = bf16[512,384]{1,0:T(8,128)(2,1)S(1)} fusion(bf16[512,2304]{1,0:T(8,128)(2,1)S(1)} %copy-done, bf16[2304,384]{0,1:T(8,128)(2,1)} %bitcast.82), kind=kOutput, calls=%fused_computation.15 | convolution fusion | flops 906166272 | bytes 4521984 | tf_op jit(solution)/shard_map/dot_general | solution.py:35
  13.5 3.9 %collective-permute-start = (bf16[3,384]{1,0:T(4,128)(2,1)S(1)}, bf16[3,384]{1,0:T(4,128)(2,1)S(1)}, u32[]{:S(2)}, u32[]{:S(2)}) collective-permute-start(bf16[3,384]{1,0:T(4,128)(2,1)S(1)} %slice.70), channel_id=1, source_target_pairs={{0,32},{32,64},{64,96},{96,128},{128,160},{160,192},{192,224},{1,3... | collective-permute-start | bytes 6920 | tf_op jit(solution)/shard_map/ppermute | solution.py:15
  18.2 2.0 fusion.33
  20.4 0.6 slice_bitcast_fusion
  21.0 0.7 fusion.59
  21.8 0.7 iota_compare_fusion.4
  22.5 0.6 fusion.54
  23.2 0.7 copy.35
  24.0 0.5 divide_multiply_fusion
  24.5 0.2 multiply_reduce_fusion.1
  24.8 0.7 slice.124
  25.4 0.2 multiply_convert_fusion
  25.7 1.1 exponential_multiply_fusion.1
  26.8 0.7 copy-done.1
  27.5 1.3 fusion.19
  28.8 40.0 %custom-call.3 = f32[8,1,64,64]{2,3,1,0:T(8,128)S(1)} custom-call(f32[8,1,64,64]{3,2,1,0:T(8,128)} %fusion.19), custom_call_target="InvertDiagBlocksLowerTriangular" | custom-call | tf_op jit(solution)/shard_map/triangular_solve | solution.py:81
  68.9 1.0 copy.36
  69.9 0.9 maximum_multiply_fusion
  70.8 0.8 fusion.31
  71.6 1.8 fusion.39
  73.4 2.0 convolution_subtract_fusion
  75.4 15.9 %while.17 = (s32[]{:T(128)}, f32[128,128]{1,0:T(8,128)S(1)}, f32[128,128]{1,0:T(8,128)S(1)}, f32[8,128,128]{2,1,0:T(8,128)}, f32[8,128,128]{2,1,0:T(8,128)}, /*i...) while((s32[]{:T(128)}, f32[128,128]{1,0:T(8,128)S(1)}, ...), condition=%wide.region_4.5_spmd.clone, body=%wide.region_3.4_spmd.clone.sunk | while | flops 50380800 | bytes 984695 | solution.py:92
  75.4 0.7 bitcast_dynamic-update-slice_fusion.3
  76.1 1.0 convolution_add_fusion.12
  77.1 0.2 fusion.100
  77.4 0.7 bitcast_dynamic-update-slice_fusion.3
  78.1 1.0 convolution_add_fusion.12
  79.1 0.2 fusion.100
  79.4 0.7 bitcast_dynamic-update-slice_fusion.3
  80.1 1.0 convolution_add_fusion.12
  81.1 0.2 fusion.100
  81.4 0.7 bitcast_dynamic-update-slice_fusion.3
  82.0 1.0 convolution_add_fusion.12
  83.4 0.7 bitcast_dynamic-update-slice_fusion.3
  84.0 1.0 convolution_add_fusion.12
  85.3 0.7 bitcast_dynamic-update-slice_fusion.3
  86.0 1.0 convolution_add_fusion.12
  87.1 0.2 fusion.100
  87.3 0.7 bitcast_dynamic-update-slice_fusion.3
  88.0 1.0 convolution_add_fusion.12
  89.3 0.7 bitcast_dynamic-update-slice_fusion.3
  90.0 1.0 convolution_add_fusion.12
  91.5 3.3 %collective-permute-start.1 = (bf16[128,128]{1,0:T(8,128)(2,1)S(1)}, bf16[128,128]{1,0:T(8,128)(2,1)S(1)}, u32[]{:S(2)}, u32[]{:S(2)}) collective-permute-start(bf16[128,128]{1,0:T(8,128)(2,1)S(1)} %fusion.21), channel_id=1, source_target_pairs={{0,32},{32,64},{64,96},{96,128},{128,160},{160,192},{192,224},{1,3... | collective-permute-start | bytes 98312 | tf_op jit(solution)/shard_map/ppermute | solution.py:15
  94.7 1.0 collective-permute-done.1
  95.9 3.6 %collective-permute-start.2 = (bf16[128,128]{1,0:T(8,128)(2,1)S(1)}, bf16[128,128]{1,0:T(8,128)(2,1)S(1)}, u32[]{:S(2)}, u32[]{:S(2)}) collective-permute-start(bf16[128,128]{1,0:T(8,128)(2,1)S(1)} %fusion.22), channel_id=1, source_target_pairs={{0,32},{32,64},{64,96},{96,128},{128,160},{160,192},{192,224},{1,3... | collective-permute-start | bytes 98312 | tf_op jit(solution)/shard_map/ppermute | solution.py:15
  99.6 1.0 collective-permute-done.2
  100.8 3.6 %collective-permute-start.3 = (bf16[128,128]{1,0:T(8,128)(2,1)S(1)}, bf16[128,128]{1,0:T(8,128)(2,1)S(1)}, u32[]{:S(2)}, u32[]{:S(2)}) collective-permute-start(bf16[128,128]{1,0:T(8,128)(2,1)S(1)} %fusion.23), channel_id=1, source_target_pairs={{0,32},{32,64},{64,96},{96,128},{128,160},{160,192},{192,224},{1,3... | collective-permute-start | bytes 98312 | tf_op jit(solution)/shard_map/ppermute | solution.py:15
  104.4 1.0 collective-permute-done.3
  105.6 3.6 %collective-permute-start.4 = (bf16[128,128]{1,0:T(8,128)(2,1)S(1)}, bf16[128,128]{1,0:T(8,128)(2,1)S(1)}, u32[]{:S(2)}, u32[]{:S(2)}) collective-permute-start(bf16[128,128]{1,0:T(8,128)(2,1)S(1)} %fusion.24), channel_id=1, source_target_pairs={{0,32},{32,64},{64,96},{96,128},{128,160},{160,192},{192,224},{1,3... | collective-permute-start | bytes 98312 | tf_op jit(solution)/shard_map/ppermute | solution.py:15
  109.3 1.0 collective-permute-done.4
  110.4 3.9 %collective-permute-start.5 = (bf16[128,128]{1,0:T(8,128)(2,1)S(1)}, bf16[128,128]{1,0:T(8,128)(2,1)S(1)}, u32[]{:S(2)}, u32[]{:S(2)}) collective-permute-start(bf16[128,128]{1,0:T(8,128)(2,1)S(1)} %fusion.25), channel_id=1, source_target_pairs={{0,32},{32,64},{64,96},{96,128},{128,160},{160,192},{192,224},{1,3... | collective-permute-start | bytes 98312 | tf_op jit(solution)/shard_map/ppermute | solution.py:15
  114.3 1.0 collective-permute-done.5
  115.5 5.8 %collective-permute-start.6 = (bf16[128,128]{1,0:T(8,128)(2,1)S(1)}, bf16[128,128]{1,0:T(8,128)(2,1)S(1)}, u32[]{:S(2)}, u32[]{:S(2)}) collective-permute-start(bf16[128,128]{1,0:T(8,128)(2,1)S(1)} %fusion.26), channel_id=1, source_target_pairs={{0,32},{32,64},{64,96},{96,128},{128,160},{160,192},{192,224},{1,3... | collective-permute-start | bytes 98312 | tf_op jit(solution)/shard_map/ppermute | solution.py:15
  121.3 1.0 collective-permute-done.6
  122.5 5.9 %collective-permute-start.7 = (bf16[128,128]{1,0:T(8,128)(2,1)S(1)}, bf16[128,128]{1,0:T(8,128)(2,1)S(1)}, u32[]{:S(2)}, u32[]{:S(2)}) collective-permute-start(bf16[128,128]{1,0:T(8,128)(2,1)S(1)} %fusion.27), channel_id=1, source_target_pairs={{0,32},{32,64},{64,96},{96,128},{128,160},{160,192},{192,224},{1,3... | collective-permute-start | bytes 98312 | tf_op jit(solution)/shard_map/ppermute | solution.py:15
  128.4 1.6 convolution_multiply_fusion
  130.1 0.4 convolution_add_fusion.1
  130.5 0.6 convolution_subtract_fusion.1
  131.1 0.6 fusion.44
  131.7 0.5 multiply_reduce_fusion
  132.5 2.0 fusion.20
  134.5 2.2 convolution_convert_fusion
  136.7 134.3 %reduce-scatter.2.cloned.1.call-done = bf16[16,2304]{1,0:T(8,128)(2,1)} async-done(((bf16[512,2304]{1,0:T(8,128)(2,1)}), bf16[16,2304]{1,0:T(8,128)(2,1)}) %reduce-scatter.2.cloned.1.call-update) | async-done | bytes 73744 | tf_op jit(solution)/shard_map/reduce_scatter | solution.py:106
  (84 shorter events, 3.0 us)
Async XLA Ops:
  6.5 4.0 %copy-start = (bf16[512,2304]{1,0:T(8,128)(2,1)S(1)}, bf16[512,2304]{1,0:T(8,128)(2,1)}, u32[]{:S(2)}) copy-start(bf16[512,2304]{1,0:T(8,128)(2,1)} %param.14) | copy-start | bytes 7077892
  6.5 264.5 %reduce-scatter.2.cloned.1.call-start = ((), (), s32[]{:S(2)}) async-start(), calls=%async_computation.1 | async-start | bytes 2433024 | tf_op jit(solution)/shard_map/reduce_scatter | solution.py:106
  10.5 7.6 %copy-start.14 = (bf16[128,128]{1,0:T(8,128)(2,1)S(1)}, bf16[128,128]{1,0:T(8,128)(2,1)}, u32[]{:S(2)}) copy-start(bf16[128,128]{1,0:T(8,128)(2,1)} %param.18) | copy-start | bytes 98308
  10.5 7.6 %copy-start.16 = (f32[128]{0:T(128)S(1)}, f32[128]{0:T(128)}, u32[]{:S(2)}) copy-start(f32[128]{0:T(128)} %param.19) | copy-start | bytes 1540
  13.4 7.5 %copy-start.11 = (bf16[2304,1]{0,1:T(2,128)(2,1)S(1)}, bf16[2304,1]{0,1:T(2,128)(2,1)}, u32[]{:S(2)}) copy-start(bf16[2304,1]{0,1:T(2,128)(2,1)} %param.21) | copy-start | bytes 13828
  13.5 10.4 %collective-permute-start = (bf16[3,384]{1,0:T(4,128)(2,1)S(1)}, bf16[3,384]{1,0:T(4,128)(2,1)S(1)}, u32[]{:S(2)}, u32[]{:S(2)}) collective-permute-start(bf16[3,384]{1,0:T(4,128)(2,1)S(1)} %slice.70), channel_id=1, source_target_pairs={{0,32},{32,64},{64,96},{96,128},{128,160},{160,192},{192,224},{1,3... | collective-permute-start | bytes 6920 | tf_op jit(solution)/shard_map/ppermute | solution.py:15
  20.2 1.5 copy-start.12
  24.0 1.7 copy-start.10
  24.5 3.0 %copy-start.7 = (f32[64,64]{1,0:T(8,128)S(1)}, f32[64,64]{1,0:T(8,128)}, u32[]{:S(2)}) copy-start(f32[64,64]{1,0:T(8,128)} %get-tuple-element.108) | copy-start | bytes 49156
  24.5 3.0 %copy-start.8 = (f32[64,64]{1,0:T(8,128)S(1)}, f32[64,64]{1,0:T(8,128)}, u32[]{:S(2)}) copy-start(f32[64,64]{1,0:T(8,128)} %get-tuple-element.113) | copy-start | bytes 49156
  24.5 3.0 %copy-start.9 = (f32[64,64]{1,0:T(8,128)S(1)}, f32[64,64]{1,0:T(8,128)}, u32[]{:S(2)}) copy-start(f32[64,64]{1,0:T(8,128)} %fusion.54) | copy-start | bytes 49156
  26.8 0.7 copy-start.1
  26.8 44.8 %copy-start.3 = (f32[8,64,128]{2,0,1:T(8,128)}, f32[8,64,128]{2,0,1:T(8,128)S(1)}, u32[]{:S(2)}) copy-start(f32[8,64,128]{2,0,1:T(8,128)S(1)} %get-tuple-element.103) | copy-start | bytes 786436
  91.2 38.8 %copy-start.5 = (f32[8,128,128]{2,1,0:T(8,128)S(1)}, f32[8,128,128]{2,1,0:T(8,128)}, u32[]{:S(2)}) copy-start(f32[8,128,128]{2,1,0:T(8,128)} %get-tuple-element.54) | copy-start | bytes 1572868
  91.2 38.8 %copy-start.6 = (f32[8,128,128]{2,1,0:T(8,128)S(1)}, f32[8,128,128]{2,1,0:T(8,128)}, u32[]{:S(2)}) copy-start(f32[8,128,128]{2,1,0:T(8,128)} %get-tuple-element.51) | copy-start | bytes 1572868
  91.5 39.6 %copy-start.2 = (f32[8,64,128]{2,0,1:T(8,128)S(1)}, f32[8,64,128]{2,0,1:T(8,128)}, u32[]{:S(2)}) copy-start(f32[8,64,128]{2,0,1:T(8,128)} %get-tuple-element.106) | copy-start | bytes 786436
  91.5 4.3 %collective-permute-start.1 = (bf16[128,128]{1,0:T(8,128)(2,1)S(1)}, bf16[128,128]{1,0:T(8,128)(2,1)S(1)}, u32[]{:S(2)}, u32[]{:S(2)}) collective-permute-start(bf16[128,128]{1,0:T(8,128)(2,1)S(1)} %fusion.21), channel_id=1, source_target_pairs={{0,32},{32,64},{64,96},{96,128},{128,160},{160,192},{192,224},{1,3... | collective-permute-start | bytes 98312 | tf_op jit(solution)/shard_map/ppermute | solution.py:15
  95.9 4.7 %collective-permute-start.2 = (bf16[128,128]{1,0:T(8,128)(2,1)S(1)}, bf16[128,128]{1,0:T(8,128)(2,1)S(1)}, u32[]{:S(2)}, u32[]{:S(2)}) collective-permute-start(bf16[128,128]{1,0:T(8,128)(2,1)S(1)} %fusion.22), channel_id=1, source_target_pairs={{0,32},{32,64},{64,96},{96,128},{128,160},{160,192},{192,224},{1,3... | collective-permute-start | bytes 98312 | tf_op jit(solution)/shard_map/ppermute | solution.py:15
  100.8 4.7 %collective-permute-start.3 = (bf16[128,128]{1,0:T(8,128)(2,1)S(1)}, bf16[128,128]{1,0:T(8,128)(2,1)S(1)}, u32[]{:S(2)}, u32[]{:S(2)}) collective-permute-start(bf16[128,128]{1,0:T(8,128)(2,1)S(1)} %fusion.23), channel_id=1, source_target_pairs={{0,32},{32,64},{64,96},{96,128},{128,160},{160,192},{192,224},{1,3... | collective-permute-start | bytes 98312 | tf_op jit(solution)/shard_map/ppermute | solution.py:15
  105.6 4.7 %collective-permute-start.4 = (bf16[128,128]{1,0:T(8,128)(2,1)S(1)}, bf16[128,128]{1,0:T(8,128)(2,1)S(1)}, u32[]{:S(2)}, u32[]{:S(2)}) collective-permute-start(bf16[128,128]{1,0:T(8,128)(2,1)S(1)} %fusion.24), channel_id=1, source_target_pairs={{0,32},{32,64},{64,96},{96,128},{128,160},{160,192},{192,224},{1,3... | collective-permute-start | bytes 98312 | tf_op jit(solution)/shard_map/ppermute | solution.py:15
  110.4 4.9 %collective-permute-start.5 = (bf16[128,128]{1,0:T(8,128)(2,1)S(1)}, bf16[128,128]{1,0:T(8,128)(2,1)S(1)}, u32[]{:S(2)}, u32[]{:S(2)}) collective-permute-start(bf16[128,128]{1,0:T(8,128)(2,1)S(1)} %fusion.25), channel_id=1, source_target_pairs={{0,32},{32,64},{64,96},{96,128},{128,160},{160,192},{192,224},{1,3... | collective-permute-start | bytes 98312 | tf_op jit(solution)/shard_map/ppermute | solution.py:15
  115.5 6.8 %collective-permute-start.6 = (bf16[128,128]{1,0:T(8,128)(2,1)S(1)}, bf16[128,128]{1,0:T(8,128)(2,1)S(1)}, u32[]{:S(2)}, u32[]{:S(2)}) collective-permute-start(bf16[128,128]{1,0:T(8,128)(2,1)S(1)} %fusion.26), channel_id=1, source_target_pairs={{0,32},{32,64},{64,96},{96,128},{128,160},{160,192},{192,224},{1,3... | collective-permute-start | bytes 98312 | tf_op jit(solution)/shard_map/ppermute | solution.py:15
  122.5 7.6 %collective-permute-start.7 = (bf16[128,128]{1,0:T(8,128)(2,1)S(1)}, bf16[128,128]{1,0:T(8,128)(2,1)S(1)}, u32[]{:S(2)}, u32[]{:S(2)}) collective-permute-start(bf16[128,128]{1,0:T(8,128)(2,1)S(1)} %fusion.27), channel_id=1, source_target_pairs={{0,32},{32,64},{64,96},{96,128},{128,160},{160,192},{192,224},{1,3... | collective-permute-start | bytes 98312 | tf_op jit(solution)/shard_map/ppermute | solution.py:15
  130.1 2.3 copy-start.13
  130.1 2.4 copy-start.15
  132.3 2.2 copy-start.4
Sparse Core Ops, SparseCore 0:
  136.8 134.1 reduce-scatter.1
where the time goes:
time: 283 us; the launch traced here: 278 us
  waiting for transfers between devices  140 us (49%)
  other arithmetic  50.1 us (18%)
  starting transfers between devices  33.7 us (12%)
  matrix products  30.6 us (11%)
  between operations  14.6 us (5%)
  local copies, waits for them, and re-layouts  8.06 us (3%)
    reduce_scatter x1, waiting for transfers between devices, on_device(): lax.psum_scatter(jnp.dot(gated, w_out, preferred_element_type=jnp.float32...  134 us
    another operation x4, other arithmetic, on_device(): lax.linalg.triangular_solve(system, target, left_side=True, lower=True, u...  41.4 us
    ppermute x8, starting transfers between devices, from_behind(): lax.ppermute(value, axis, [(source, source + steps) for source in range(f...  33.7 us
    dot_general x23, matrix products, product(): return jnp.dot(left, right, precision=HIGHEST)  11.2 us
    ppermute x8, waiting for transfers between devices, from_behind(): lax.ppermute(value, axis, [(source, source + steps) for source in range(f...  6.02 us
  transfers between devices with their start and end apart: 9, of which 7 were waited for; matrix products, arithmetic and copies ran while one was open for 3% of the time, Pallas kernels for 0%

commit v1 on v0

v1 whole, which is shorter than its diff:
```python
import functools

import jax
import jax.numpy as jnp
from jax import lax
from jax.experimental import pallas as pl
from jax.experimental.pallas import tpu as pltpu
from jax.sharding import PartitionSpec as P

BLOCK = 64
GROUP = 256
F32 = jnp.float32
BF16 = jnp.bfloat16
HIGHEST = lax.Precision.HIGHEST
VMEM = pl.BlockSpec(memory_space=pltpu.VMEM)
SMEM = pl.BlockSpec(memory_space=pltpu.SMEM)
LIMIT = pltpu.CompilerParams(vmem_limit_bytes=40 * 1024 * 1024)


def mm(left, right):
    return jnp.dot(left.astype(BF16), right.astype(BF16), preferred_element_type=F32)


def mm_nt(left, right):
    return lax.dot_general(
        left.astype(BF16), right.astype(BF16), (((1,), (1,)), ((), ())), preferred_element_type=F32
    )


def mm_tn(left, right):
    return lax.dot_general(
        left.astype(BF16), right.astype(BF16), (((0,), (0,)), ((), ())), preferred_element_type=F32
    )


def split(value):
    high = value.astype(BF16)
    return high, (value - high.astype(F32)).astype(BF16)


def mm3(left, right):
    lh, ll = split(left)
    rh, rl = split(right)
    dot = functools.partial(jnp.dot, preferred_element_type=F32)
    return dot(lh, rh) + (dot(lh, rl) + dot(ll, rh))


def project(
    alog, tokens, w3, f_down, f_up, bias, w_beta, o_down, o_up, raw_out, cum_out, beta_out, gate_out
):
    head = f_up.shape[0]
    tok = tokens[...]
    for part in range(3):
        raw_out[:, part * head : (part + 1) * head] = jnp.dot(
            tok, w3[part], preferred_element_type=F32
        ).astype(BF16)
    low = jnp.dot(tok, f_down[...], preferred_element_type=F32).astype(BF16)
    logit = jnp.dot(low, f_up[...], preferred_element_type=F32) + bias[...]
    decays = -jnp.exp(jnp.full((1, 1), alog[0], F32)) * jax.nn.softplus(logit)
    row = lax.broadcasted_iota(jnp.int32, (GROUP, GROUP), 0)
    col = lax.broadcasted_iota(jnp.int32, (GROUP, GROUP), 1)
    tri = jnp.where((row >= col) & ((row // BLOCK) == (col // BLOCK)), 1.0, 0.0).astype(F32)
    cum_out[...] = jnp.dot(tri, decays, precision=HIGHEST, preferred_element_type=F32)
    beta_out[...] = jax.nn.sigmoid(
        mm_nt(tok, jnp.broadcast_to(w_beta[...].astype(F32), (head, w_beta.shape[1])))
    )
    out_low = jnp.dot(tok, o_down[...], preferred_element_type=F32).astype(BF16)
    gate_out[...] = jax.nn.sigmoid(jnp.dot(out_low, o_up[...], preferred_element_type=F32))


def delta(raw, rim, taps, cum_ref, beta_ref, c_out, w_out, padded):
    rows, width = raw.shape
    head = width // 3
    count = rows // BLOCK
    padded[0:8, :] = rim[...].astype(F32)[rim.shape[0] - 8 :]
    padded[8:, :] = raw[...].astype(F32)
    conv_taps = taps.shape[1]
    active = []
    for part in range(3):
        lanes = slice(part * head, (part + 1) * head)
        mixed = padded[9 - conv_taps : 9 - conv_taps + rows, lanes] * taps[part, 0:1, :]
        for tap in range(1, conv_taps):
            start = 9 - conv_taps + tap
            mixed = mixed + padded[start : start + rows, lanes] * taps[part, tap : tap + 1, :]
        active.append(jax.nn.silu(mixed))
    query_raw, key_raw, value_raw = active
    queries = query_raw * lax.rsqrt(
        jnp.sum(query_raw * query_raw, axis=-1, keepdims=True) + 1e-06
    ) * (head ** (-0.5))
    keyset = key_raw * lax.rsqrt(jnp.sum(key_raw * key_raw, axis=-1, keepdims=True) + 1e-06)
    queries = queries.astype(BF16).astype(F32)
    keyset = keyset.astype(BF16).astype(F32)
    values = value_raw.astype(BF16).astype(F32)
    cumulative = cum_ref[...]
    beta = beta_ref[...]
    rising = jnp.exp(cumulative)
    falling = jnp.exp(-cumulative)
    key_rise = keyset * rising
    key_fall = (keyset * falling).astype(BF16)
    query_rise = queries * rising
    blocked = cumulative.reshape(count, BLOCK, head)
    ends = blocked[:, BLOCK - 1 : BLOCK, :]
    tail = (keyset.reshape(count, BLOCK, head) * jnp.exp(ends - blocked)).reshape(rows, head)
    tail = tail.astype(BF16)
    target = jnp.concatenate([beta * values, beta * key_rise], axis=1).astype(BF16)
    row = lax.broadcasted_iota(jnp.int32, (GROUP, GROUP), 0)
    col = lax.broadcasted_iota(jnp.int32, (GROUP, GROUP), 1)
    differ = row ^ col
    same = differ < BLOCK
    lower = row > col
    unit = jnp.where(row == col, 1.0, 0.0).astype(F32)
    systems, scores, inverse = [], [], []
    for group in range(rows // GROUP):
        rng = slice(group * GROUP, (group + 1) * GROUP)
        inner = mm_nt(key_rise[rng], key_fall[rng])
        wide = jnp.concatenate([beta[rng], beta[rng]], axis=1)
        systems.append(jnp.where(lower & same, inner * wide, 0.0))
        scores.append(
            jnp.where((row >= col) & same, mm_nt(query_rise[rng], key_fall[rng]), 0.0).astype(BF16)
        )
        inverse.append(unit - jnp.where(differ == 1, systems[-1], 0.0))
    size = 2
    while size < BLOCK:
        here = (differ >= size) & (differ < 2 * size)
        steps = [mm(jnp.where(here, s, 0.0), d) for s, d in zip(systems, inverse)]
        inverse = [d - mm(d, x) for d, x in zip(inverse, steps)]
        size *= 2
    mixing, adding, moving = [], [], []
    for group in range(rows // GROUP):
        rng = slice(group * GROUP, (group + 1) * GROUP)
        solved = mm(inverse[group], target[rng]).astype(BF16)
        local = mm(scores[group], solved)
        local_value, local_key = local[:, :head], query_rise[rng] - local[:, head:]
        for inside in range(GROUP // BLOCK):
            sub = slice(inside * BLOCK, (inside + 1) * BLOCK)
            mixing.append((local_value[sub], local_key[sub].astype(BF16)))
            pair = mm_tn(tail[group * GROUP + inside * BLOCK :][:BLOCK], solved[sub])
            adding.append(pair[:, :head])
            moving.append(pair[:, head:])
    shrink = jnp.transpose(jnp.exp(ends.reshape(count, head)))
    ident = unit[:head, :head]
    state = jnp.concatenate([jnp.zeros((head, head), F32), ident], axis=1)
    for block in range(count):
        low = state.astype(BF16)
        value_part, key_part = mixing[block]
        across = jnp.dot(key_part, low, preferred_element_type=F32)
        rng = slice(block * BLOCK, (block + 1) * BLOCK)
        c_out[rng, :head] = across[:, :head] + value_part
        c_out[rng, head:] = across[:, head:]
        step = mm(moving[block], low)
        state = shrink[:, block : block + 1] * state - step
        state = jnp.concatenate([state[:, :head] + adding[block], state[:, head:]], axis=1)
    final = state.astype(BF16)
    for copy in range(w_out.shape[0]):
        w_out[copy] = final


def finish(place, c_ref, gate, gain, states, own, to_core, to_far, to_both, gated):
    rows, head = gate.shape
    ctx, sub = place[0], place[1]
    state = jnp.zeros((head, head), F32)
    for step in range(states.shape[0] - 1):
        moved = jnp.dot(states[step, :, head:], state.astype(BF16), preferred_element_type=F32)
        state = jnp.where(step < ctx, moved + states[step, :, :head].astype(F32), state)
    core = c_ref[:, :head] + mm(c_ref[:, head:], state)
    scale = lax.rsqrt(jnp.mean(core * core, axis=-1, keepdims=True) + 1e-05)
    result = core * scale * gain[...] * gate[...]
    gated[...] = result.reshape(gated.shape)
    for out, flip in ((own, 0), (to_core, 1), (to_far, 2), (to_both, 3)):
        out[...] = gated[:, pl.ds(sub ^ flip, 1)].reshape(out.shape).astype(BF16)


def spread(place, g0, g1, g2, g3, w0, w1, w2, w3, out, left):
    zs, rows, head = g0.shape
    z = place[2]
    for lane, ref in enumerate((g0, g1, g2, g3)):
        for k in range(zs):
            left[k, :, lane * head : (lane + 1) * head] = ref[(z + k) % zs]
    full = left[...].reshape(zs * rows, 4 * head)
    total = jnp.dot(full[:, :head], w0[...], preferred_element_type=F32)
    for lane, ref in ((1, w1), (2, w2), (3, w3)):
        total = total + jnp.dot(
            full[:, lane * head : (lane + 1) * head], ref[...], preferred_element_type=F32
        )
    out[...] = total.astype(BF16).reshape(out.shape)


def on_device(
    tokens, w_qkv, conv_weight, f_down, f_up, dt_bias, a_log, w_beta, o_down, o_up, norm_gain, w_out
):
    rows, model = tokens.shape
    head = f_up.shape[1]
    ctx_count, head_count = lax.axis_size("ctx"), lax.axis_size("head")
    zs = head_count // 4
    shape = jax.ShapeDtypeStruct
    ctx, which = lax.axis_index("ctx"), lax.axis_index("head")
    place = jnp.stack([ctx, which % 4, which // 4]).astype(jnp.int32)

    def flip(value, mask):
        return lax.ppermute(value, "head", [(h, h ^ mask) for h in range(head_count)])

    with jax.named_scope("rim"):
        rim_tokens = lax.ppermute(
            tokens[rows - 16 :], "ctx", [(i, i + 1) for i in range(ctx_count - 1)]
        )
    with jax.named_scope("weights"):
        w_core, w_far = flip(w_out, 1), flip(w_out, 2)
        w_both = flip(w_far, 1)
    w3 = jnp.transpose(w_qkv, (1, 0, 2))
    tile = pl.BlockSpec((GROUP, head), lambda i: (i, 0))
    whole = lambda *dims: pl.BlockSpec(dims, lambda i: (0,) * len(dims))
    with jax.named_scope("project"):
        raw, cum, beta, gate = pl.pallas_call(
            project,
            grid=(rows // GROUP,),
            in_specs=[
                SMEM,
                pl.BlockSpec((GROUP, model), lambda i: (i, 0)),
                whole(3, model, head),
                whole(model, head),
                whole(head, head),
                whole(1, head),
                whole(1, model),
                whole(model, head),
                whole(head, head),
            ],
            out_specs=[pl.BlockSpec((GROUP, 3 * head), lambda i: (i, 0)), tile, tile, tile],
            out_shape=[
                shape((rows, 3 * head), BF16),
                shape((rows, head), F32),
                shape((rows, head), F32),
                shape((rows, head), F32),
            ],
            compiler_params=LIMIT,
            cost_estimate=pl.CostEstimate(
                flops=2 * rows * model * 6 * head, bytes_accessed=6_000_000, transcendentals=0
            ),
        )(
            a_log,
            tokens,
            w3,
            f_down,
            f_up,
            dt_bias.reshape(1, head),
            w_beta.reshape(1, model),
            o_down,
            o_up,
        )
    with jax.named_scope("rim_raw"):
        rim = lax.dot_general(
            rim_tokens, w3, (((1,), (1,)), ((), ())), preferred_element_type=F32
        ).astype(BF16).reshape(16, 3 * head)
    with jax.named_scope("delta"):
        c_parts, states = pl.pallas_call(
            delta,
            in_specs=[VMEM] * 5,
            out_specs=[VMEM] * 2,
            out_shape=[shape((rows, 2 * head), F32), shape((ctx_count, head, 2 * head), BF16)],
            scratch_shapes=[pltpu.VMEM((rows + 8, 3 * head), F32)],
            compiler_params=LIMIT,
            cost_estimate=pl.CostEstimate(
                flops=4_000_000_000, bytes_accessed=30_000_000, transcendentals=0
            ),
        )(raw, rim, jnp.transpose(conv_weight, (1, 0, 2)), cum, beta)
    with jax.named_scope("states"):
        states = lax.all_to_all(states, "ctx", 0, 0, tiled=True)
    part = shape((zs, 16, head), BF16)
    with jax.named_scope("finish"):
        own, to_core, to_far, to_both = pl.pallas_call(
            finish,
            in_specs=[SMEM] + [VMEM] * 4,
            out_specs=[VMEM] * 4,
            out_shape=[part] * 4,
            scratch_shapes=[pltpu.VMEM((zs, 4, 16, head), F32)],
            compiler_params=LIMIT,
        )(place, c_parts, gate, norm_gain.reshape(1, head), states)
    with jax.named_scope("exchange"):
        from_both, from_far, from_core = flip(to_both, 3), flip(to_far, 2), flip(to_core, 1)
    with jax.named_scope("spread"):
        parts = pl.pallas_call(
            spread,
            in_specs=[SMEM] + [VMEM] * 8,
            out_specs=VMEM,
            out_shape=shape((zs, 16, model), BF16),
            scratch_shapes=[pltpu.VMEM((zs, 16, 4 * head), BF16)],
            compiler_params=LIMIT,
        )(place, own, from_core, from_far, from_both, w_out, w_core, w_far, w_both)
    with jax.named_scope("reduce"):
        return reduce_z(parts, zs, head_count)


def reduce_z(parts, zs, head_count):
    def send(value, k):
        return lax.ppermute(
            value, "head", [(h, (h + 4 * k) % head_count) for h in range(head_count)]
        )

    total = parts[0].astype(F32)
    order = sorted(range(1, zs), key=lambda k: -min(k, zs - k))
    for got in [send(parts[k], k) for k in order]:
        total = total + got.astype(F32)
    return total.astype(BF16)


def solution(mesh):
    in_specs = (
        P("ctx", None),
        P(None, None, "head"),
        P(None, None, "head"),
        P(),
        P(None, "head"),
        P("head"),
        P("head"),
        P(None, "head"),
        P(),
        P(None, "head"),
        P(),
        P("head", None),
    )
    out_specs = P(("ctx", "head"), None)
    return jax.shard_map(
        on_device, mesh=mesh, in_specs=in_specs, out_specs=out_specs, check_vma=False
    )
```

time: 283 us -> 78.6 us (0.28)
  the two profiles are of different devices: /device:TPU:1 before, /device:TPU:2 now
where the time goes in v1:
time: 78.6 us; the launch traced here: 77.9 us
  starting transfers between devices  34.8 us (44%)
  waiting for transfers between devices  17.5 us (22%)
  Pallas kernels  12.9 us (16%)
  local copies, waits for them, and re-layouts  10.8 us (14%)
  between operations  0.8 us (1%)
  other arithmetic  0.79 us (1%)
    ppermute x7, starting transfers between devices, send(): lax.ppermute(value, 'head', [(h, (h + 4 * k) % head_count) for h in range...  19.7 us
    unnamed x28, local copies, waits for them, and re-layouts  9.89 us
    all_to_all x1, waiting for transfers between devices, on_device(): states = lax.all_to_all(states, 'ctx', 0, 0, tiled=True)  9.28 us
    ppermute x6, starting transfers between devices, flip(): lax.ppermute(value, 'head', [(h, h ^ mask) for h in range(head_count)])  6.98 us
    pallas_call x1, Pallas kernels, on_device(): pl.pallas_call(project, grid=(rows // GROUP,), in_specs=[SMEM, pl.BlockSp...  5.22 us
    all_to_all x1, starting transfers between devices, on_device(): states = lax.all_to_all(states, 'ctx', 0, 0, tiled=True)  4.78 us
    ppermute x7, waiting for transfers between devices, send(): lax.ppermute(value, 'head', [(h, (h + 4 * k) % head_count) for h in range...  4.74 us
    pallas_call x1, Pallas kernels, on_device(): pl.pallas_call(delta, in_specs=[VMEM] * 5, out_specs=[VMEM] * 2, out_shap...  4.6 us
  transfers between devices with their start and end apart: 15, of which 5 were waited for; matrix products, arithmetic and copies ran while one was open for 2% of the time, Pallas kernels for 15%

profile of v1, /device:TPU:2, one launch (start us, length us, event | category | flops | bytes accessed | tf_op | source)
XLA Modules:
  0.0 77.9 jit_solution(15461653813542896961)
XLA Ops:
  0.0 3.2 %collective-permute-start.5 = (bf16[128,2304]{1,0:T(8,128)(2,1)}, bf16[128,2304]{1,0:T(8,128)(2,1)S(1)}, u32[]{:S(2)}, u32[]{:S(2)}) collective-permute-start(bf16[128,2304]{1,0:T(8,128)(2,1)} %w0.1), channel_id=1, source_target_pairs={{0,2},{1,3},{2,0},{3,1},{4,6},{5,7},{6,4},{7,5},{8,10},{9,11},{10,... | collective-permute-start | bytes 1769480 | tf_op jit(solution)/shard_map/weights/ppermute | solution.py:200
  3.2 0.0 collective-permute-start.4
  3.2 0.9 %slice.27 = bf16[16,2304]{1,0:T(8,128)(2,1)S(1)} slice(bf16[512,2304]{1,0:T(8,128)(2,1)} %tokens.1), slice={[496:512], [0:2304]} | slice | bytes 147456 | tf_op jit(solution)/shard_map/rim/slice | solution.py:204
  4.1 3.4 %collective-permute-start = (bf16[16,2304]{1,0:T(8,128)(2,1)S(1)}, bf16[16,2304]{1,0:T(8,128)(2,1)S(1)}, u32[]{:S(2)}, u32[]{:S(2)}) collective-permute-start(bf16[16,2304]{1,0:T(8,128)(2,1)S(1)} %slice.27), channel_id=1, source_target_pairs={{0,32},{32,64},{64,96},{96,128},{128,160},{160,192},{192,224},{1,3... | collective-permute-start | bytes 221192 | tf_op jit(solution)/shard_map/rim/ppermute | solution.py:203
  8.1 0.0 copy-start
  8.1 1.5 %copy-done = bf16[2304,3,128]{2,0,1:T(8,128)(2,1)S(1)} copy-done((bf16[2304,3,128]{2,0,1:T(8,128)(2,1)S(1)}, bf16[2304,3,128]{2,0,1:T(8,128)(2,1)}, u32[]{:S(2)}) %copy-start) | copy-done | bytes 1769496
  9.6 0.0 copy-start.5
  9.6 1.7 %copy-done.5 = bf16[512,2304]{1,0:T(8,128)(2,1)S(1)} copy-done((bf16[512,2304]{1,0:T(8,128)(2,1)S(1)}, bf16[512,2304]{1,0:T(8,128)(2,1)}, u32[]{:S(2)}) %copy-start.5) | copy-done | bytes 2359320
  11.3 0.0 copy-start.7
  11.3 1.1 %copy-done.7 = bf16[2304,128]{1,0:T(8,128)(2,1)S(1)} copy-done((bf16[2304,128]{1,0:T(8,128)(2,1)S(1)}, bf16[2304,128]{1,0:T(8,128)(2,1)}, u32[]{:S(2)}) %copy-start.7) | copy-done | bytes 589848
  12.3 0.0 copy-start.8
  12.3 1.1 %copy-done.8 = bf16[2304,128]{1,0:T(8,128)(2,1)S(1)} copy-done((bf16[2304,128]{1,0:T(8,128)(2,1)S(1)}, bf16[2304,128]{1,0:T(8,128)(2,1)}, u32[]{:S(2)}) %copy-start.8) | copy-done | bytes 589848
  13.4 0.0 copy-start.9
  13.4 0.8 copy-done.9
  14.2 0.0 copy-start.10
  14.2 0.8 copy-done.10
  14.9 0.0 copy-start.11
  14.9 0.7 copy-done.11
  15.6 0.0 copy-start.13
  15.6 0.7 copy-done.13
  16.3 5.2 %project.1 = (bf16[512,384]{1,0:T(8,128)(2,1)S(1)}, f32[512,128]{1,0:T(8,128)S(1)}, f32[512,128]{1,0:T(8,128)S(1)}, f32[512,128]{1,0:T(8,128)S(1)}) custom-call(f32[1]{0:T(128)S(6)} %copy.18.alog, bf16[512,2304]{1,0:T(8,128)(2,1)S(1)} %copy-done.5, bf16[3,2304,128]{2,1,0:T(8,128)(2,1)S(1)} %bitcast.37, bf16[2304,128]{1,0:T(8,128)(2,1)S(1)} %copy-done.7, ...), custom_call_target="tpu_custom_call" | custom-call | flops 1811939328 | bytes 6000000 | tf_op jit(solution)/shard_map/project/pallas_call | solution.py:213
  21.5 0.0 copy-start.3
  21.5 0.0 copy-start.12
  21.5 0.0 collective-permute-done
  21.5 0.3 fusion
  21.9 0.0 collective-permute-done.5.w2
  21.9 0.3 collective-permute-start.6
  22.2 0.0 copy-done.12
  22.2 0.0 copy-start.6
  22.2 4.6 %delta.1 = (f32[512,256]{1,0:T(8,128)S(1)}, bf16[8,128,256]{2,1,0:T(8,128)(2,1)S(1)}) custom-call(bf16[512,384]{1,0:T(8,128)(2,1)S(1)} %get-tuple-element.15.raw, bf16[16,384]{1,0:T(8,128)(2,1)S(1)} %bitcast.38, f32[3,4,128]{2,1,0:T(4,128)S(1)} %bitcast.41, f32[512,128]{1,0:T(8,128)S(1)} %get-tuple-element.16.cum_ref, f32[512,128]{1,0:T(8,128)S(1)} %get-tuple-element.17.beta_ref), custom_call_target="tpu_custom_call" | custom-call | flops 4000000000 | bytes 30000000 | tf_op jit(solution)/shard_map/delta/pallas_call | solution.py:254
  26.9 0.0 copy-done.3
  26.9 0.0 copy-start.2
  26.9 0.8 %copy-done.2 = bf16[8,128,256]{2,1,0:T(8,128)(2,1)} copy-done((bf16[8,128,256]{2,1,0:T(8,128)(2,1)}, bf16[8,128,256]{2,1,0:T(8,128)(2,1)S(1)}, u32[]{:S(2)}) %copy-start.2) | copy-done | bytes 524312
  27.7 4.8 %all-to-all-start = ((bf16[8,128,256]{2,1,0:T(8,128)(2,1)}), bf16[8,128,256]{2,1,0:T(8,128)(2,1)S(1)}, u32[]{:S(2)}, u32[]{:S(2)}) async-start(bf16[8,128,256]{2,1,0:T(8,128)(2,1)} %copy-done.2), calls=%async_computation | async-start | bytes 1048576 | tf_op jit(solution)/shard_map/states/all_to_all | solution.py:266
  32.4 0.1 pad_add_fusion.place
  32.5 9.3 %all-to-all-done.states = bf16[8,128,256]{2,1,0:T(8,128)(2,1)S(1)} async-done(((bf16[8,128,256]{2,1,0:T(8,128)(2,1)}), bf16[8,128,256]{2,1,0:T(8,128)(2,1)S(1)}, u32[]{:S(2)}, u32[]{:S(2)}) %all-to-all-start) | async-done | bytes 524320 | tf_op jit(solution)/shard_map/states/all_to_all | solution.py:266
  41.8 0.0 copy-done.6
  41.8 0.9 %copy-done.4 = f32[512,128]{1,0:T(8,128)S(1)} copy-done((f32[512,128]{1,0:T(8,128)S(1)}, f32[512,128]{1,0:T(8,128)}, u32[]{:S(2)}) %copy-start.4) | copy-done | bytes 262168
  42.7 1.8 %finish.1 = (bf16[8,16,128]{2,1,0:T(8,128)(2,1)S(1)}, bf16[8,16,128]{2,1,0:T(8,128)(2,1)S(1)}, bf16[8,16,128]{2,1,0:T(8,128)(2,1)S(1)}, bf16[8,16,128]{2,1,0:T(8,128)(2,1)S(1)}) custom-call(s32[3]{0:T(128)S(1)} %pad_add_fusion.place, f32[512,256]{1,0:T(8,128)S(1)} %get-tuple-element.18.c_ref, f32[512,128]{1,0:T(8,128)S(1)} %copy-done.4, ...), custom_call_target="tpu_custom_call" | custom-call | tf_op jit(solution)/shard_map/finish/pallas_call | solution.py:269
  44.5 0.1 collective-permute-start.1
  44.6 1.9 %collective-permute-start.2 = (bf16[8,16,128]{2,1,0:T(8,128)(2,1)S(1)}, bf16[8,16,128]{2,1,0:T(8,128)(2,1)S(1)}, u32[]{:S(2)}, u32[]{:S(2)}) collective-permute-start(bf16[8,16,128]{2,1,0:T(8,128)(2,1)S(1)} %get-tuple-element.23), channel_id=1, source_target_pairs={{0,2},{1,3},{2,0},{3,1},{4,6},{5,7},{6,4},{7,5},{8,10},{9,11},{10,... | collective-permute-start | bytes 98312 | tf_op jit(solution)/shard_map/exchange/ppermute | solution.py:200
  46.6 1.4 %collective-permute-start.3 = (bf16[8,16,128]{2,1,0:T(8,128)(2,1)S(1)}, bf16[8,16,128]{2,1,0:T(8,128)(2,1)S(1)}, u32[]{:S(2)}, u32[]{:S(2)}) collective-permute-start(bf16[8,16,128]{2,1,0:T(8,128)(2,1)S(1)} %get-tuple-element.24), channel_id=1, source_target_pairs={{0,3},{1,2},{2,1},{3,0},{4,7},{5,6},{6,5},{7,4},{8,11},{9,10},{10,... | collective-permute-start | bytes 98312 | tf_op jit(solution)/shard_map/exchange/ppermute | solution.py:200
  48.0 0.0 collective-permute-done.1.g1
  48.0 2.1 %collective-permute-done.2.g2 = bf16[8,16,128]{2,1,0:T(8,128)(2,1)S(1)} collective-permute-done((bf16[8,16,128]{2,1,0:T(8,128)(2,1)S(1)}, bf16[8,16,128]{2,1,0:T(8,128)(2,1)S(1)}, u32[]{:S(2)}, u32[]{:S(2)}) %collective-permute-start.2) | collective-permute-done | bytes 32800 | tf_op jit(solution)/shard_map/exchange/ppermute | solution.py:200
  50.1 1.3 %collective-permute-done.3.g3 = bf16[8,16,128]{2,1,0:T(8,128)(2,1)S(1)} collective-permute-done((bf16[8,16,128]{2,1,0:T(8,128)(2,1)S(1)}, bf16[8,16,128]{2,1,0:T(8,128)(2,1)S(1)}, u32[]{:S(2)}, u32[]{:S(2)}) %collective-permute-start.3) | collective-permute-done | bytes 32800 | tf_op jit(solution)/shard_map/exchange/ppermute | solution.py:200
  51.4 0.0 collective-permute-done.4.w1
  51.4 0.0 collective-permute-done.6.w3
  51.4 0.0 copy-done.1
  51.4 1.3 %spread.1 = bf16[8,16,2304]{2,1,0:T(8,128)(2,1)S(1)} custom-call(s32[3]{0:T(128)S(1)} %pad_add_fusion.place, bf16[8,16,128]{2,1,0:T(8,128)(2,1)S(1)} %get-tuple-element.21.g0, bf16[8,16,128]{2,1,0:T(8,128)(2,1)S(1)} %collective-permute-done.1.g1, bf16[8,16,128]{2,1,0:T(8,128)(2,1)S(1)} %collective-permute-done.2.g2, ...), custom_call_target="tpu_custom_call" | custom-call | tf_op jit(solution)/shard_map/spread/pallas_call | solution.py:280
  52.8 3.3 %collective-permute-start.10 = (bf16[16,2304]{1,0:T(8,128)(2,1)S(1)}, bf16[16,2304]{1,0:T(8,128)(2,1)S(1)}, u32[]{:S(2)}, u32[]{:S(2)}) collective-permute-start(bf16[16,2304]{1,0:T(8,128)(2,1)S(1)} %get-tuple-element.29), channel_id=1, source_target_pairs={{0,8},{1,9},{2,10},{3,11},{4,12},{5,13},{6,14},{7,15},{8,16},{9,17... | collective-permute-start | bytes 221192 | tf_op jit(solution)/shard_map/reduce/ppermute | solution.py:294
  56.1 3.3 %collective-permute-start.11 = (bf16[16,2304]{1,0:T(8,128)(2,1)S(1)}, bf16[16,2304]{1,0:T(8,128)(2,1)S(1)}, u32[]{:S(2)}, u32[]{:S(2)}) collective-permute-start(bf16[16,2304]{1,0:T(8,128)(2,1)S(1)} %get-tuple-element.28), channel_id=1, source_target_pairs={{0,24},{1,25},{2,26},{3,27},{4,28},{5,29},{6,30},{7,31},{8,0},{9,1... | collective-permute-start | bytes 221192 | tf_op jit(solution)/shard_map/reduce/ppermute | solution.py:294
  59.4 1.0 %collective-permute-start.12 = (bf16[16,2304]{1,0:T(8,128)(2,1)S(1)}, bf16[16,2304]{1,0:T(8,128)(2,1)S(1)}, u32[]{:S(2)}, u32[]{:S(2)}) collective-permute-start(bf16[16,2304]{1,0:T(8,128)(2,1)S(1)} %get-tuple-element.27), channel_id=1, source_target_pairs={{0,4},{1,5},{2,6},{3,7},{4,8},{5,9},{6,10},{7,11},{8,12},{9,13},{1... | collective-permute-start | bytes 221192 | tf_op jit(solution)/shard_map/reduce/ppermute | solution.py:294
  60.5 2.2 %collective-permute-start.13 = (bf16[16,2304]{1,0:T(8,128)(2,1)S(1)}, bf16[16,2304]{1,0:T(8,128)(2,1)S(1)}, u32[]{:S(2)}, u32[]{:S(2)}) collective-permute-start(bf16[16,2304]{1,0:T(8,128)(2,1)S(1)} %get-tuple-element.26), channel_id=1, source_target_pairs={{0,28},{1,29},{2,30},{3,31},{4,0},{5,1},{6,2},{7,3},{8,4},{9,5},{1... | collective-permute-start | bytes 221192 | tf_op jit(solution)/shard_map/reduce/ppermute | solution.py:294
  62.7 4.8 %collective-permute-start.7 = (bf16[16,2304]{1,0:T(8,128)(2,1)S(1)}, bf16[16,2304]{1,0:T(8,128)(2,1)S(1)}, u32[]{:S(2)}, u32[]{:S(2)}) collective-permute-start(bf16[16,2304]{1,0:T(8,128)(2,1)S(1)} %get-tuple-element.25), channel_id=1, source_target_pairs={{0,16},{1,17},{2,18},{3,19},{4,20},{5,21},{6,22},{7,23},{8,24},{9,... | collective-permute-start | bytes 221192 | tf_op jit(solution)/shard_map/reduce/ppermute | solution.py:294
  67.4 0.0 collective-permute-done.10
  67.4 0.0 collective-permute-start.8
  67.4 0.0 collective-permute-done.11
  67.4 5.0 %collective-permute-start.9 = (bf16[16,2304]{1,0:T(8,128)(2,1)S(1)}, bf16[16,2304]{1,0:T(8,128)(2,1)S(1)}, u32[]{:S(2)}, u32[]{:S(2)}) collective-permute-start(bf16[16,2304]{1,0:T(8,128)(2,1)S(1)} %get-tuple-element.30), channel_id=1, source_target_pairs={{0,20},{1,21},{2,22},{3,23},{4,24},{5,25},{6,26},{7,27},{8,28},{9,... | collective-permute-start | bytes 221192 | tf_op jit(solution)/shard_map/reduce/ppermute | solution.py:294
  72.5 0.0 collective-permute-done.12
  72.5 0.0 collective-permute-done.13
  72.5 3.3 %collective-permute-done.7 = bf16[16,2304]{1,0:T(8,128)(2,1)S(1)} collective-permute-done((bf16[16,2304]{1,0:T(8,128)(2,1)S(1)}, bf16[16,2304]{1,0:T(8,128)(2,1)S(1)}, u32[]{:S(2)}, u32[]{:S(2)}) %collective-permute-start.7) | collective-permute-done | bytes 73760 | tf_op jit(solution)/shard_map/reduce/ppermute | solution.py:294
  75.8 1.4 %collective-permute-done.8 = bf16[16,2304]{1,0:T(8,128)(2,1)S(1)} collective-permute-done((bf16[16,2304]{1,0:T(8,128)(2,1)S(1)}, bf16[16,2304]{1,0:T(8,128)(2,1)S(1)}, u32[]{:S(2)}, u32[]{:S(2)}) %collective-permute-start.8) | collective-permute-done | bytes 73760 | tf_op jit(solution)/shard_map/reduce/ppermute | solution.py:294
  77.2 0.0 collective-permute-done.9
  77.2 0.7 fusion.7
  (4 shorter events, 0.0 us)
Async XLA Ops:
  0.0 21.9 %collective-permute-start.5 = (bf16[128,2304]{1,0:T(8,128)(2,1)}, bf16[128,2304]{1,0:T(8,128)(2,1)S(1)}, u32[]{:S(2)}, u32[]{:S(2)}) collective-permute-start(bf16[128,2304]{1,0:T(8,128)(2,1)} %w0.1), channel_id=1, source_target_pairs={{0,2},{1,3},{2,0},{3,1},{4,6},{5,7},{6,4},{7,5},{8,10},{9,11},{10,... | collective-permute-start | bytes 1769480 | tf_op jit(solution)/shard_map/weights/ppermute | solution.py:200
  3.2 48.2 %collective-permute-start.4 = (bf16[128,2304]{1,0:T(8,128)(2,1)}, bf16[128,2304]{1,0:T(8,128)(2,1)S(1)}, u32[]{:S(2)}, u32[]{:S(2)}) collective-permute-start(bf16[128,2304]{1,0:T(8,128)(2,1)} %w0.1), channel_id=1, source_target_pairs={{0,1},{1,0},{2,3},{3,2},{4,5},{5,4},{6,7},{7,6},{8,9},{9,8},{10,11... | collective-permute-start | bytes 1769480 | tf_op jit(solution)/shard_map/weights/ppermute | solution.py:200
  4.1 17.4 %collective-permute-start = (bf16[16,2304]{1,0:T(8,128)(2,1)S(1)}, bf16[16,2304]{1,0:T(8,128)(2,1)S(1)}, u32[]{:S(2)}, u32[]{:S(2)}) collective-permute-start(bf16[16,2304]{1,0:T(8,128)(2,1)S(1)} %slice.27), channel_id=1, source_target_pairs={{0,32},{32,64},{64,96},{96,128},{128,160},{160,192},{192,224},{1,3... | collective-permute-start | bytes 221192 | tf_op jit(solution)/shard_map/rim/ppermute | solution.py:203
  8.1 1.5 %copy-start = (bf16[2304,3,128]{2,0,1:T(8,128)(2,1)S(1)}, bf16[2304,3,128]{2,0,1:T(8,128)(2,1)}, u32[]{:S(2)}) copy-start(bf16[2304,3,128]{2,0,1:T(8,128)(2,1)} %param.13) | copy-start | bytes 5308420
  9.6 1.7 %copy-start.5 = (bf16[512,2304]{1,0:T(8,128)(2,1)S(1)}, bf16[512,2304]{1,0:T(8,128)(2,1)}, u32[]{:S(2)}) copy-start(bf16[512,2304]{1,0:T(8,128)(2,1)} %tokens.1) | copy-start | bytes 7077892
  11.3 1.1 %copy-start.7 = (bf16[2304,128]{1,0:T(8,128)(2,1)S(1)}, bf16[2304,128]{1,0:T(8,128)(2,1)}, u32[]{:S(2)}) copy-start(bf16[2304,128]{1,0:T(8,128)(2,1)} %f_down.1) | copy-start | bytes 1769476
  12.3 1.1 %copy-start.8 = (bf16[2304,128]{1,0:T(8,128)(2,1)S(1)}, bf16[2304,128]{1,0:T(8,128)(2,1)}, u32[]{:S(2)}) copy-start(bf16[2304,128]{1,0:T(8,128)(2,1)} %o_down.1) | copy-start | bytes 1769476
  13.4 0.8 copy-start.9
  14.2 0.8 copy-start.10
  14.9 0.7 copy-start.11
  15.6 0.7 copy-start.13
  21.5 5.3 %copy-start.3 = (f32[512,128]{1,0:T(8,128)}, f32[512,128]{1,0:T(8,128)S(1)}, u32[]{:S(2)}) copy-start(f32[512,128]{1,0:T(8,128)S(1)} %get-tuple-element.19.gate) | copy-start | bytes 786436
  21.5 0.7 copy-start.12
  21.9 29.5 %collective-permute-start.6 = (bf16[128,2304]{1,0:T(8,128)(2,1)S(1)}, bf16[128,2304]{1,0:T(8,128)(2,1)S(1)}, u32[]{:S(2)}, u32[]{:S(2)}) collective-permute-start(bf16[128,2304]{1,0:T(8,128)(2,1)S(1)} %collective-permute-done.5.w2), channel_id=1, source_target_pairs={{0,1},{1,0},{2,3},{3,2},{4,5},{5,4},{6,7},{7,6},{8,9},{9,8},{10,11... | collective-permute-start | bytes 1769480 | tf_op jit(solution)/shard_map/weights/ppermute | solution.py:200
  22.2 19.6 %copy-start.6 = (f32[128]{0:T(128)S(1)}, f32[128]{0:T(128)}, u32[]{:S(2)}) copy-start(f32[128]{0:T(128)} %param.22) | copy-start | bytes 1540
  26.9 0.8 %copy-start.2 = (bf16[8,128,256]{2,1,0:T(8,128)(2,1)}, bf16[8,128,256]{2,1,0:T(8,128)(2,1)S(1)}, u32[]{:S(2)}) copy-start(bf16[8,128,256]{2,1,0:T(8,128)(2,1)S(1)} %get-tuple-element.20) | copy-start | bytes 1572868
  27.7 23.8 %copy-start.1 = (bf16[128,2304]{1,0:T(8,128)(2,1)S(1)}, bf16[128,2304]{1,0:T(8,128)(2,1)}, u32[]{:S(2)}) copy-start(bf16[128,2304]{1,0:T(8,128)(2,1)} %w0.1) | copy-start | bytes 1769476
  27.7 14.1 %all-to-all-start = ((bf16[8,128,256]{2,1,0:T(8,128)(2,1)}), bf16[8,128,256]{2,1,0:T(8,128)(2,1)S(1)}, u32[]{:S(2)}, u32[]{:S(2)}) async-start(bf16[8,128,256]{2,1,0:T(8,128)(2,1)} %copy-done.2), calls=%async_computation | async-start | bytes 1048576 | tf_op jit(solution)/shard_map/states/all_to_all | solution.py:266
  41.8 1.0 %copy-start.4 = (f32[512,128]{1,0:T(8,128)S(1)}, f32[512,128]{1,0:T(8,128)}, u32[]{:S(2)}) copy-start(f32[512,128]{1,0:T(8,128)} %copy-done.3) | copy-start | bytes 786436
  44.5 3.5 %collective-permute-start.1 = (bf16[8,16,128]{2,1,0:T(8,128)(2,1)S(1)}, bf16[8,16,128]{2,1,0:T(8,128)(2,1)S(1)}, u32[]{:S(2)}, u32[]{:S(2)}) collective-permute-start(bf16[8,16,128]{2,1,0:T(8,128)(2,1)S(1)} %get-tuple-element.22), channel_id=1, source_target_pairs={{0,1},{1,0},{2,3},{3,2},{4,5},{5,4},{6,7},{7,6},{8,9},{9,8},{10,11... | collective-permute-start | bytes 98312 | tf_op jit(solution)/shard_map/exchange/ppermute | solution.py:200
  44.6 5.5 %collective-permute-start.2 = (bf16[8,16,128]{2,1,0:T(8,128)(2,1)S(1)}, bf16[8,16,128]{2,1,0:T(8,128)(2,1)S(1)}, u32[]{:S(2)}, u32[]{:S(2)}) collective-permute-start(bf16[8,16,128]{2,1,0:T(8,128)(2,1)S(1)} %get-tuple-element.23), channel_id=1, source_target_pairs={{0,2},{1,3},{2,0},{3,1},{4,6},{5,7},{6,4},{7,5},{8,10},{9,11},{10,... | collective-permute-start | bytes 98312 | tf_op jit(solution)/shard_map/exchange/ppermute | solution.py:200
  46.6 4.9 %collective-permute-start.3 = (bf16[8,16,128]{2,1,0:T(8,128)(2,1)S(1)}, bf16[8,16,128]{2,1,0:T(8,128)(2,1)S(1)}, u32[]{:S(2)}, u32[]{:S(2)}) collective-permute-start(bf16[8,16,128]{2,1,0:T(8,128)(2,1)S(1)} %get-tuple-element.24), channel_id=1, source_target_pairs={{0,3},{1,2},{2,1},{3,0},{4,7},{5,6},{6,5},{7,4},{8,11},{9,10},{10,... | collective-permute-start | bytes 98312 | tf_op jit(solution)/shard_map/exchange/ppermute | solution.py:200
  52.8 14.6 %collective-permute-start.10 = (bf16[16,2304]{1,0:T(8,128)(2,1)S(1)}, bf16[16,2304]{1,0:T(8,128)(2,1)S(1)}, u32[]{:S(2)}, u32[]{:S(2)}) collective-permute-start(bf16[16,2304]{1,0:T(8,128)(2,1)S(1)} %get-tuple-element.29), channel_id=1, source_target_pairs={{0,8},{1,9},{2,10},{3,11},{4,12},{5,13},{6,14},{7,15},{8,16},{9,17... | collective-permute-start | bytes 221192 | tf_op jit(solution)/shard_map/reduce/ppermute | solution.py:294
  56.1 11.3 %collective-permute-start.11 = (bf16[16,2304]{1,0:T(8,128)(2,1)S(1)}, bf16[16,2304]{1,0:T(8,128)(2,1)S(1)}, u32[]{:S(2)}, u32[]{:S(2)}) collective-permute-start(bf16[16,2304]{1,0:T(8,128)(2,1)S(1)} %get-tuple-element.28), channel_id=1, source_target_pairs={{0,24},{1,25},{2,26},{3,27},{4,28},{5,29},{6,30},{7,31},{8,0},{9,1... | collective-permute-start | bytes 221192 | tf_op jit(solution)/shard_map/reduce/ppermute | solution.py:294
  59.4 13.0 %collective-permute-start.12 = (bf16[16,2304]{1,0:T(8,128)(2,1)S(1)}, bf16[16,2304]{1,0:T(8,128)(2,1)S(1)}, u32[]{:S(2)}, u32[]{:S(2)}) collective-permute-start(bf16[16,2304]{1,0:T(8,128)(2,1)S(1)} %get-tuple-element.27), channel_id=1, source_target_pairs={{0,4},{1,5},{2,6},{3,7},{4,8},{5,9},{6,10},{7,11},{8,12},{9,13},{1... | collective-permute-start | bytes 221192 | tf_op jit(solution)/shard_map/reduce/ppermute | solution.py:294
  60.5 12.0 %collective-permute-start.13 = (bf16[16,2304]{1,0:T(8,128)(2,1)S(1)}, bf16[16,2304]{1,0:T(8,128)(2,1)S(1)}, u32[]{:S(2)}, u32[]{:S(2)}) collective-permute-start(bf16[16,2304]{1,0:T(8,128)(2,1)S(1)} %get-tuple-element.26), channel_id=1, source_target_pairs={{0,28},{1,29},{2,30},{3,31},{4,0},{5,1},{6,2},{7,3},{8,4},{9,5},{1... | collective-permute-start | bytes 221192 | tf_op jit(solution)/shard_map/reduce/ppermute | solution.py:294
  62.7 13.1 %collective-permute-start.7 = (bf16[16,2304]{1,0:T(8,128)(2,1)S(1)}, bf16[16,2304]{1,0:T(8,128)(2,1)S(1)}, u32[]{:S(2)}, u32[]{:S(2)}) collective-permute-start(bf16[16,2304]{1,0:T(8,128)(2,1)S(1)} %get-tuple-element.25), channel_id=1, source_target_pairs={{0,16},{1,17},{2,18},{3,19},{4,20},{5,21},{6,22},{7,23},{8,24},{9,... | collective-permute-start | bytes 221192 | tf_op jit(solution)/shard_map/reduce/ppermute | solution.py:294
  67.4 9.8 %collective-permute-start.8 = (bf16[16,2304]{1,0:T(8,128)(2,1)S(1)}, bf16[16,2304]{1,0:T(8,128)(2,1)S(1)}, u32[]{:S(2)}, u32[]{:S(2)}) collective-permute-start(bf16[16,2304]{1,0:T(8,128)(2,1)S(1)} %get-tuple-element.31), channel_id=1, source_target_pairs={{0,12},{1,13},{2,14},{3,15},{4,16},{5,17},{6,18},{7,19},{8,20},{9,... | collective-permute-start | bytes 221192 | tf_op jit(solution)/shard_map/reduce/ppermute | solution.py:294
  67.4 9.8 %collective-permute-start.9 = (bf16[16,2304]{1,0:T(8,128)(2,1)S(1)}, bf16[16,2304]{1,0:T(8,128)(2,1)S(1)}, u32[]{:S(2)}, u32[]{:S(2)}) collective-permute-start(bf16[16,2304]{1,0:T(8,128)(2,1)S(1)} %get-tuple-element.30), channel_id=1, source_target_pairs={{0,20},{1,21},{2,22},{3,23},{4,24},{5,25},{6,26},{7,27},{8,28},{9,... | collective-permute-start | bytes 221192 | tf_op jit(solution)/shard_map/reduce/ppermute | solution.py:294

commit v2 on v0

v2 whole, which is shorter than its diff:
```python
import functools

import jax
import jax.numpy as jnp
from jax import lax
from jax.experimental import pallas as pl
from jax.experimental.pallas import tpu as pltpu
from jax.sharding import PartitionSpec as P

BLOCK = 64
GROUP = 128
SPAN = 256
SUBS = 8
CHUNKS = 3
F32 = jnp.float32
BF16 = jnp.bfloat16
HIGHEST = lax.Precision.HIGHEST
VMEM = pl.BlockSpec(memory_space=pltpu.VMEM)
HBM = pl.BlockSpec(memory_space=pltpu.HBM)
SMEM = pl.BlockSpec(memory_space=pltpu.SMEM)
FULL = pltpu.CompilerParams(vmem_limit_bytes=62 * 1024 * 1024)
LIMIT = pltpu.CompilerParams(vmem_limit_bytes=16 * 1024 * 1024)


def cost(us):
    return pl.CostEstimate(flops=0, bytes_accessed=int(us * 3_690_000), transcendentals=0)


def mm(left, right):
    return jnp.dot(left.astype(BF16), right.astype(BF16), preferred_element_type=F32)


def mm_nt(left, right):
    return lax.dot_general(
        left.astype(BF16), right.astype(BF16), (((1,), (1,)), ((), ())), preferred_element_type=F32
    )


def mm_tn(left, right):
    return lax.dot_general(
        left.astype(BF16), right.astype(BF16), (((0,), (0,)), ((), ())), preferred_element_type=F32
    )


def split(value):
    high = value.astype(BF16)
    return high, (value - high.astype(F32)).astype(BF16)


def mm3(left, right):
    lh, ll = split(left)
    rh, rl = split(right)
    dot = functools.partial(jnp.dot, preferred_element_type=F32)
    return dot(lh, rh) + (dot(lh, rl) + dot(ll, rh))


def masks(size):
    row = lax.broadcasted_iota(jnp.int32, (size, size), 0)
    col = lax.broadcasted_iota(jnp.int32, (size, size), 1)
    return row, col, row ^ col


def load(pairs, sems):
    copies = []
    for place, (source, target) in enumerate(pairs):
        copies.append(pltpu.make_async_copy(source, target, sems.at[place]))
        copies[-1].start()
    return copies


def convolve(total, taps, padded, rows, part):
    head = taps.shape[2]
    conv_taps = taps.shape[1]
    lanes = slice(part * head, (part + 1) * head)
    edge = total[rows:, lanes].astype(BF16).astype(F32)[total.shape[0] - rows - 8 :]
    padded[0:8, lanes] = jnp.where(lax.axis_index("ctx") > 0, edge, 0.0)
    padded[8:, lanes] = total[:rows, lanes].astype(BF16).astype(F32)
    mixed = padded[9 - conv_taps : 9 - conv_taps + rows, lanes] * taps[part, 0:1, :]
    for tap in range(1, conv_taps):
        start = 9 - conv_taps + tap
        mixed = mixed + padded[start : start + rows, lanes] * taps[part, tap : tap + 1, :]
    return jax.nn.silu(mixed)


def unit_rows(value):
    return value * lax.rsqrt(jnp.sum(value * value, axis=-1, keepdims=True) + 1e-06)


def front(
    alog, tokens_hbm, rim_hbm, w3_hbm, f_down_hbm, o_down_hbm, f_up_hbm, o_up_hbm, bias_hbm,
    w_beta_hbm, taps_hbm, plain_out, carry_out, half_out, gate_out, sends, tok, w3, f_down, o_down,
    wide, f_up, o_up, bias, w_beta, taps, total, padded, final, sems, out_sems,
):
    rows, model = tokens_hbm.shape
    head = f_up.shape[0]
    count = rows // BLOCK
    inside = SPAN // BLOCK
    chunk = model // CHUNKS
    pairs = [(w_beta_hbm, w_beta), (rim_hbm, tok.at[pl.ds(rows, rim_hbm.shape[0])])]
    for step in range(CHUNKS):
        rng = pl.ds(step * chunk, chunk)
        pairs.append((tokens_hbm.at[:, rng], tok.at[pl.ds(0, rows), rng]))
        pairs += [(w3_hbm.at[part, rng], w3.at[part, rng]) for part in range(3)]
        pairs.append((f_down_hbm.at[rng], f_down.at[rng]))
        pairs.append((o_down_hbm.at[rng], o_down.at[rng]))
    pairs += [(f_up_hbm, f_up), (o_up_hbm, o_up), (bias_hbm, bias), (taps_hbm, taps)]
    copies = load(pairs, sems)
    wide[...] = jnp.zeros_like(wide)
    copies[0].wait()
    column = jnp.transpose(jnp.broadcast_to(w_beta[...].astype(F32), (8, model)))
    wide[:, 0:8] = column.astype(BF16)
    copies[1].wait()
    for step in range(CHUNKS):
        for copy in copies[2 + 6 * step : 8 + 6 * step]:
            copy.wait()
        rng = slice(step * chunk, (step + 1) * chunk)
        joined = [w3[part, rng] for part in range(3)] + [f_down[rng], o_down[rng], wide[rng]]
        piece = jnp.dot(tok[:, rng], jnp.concatenate(joined, axis=1), preferred_element_type=F32)
        if step == 0:
            total[...] = piece
        else:
            total[...] += piece
    for copy in copies[2 + 6 * CHUNKS :]:
        copy.wait()
    low = total[:rows, 3 * head : 4 * head].astype(BF16)
    logit = jnp.dot(low, f_up[...], preferred_element_type=F32) + bias[...]
    decays = -jnp.exp(jnp.full((1, 1), alog[0], F32)) * jax.nn.softplus(logit)
    out_low = total[:rows, 4 * head : 5 * head].astype(BF16)
    gate_out[...] = jax.nn.sigmoid(jnp.dot(out_low, o_up[...], preferred_element_type=F32))
    beta = jnp.broadcast_to(jax.nn.sigmoid(total[:rows, 5 * head : 5 * head + 1]), (rows, head))
    row, col, differ = masks(GROUP)
    strict = (row > col) & (differ < BLOCK)
    causal = (row >= col) & (differ < BLOCK)
    unit = jnp.where(row == col, 1.0, 0.0).astype(F32)
    tri = jnp.where(causal, 1.0, 0.0).astype(BF16)
    high, rest = split(decays)
    middle, least = split(decays - high.astype(F32) - rest.astype(F32))
    terms = jnp.concatenate([high, rest, middle], axis=1)
    sums = [
        jnp.dot(tri, terms[s : s + GROUP], preferred_element_type=F32) for s in range(0, rows, GROUP)
    ]
    sums = jnp.concatenate(sums, axis=0)
    cumulative = sums[:, :head] + (sums[:, head : 2 * head] + sums[:, 2 * head :])
    key_raw = convolve(total, taps, padded, rows, 1)
    value_raw = convolve(total, taps, padded, rows, 2)
    query_raw = convolve(total, taps, padded, rows, 0)
    keyset = unit_rows(key_raw).astype(BF16).astype(F32)
    values = value_raw.astype(BF16).astype(F32)
    rising = jnp.exp(cumulative)
    key_rise = keyset * rising
    key_fall = (keyset * jnp.exp(-cumulative)).astype(BF16)
    blocked = cumulative.reshape(count, BLOCK, head)
    ends = blocked[:, BLOCK - 1 : BLOCK, :]
    tail = (keyset.reshape(count, BLOCK, head) * jnp.exp(ends - blocked)).reshape(rows, head)
    tail = tail.astype(BF16)
    shrink = jnp.transpose(jnp.exp(ends.reshape(count, head)))
    target = jnp.concatenate([beta * values, beta * key_rise], axis=1).astype(BF16)
    systems, inverse = [], []
    for start in range(0, rows, GROUP):
        rng = slice(start, start + GROUP)
        inner = mm_nt(key_rise[rng], key_fall[rng])
        systems.append(jnp.where(strict, inner * beta[rng], 0.0))
        inverse.append(unit - jnp.where(differ == 1, systems[-1], 0.0))
    size = 2
    while size < BLOCK:
        here = (differ >= size) & (differ < 2 * size)
        steps = [mm(jnp.where(here, s, 0.0), d) for s, d in zip(systems, inverse)]
        inverse = [d - mm(d, x) for d, x in zip(inverse, steps)]
        size *= 2
    pairs, solves, starts = [], [], {}
    for group, start in enumerate(range(0, rows, GROUP)):
        solved = mm(inverse[group], target[start : start + GROUP]).astype(BF16)
        solves.append(solved)
        for block in range(GROUP // BLOCK):
            sub = slice(block * BLOCK, (block + 1) * BLOCK)
            pairs.append(mm_tn(tail[start + block * BLOCK :][:BLOCK], solved[sub]))
    fresh = jnp.concatenate([jnp.zeros((head, head), F32), unit], axis=1)
    states = [fresh] * (rows // SPAN)
    for block in range(inside):
        for group in range(rows // SPAN):
            at = group * inside + block
            state = states[group]
            short = state.astype(BF16)
            starts[at] = short
            step = mm(pairs[at][:, head:], short)
            state = shrink[:, at : at + 1] * state - step
            states[group] = jnp.concatenate(
                [state[:, :head] + pairs[at][:, :head], state[:, head:]], axis=1
            )
    half_out[...] = states[0].astype(BF16)
    whole = mm(states[1][:, head:], states[0])
    final[...] = jnp.concatenate(
        [whole[:, :head] + states[1][:, :head], whole[:, head:]], axis=1
    ).astype(BF16)
    copies = load([(final, sends.at[i]) for i in range(sends.shape[0])], out_sems)
    queries = (unit_rows(query_raw) * (head ** (-0.5))).astype(BF16).astype(F32)
    query_rise = queries * rising
    for group, start in enumerate(range(0, rows, GROUP)):
        rng = slice(start, start + GROUP)
        scores = jnp.where(causal, mm_nt(query_rise[rng], key_fall[rng]), 0.0)
        local = mm(scores, solves[group])
        local_key = (query_rise[rng] - local[:, head:]).astype(BF16)
        for block in range(GROUP // BLOCK):
            sub = slice(block * BLOCK, (block + 1) * BLOCK)
            out = slice(start + block * BLOCK, start + (block + 1) * BLOCK)
            across = jnp.dot(
                local_key[sub], starts[(start // BLOCK) + block], preferred_element_type=F32
            )
            plain_out[out] = across[:, :head] + local[sub, :head]
            carry_out[out] = across[:, head:].astype(BF16)
    for copy in copies:
        copy.wait()


def stage(plain, carry, half, gate, gain, plain_out, carry_out, half_out, gate_out):
    plain_out[...] = plain[...]
    carry_out[...] = carry[...]
    half_out[...] = half[...]
    gate_out[...] = gate[...] * gain[...]


def finish(plain, carry, half, gate, states, own, other, gated):
    rows, head = gate.shape
    ctx = lax.axis_index("ctx")
    core_at = lax.rem(lax.axis_index("head"), 2)
    state = jnp.zeros((head, head), F32)
    for step in range(states.shape[0] - 1):
        moved = jnp.dot(states[step, :, head:], state.astype(BF16), preferred_element_type=F32)
        state = jnp.where(step < ctx, moved + states[step, :, :head].astype(F32), state)
    middle = jnp.dot(half[:, head:], state.astype(BF16), preferred_element_type=F32)
    middle = middle + half[:, :head].astype(F32)
    cores = []
    for group, start in enumerate((state, middle)):
        rng = slice(group * SPAN, (group + 1) * SPAN)
        cores.append(plain[rng] + mm(carry[rng], start))
    core = jnp.concatenate(cores, axis=0)
    scale = lax.rsqrt(jnp.mean(core * core, axis=-1, keepdims=True) + 1e-05)
    result = core * scale * gate[...]
    gated[...] = result.astype(BF16).reshape(gated.shape)
    for pair in range(own.shape[0]):
        own[pair] = gated[:, pair, pl.ds(core_at, 1)].reshape(own.shape[1:])
        other[pair] = gated[:, pair, pl.ds(1 - core_at, 1)].reshape(own.shape[1:])


def regroup(own, sibling, *outs):
    mine = lax.rem(lax.axis_index("head") // 2, own.shape[0])
    for flip, out in enumerate(outs):
        at = mine ^ flip
        out[0] = own[pl.ds(at, 1)].reshape(out.shape[1:])
        out[1] = sibling[pl.ds(at, 1)].reshape(out.shape[1:])


def spread(part, w_one, w_two, *refs):
    rest, held, out, left = refs[:-3], refs[-3], refs[-2], refs[-1]
    turn(part, left)
    joined = jnp.concatenate([w_one[...], w_two[...]], axis=0)
    out[...] = jnp.dot(left[...], joined, preferred_element_type=F32)
    head = w_one.shape[0]
    for at, ref in enumerate(rest):
        held[at * head : (at + 1) * head] = ref[...]


def turn(part, left):
    mine = lax.axis_index("head") // SUBS
    sides, zs, rows, head = part.shape
    for side in range(sides):
        for k in range(zs):
            piece = part[side, pl.ds(mine ^ k, 1)].reshape(rows, head)
            left[k * rows : (k + 1) * rows, side * head : (side + 1) * head] = piece


def combine(begun, *refs):
    parts, (held, w_one, w_two, out, left) = refs[:3], refs[3:]
    total = begun[...]
    depth = left.shape[-1]
    for which, part in enumerate(parts):
        turn(part, left.at[which])
        if which < 2:
            weight = held[which * depth : (which + 1) * depth]
        else:
            weight = jnp.concatenate([w_one[...], w_two[...]], axis=0)
        total = total + jnp.dot(left[which], weight, preferred_element_type=F32)
    out[...] = total.astype(BF16).reshape(out.shape)


def on_device(
    tokens, w_qkv, conv_weight, f_down, f_up, dt_bias, a_log, w_beta, o_down, o_up, norm_gain, w_out
):
    rows, model = tokens.shape
    head = f_up.shape[1]
    ctx_count, head_count = lax.axis_size("ctx"), lax.axis_size("head")
    zs = head_count // SUBS
    shape = jax.ShapeDtypeStruct
    dma = pltpu.SemaphoreType.DMA

    def flip(value, mask):
        return lax.ppermute(value, "head", [(h, h ^ mask) for h in range(head_count)])

    w3 = jnp.transpose(w_qkv, (1, 0, 2))
    taps = jnp.transpose(conv_weight, (1, 0, 2))
    edge = tokens[rows - 16 :]
    with jax.named_scope("rim"):
        rim = lax.ppermute(edge, "ctx", [(i, (i + 1) % ctx_count) for i in range(ctx_count)])
    (w_sent,) = after((w_out,), edge)
    with jax.named_scope("weights"):
        w_far, w_next, w_core = flip(w_sent, 2), flip(w_sent, 4), flip(w_sent, 1)
    with jax.named_scope("front"):
        plain, carry, half, gate, sends = pl.pallas_call(
            front,
            in_specs=[SMEM] + [HBM] * 10,
            out_specs=[VMEM] * 4 + [HBM],
            out_shape=[
                shape((rows, head), F32),
                shape((rows, head), BF16),
                shape((head, 2 * head), BF16),
                shape((rows, head), F32),
                shape((ctx_count, head, 2 * head), BF16),
            ],
            scratch_shapes=[
                pltpu.VMEM((rows + 16, model), BF16),
                pltpu.VMEM((3, model, head), BF16),
                pltpu.VMEM((model, head), BF16),
                pltpu.VMEM((model, head), BF16),
                pltpu.VMEM((model, head), BF16),
                pltpu.VMEM((head, head), BF16),
                pltpu.VMEM((head, head), BF16),
                pltpu.VMEM((1, head), F32),
                pltpu.VMEM((1, model), BF16),
                pltpu.VMEM(taps.shape, F32),
                pltpu.VMEM((rows + 16, 6 * head), F32),
                pltpu.VMEM((rows + 8, 3 * head), F32),
                pltpu.VMEM((head, 2 * head), BF16),
                dma((6 + 6 * CHUNKS,)),
                dma((ctx_count,)),
            ],
            compiler_params=FULL,
            cost_estimate=cost(9),
        )(
            a_log,
            tokens,
            rim,
            w3,
            f_down,
            o_down,
            f_up,
            o_up,
            dt_bias.reshape(1, head),
            w_beta.reshape(1, model),
            taps,
        )
    with jax.named_scope("states"):
        states = lax.all_to_all(sends, "ctx", 0, 0, tiled=True)
    w_late, w_near = after((w_far, w_next), half)
    with jax.named_scope("weights"):
        w_both = flip(w_late, 4)
        w_far_core, w_next_core = flip(w_late, 1), flip(w_near, 1)
    with jax.named_scope("stage"):
        kinds = [shape(v.shape, v.dtype) for v in (plain, carry, half, gate)]
        staged = pl.pallas_call(
            stage,
            in_specs=[VMEM] * 5,
            out_specs=[VMEM] * 4,
            out_shape=kinds,
            compiler_params=LIMIT,
            cost_estimate=cost(0.5),
        )(plain, carry, half, gate, norm_gain.reshape(1, head))
    with jax.named_scope("finish"):
        own, other = pl.pallas_call(
            finish,
            in_specs=[VMEM] * 5,
            out_specs=[VMEM] * 2,
            out_shape=[shape((SUBS // 2, zs, 16, head), BF16)] * 2,
            scratch_shapes=[pltpu.VMEM((zs, SUBS // 2, 2, 16, head), BF16)],
            compiler_params=LIMIT,
            cost_estimate=cost(1.8),
        )(*staged, states)
    with jax.named_scope("exchange"):
        sibling = flip(other, 1)
        kept, *sent = pl.pallas_call(
            regroup,
            in_specs=[VMEM] * 2,
            out_specs=[VMEM] * 4,
            out_shape=[shape((2, zs, 16, head), BF16)] * 4,
            compiler_params=LIMIT,
            cost_estimate=cost(0.5),
        )(own, sibling)
        got = {f: flip(sent[f - 1], 2 * f) for f in (3, 1, 2)}
    with jax.named_scope("spread"):
        held, begun = pl.pallas_call(
            spread,
            in_specs=[VMEM] * 7,
            out_specs=[VMEM] * 2,
            out_shape=[shape((4 * head, model), BF16), shape((zs * 16, model), F32)],
            scratch_shapes=[pltpu.VMEM((zs * 16, 2 * head), BF16)],
            compiler_params=LIMIT,
            cost_estimate=cost(2.5),
        )(kept, w_out, w_core, w_far, w_far_core, w_next, w_next_core)
        (w_late,) = after((w_both,), own)
        w_both_core = flip(w_late, 1)
        parts = pl.pallas_call(
            combine,
            in_specs=[VMEM] * 7,
            out_specs=VMEM,
            out_shape=shape((zs, 16, model), BF16),
            scratch_shapes=[pltpu.VMEM((3, zs * 16, 2 * head), BF16)],
            compiler_params=LIMIT,
            cost_estimate=cost(1.0),
        )(begun, got[1], got[2], got[3], held, w_both, w_both_core)
    with jax.named_scope("reduce"):
        total = parts[0].astype(F32)
        for part in [flip(parts[k], SUBS * k) for k in (2, 1, 3)]:
            total = total + part.astype(F32)
        return total.astype(BF16)


def after(values, token):
    return lax.optimization_barrier((*values, token))[: len(values)]


def solution(mesh):
    in_specs = (
        P("ctx", None),
        P(None, None, "head"),
        P(None, None, "head"),
        P(),
        P(None, "head"),
        P("head"),
        P("head"),
        P(None, "head"),
        P(),
        P(None, "head"),
        P(),
        P("head", None),
    )
    out_specs = P(("ctx", "head"), None)
    return jax.shard_map(
        on_device, mesh=mesh, in_specs=in_specs, out_specs=out_specs, check_vma=False
    )
```

time: 283 us -> 66.3 us (0.23)
  the two profiles are of different devices: /device:TPU:1 before, /device:TPU:32 now
where the time goes in v2:
time: 66.3 us; the launch traced here: 65.9 us
  starting transfers between devices  23.9 us (36%)
  waiting for transfers between devices  18.8 us (28%)
  Pallas kernels  14.4 us (22%)
  local copies, waits for them, and re-layouts  7.3 us (11%)
  between operations  0.78 us (1%)
  other arithmetic  0.68 us (1%)
    ppermute x14, starting transfers between devices, flip(): lax.ppermute(value, 'head', [(h, h ^ mask) for h in range(head_count)])  19 us
    ppermute x14, waiting for transfers between devices, flip(): lax.ppermute(value, 'head', [(h, h ^ mask) for h in range(head_count)])  11.3 us
    pallas_call x1, Pallas kernels, on_device(): pl.pallas_call(front, in_specs=[SMEM] + [HBM] * 10, out_specs=[VMEM] * 4...  10.5 us
    unnamed x18, local copies, waits for them, and re-layouts  6.4 us
    ppermute x1, waiting for transfers between devices, on_device(): lax.ppermute(edge, 'ctx', [(i, (i + 1) % ctx_count) for i in range(ctx_co...  4.42 us
    all_to_all x1, starting transfers between devices, on_device(): states = lax.all_to_all(sends, 'ctx', 0, 0, tiled=True)  3.49 us
    all_to_all x1, waiting for transfers between devices, on_device(): states = lax.all_to_all(sends, 'ctx', 0, 0, tiled=True)  3.03 us
    pallas_call x1, Pallas kernels, on_device(): pl.pallas_call(spread, in_specs=[VMEM] * 7, out_specs=[VMEM] * 2, out_sha...  1.73 us
  transfers between devices with their start and end apart: 16, of which 7 were waited for; matrix products, arithmetic and copies ran while one was open for 0% of the time, Pallas kernels for 21%

profile of v2, /device:TPU:32, one launch (start us, length us, event | category | flops | bytes accessed | tf_op | source)
XLA Modules:
  0.0 65.9 jit_solution(14763925344503606644)
XLA Ops:
  0.0 0.9 %slice.15 = bf16[16,2304]{1,0:T(8,128)(2,1)S(1)} slice(bf16[512,2304]{1,0:T(8,128)(2,1)} %tokens_hbm.1), slice={[496:512], [0:2304]} | slice | bytes 147456 | tf_op jit(solution)/shard_map/slice | solution.py:301
  0.9 3.2 %collective-permute-start.3 = (bf16[128,2304]{1,0:T(8,128)(2,1)}, bf16[128,2304]{1,0:T(8,128)(2,1)S(1)}, u32[]{:S(2)}, u32[]{:S(2)}) collective-permute-start(bf16[128,2304]{1,0:T(8,128)(2,1)} %w_one.1), channel_id=1, source_target_pairs={{0,2},{1,3},{2,0},{3,1},{4,6},{5,7},{6,4},{7,5},{8,10},{9,11},{10,... | collective-permute-start | bytes 1769480 | tf_op jit(solution)/shard_map/weights/ppermute | solution.py:297
  4.1 0.1 collective-permute-start.4
  4.2 1.5 %collective-permute-start = (bf16[16,2304]{1,0:T(8,128)(2,1)S(1)}, bf16[16,2304]{1,0:T(8,128)(2,1)S(1)}, u32[]{:S(2)}, u32[]{:S(2)}) collective-permute-start(bf16[16,2304]{1,0:T(8,128)(2,1)S(1)} %slice.15), channel_id=1, source_target_pairs={{0,32},{32,64},{64,96},{96,128},{128,160},{160,192},{192,224},{224... | collective-permute-start | bytes 221192 | tf_op jit(solution)/shard_map/rim/ppermute | solution.py:303
  6.3 4.4 %collective-permute-done.rim_hbm = bf16[16,2304]{1,0:T(8,128)(2,1)S(1)} collective-permute-done((bf16[16,2304]{1,0:T(8,128)(2,1)S(1)}, bf16[16,2304]{1,0:T(8,128)(2,1)S(1)}, u32[]{:S(2)}, u32[]{:S(2)}) %collective-permute-start) | collective-permute-done | bytes 73760 | tf_op jit(solution)/shard_map/rim/ppermute | solution.py:303
  10.8 0.0 copy-start.8
  10.8 0.6 copy-done.8
  11.4 0.0 copy-start
  11.4 10.5 %front.1 = (f32[512,128]{1,0:T(8,128)}, bf16[512,128]{1,0:T(8,128)(2,1)}, bf16[128,256]{1,0:T(8,128)(2,1)}, f32[512,128]{1,0:T(8,128)}, bf16[8,128,256]{2,1,0:T(8,128)(2,1)}) custom-call(f32[1]{0:T(128)S(6)} %copy.13.alog, bf16[512,2304]{1,0:T(8,128)(2,1)} %tokens_hbm.1, bf16[16,2304]{1,0:T(8,128)(2,1)} %copy-done.8, bf16[3,2304,128]{2,1,0:T(8,128)(2,1)} %bitcast.17, ...), custom_call_target="tpu_custom_call" | custom-call | bytes 33210000 | tf_op jit(solution)/shard_map/front/pallas_call | solution.py:308
  21.9 0.0 collective-permute-done.3.refs_0_
  21.9 0.0 collective-permute-done.4.refs_2_
  21.9 2.0 %collective-permute-start.10 = (bf16[128,2304]{1,0:T(8,128)(2,1)S(1)}, bf16[128,2304]{1,0:T(8,128)(2,1)S(1)}, u32[]{:S(2)}, u32[]{:S(2)}) collective-permute-start(bf16[128,2304]{1,0:T(8,128)(2,1)S(1)} %collective-permute-done.3.refs_0_), channel_id=1, source_target_pairs={{0,4},{1,5},{2,6},{3,7},{4,0},{5,1},{6,2},{7,3},{8,12},{9,13},{10,... | collective-permute-start | bytes 1769480 | tf_op jit(solution)/shard_map/weights/ppermute | solution.py:297
  23.9 3.5 %all-to-all-start = ((bf16[8,128,256]{2,1,0:T(8,128)(2,1)}), bf16[8,128,256]{2,1,0:T(8,128)(2,1)S(1)}, u32[]{:S(2)}, u32[]{:S(2)}) async-start(bf16[8,128,256]{2,1,0:T(8,128)(2,1)} %get-tuple-element.34), calls=%async_computation | async-start | bytes 1048576 | tf_op jit(solution)/shard_map/states/all_to_all | solution.py:352
  27.4 0.0 copy-done
  27.5 0.1 collective-permute-start.2
  27.6 0.5 collective-permute-start.5
  28.1 0.0 copy-start.1
  28.1 0.9 %copy-done.1 = f32[512,128]{1,0:T(8,128)S(1)} copy-done((f32[512,128]{1,0:T(8,128)S(1)}, f32[512,128]{1,0:T(8,128)}, u32[]{:S(2)}) %copy-start.1) | copy-done | bytes 262168
  29.0 0.0 copy-start.2
  29.0 0.9 %copy-done.2 = f32[512,128]{1,0:T(8,128)S(1)} copy-done((f32[512,128]{1,0:T(8,128)S(1)}, f32[512,128]{1,0:T(8,128)}, u32[]{:S(2)}) %copy-start.2) | copy-done | bytes 262168
  30.0 0.0 copy-start.3
  30.0 0.9 %copy-done.3 = bf16[512,128]{1,0:T(8,128)(2,1)S(1)} copy-done((bf16[512,128]{1,0:T(8,128)(2,1)S(1)}, bf16[512,128]{1,0:T(8,128)(2,1)}, u32[]{:S(2)}) %copy-start.3) | copy-done | bytes 131096
  30.9 0.0 copy-start.4
  30.9 0.8 %copy-done.4 = bf16[128,256]{1,0:T(8,128)(2,1)S(1)} copy-done((bf16[128,256]{1,0:T(8,128)(2,1)S(1)}, bf16[128,256]{1,0:T(8,128)(2,1)}, u32[]{:S(2)}) %copy-start.4) | copy-done | bytes 65560
  31.7 0.0 copy-start.7
  31.7 0.7 copy-done.7
  32.4 0.0 copy-start.5
  32.4 0.6 copy-done.5
  33.0 3.0 %all-to-all-done.states = bf16[8,128,256]{2,1,0:T(8,128)(2,1)S(1)} async-done(((bf16[8,128,256]{2,1,0:T(8,128)(2,1)}), bf16[8,128,256]{2,1,0:T(8,128)(2,1)S(1)}, u32[]{:S(2)}, u32[]{:S(2)}) %all-to-all-start) | async-done | bytes 524320 | tf_op jit(solution)/shard_map/states/all_to_all | solution.py:352
  36.1 0.0 copy-start.6
  36.1 0.8 %copy-done.6 = bf16[128,256]{1,0:T(8,128)(2,1)S(1)} copy-done((bf16[128,256]{1,0:T(8,128)(2,1)S(1)}, bf16[128,256]{1,0:T(8,128)(2,1)}, u32[]{:S(2)}) %copy-start.6) | copy-done | bytes 65560
  36.9 1.3 %finish.1 = (bf16[4,4,16,128]{3,2,1,0:T(8,128)(2,1)S(1)}, bf16[4,4,16,128]{3,2,1,0:T(8,128)(2,1)S(1)}) custom-call(f32[512,128]{1,0:T(8,128)S(1)} %get-tuple-element.30.plain, bf16[512,128]{1,0:T(8,128)(2,1)S(1)} %get-tuple-element.31.carry, bf16[128,256]{1,0:T(8,128)(2,1)S(1)} %copy-done.6, f32[512,128]{1,0:T(8,128)S(1)} %get-tuple-element.33.gate, ...), custom_call_target="tpu_custom_call" | custom-call | bytes 6642000 | tf_op jit(solution)/shard_map/finish/pallas_call | solution.py:368
  38.3 0.1 collective-permute-start.6
  38.4 0.0 collective-permute-done.10.refs_4_
  38.4 0.5 collective-permute-start.11
  38.9 0.1 collective-permute-start.1
  39.0 2.3 %collective-permute-done.1.sibling = bf16[4,4,16,128]{3,2,1,0:T(8,128)(2,1)S(1)} collective-permute-done((bf16[4,4,16,128]{3,2,1,0:T(8,128)(2,1)S(1)}, bf16[4,4,16,128]{3,2,1,0:T(8,128)(2,1)S(1)}, u32[]{:S(2)}, u32[]{:S(2)}) %collective-permute-start.1) | collective-permute-done | bytes 65568 | tf_op jit(solution)/shard_map/exchange/ppermute | solution.py:297
  41.3 0.7 %collective-permute-start.7 = (bf16[2,4,16,128]{3,2,1,0:T(8,128)(2,1)S(1)}, bf16[2,4,16,128]{3,2,1,0:T(8,128)(2,1)S(1)}, u32[]{:S(2)}, u32[]{:S(2)}) collective-permute-start(bf16[2,4,16,128]{3,2,1,0:T(8,128)(2,1)S(1)} %get-tuple-element.42), channel_id=1, source_target_pairs={{0,2},{1,3},{2,0},{3,1},{4,6},{5,7},{6,4},{7,5},{8,10},{9,11},{10,... | collective-permute-start | bytes 98312 | tf_op jit(solution)/shard_map/exchange/ppermute | solution.py:297
  42.0 0.0 collective-permute-done.2.w_two
  42.0 1.6 %collective-permute-start.8 = (bf16[2,4,16,128]{3,2,1,0:T(8,128)(2,1)S(1)}, bf16[2,4,16,128]{3,2,1,0:T(8,128)(2,1)S(1)}, u32[]{:S(2)}, u32[]{:S(2)}) collective-permute-start(bf16[2,4,16,128]{3,2,1,0:T(8,128)(2,1)S(1)} %get-tuple-element.43), channel_id=1, source_target_pairs={{0,4},{1,5},{2,6},{3,7},{4,0},{5,1},{6,2},{7,3},{8,12},{9,13},{10,... | collective-permute-start | bytes 98312 | tf_op jit(solution)/shard_map/exchange/ppermute | solution.py:297
  43.6 0.0 collective-permute-done.5.refs_1_
  43.6 2.8 %collective-permute-start.9 = (bf16[2,4,16,128]{3,2,1,0:T(8,128)(2,1)S(1)}, bf16[2,4,16,128]{3,2,1,0:T(8,128)(2,1)S(1)}, u32[]{:S(2)}, u32[]{:S(2)}) collective-permute-start(bf16[2,4,16,128]{3,2,1,0:T(8,128)(2,1)S(1)} %get-tuple-element.44), channel_id=1, source_target_pairs={{0,6},{1,7},{2,4},{3,5},{4,2},{5,3},{6,0},{7,1},{8,14},{9,15},{10,... | collective-permute-start | bytes 98312 | tf_op jit(solution)/shard_map/exchange/ppermute | solution.py:297
  46.4 0.0 collective-permute-done.6.refs_3_
  46.4 1.7 %spread.2 = (bf16[512,2304]{1,0:T(8,128)(2,1)S(1)}, f32[64,2304]{1,0:T(8,128)S(1)}) custom-call(bf16[2,4,16,128]{3,2,1,0:T(8,128)(2,1)S(1)} %get-tuple-element.37.part, bf16[128,2304]{1,0:T(8,128)(2,1)S(1)} %copy-done, bf16[128,2304]{1,0:T(8,128)(2,1)} %collective-permute-done.2.w_two, bf16[128,2304]{1,0:T(8,128)(2,1)S(1)} %collective-permute-done.3.refs_0_, ...), custom_call_target="tpu_custom_call" | custom-call | bytes 9225000 | tf_op jit(solution)/shard_map/spread/pallas_call | solution.py:389
  48.1 0.0 collective-permute-done.7.refs_0_
  48.1 0.0 collective-permute-done.8.refs_1_
  48.1 1.8 %collective-permute-done.9.refs_2_ = bf16[2,4,16,128]{3,2,1,0:T(8,128)(2,1)S(1)} collective-permute-done((bf16[2,4,16,128]{3,2,1,0:T(8,128)(2,1)S(1)}, bf16[2,4,16,128]{3,2,1,0:T(8,128)(2,1)S(1)}, u32[]{:S(2)}, u32[]{:S(2)}) %collective-permute-start.9) | collective-permute-done | bytes 32800 | tf_op jit(solution)/shard_map/exchange/ppermute | solution.py:297
  49.9 0.0 collective-permute-done.11.refs_5_
  49.9 0.7 %spread.3 = bf16[4,16,2304]{2,1,0:T(8,128)(2,1)S(1)} custom-call(f32[64,2304]{1,0:T(8,128)S(1)} %get-tuple-element.41.begun, bf16[2,4,16,128]{3,2,1,0:T(8,128)(2,1)S(1)} %collective-permute-done.7.refs_0_, bf16[2,4,16,128]{3,2,1,0:T(8,128)(2,1)S(1)} %collective-permute-done.8.refs_1_, bf16[2,4,16,128]{3,2,1,0:T(8,128)(2,1)S(1)} %collective-permute-done.9.refs_2_, ...), custom_call_target="tpu_custom_call" | custom-call | bytes 3690000 | tf_op jit(solution)/shard_map/spread/pallas_call | solution.py:400
  50.7 5.8 %collective-permute-start.12 = (bf16[16,2304]{1,0:T(8,128)(2,1)S(1)}, bf16[16,2304]{1,0:T(8,128)(2,1)S(1)}, u32[]{:S(2)}, u32[]{:S(2)}) collective-permute-start(bf16[16,2304]{1,0:T(8,128)(2,1)S(1)} %get-tuple-element.47), channel_id=1, source_target_pairs={{0,16},{1,17},{2,18},{3,19},{4,20},{5,21},{6,22},{7,23},{8,24},{9,... | collective-permute-start | bytes 221192 | tf_op jit(solution)/shard_map/reduce/ppermute | solution.py:297
  56.5 1.5 %collective-permute-start.13 = (bf16[16,2304]{1,0:T(8,128)(2,1)S(1)}, bf16[16,2304]{1,0:T(8,128)(2,1)S(1)}, u32[]{:S(2)}, u32[]{:S(2)}) collective-permute-start(bf16[16,2304]{1,0:T(8,128)(2,1)S(1)} %get-tuple-element.49), channel_id=1, source_target_pairs={{0,8},{1,9},{2,10},{3,11},{4,12},{5,13},{6,14},{7,15},{8,0},{9,1},... | collective-permute-start | bytes 221192 | tf_op jit(solution)/shard_map/reduce/ppermute | solution.py:297
  57.9 0.0 collective-permute-start.14
  58.0 1.3 %collective-permute-done.12 = bf16[16,2304]{1,0:T(8,128)(2,1)S(1)} collective-permute-done((bf16[16,2304]{1,0:T(8,128)(2,1)S(1)}, bf16[16,2304]{1,0:T(8,128)(2,1)S(1)}, u32[]{:S(2)}, u32[]{:S(2)}) %collective-permute-start.12) | collective-permute-done | bytes 73760 | tf_op jit(solution)/shard_map/reduce/ppermute | solution.py:297
  59.3 3.1 %collective-permute-done.13 = bf16[16,2304]{1,0:T(8,128)(2,1)S(1)} collective-permute-done((bf16[16,2304]{1,0:T(8,128)(2,1)S(1)}, bf16[16,2304]{1,0:T(8,128)(2,1)S(1)}, u32[]{:S(2)}, u32[]{:S(2)}) %collective-permute-start.13) | collective-permute-done | bytes 73760 | tf_op jit(solution)/shard_map/reduce/ppermute | solution.py:297
  62.4 2.8 %collective-permute-done.14 = bf16[16,2304]{1,0:T(8,128)(2,1)S(1)} collective-permute-done((bf16[16,2304]{1,0:T(8,128)(2,1)S(1)}, bf16[16,2304]{1,0:T(8,128)(2,1)S(1)}, u32[]{:S(2)}, u32[]{:S(2)}) %collective-permute-start.14) | collective-permute-done | bytes 73760 | tf_op jit(solution)/shard_map/reduce/ppermute | solution.py:297
  65.2 0.7 %fusion.2 = bf16[16,2304]{1,0:T(8,128)(2,1)} fusion(bf16[16,2304]{1,0:T(8,128)(2,1)S(1)} %collective-permute-done.14, bf16[16,2304]{1,0:T(8,128)(2,1)S(1)} %collective-permute-done.13, bf16[16,2304]{1,0:T(8,128)(2,1)S(1)} %collective-permute-done.12, bf16[4,16,2304]{2,1,0:T(8,128)(2,1)S(1)} %spread.3), kind=kLoop, calls=%fused_computation.3 | loop fusion | flops 294912 | bytes 368640 | tf_op jit(solution)/shard_map/reduce/convert_element_type | solution.py:413
  (3 shorter events, 0.1 us)
Async XLA Ops:
  0.9 21.0 %collective-permute-start.3 = (bf16[128,2304]{1,0:T(8,128)(2,1)}, bf16[128,2304]{1,0:T(8,128)(2,1)S(1)}, u32[]{:S(2)}, u32[]{:S(2)}) collective-permute-start(bf16[128,2304]{1,0:T(8,128)(2,1)} %w_one.1), channel_id=1, source_target_pairs={{0,2},{1,3},{2,0},{3,1},{4,6},{5,7},{6,4},{7,5},{8,10},{9,11},{10,... | collective-permute-start | bytes 1769480 | tf_op jit(solution)/shard_map/weights/ppermute | solution.py:297
  4.1 17.8 %collective-permute-start.4 = (bf16[128,2304]{1,0:T(8,128)(2,1)}, bf16[128,2304]{1,0:T(8,128)(2,1)S(1)}, u32[]{:S(2)}, u32[]{:S(2)}) collective-permute-start(bf16[128,2304]{1,0:T(8,128)(2,1)} %w_one.1), channel_id=1, source_target_pairs={{0,4},{1,5},{2,6},{3,7},{4,0},{5,1},{6,2},{7,3},{8,12},{9,13},{10,... | collective-permute-start | bytes 1769480 | tf_op jit(solution)/shard_map/weights/ppermute | solution.py:297
  4.2 6.6 %collective-permute-start = (bf16[16,2304]{1,0:T(8,128)(2,1)S(1)}, bf16[16,2304]{1,0:T(8,128)(2,1)S(1)}, u32[]{:S(2)}, u32[]{:S(2)}) collective-permute-start(bf16[16,2304]{1,0:T(8,128)(2,1)S(1)} %slice.15), channel_id=1, source_target_pairs={{0,32},{32,64},{64,96},{96,128},{128,160},{160,192},{192,224},{224... | collective-permute-start | bytes 221192 | tf_op jit(solution)/shard_map/rim/ppermute | solution.py:303
  10.8 0.6 copy-start.8
  11.4 16.1 %copy-start = (bf16[128,2304]{1,0:T(8,128)(2,1)S(1)}, bf16[128,2304]{1,0:T(8,128)(2,1)}, u32[]{:S(2)}) copy-start(bf16[128,2304]{1,0:T(8,128)(2,1)} %w_one.1) | copy-start | bytes 1769476
  21.9 16.4 %collective-permute-start.10 = (bf16[128,2304]{1,0:T(8,128)(2,1)S(1)}, bf16[128,2304]{1,0:T(8,128)(2,1)S(1)}, u32[]{:S(2)}, u32[]{:S(2)}) collective-permute-start(bf16[128,2304]{1,0:T(8,128)(2,1)S(1)} %collective-permute-done.3.refs_0_), channel_id=1, source_target_pairs={{0,4},{1,5},{2,6},{3,7},{4,0},{5,1},{6,2},{7,3},{8,12},{9,13},{10,... | collective-permute-start | bytes 1769480 | tf_op jit(solution)/shard_map/weights/ppermute | solution.py:297
  23.9 12.1 %all-to-all-start = ((bf16[8,128,256]{2,1,0:T(8,128)(2,1)}), bf16[8,128,256]{2,1,0:T(8,128)(2,1)S(1)}, u32[]{:S(2)}, u32[]{:S(2)}) async-start(bf16[8,128,256]{2,1,0:T(8,128)(2,1)} %get-tuple-element.34), calls=%async_computation | async-start | bytes 1048576 | tf_op jit(solution)/shard_map/states/all_to_all | solution.py:352
  27.5 14.5 %collective-permute-start.2 = (bf16[128,2304]{1,0:T(8,128)(2,1)S(1)}, bf16[128,2304]{1,0:T(8,128)(2,1)}, u32[]{:S(2)}, u32[]{:S(2)}) collective-permute-start(bf16[128,2304]{1,0:T(8,128)(2,1)S(1)} %copy-done), channel_id=1, source_target_pairs={{0,1},{1,0},{2,3},{3,2},{4,5},{5,4},{6,7},{7,6},{8,9},{9,8},{10,11... | collective-permute-start | bytes 1769480 | tf_op jit(solution)/shard_map/weights/ppermute | solution.py:297
  27.6 16.0 %collective-permute-start.5 = (bf16[128,2304]{1,0:T(8,128)(2,1)S(1)}, bf16[128,2304]{1,0:T(8,128)(2,1)}, u32[]{:S(2)}, u32[]{:S(2)}) collective-permute-start(bf16[128,2304]{1,0:T(8,128)(2,1)S(1)} %collective-permute-done.3.refs_0_), channel_id=1, source_target_pairs={{0,1},{1,0},{2,3},{3,2},{4,5},{5,4},{6,7},{7,6},{8,9},{9,8},{10,11... | collective-permute-start | bytes 1769480 | tf_op jit(solution)/shard_map/weights/ppermute | solution.py:297
  28.1 0.9 %copy-start.1 = (f32[512,128]{1,0:T(8,128)S(1)}, f32[512,128]{1,0:T(8,128)}, u32[]{:S(2)}) copy-start(f32[512,128]{1,0:T(8,128)} %get-tuple-element.26.plain) | copy-start | bytes 786436
  29.0 0.9 %copy-start.2 = (f32[512,128]{1,0:T(8,128)S(1)}, f32[512,128]{1,0:T(8,128)}, u32[]{:S(2)}) copy-start(f32[512,128]{1,0:T(8,128)} %get-tuple-element.29.gate) | copy-start | bytes 786436
  30.0 0.9 %copy-start.3 = (bf16[512,128]{1,0:T(8,128)(2,1)S(1)}, bf16[512,128]{1,0:T(8,128)(2,1)}, u32[]{:S(2)}) copy-start(bf16[512,128]{1,0:T(8,128)(2,1)} %get-tuple-element.27.carry) | copy-start | bytes 393220
  30.9 0.8 %copy-start.4 = (bf16[128,256]{1,0:T(8,128)(2,1)S(1)}, bf16[128,256]{1,0:T(8,128)(2,1)}, u32[]{:S(2)}) copy-start(bf16[128,256]{1,0:T(8,128)(2,1)} %get-tuple-element.28.half) | copy-start | bytes 196612
  31.7 0.7 copy-start.7
  32.4 0.6 copy-start.5
  36.1 0.8 %copy-start.6 = (bf16[128,256]{1,0:T(8,128)(2,1)S(1)}, bf16[128,256]{1,0:T(8,128)(2,1)}, u32[]{:S(2)}) copy-start(bf16[128,256]{1,0:T(8,128)(2,1)} %copy-done.5) | copy-start | bytes 196612
  38.3 8.1 %collective-permute-start.6 = (bf16[128,2304]{1,0:T(8,128)(2,1)S(1)}, bf16[128,2304]{1,0:T(8,128)(2,1)S(1)}, u32[]{:S(2)}, u32[]{:S(2)}) collective-permute-start(bf16[128,2304]{1,0:T(8,128)(2,1)S(1)} %collective-permute-done.4.refs_2_), channel_id=1, source_target_pairs={{0,1},{1,0},{2,3},{3,2},{4,5},{5,4},{6,7},{7,6},{8,9},{9,8},{10,11... | collective-permute-start | bytes 1769480 | tf_op jit(solution)/shard_map/weights/ppermute | solution.py:297
  38.4 11.5 %collective-permute-start.11 = (bf16[128,2304]{1,0:T(8,128)(2,1)S(1)}, bf16[128,2304]{1,0:T(8,128)(2,1)S(1)}, u32[]{:S(2)}, u32[]{:S(2)}) collective-permute-start(bf16[128,2304]{1,0:T(8,128)(2,1)S(1)} %collective-permute-done.10.refs_4_), channel_id=1, source_target_pairs={{0,1},{1,0},{2,3},{3,2},{4,5},{5,4},{6,7},{7,6},{8,9},{9,8},{10,11... | collective-permute-start | bytes 1769480 | tf_op jit(solution)/shard_map/spread/ppermute | solution.py:297
  38.9 2.4 %collective-permute-start.1 = (bf16[4,4,16,128]{3,2,1,0:T(8,128)(2,1)S(1)}, bf16[4,4,16,128]{3,2,1,0:T(8,128)(2,1)S(1)}, u32[]{:S(2)}, u32[]{:S(2)}) collective-permute-start(bf16[4,4,16,128]{3,2,1,0:T(8,128)(2,1)S(1)} %get-tuple-element.36), channel_id=1, source_target_pairs={{0,1},{1,0},{2,3},{3,2},{4,5},{5,4},{6,7},{7,6},{8,9},{9,8},{10,11... | collective-permute-start | bytes 196616 | tf_op jit(solution)/shard_map/exchange/ppermute | solution.py:297
  41.3 6.8 %collective-permute-start.7 = (bf16[2,4,16,128]{3,2,1,0:T(8,128)(2,1)S(1)}, bf16[2,4,16,128]{3,2,1,0:T(8,128)(2,1)S(1)}, u32[]{:S(2)}, u32[]{:S(2)}) collective-permute-start(bf16[2,4,16,128]{3,2,1,0:T(8,128)(2,1)S(1)} %get-tuple-element.42), channel_id=1, source_target_pairs={{0,2},{1,3},{2,0},{3,1},{4,6},{5,7},{6,4},{7,5},{8,10},{9,11},{10,... | collective-permute-start | bytes 98312 | tf_op jit(solution)/shard_map/exchange/ppermute | solution.py:297
  42.0 6.1 %collective-permute-start.8 = (bf16[2,4,16,128]{3,2,1,0:T(8,128)(2,1)S(1)}, bf16[2,4,16,128]{3,2,1,0:T(8,128)(2,1)S(1)}, u32[]{:S(2)}, u32[]{:S(2)}) collective-permute-start(bf16[2,4,16,128]{3,2,1,0:T(8,128)(2,1)S(1)} %get-tuple-element.43), channel_id=1, source_target_pairs={{0,4},{1,5},{2,6},{3,7},{4,0},{5,1},{6,2},{7,3},{8,12},{9,13},{10,... | collective-permute-start | bytes 98312 | tf_op jit(solution)/shard_map/exchange/ppermute | solution.py:297
  43.6 6.3 %collective-permute-start.9 = (bf16[2,4,16,128]{3,2,1,0:T(8,128)(2,1)S(1)}, bf16[2,4,16,128]{3,2,1,0:T(8,128)(2,1)S(1)}, u32[]{:S(2)}, u32[]{:S(2)}) collective-permute-start(bf16[2,4,16,128]{3,2,1,0:T(8,128)(2,1)S(1)} %get-tuple-element.44), channel_id=1, source_target_pairs={{0,6},{1,7},{2,4},{3,5},{4,2},{5,3},{6,0},{7,1},{8,14},{9,15},{10,... | collective-permute-start | bytes 98312 | tf_op jit(solution)/shard_map/exchange/ppermute | solution.py:297
  50.7 8.6 %collective-permute-start.12 = (bf16[16,2304]{1,0:T(8,128)(2,1)S(1)}, bf16[16,2304]{1,0:T(8,128)(2,1)S(1)}, u32[]{:S(2)}, u32[]{:S(2)}) collective-permute-start(bf16[16,2304]{1,0:T(8,128)(2,1)S(1)} %get-tuple-element.47), channel_id=1, source_target_pairs={{0,16},{1,17},{2,18},{3,19},{4,20},{5,21},{6,22},{7,23},{8,24},{9,... | collective-permute-start | bytes 221192 | tf_op jit(solution)/shard_map/reduce/ppermute | solution.py:297
  56.5 5.9 %collective-permute-start.13 = (bf16[16,2304]{1,0:T(8,128)(2,1)S(1)}, bf16[16,2304]{1,0:T(8,128)(2,1)S(1)}, u32[]{:S(2)}, u32[]{:S(2)}) collective-permute-start(bf16[16,2304]{1,0:T(8,128)(2,1)S(1)} %get-tuple-element.49), channel_id=1, source_target_pairs={{0,8},{1,9},{2,10},{3,11},{4,12},{5,13},{6,14},{7,15},{8,0},{9,1},... | collective-permute-start | bytes 221192 | tf_op jit(solution)/shard_map/reduce/ppermute | solution.py:297
  57.9 7.3 %collective-permute-start.14 = (bf16[16,2304]{1,0:T(8,128)(2,1)S(1)}, bf16[16,2304]{1,0:T(8,128)(2,1)S(1)}, u32[]{:S(2)}, u32[]{:S(2)}) collective-permute-start(bf16[16,2304]{1,0:T(8,128)(2,1)S(1)} %get-tuple-element.48), channel_id=1, source_target_pairs={{0,24},{1,25},{2,26},{3,27},{4,28},{5,29},{6,30},{7,31},{8,16},{9,... | collective-permute-start | bytes 221192 | tf_op jit(solution)/shard_map/reduce/ppermute | solution.py:297

commit v3 on v2

--- a/solution.py
+++ b/solution.py
@@ -22,8 +22,10 @@
 LIMIT = pltpu.CompilerParams(vmem_limit_bytes=16 * 1024 * 1024)
 
 
-def cost(us):
-    return pl.CostEstimate(flops=0, bytes_accessed=int(us * 3_690_000), transcendentals=0)
+def cost(us, flops=0):
+    return pl.CostEstimate(
+        flops=int(flops * 1_000_000_000), bytes_accessed=int(us * 3_690_000), transcendentals=0
+    )
 
 
 def mm(left, right):
@@ -87,9 +89,9 @@
 
 
 def front(
-    alog, tokens_hbm, rim_hbm, w3_hbm, f_down_hbm, o_down_hbm, f_up_hbm, o_up_hbm, bias_hbm,
-    w_beta_hbm, taps_hbm, plain_out, carry_out, half_out, gate_out, sends, tok, w3, f_down, o_down,
-    wide, f_up, o_up, bias, w_beta, taps, total, padded, final, sems, out_sems,
+    tokens_hbm, rim_hbm, alog_hbm, w3_hbm, f_down_hbm, o_down_hbm, f_up_hbm, o_up_hbm, bias_hbm,
+    w_beta_hbm, taps_hbm, pack_hbm, sends, tok, w3, f_down, o_down,
+    wide, f_up, o_up, bias, w_beta, taps, alog, total, padded, final, pack, sems, out_sems, pack_sems,
 ):
     rows, model = tokens_hbm.shape
     head = f_up.shape[0]
@@ -104,6 +106,7 @@
         pairs.append((f_down_hbm.at[rng], f_down.at[rng]))
         pairs.append((o_down_hbm.at[rng], o_down.at[rng]))
     pairs += [(f_up_hbm, f_up), (o_up_hbm, o_up), (bias_hbm, bias), (taps_hbm, taps)]
+    pairs.append((alog_hbm, alog))
     copies = load(pairs, sems)
     wide[...] = jnp.zeros_like(wide)
     copies[0].wait()
@@ -124,9 +127,16 @@
         copy.wait()
     low = total[:rows, 3 * head : 4 * head].astype(BF16)
     logit = jnp.dot(low, f_up[...], preferred_element_type=F32) + bias[...]
-    decays = -jnp.exp(jnp.full((1, 1), alog[0], F32)) * jax.nn.softplus(logit)
+    decays = -jnp.exp(alog[...]) * jax.nn.softplus(logit)
     out_low = total[:rows, 4 * head : 5 * head].astype(BF16)
-    gate_out[...] = jax.nn.sigmoid(jnp.dot(out_low, o_up[...], preferred_element_type=F32))
+    pack[:rows, 2 * head :] = jax.nn.sigmoid(jnp.dot(out_low, o_up[...], preferred_element_type=F32))
+    stores = []
+
+    def store(at):
+        stores.append(pltpu.make_async_copy(pack.at[at], pack_hbm.at[at], pack_sems.at[len(stores)]))
+        stores[-1].start()
+
+    store((pl.ds(0, rows), pl.ds(2 * head, head)))
     beta = jnp.broadcast_to(jax.nn.sigmoid(total[:rows, 5 * head : 5 * head + 1]), (rows, head))
     row, col, differ = masks(GROUP)
     strict = (row > col) & (differ < BLOCK)
@@ -187,7 +197,8 @@
             states[group] = jnp.concatenate(
                 [state[:, :head] + pairs[at][:, :head], state[:, head:]], axis=1
             )
-    half_out[...] = states[0].astype(BF16)
+    pack[rows:, : 2 * head] = states[0]
+    store((pl.ds(rows, head), pl.ds(0, 2 * head)))
     whole = mm(states[1][:, head:], states[0])
     final[...] = jnp.concatenate(
         [whole[:, :head] + states[1][:, :head], whole[:, head:]], axis=1
@@ -206,36 +217,37 @@
             across = jnp.dot(
                 local_key[sub], starts[(start // BLOCK) + block], preferred_element_type=F32
             )
-            plain_out[out] = across[:, :head] + local[sub, :head]
-            carry_out[out] = across[:, head:].astype(BF16)
-    for copy in copies:
+            pack[out, :head] = across[:, :head] + local[sub, :head]
+            pack[out, head : 2 * head] = across[:, head:]
+        store((pl.ds(start, GROUP), pl.ds(0, 2 * head)))
+    for copy in copies + stores:
         copy.wait()
 
 
-def stage(plain, carry, half, gate, gain, plain_out, carry_out, half_out, gate_out):
-    plain_out[...] = plain[...]
-    carry_out[...] = carry[...]
-    half_out[...] = half[...]
-    gate_out[...] = gate[...] * gain[...]
-
-
-def finish(plain, carry, half, gate, states, own, other, gated):
-    rows, head = gate.shape
+def stage(pack, gain, out):
+    head = gain.shape[1]
+    rows = pack.shape[0] - head
+    out[:, : 2 * head] = pack[:, : 2 * head]
+    out[:rows, 2 * head :] = pack[:rows, 2 * head :] * gain[...]
+
+
+def finish(pack, states, own, other, gated):
+    head = states.shape[1]
+    rows = pack.shape[0] - head
     ctx = lax.axis_index("ctx")
     core_at = lax.rem(lax.axis_index("head"), 2)
     state = jnp.zeros((head, head), F32)
     for step in range(states.shape[0] - 1):
         moved = jnp.dot(states[step, :, head:], state.astype(BF16), preferred_element_type=F32)
         state = jnp.where(step < ctx, moved + states[step, :, :head].astype(F32), state)
-    middle = jnp.dot(half[:, head:], state.astype(BF16), preferred_element_type=F32)
-    middle = middle + half[:, :head].astype(F32)
+    middle = mm(pack[rows:, head : 2 * head], state) + pack[rows:, :head]
     cores = []
     for group, start in enumerate((state, middle)):
         rng = slice(group * SPAN, (group + 1) * SPAN)
-        cores.append(plain[rng] + mm(carry[rng], start))
+        cores.append(pack[rng, :head] + mm(pack[rng, head : 2 * head], start))
     core = jnp.concatenate(cores, axis=0)
     scale = lax.rsqrt(jnp.mean(core * core, axis=-1, keepdims=True) + 1e-05)
-    result = core * scale * gate[...]
+    result = core * scale * pack[:rows, 2 * head :]
     gated[...] = result.astype(BF16).reshape(gated.shape)
     for pair in range(own.shape[0]):
         own[pair] = gated[:, pair, pl.ds(core_at, 1)].reshape(own.shape[1:])
@@ -275,8 +287,8 @@
     depth = left.shape[-1]
     for which, part in enumerate(parts):
         turn(part, left.at[which])
-        if which < 2:
-            weight = held[which * depth : (which + 1) * depth]
+        if which > 0:
+            weight = held[(which - 1) * depth : which * depth]
         else:
             weight = jnp.concatenate([w_one[...], w_two[...]], axis=0)
         total = total + jnp.dot(left[which], weight, preferred_element_type=F32)
@@ -303,17 +315,14 @@
         rim = lax.ppermute(edge, "ctx", [(i, (i + 1) % ctx_count) for i in range(ctx_count)])
     (w_sent,) = after((w_out,), edge)
     with jax.named_scope("weights"):
-        w_far, w_next, w_core = flip(w_sent, 2), flip(w_sent, 4), flip(w_sent, 1)
+        w_far, w_next = flip(w_sent, 2), flip(w_sent, 4)
     with jax.named_scope("front"):
-        plain, carry, half, gate, sends = pl.pallas_call(
+        pack, sends = pl.pallas_call(
             front,
-            in_specs=[SMEM] + [HBM] * 10,
-            out_specs=[VMEM] * 4 + [HBM],
+            in_specs=[HBM] * 11,
+            out_specs=[HBM] * 2,
             out_shape=[
-                shape((rows, head), F32),
-                shape((rows, head), BF16),
-                shape((head, 2 * head), BF16),
-                shape((rows, head), F32),
+                shape((rows + head, 3 * head), F32),
                 shape((ctx_count, head, 2 * head), BF16),
             ],
             scratch_shapes=[
@@ -327,18 +336,21 @@
                 pltpu.VMEM((1, head), F32),
                 pltpu.VMEM((1, model), BF16),
                 pltpu.VMEM(taps.shape, F32),
+                pltpu.VMEM((1, 1), F32),
                 pltpu.VMEM((rows + 16, 6 * head), F32),
                 pltpu.VMEM((rows + 8, 3 * head), F32),
                 pltpu.VMEM((head, 2 * head), BF16),
-                dma((6 + 6 * CHUNKS,)),
+                pltpu.VMEM((rows + head, 3 * head), F32),
+                dma((7 + 6 * CHUNKS,)),
                 dma((ctx_count,)),
+                dma((2 + rows // GROUP,)),
             ],
             compiler_params=FULL,
-            cost_estimate=cost(9),
+            cost_estimate=cost(9, 40),
         )(
-            a_log,
             tokens,
             rim,
+            a_log.reshape(1, 1),
             w3,
             f_down,
             o_down,
@@ -350,30 +362,31 @@
         )
     with jax.named_scope("states"):
         states = lax.all_to_all(sends, "ctx", 0, 0, tiled=True)
-    w_late, w_near = after((w_far, w_next), half)
+    (w_early,) = after((w_far,), pack)
     with jax.named_scope("weights"):
-        w_both = flip(w_late, 4)
-        w_far_core, w_next_core = flip(w_late, 1), flip(w_near, 1)
+        w_both = flip(w_early, 4)
     with jax.named_scope("stage"):
-        kinds = [shape(v.shape, v.dtype) for v in (plain, carry, half, gate)]
         staged = pl.pallas_call(
             stage,
-            in_specs=[VMEM] * 5,
-            out_specs=[VMEM] * 4,
-            out_shape=kinds,
+            in_specs=[VMEM] * 2,
+            out_specs=VMEM,
+            out_shape=shape(pack.shape, F32),
             compiler_params=LIMIT,
-            cost_estimate=cost(0.5),
-        )(plain, carry, half, gate, norm_gain.reshape(1, head))
+            cost_estimate=cost(0.5, 0),
+        )(pack, norm_gain.reshape(1, head))
+    w_late, w_near, w_mine = after((w_far, w_next, w_out), staged)
+    with jax.named_scope("weights"):
+        w_core, w_far_core, w_next_core = flip(w_mine, 1), flip(w_late, 1), flip(w_near, 1)
     with jax.named_scope("finish"):
         own, other = pl.pallas_call(
             finish,
-            in_specs=[VMEM] * 5,
+            in_specs=[VMEM] * 2,
             out_specs=[VMEM] * 2,
             out_shape=[shape((SUBS // 2, zs, 16, head), BF16)] * 2,
             scratch_shapes=[pltpu.VMEM((zs, SUBS // 2, 2, 16, head), BF16)],
             compiler_params=LIMIT,
-            cost_estimate=cost(1.8),
-        )(*staged, states)
+            cost_estimate=cost(2, 0.5),
+        )(staged, states)
     with jax.named_scope("exchange"):
         sibling = flip(other, 1)
         kept, *sent = pl.pallas_call(
@@ -382,7 +395,7 @@
             out_specs=[VMEM] * 4,
             out_shape=[shape((2, zs, 16, head), BF16)] * 4,
             compiler_params=LIMIT,
-            cost_estimate=cost(0.5),
+            cost_estimate=cost(0.5, 0),
         )(own, sibling)
         got = {f: flip(sent[f - 1], 2 * f) for f in (3, 1, 2)}
     with jax.named_scope("spread"):
@@ -393,9 +406,9 @@
             out_shape=[shape((4 * head, model), BF16), shape((zs * 16, model), F32)],
             scratch_shapes=[pltpu.VMEM((zs * 16, 2 * head), BF16)],
             compiler_params=LIMIT,
-            cost_estimate=cost(2.5),
+            cost_estimate=cost(2, 0),
         )(kept, w_out, w_core, w_far, w_far_core, w_next, w_next_core)
-        (w_late,) = after((w_both,), own)
+        (w_late,) = after((w_both,), kept)
         w_both_core = flip(w_late, 1)
         parts = pl.pallas_call(
             combine,
@@ -404,8 +417,8 @@
             out_shape=shape((zs, 16, model), BF16),
             scratch_shapes=[pltpu.VMEM((3, zs * 16, 2 * head), BF16)],
             compiler_params=LIMIT,
-            cost_estimate=cost(1.0),
-        )(begun, got[1], got[2], got[3], held, w_both, w_both_core)
+            cost_estimate=cost(1, 0),
+        )(begun, got[3], got[1], got[2], held, w_both, w_both_core)
     with jax.named_scope("reduce"):
         total = parts[0].astype(F32)
         for part in [flip(parts[k], SUBS * k) for k in (2, 1, 3)]:

time: 66.3 us -> 64.6 us (0.974)
  the two profiles are of different devices: /device:TPU:32 before, /device:TPU:1 now
where the time goes in v3:
time: 64.6 us; the launch traced here: 64.2 us
  starting transfers between devices  29 us (45%)
  waiting for transfers between devices  17.4 us (27%)
  Pallas kernels  13.6 us (21%)
  local copies, waits for them, and re-layouts  2.74 us (4%)
  between operations  0.75 us (1%)
  other arithmetic  0.68 us (1%)
    ppermute x14, starting transfers between devices, flip(): lax.ppermute(value, 'head', [(h, h ^ mask) for h in range(head_count)])  22.7 us
    ppermute x14, waiting for transfers between devices, flip(): lax.ppermute(value, 'head', [(h, h ^ mask) for h in range(head_count)])  10.4 us
    pallas_call x1, Pallas kernels, on_device(): pl.pallas_call(front, in_specs=[HBM] * 11, out_specs=[HBM] * 2, out_shape...  10 us
    all_to_all x1, waiting for transfers between devices, on_device(): states = lax.all_to_all(sends, 'ctx', 0, 0, tiled=True)  6.93 us
    all_to_all x1, starting transfers between devices, on_device(): states = lax.all_to_all(sends, 'ctx', 0, 0, tiled=True)  4.27 us
    pallas_call x1, Pallas kernels, on_device(): pl.pallas_call(finish, in_specs=[VMEM] * 2, out_specs=[VMEM] * 2, out_sha...  2.37 us
    ppermute x1, starting transfers between devices, on_device(): lax.ppermute(edge, 'ctx', [(i, (i + 1) % ctx_count) for i in range(ctx_co...  2.04 us
    unnamed x8, local copies, waits for them, and re-layouts  1.83 us
  transfers between devices with their start and end apart: 16, of which 7 were waited for; matrix products, arithmetic and copies ran while one was open for 0% of the time, Pallas kernels for 20%

profile of v3, /device:TPU:1, one launch (start us, length us, event | category | flops | bytes accessed | tf_op | source)
XLA Modules:
  0.0 64.2 jit_solution(1644415788224635315)
XLA Ops:
  0.0 0.9 %slice.15 = bf16[16,2304]{1,0:T(8,128)(2,1)S(1)} slice(bf16[512,2304]{1,0:T(8,128)(2,1)} %tokens_hbm.1), slice={[496:512], [0:2304]} | slice | bytes 147456 | tf_op jit(solution)/shard_map/slice | solution.py:313
  0.9 2.0 %collective-permute-start = (bf16[16,2304]{1,0:T(8,128)(2,1)S(1)}, bf16[16,2304]{1,0:T(8,128)(2,1)S(1)}, u32[]{:S(2)}, u32[]{:S(2)}) collective-permute-start(bf16[16,2304]{1,0:T(8,128)(2,1)S(1)} %slice.15), channel_id=1, source_target_pairs={{0,32},{32,64},{64,96},{96,128},{128,160},{160,192},{192,224},{224... | collective-permute-start | bytes 221192 | tf_op jit(solution)/shard_map/rim/ppermute | solution.py:315
  2.9 2.9 %collective-permute-start.2 = (bf16[128,2304]{1,0:T(8,128)(2,1)}, bf16[128,2304]{1,0:T(8,128)(2,1)S(1)}, u32[]{:S(2)}, u32[]{:S(2)}) collective-permute-start(bf16[128,2304]{1,0:T(8,128)(2,1)} %w_one.1), channel_id=1, source_target_pairs={{0,2},{1,3},{2,0},{3,1},{4,6},{5,7},{6,4},{7,5},{8,10},{9,11},{10,... | collective-permute-start | bytes 1769480 | tf_op jit(solution)/shard_map/weights/ppermute | solution.py:309
  5.8 1.6 %collective-permute-start.3 = (bf16[128,2304]{1,0:T(8,128)(2,1)}, bf16[128,2304]{1,0:T(8,128)(2,1)S(1)}, u32[]{:S(2)}, u32[]{:S(2)}) collective-permute-start(bf16[128,2304]{1,0:T(8,128)(2,1)} %w_one.1), channel_id=1, source_target_pairs={{0,4},{1,5},{2,6},{3,7},{4,0},{5,1},{6,2},{7,3},{8,12},{9,13},{10,... | collective-permute-start | bytes 1769480 | tf_op jit(solution)/shard_map/weights/ppermute | solution.py:309
  8.1 0.0 collective-permute-done.rim_hbm
  8.1 0.0 copy-start.3
  8.2 0.6 copy-done.3
  8.8 0.0 copy-start.2
  8.8 10.0 %front.1 = (f32[640,384]{1,0:T(8,128)}, bf16[8,128,256]{2,1,0:T(8,128)(2,1)}) custom-call(bf16[512,2304]{1,0:T(8,128)(2,1)} %tokens_hbm.1, bf16[16,2304]{1,0:T(8,128)(2,1)} %copy-done.3, f32[1,1]{1,0:T(1,128)} %bitcast.17.alog_hbm, bf16[3,2304,128]{2,1,0:T(8,128)(2,1)} %bitcast.19, bf16[2304,128]{1,0:T(8,128)(2,1)} %f_down_hbm.1, ...), custom_call_target="tpu_custom_call" | custom-call | flops 40000000000 | bytes 33210000 | tf_op jit(solution)/shard_map/front/pallas_call | solution.py:320
  18.8 1.0 %collective-permute-done.2.refs_0_ = bf16[128,2304]{1,0:T(8,128)(2,1)S(1)} collective-permute-done((bf16[128,2304]{1,0:T(8,128)(2,1)}, bf16[128,2304]{1,0:T(8,128)(2,1)S(1)}, u32[]{:S(2)}, u32[]{:S(2)}) %collective-permute-start.2) | collective-permute-done | bytes 589856 | tf_op jit(solution)/shard_map/weights/ppermute | solution.py:309
  19.8 2.0 %collective-permute-start.10 = (bf16[128,2304]{1,0:T(8,128)(2,1)S(1)}, bf16[128,2304]{1,0:T(8,128)(2,1)S(1)}, u32[]{:S(2)}, u32[]{:S(2)}) collective-permute-start(bf16[128,2304]{1,0:T(8,128)(2,1)S(1)} %collective-permute-done.2.refs_0_), channel_id=1, source_target_pairs={{0,4},{1,5},{2,6},{3,7},{4,0},{5,1},{6,2},{7,3},{8,12},{9,13},{10,... | collective-permute-start | bytes 1769480 | tf_op jit(solution)/shard_map/weights/ppermute | solution.py:309
  21.7 0.0 copy-start.1
  21.7 4.3 %all-to-all-start = ((bf16[8,128,256]{2,1,0:T(8,128)(2,1)}), bf16[8,128,256]{2,1,0:T(8,128)(2,1)}, u32[]{:S(2)}, u32[]{:S(2)}) async-start(bf16[8,128,256]{2,1,0:T(8,128)(2,1)} %get-tuple-element.22), calls=%async_computation | async-start | bytes 1048576 | tf_op jit(solution)/shard_map/states/all_to_all | solution.py:364
  26.0 0.0 copy-done.2
  26.0 0.0 copy-start
  26.0 1.2 %copy-done = f32[640,384]{1,0:T(8,128)S(1)} copy-done((f32[640,384]{1,0:T(8,128)S(1)}, f32[640,384]{1,0:T(8,128)}, u32[]{:S(2)}) %copy-start) | copy-done | bytes 983064
  27.2 0.1 stage.1.pack
  27.3 6.9 %all-to-all-done.states = bf16[8,128,256]{2,1,0:T(8,128)(2,1)} async-done(((bf16[8,128,256]{2,1,0:T(8,128)(2,1)}), bf16[8,128,256]{2,1,0:T(8,128)(2,1)}, u32[]{:S(2)}, u32[]{:S(2)}) %all-to-all-start) | async-done | bytes 524320 | tf_op jit(solution)/shard_map/states/all_to_all | solution.py:364
  34.2 2.4 %finish.1 = (bf16[4,4,16,128]{3,2,1,0:T(8,128)(2,1)S(1)}, bf16[4,4,16,128]{3,2,1,0:T(8,128)(2,1)S(1)}) custom-call(f32[640,384]{1,0:T(8,128)S(1)} %stage.1.pack, bf16[8,128,256]{2,1,0:T(8,128)(2,1)} %all-to-all-done.states), custom_call_target="tpu_custom_call" | custom-call | flops 500000000 | bytes 7380000 | tf_op jit(solution)/shard_map/finish/pallas_call | solution.py:381
  36.6 2.9 %collective-permute-start.1 = (bf16[4,4,16,128]{3,2,1,0:T(8,128)(2,1)S(1)}, bf16[4,4,16,128]{3,2,1,0:T(8,128)(2,1)S(1)}, u32[]{:S(2)}, u32[]{:S(2)}) collective-permute-start(bf16[4,4,16,128]{3,2,1,0:T(8,128)(2,1)S(1)} %get-tuple-element.24), channel_id=1, source_target_pairs={{0,1},{1,0},{2,3},{3,2},{4,5},{5,4},{6,7},{7,6},{8,9},{9,8},{10,11... | collective-permute-start | bytes 196616 | tf_op jit(solution)/shard_map/exchange/ppermute | solution.py:309
  39.5 0.0 collective-permute-done.3.refs_2_
  39.5 0.0 copy-done.1
  39.5 0.1 collective-permute-start.4
  39.7 0.4 collective-permute-start.5
  40.1 0.1 collective-permute-start.6
  40.2 0.3 collective-permute-done.1.sibling
  40.5 0.0 collective-permute-done.10.refs_4_
  40.5 0.4 collective-permute-start.11
  40.9 2.6 %collective-permute-start.7 = (bf16[2,4,16,128]{3,2,1,0:T(8,128)(2,1)S(1)}, bf16[2,4,16,128]{3,2,1,0:T(8,128)(2,1)S(1)}, u32[]{:S(2)}, u32[]{:S(2)}) collective-permute-start(bf16[2,4,16,128]{3,2,1,0:T(8,128)(2,1)S(1)} %get-tuple-element.31), channel_id=1, source_target_pairs={{0,6},{1,7},{2,4},{3,5},{4,2},{5,3},{6,0},{7,1},{8,14},{9,15},{10,... | collective-permute-start | bytes 98312 | tf_op jit(solution)/shard_map/exchange/ppermute | solution.py:309
  43.5 0.0 collective-permute-done.4.w_two
  43.5 0.9 %collective-permute-start.8 = (bf16[2,4,16,128]{3,2,1,0:T(8,128)(2,1)S(1)}, bf16[2,4,16,128]{3,2,1,0:T(8,128)(2,1)S(1)}, u32[]{:S(2)}, u32[]{:S(2)}) collective-permute-start(bf16[2,4,16,128]{3,2,1,0:T(8,128)(2,1)S(1)} %get-tuple-element.32), channel_id=1, source_target_pairs={{0,2},{1,3},{2,0},{3,1},{4,6},{5,7},{6,4},{7,5},{8,10},{9,11},{10,... | collective-permute-start | bytes 98312 | tf_op jit(solution)/shard_map/exchange/ppermute | solution.py:309
  44.5 0.0 collective-permute-done.5.refs_1_
  44.5 0.6 collective-permute-start.9
  45.1 0.0 collective-permute-done.6.refs_3_
  45.1 0.4 spread.2
  45.5 0.6 collective-permute-done.7.refs_0_
  46.1 1.7 %collective-permute-done.8.refs_1_ = bf16[2,4,16,128]{3,2,1,0:T(8,128)(2,1)S(1)} collective-permute-done((bf16[2,4,16,128]{3,2,1,0:T(8,128)(2,1)S(1)}, bf16[2,4,16,128]{3,2,1,0:T(8,128)(2,1)S(1)}, u32[]{:S(2)}, u32[]{:S(2)}) %collective-permute-start.8) | collective-permute-done | bytes 32800 | tf_op jit(solution)/shard_map/exchange/ppermute | solution.py:309
  47.8 0.0 collective-permute-done.9.refs_2_
  47.8 0.0 collective-permute-done.11.refs_5_
  47.8 0.7 %spread.3 = bf16[4,16,2304]{2,1,0:T(8,128)(2,1)S(1)} custom-call(f32[64,2304]{1,0:T(8,128)S(1)} %get-tuple-element.30.begun, bf16[2,4,16,128]{3,2,1,0:T(8,128)(2,1)S(1)} %collective-permute-done.7.refs_0_, bf16[2,4,16,128]{3,2,1,0:T(8,128)(2,1)S(1)} %collective-permute-done.8.refs_1_, bf16[2,4,16,128]{3,2,1,0:T(8,128)(2,1)S(1)} %collective-permute-done.9.refs_2_, ...), custom_call_target="tpu_custom_call" | custom-call | bytes 3690000 | tf_op jit(solution)/shard_map/spread/pallas_call | solution.py:413
  48.6 6.8 %collective-permute-start.12 = (bf16[16,2304]{1,0:T(8,128)(2,1)S(1)}, bf16[16,2304]{1,0:T(8,128)(2,1)S(1)}, u32[]{:S(2)}, u32[]{:S(2)}) collective-permute-start(bf16[16,2304]{1,0:T(8,128)(2,1)S(1)} %get-tuple-element.37), channel_id=1, source_target_pairs={{0,16},{1,17},{2,18},{3,19},{4,20},{5,21},{6,22},{7,23},{8,24},{9,... | collective-permute-start | bytes 221192 | tf_op jit(solution)/shard_map/reduce/ppermute | solution.py:309
  55.4 1.2 %collective-permute-start.13 = (bf16[16,2304]{1,0:T(8,128)(2,1)S(1)}, bf16[16,2304]{1,0:T(8,128)(2,1)S(1)}, u32[]{:S(2)}, u32[]{:S(2)}) collective-permute-start(bf16[16,2304]{1,0:T(8,128)(2,1)S(1)} %get-tuple-element.39), channel_id=1, source_target_pairs={{0,8},{1,9},{2,10},{3,11},{4,12},{5,13},{6,14},{7,15},{8,0},{9,1},... | collective-permute-start | bytes 221192 | tf_op jit(solution)/shard_map/reduce/ppermute | solution.py:309
  56.6 0.0 collective-permute-start.14
  56.6 0.7 %collective-permute-done.12 = bf16[16,2304]{1,0:T(8,128)(2,1)S(1)} collective-permute-done((bf16[16,2304]{1,0:T(8,128)(2,1)S(1)}, bf16[16,2304]{1,0:T(8,128)(2,1)S(1)}, u32[]{:S(2)}, u32[]{:S(2)}) %collective-permute-start.12) | collective-permute-done | bytes 73760 | tf_op jit(solution)/shard_map/reduce/ppermute | solution.py:309
  57.3 6.2 %collective-permute-done.13 = bf16[16,2304]{1,0:T(8,128)(2,1)S(1)} collective-permute-done((bf16[16,2304]{1,0:T(8,128)(2,1)S(1)}, bf16[16,2304]{1,0:T(8,128)(2,1)S(1)}, u32[]{:S(2)}, u32[]{:S(2)}) %collective-permute-start.13) | collective-permute-done | bytes 73760 | tf_op jit(solution)/shard_map/reduce/ppermute | solution.py:309
  63.5 0.0 collective-permute-done.14
  63.5 0.7 %fusion.2 = bf16[16,2304]{1,0:T(8,128)(2,1)} fusion(bf16[16,2304]{1,0:T(8,128)(2,1)S(1)} %collective-permute-done.14, bf16[16,2304]{1,0:T(8,128)(2,1)S(1)} %collective-permute-done.13, bf16[16,2304]{1,0:T(8,128)(2,1)S(1)} %collective-permute-done.12, bf16[4,16,2304]{2,1,0:T(8,128)(2,1)S(1)} %spread.3), kind=kLoop, calls=%fused_computation.3 | loop fusion | flops 294912 | bytes 368640 | tf_op jit(solution)/shard_map/reduce/convert_element_type | solution.py:426
  (2 shorter events, 0.0 us)
Async XLA Ops:
  0.9 7.2 %collective-permute-start = (bf16[16,2304]{1,0:T(8,128)(2,1)S(1)}, bf16[16,2304]{1,0:T(8,128)(2,1)S(1)}, u32[]{:S(2)}, u32[]{:S(2)}) collective-permute-start(bf16[16,2304]{1,0:T(8,128)(2,1)S(1)} %slice.15), channel_id=1, source_target_pairs={{0,32},{32,64},{64,96},{96,128},{128,160},{160,192},{192,224},{224... | collective-permute-start | bytes 221192 | tf_op jit(solution)/shard_map/rim/ppermute | solution.py:315
  2.9 16.8 %collective-permute-start.2 = (bf16[128,2304]{1,0:T(8,128)(2,1)}, bf16[128,2304]{1,0:T(8,128)(2,1)S(1)}, u32[]{:S(2)}, u32[]{:S(2)}) collective-permute-start(bf16[128,2304]{1,0:T(8,128)(2,1)} %w_one.1), channel_id=1, source_target_pairs={{0,2},{1,3},{2,0},{3,1},{4,6},{5,7},{6,4},{7,5},{8,10},{9,11},{10,... | collective-permute-start | bytes 1769480 | tf_op jit(solution)/shard_map/weights/ppermute | solution.py:309
  5.8 33.7 %collective-permute-start.3 = (bf16[128,2304]{1,0:T(8,128)(2,1)}, bf16[128,2304]{1,0:T(8,128)(2,1)S(1)}, u32[]{:S(2)}, u32[]{:S(2)}) collective-permute-start(bf16[128,2304]{1,0:T(8,128)(2,1)} %w_one.1), channel_id=1, source_target_pairs={{0,4},{1,5},{2,6},{3,7},{4,0},{5,1},{6,2},{7,3},{8,12},{9,13},{10,... | collective-permute-start | bytes 1769480 | tf_op jit(solution)/shard_map/weights/ppermute | solution.py:309
  8.1 0.6 copy-start.3
  8.8 17.2 %copy-start.2 = (f32[128]{0:T(128)S(1)}, f32[128]{0:T(128)}, u32[]{:S(2)}) copy-start(f32[128]{0:T(128)} %param.22) | copy-start | bytes 1540
  19.8 20.7 %collective-permute-start.10 = (bf16[128,2304]{1,0:T(8,128)(2,1)S(1)}, bf16[128,2304]{1,0:T(8,128)(2,1)S(1)}, u32[]{:S(2)}, u32[]{:S(2)}) collective-permute-start(bf16[128,2304]{1,0:T(8,128)(2,1)S(1)} %collective-permute-done.2.refs_0_), channel_id=1, source_target_pairs={{0,4},{1,5},{2,6},{3,7},{4,0},{5,1},{6,2},{7,3},{8,12},{9,13},{10,... | collective-permute-start | bytes 1769480 | tf_op jit(solution)/shard_map/weights/ppermute | solution.py:309
  21.7 17.8 %copy-start.1 = (bf16[128,2304]{1,0:T(8,128)(2,1)S(1)}, bf16[128,2304]{1,0:T(8,128)(2,1)}, u32[]{:S(2)}) copy-start(bf16[128,2304]{1,0:T(8,128)(2,1)} %w_one.1) | copy-start | bytes 1769476
  21.7 12.5 %all-to-all-start = ((bf16[8,128,256]{2,1,0:T(8,128)(2,1)}), bf16[8,128,256]{2,1,0:T(8,128)(2,1)}, u32[]{:S(2)}, u32[]{:S(2)}) async-start(bf16[8,128,256]{2,1,0:T(8,128)(2,1)} %get-tuple-element.22), calls=%async_computation | async-start | bytes 1048576 | tf_op jit(solution)/shard_map/states/all_to_all | solution.py:364
  26.0 1.2 %copy-start = (f32[640,384]{1,0:T(8,128)S(1)}, f32[640,384]{1,0:T(8,128)}, u32[]{:S(2)}) copy-start(f32[640,384]{1,0:T(8,128)} %get-tuple-element.21.pack) | copy-start | bytes 2949124
  36.6 3.8 %collective-permute-start.1 = (bf16[4,4,16,128]{3,2,1,0:T(8,128)(2,1)S(1)}, bf16[4,4,16,128]{3,2,1,0:T(8,128)(2,1)S(1)}, u32[]{:S(2)}, u32[]{:S(2)}) collective-permute-start(bf16[4,4,16,128]{3,2,1,0:T(8,128)(2,1)S(1)} %get-tuple-element.24), channel_id=1, source_target_pairs={{0,1},{1,0},{2,3},{3,2},{4,5},{5,4},{6,7},{7,6},{8,9},{9,8},{10,11... | collective-permute-start | bytes 196616 | tf_op jit(solution)/shard_map/exchange/ppermute | solution.py:309
  39.5 4.0 %collective-permute-start.4 = (bf16[128,2304]{1,0:T(8,128)(2,1)S(1)}, bf16[128,2304]{1,0:T(8,128)(2,1)S(1)}, u32[]{:S(2)}, u32[]{:S(2)}) collective-permute-start(bf16[128,2304]{1,0:T(8,128)(2,1)S(1)} %copy-done.1), channel_id=1, source_target_pairs={{0,1},{1,0},{2,3},{3,2},{4,5},{5,4},{6,7},{7,6},{8,9},{9,8},{10,11... | collective-permute-start | bytes 1769480 | tf_op jit(solution)/shard_map/weights/ppermute | solution.py:309
  39.7 4.8 %collective-permute-start.5 = (bf16[128,2304]{1,0:T(8,128)(2,1)S(1)}, bf16[128,2304]{1,0:T(8,128)(2,1)S(1)}, u32[]{:S(2)}, u32[]{:S(2)}) collective-permute-start(bf16[128,2304]{1,0:T(8,128)(2,1)S(1)} %collective-permute-done.2.refs_0_), channel_id=1, source_target_pairs={{0,1},{1,0},{2,3},{3,2},{4,5},{5,4},{6,7},{7,6},{8,9},{9,8},{10,11... | collective-permute-start | bytes 1769480 | tf_op jit(solution)/shard_map/weights/ppermute | solution.py:309
  40.1 5.1 %collective-permute-start.6 = (bf16[128,2304]{1,0:T(8,128)(2,1)S(1)}, bf16[128,2304]{1,0:T(8,128)(2,1)S(1)}, u32[]{:S(2)}, u32[]{:S(2)}) collective-permute-start(bf16[128,2304]{1,0:T(8,128)(2,1)S(1)} %collective-permute-done.3.refs_2_), channel_id=1, source_target_pairs={{0,1},{1,0},{2,3},{3,2},{4,5},{5,4},{6,7},{7,6},{8,9},{9,8},{10,11... | collective-permute-start | bytes 1769480 | tf_op jit(solution)/shard_map/weights/ppermute | solution.py:309
  40.5 7.4 %collective-permute-start.11 = (bf16[128,2304]{1,0:T(8,128)(2,1)S(1)}, bf16[128,2304]{1,0:T(8,128)(2,1)S(1)}, u32[]{:S(2)}, u32[]{:S(2)}) collective-permute-start(bf16[128,2304]{1,0:T(8,128)(2,1)S(1)} %collective-permute-done.10.refs_4_), channel_id=1, source_target_pairs={{0,1},{1,0},{2,3},{3,2},{4,5},{5,4},{6,7},{7,6},{8,9},{9,8},{10,11... | collective-permute-start | bytes 1769480 | tf_op jit(solution)/shard_map/spread/ppermute | solution.py:309
  40.9 5.2 %collective-permute-start.7 = (bf16[2,4,16,128]{3,2,1,0:T(8,128)(2,1)S(1)}, bf16[2,4,16,128]{3,2,1,0:T(8,128)(2,1)S(1)}, u32[]{:S(2)}, u32[]{:S(2)}) collective-permute-start(bf16[2,4,16,128]{3,2,1,0:T(8,128)(2,1)S(1)} %get-tuple-element.31), channel_id=1, source_target_pairs={{0,6},{1,7},{2,4},{3,5},{4,2},{5,3},{6,0},{7,1},{8,14},{9,15},{10,... | collective-permute-start | bytes 98312 | tf_op jit(solution)/shard_map/exchange/ppermute | solution.py:309
  43.5 4.3 %collective-permute-start.8 = (bf16[2,4,16,128]{3,2,1,0:T(8,128)(2,1)S(1)}, bf16[2,4,16,128]{3,2,1,0:T(8,128)(2,1)S(1)}, u32[]{:S(2)}, u32[]{:S(2)}) collective-permute-start(bf16[2,4,16,128]{3,2,1,0:T(8,128)(2,1)S(1)} %get-tuple-element.32), channel_id=1, source_target_pairs={{0,2},{1,3},{2,0},{3,1},{4,6},{5,7},{6,4},{7,5},{8,10},{9,11},{10,... | collective-permute-start | bytes 98312 | tf_op jit(solution)/shard_map/exchange/ppermute | solution.py:309
  44.5 3.3 %collective-permute-start.9 = (bf16[2,4,16,128]{3,2,1,0:T(8,128)(2,1)S(1)}, bf16[2,4,16,128]{3,2,1,0:T(8,128)(2,1)S(1)}, u32[]{:S(2)}, u32[]{:S(2)}) collective-permute-start(bf16[2,4,16,128]{3,2,1,0:T(8,128)(2,1)S(1)} %get-tuple-element.33), channel_id=1, source_target_pairs={{0,4},{1,5},{2,6},{3,7},{4,0},{5,1},{6,2},{7,3},{8,12},{9,13},{10,... | collective-permute-start | bytes 98312 | tf_op jit(solution)/shard_map/exchange/ppermute | solution.py:309
  48.6 8.7 %collective-permute-start.12 = (bf16[16,2304]{1,0:T(8,128)(2,1)S(1)}, bf16[16,2304]{1,0:T(8,128)(2,1)S(1)}, u32[]{:S(2)}, u32[]{:S(2)}) collective-permute-start(bf16[16,2304]{1,0:T(8,128)(2,1)S(1)} %get-tuple-element.37), channel_id=1, source_target_pairs={{0,16},{1,17},{2,18},{3,19},{4,20},{5,21},{6,22},{7,23},{8,24},{9,... | collective-permute-start | bytes 221192 | tf_op jit(solution)/shard_map/reduce/ppermute | solution.py:309
  55.4 8.1 %collective-permute-start.13 = (bf16[16,2304]{1,0:T(8,128)(2,1)S(1)}, bf16[16,2304]{1,0:T(8,128)(2,1)S(1)}, u32[]{:S(2)}, u32[]{:S(2)}) collective-permute-start(bf16[16,2304]{1,0:T(8,128)(2,1)S(1)} %get-tuple-element.39), channel_id=1, source_target_pairs={{0,8},{1,9},{2,10},{3,11},{4,12},{5,13},{6,14},{7,15},{8,0},{9,1},... | collective-permute-start | bytes 221192 | tf_op jit(solution)/shard_map/reduce/ppermute | solution.py:309
  56.6 6.9 %collective-permute-start.14 = (bf16[16,2304]{1,0:T(8,128)(2,1)S(1)}, bf16[16,2304]{1,0:T(8,128)(2,1)S(1)}, u32[]{:S(2)}, u32[]{:S(2)}) collective-permute-start(bf16[16,2304]{1,0:T(8,128)(2,1)S(1)} %get-tuple-element.38), channel_id=1, source_target_pairs={{0,24},{1,25},{2,26},{3,27},{4,28},{5,29},{6,30},{7,31},{8,16},{9,... | collective-permute-start | bytes 221192 | tf_op jit(solution)/shard_map/reduce/ppermute | solution.py:309

commit v4 on v3

--- a/solution.py
+++ b/solution.py
@@ -305,6 +305,15 @@
     shape = jax.ShapeDtypeStruct
     dma = pltpu.SemaphoreType.DMA
 
+    def across(value):
+        half = ctx_count // 2
+        pairs = [
+            (c * head_count + h, ((c + half) % ctx_count) * head_count + (h ^ 2))
+            for c in range(ctx_count)
+            for h in range(head_count)
+        ]
+        return lax.ppermute(value, ("ctx", "head"), pairs)
+
     def flip(value, mask):
         return lax.ppermute(value, "head", [(h, h ^ mask) for h in range(head_count)])
 
@@ -315,7 +324,7 @@
         rim = lax.ppermute(edge, "ctx", [(i, (i + 1) % ctx_count) for i in range(ctx_count)])
     (w_sent,) = after((w_out,), edge)
     with jax.named_scope("weights"):
-        w_far, w_next = flip(w_sent, 2), flip(w_sent, 4)
+        w_far, w_next = across(w_sent), flip(w_sent, 4)
     with jax.named_scope("front"):
         pack, sends = pl.pallas_call(
             front,
@@ -372,7 +381,7 @@
             out_specs=VMEM,
             out_shape=shape(pack.shape, F32),
             compiler_params=LIMIT,
-            cost_estimate=cost(0.5, 0),
+            cost_estimate=cost(0.5, 0.5),
         )(pack, norm_gain.reshape(1, head))
     w_late, w_near, w_mine = after((w_far, w_next, w_out), staged)
     with jax.named_scope("weights"):
@@ -385,7 +394,7 @@
             out_shape=[shape((SUBS // 2, zs, 16, head), BF16)] * 2,
             scratch_shapes=[pltpu.VMEM((zs, SUBS // 2, 2, 16, head), BF16)],
             compiler_params=LIMIT,
-            cost_estimate=cost(2, 0.5),
+            cost_estimate=cost(2, 2),
         )(staged, states)
     with jax.named_scope("exchange"):
         sibling = flip(other, 1)
@@ -395,7 +404,7 @@
             out_specs=[VMEM] * 4,
             out_shape=[shape((2, zs, 16, head), BF16)] * 4,
             compiler_params=LIMIT,
-            cost_estimate=cost(0.5, 0),
+            cost_estimate=cost(0.5, 0.5),
         )(own, sibling)
         got = {f: flip(sent[f - 1], 2 * f) for f in (3, 1, 2)}
     with jax.named_scope("spread"):
@@ -406,7 +415,7 @@
             out_shape=[shape((4 * head, model), BF16), shape((zs * 16, model), F32)],
             scratch_shapes=[pltpu.VMEM((zs * 16, 2 * head), BF16)],
             compiler_params=LIMIT,
-            cost_estimate=cost(2, 0),
+            cost_estimate=cost(2, 2),
         )(kept, w_out, w_core, w_far, w_far_core, w_next, w_next_core)
         (w_late,) = after((w_both,), kept)
         w_both_core = flip(w_late, 1)
@@ -417,7 +426,7 @@
             out_shape=shape((zs, 16, model), BF16),
             scratch_shapes=[pltpu.VMEM((3, zs * 16, 2 * head), BF16)],
             compiler_params=LIMIT,
-            cost_estimate=cost(1, 0),
+            cost_estimate=cost(1, 1),
         )(begun, got[3], got[1], got[2], held, w_both, w_both_core)
     with jax.named_scope("reduce"):
         total = parts[0].astype(F32)

time: 64.6 us -> 61.9 us (0.958)
  waiting for transfers between devices: 17.4 us -> 12.5 us
  starting transfers between devices: 29 us -> 30.5 us
  Pallas kernels: 13.6 us -> 14.3 us
    all_to_all x1, waiting for transfers between devices: 6.93 us -> 3.49 us  [on_device(): states = lax.all_to_all(sends, 'ctx', 0, 0, tiled=True)]
    ppermute x0 -> x1, starting transfers between devices: none -> 2.73 us  [across(): return lax.ppermute(value, ('ctx', 'head'), pairs)]
    pallas_call x1, Pallas kernels: 0.4 us -> 2.08 us  [on_device(): pl.pallas_call(spread, in_specs=[VMEM] * 7, out_specs=[VMEM] * 2, out_sha...]
    ppermute x14 -> x13, waiting for transfers between devices: 10.4 us -> 9.04 us  [flip(): lax.ppermute(value, 'head', [(h, h ^ mask) for h in range(head_count)])]
    pallas_call x1, Pallas kernels: 2.37 us -> 1.33 us  [on_device(): pl.pallas_call(finish, in_specs=[VMEM] * 2, out_specs=[VMEM] * 2, out_sha...]
    ppermute x14 -> x13, starting transfers between devices: 22.7 us -> 21.9 us  [flip(): lax.ppermute(value, 'head', [(h, h ^ mask) for h in range(head_count)])]
  transfers between devices with their start and end apart: 16 -> 16, of which waited for: 7 -> 5; matrix products, arithmetic and copies ran while one was open for 0% -> 0% of each run, Pallas kernels for 20% -> 22%
where the time goes in v4:
time: 61.9 us; the launch traced here: 61.5 us
  starting transfers between devices  30.5 us (49%)
  Pallas kernels  14.3 us (23%)
  waiting for transfers between devices  12.5 us (20%)
  local copies, waits for them, and re-layouts  2.75 us (4%)
  between operations  0.75 us (1%)
  other arithmetic  0.68 us (1%)
    ppermute x13, starting transfers between devices, flip(): lax.ppermute(value, 'head', [(h, h ^ mask) for h in range(head_count)])  21.9 us
    pallas_call x1, Pallas kernels, on_device(): pl.pallas_call(front, in_specs=[HBM] * 11, out_specs=[HBM] * 2, out_shape...  10 us
    ppermute x13, waiting for transfers between devices, flip(): lax.ppermute(value, 'head', [(h, h ^ mask) for h in range(head_count)])  9.04 us
    all_to_all x1, starting transfers between devices, on_device(): states = lax.all_to_all(sends, 'ctx', 0, 0, tiled=True)  3.87 us
    all_to_all x1, waiting for transfers between devices, on_device(): states = lax.all_to_all(sends, 'ctx', 0, 0, tiled=True)  3.49 us
    ppermute x1, starting transfers between devices, across(): return lax.ppermute(value, ('ctx', 'head'), pairs)  2.73 us
    pallas_call x1, Pallas kernels, on_device(): pl.pallas_call(spread, in_specs=[VMEM] * 7, out_specs=[VMEM] * 2, out_sha...  2.08 us
    ppermute x1, starting transfers between devices, on_device(): lax.ppermute(edge, 'ctx', [(i, (i + 1) % ctx_count) for i in range(ctx_co...  2.04 us
  transfers between devices with their start and end apart: 16, of which 5 were waited for; matrix products, arithmetic and copies ran while one was open for 0% of the time, Pallas kernels for 22%

profile of v4, /device:TPU:1, one launch (start us, length us, event | category | flops | bytes accessed | tf_op | source)
XLA Modules:
  0.0 61.5 jit_solution(9296195427773333693)
XLA Ops:
  0.0 0.9 %slice.15 = bf16[16,2304]{1,0:T(8,128)(2,1)S(1)} slice(bf16[512,2304]{1,0:T(8,128)(2,1)} %tokens_hbm.1), slice={[496:512], [0:2304]} | slice | bytes 147456 | tf_op jit(solution)/shard_map/slice | solution.py:322
  0.9 2.0 %collective-permute-start = (bf16[16,2304]{1,0:T(8,128)(2,1)S(1)}, bf16[16,2304]{1,0:T(8,128)(2,1)S(1)}, u32[]{:S(2)}, u32[]{:S(2)}) collective-permute-start(bf16[16,2304]{1,0:T(8,128)(2,1)S(1)} %slice.15), channel_id=1, source_target_pairs={{0,32},{32,64},{64,96},{96,128},{128,160},{160,192},{192,224},{224... | collective-permute-start | bytes 221192 | tf_op jit(solution)/shard_map/rim/ppermute | solution.py:324
  2.9 2.7 %collective-permute-start.2 = (bf16[128,2304]{1,0:T(8,128)(2,1)}, bf16[128,2304]{1,0:T(8,128)(2,1)S(1)}, u32[]{:S(2)}, u32[]{:S(2)}) collective-permute-start(bf16[128,2304]{1,0:T(8,128)(2,1)} %w_one.1), channel_id=1, source_target_pairs={{0,130},{1,131},{2,128},{3,129},{4,134},{5,135},{6,132},{7,133},{8... | collective-permute-start | bytes 1769480 | tf_op jit(solution)/shard_map/weights/ppermute | solution.py:315
  5.7 1.6 %collective-permute-start.3 = (bf16[128,2304]{1,0:T(8,128)(2,1)}, bf16[128,2304]{1,0:T(8,128)(2,1)}, u32[]{:S(2)}, u32[]{:S(2)}) collective-permute-start(bf16[128,2304]{1,0:T(8,128)(2,1)} %w_one.1), channel_id=1, source_target_pairs={{0,4},{1,5},{2,6},{3,7},{4,0},{5,1},{6,2},{7,3},{8,12},{9,13},{10,... | collective-permute-start | bytes 1769480 | tf_op jit(solution)/shard_map/weights/ppermute | solution.py:318
  8.0 0.0 collective-permute-done.rim_hbm
  8.0 0.0 copy-start.3
  8.0 0.6 %copy-done.3 = bf16[16,2304]{1,0:T(8,128)(2,1)} copy-done((bf16[16,2304]{1,0:T(8,128)(2,1)}, bf16[16,2304]{1,0:T(8,128)(2,1)S(1)}, u32[]{:S(2)}) %copy-start.3) | copy-done | bytes 73752
  8.6 0.0 copy-start.1
  8.6 10.0 %front.1 = (f32[640,384]{1,0:T(8,128)}, bf16[8,128,256]{2,1,0:T(8,128)(2,1)}) custom-call(bf16[512,2304]{1,0:T(8,128)(2,1)} %tokens_hbm.1, bf16[16,2304]{1,0:T(8,128)(2,1)} %copy-done.3, f32[1,1]{1,0:T(1,128)} %bitcast.17.alog_hbm, bf16[3,2304,128]{2,1,0:T(8,128)(2,1)} %bitcast.19, bf16[2304,128]{1,0:T(8,128)(2,1)} %f_down_hbm.1, ...), custom_call_target="tpu_custom_call" | custom-call | flops 40000000000 | bytes 33210000 | tf_op jit(solution)/shard_map/front/pallas_call | solution.py:329
  18.6 0.0 copy-start.2
  18.7 3.9 %all-to-all-start = ((bf16[8,128,256]{2,1,0:T(8,128)(2,1)}), bf16[8,128,256]{2,1,0:T(8,128)(2,1)S(1)}, u32[]{:S(2)}, u32[]{:S(2)}) async-start(bf16[8,128,256]{2,1,0:T(8,128)(2,1)} %get-tuple-element.22), calls=%async_computation | async-start | bytes 1048576 | tf_op jit(solution)/shard_map/states/all_to_all | solution.py:373
  22.5 0.0 collective-permute-done.2.refs_0_
  22.5 0.6 collective-permute-start.10
  23.1 0.0 copy-done.1
  23.1 0.0 copy-start
  23.1 1.2 %copy-done = f32[640,384]{1,0:T(8,128)S(1)} copy-done((f32[640,384]{1,0:T(8,128)S(1)}, f32[640,384]{1,0:T(8,128)}, u32[]{:S(2)}) %copy-start) | copy-done | bytes 983064
  24.3 0.1 stage.1.pack
  24.4 0.0 collective-permute-done.3.refs_2_
  24.4 0.0 copy-done.2
  24.4 2.2 %collective-permute-start.4 = (bf16[128,2304]{1,0:T(8,128)(2,1)S(1)}, bf16[128,2304]{1,0:T(8,128)(2,1)}, u32[]{:S(2)}, u32[]{:S(2)}) collective-permute-start(bf16[128,2304]{1,0:T(8,128)(2,1)S(1)} %copy-done.2), channel_id=1, source_target_pairs={{0,1},{1,0},{2,3},{3,2},{4,5},{5,4},{6,7},{7,6},{8,9},{9,8},{10,11... | collective-permute-start | bytes 1769480 | tf_op jit(solution)/shard_map/weights/ppermute | solution.py:318
  26.6 0.1 collective-permute-start.5
  26.7 0.4 collective-permute-start.6
  27.1 3.5 %all-to-all-done.states = bf16[8,128,256]{2,1,0:T(8,128)(2,1)S(1)} async-done(((bf16[8,128,256]{2,1,0:T(8,128)(2,1)}), bf16[8,128,256]{2,1,0:T(8,128)(2,1)S(1)}, u32[]{:S(2)}, u32[]{:S(2)}) %all-to-all-start) | async-done | bytes 524320 | tf_op jit(solution)/shard_map/states/all_to_all | solution.py:373
  30.6 1.3 %finish.1 = (bf16[4,4,16,128]{3,2,1,0:T(8,128)(2,1)S(1)}, bf16[4,4,16,128]{3,2,1,0:T(8,128)(2,1)S(1)}) custom-call(f32[640,384]{1,0:T(8,128)S(1)} %stage.1.pack, bf16[8,128,256]{2,1,0:T(8,128)(2,1)S(1)} %all-to-all-done.states), custom_call_target="tpu_custom_call" | custom-call | flops 2000000000 | bytes 7380000 | tf_op jit(solution)/shard_map/finish/pallas_call | solution.py:390
  31.9 3.1 %collective-permute-start.1 = (bf16[4,4,16,128]{3,2,1,0:T(8,128)(2,1)S(1)}, bf16[4,4,16,128]{3,2,1,0:T(8,128)(2,1)S(1)}, u32[]{:S(2)}, u32[]{:S(2)}) collective-permute-start(bf16[4,4,16,128]{3,2,1,0:T(8,128)(2,1)S(1)} %get-tuple-element.24), channel_id=1, source_target_pairs={{0,1},{1,0},{2,3},{3,2},{4,5},{5,4},{6,7},{7,6},{8,9},{9,8},{10,11... | collective-permute-start | bytes 196616 | tf_op jit(solution)/shard_map/exchange/ppermute | solution.py:318
  35.0 0.9 %collective-permute-done.1.sibling = bf16[4,4,16,128]{3,2,1,0:T(8,128)(2,1)S(1)} collective-permute-done((bf16[4,4,16,128]{3,2,1,0:T(8,128)(2,1)S(1)}, bf16[4,4,16,128]{3,2,1,0:T(8,128)(2,1)S(1)}, u32[]{:S(2)}, u32[]{:S(2)}) %collective-permute-start.1) | collective-permute-done | bytes 65568 | tf_op jit(solution)/shard_map/exchange/ppermute | solution.py:318
  35.9 0.0 collective-permute-done.10.refs_4_
  35.9 2.4 %collective-permute-start.11 = (bf16[128,2304]{1,0:T(8,128)(2,1)S(1)}, bf16[128,2304]{1,0:T(8,128)(2,1)S(1)}, u32[]{:S(2)}, u32[]{:S(2)}) collective-permute-start(bf16[128,2304]{1,0:T(8,128)(2,1)S(1)} %collective-permute-done.10.refs_4_), channel_id=1, source_target_pairs={{0,1},{1,0},{2,3},{3,2},{4,5},{5,4},{6,7},{7,6},{8,9},{9,8},{10,11... | collective-permute-start | bytes 1769480 | tf_op jit(solution)/shard_map/spread/ppermute | solution.py:318
  38.4 3.1 %collective-permute-start.7 = (bf16[2,4,16,128]{3,2,1,0:T(8,128)(2,1)S(1)}, bf16[2,4,16,128]{3,2,1,0:T(8,128)(2,1)S(1)}, u32[]{:S(2)}, u32[]{:S(2)}) collective-permute-start(bf16[2,4,16,128]{3,2,1,0:T(8,128)(2,1)S(1)} %get-tuple-element.31), channel_id=1, source_target_pairs={{0,6},{1,7},{2,4},{3,5},{4,2},{5,3},{6,0},{7,1},{8,14},{9,15},{10,... | collective-permute-start | bytes 98312 | tf_op jit(solution)/shard_map/exchange/ppermute | solution.py:318
  41.5 0.0 collective-permute-done.4.w_two
  41.5 0.1 collective-permute-start.8
  41.5 0.0 collective-permute-done.5.refs_1_
  41.5 1.0 %collective-permute-start.9 = (bf16[2,4,16,128]{3,2,1,0:T(8,128)(2,1)S(1)}, bf16[2,4,16,128]{3,2,1,0:T(8,128)(2,1)S(1)}, u32[]{:S(2)}, u32[]{:S(2)}) collective-permute-start(bf16[2,4,16,128]{3,2,1,0:T(8,128)(2,1)S(1)} %get-tuple-element.33), channel_id=1, source_target_pairs={{0,4},{1,5},{2,6},{3,7},{4,0},{5,1},{6,2},{7,3},{8,12},{9,13},{10,... | collective-permute-start | bytes 98312 | tf_op jit(solution)/shard_map/exchange/ppermute | solution.py:318
  42.5 0.0 collective-permute-done.6.refs_3_
  42.5 2.1 %spread.2 = (bf16[512,2304]{1,0:T(8,128)(2,1)S(1)}, f32[64,2304]{1,0:T(8,128)S(1)}) custom-call(bf16[2,4,16,128]{3,2,1,0:T(8,128)(2,1)S(1)} %get-tuple-element.25.part, bf16[128,2304]{1,0:T(8,128)(2,1)S(1)} %copy-done.2, bf16[128,2304]{1,0:T(8,128)(2,1)} %collective-permute-done.4.w_two, bf16[128,2304]{1,0:T(8,128)(2,1)S(1)} %collective-permute-done.2.refs_0_, ...), custom_call_target="tpu_custom_call" | custom-call | flops 2000000000 | bytes 7380000 | tf_op jit(solution)/shard_map/spread/pallas_call | solution.py:411
  44.6 0.0 collective-permute-done.7.refs_0_
  44.6 1.1 %collective-permute-done.8.refs_1_ = bf16[2,4,16,128]{3,2,1,0:T(8,128)(2,1)S(1)} collective-permute-done((bf16[2,4,16,128]{3,2,1,0:T(8,128)(2,1)S(1)}, bf16[2,4,16,128]{3,2,1,0:T(8,128)(2,1)S(1)}, u32[]{:S(2)}, u32[]{:S(2)}) %collective-permute-start.8) | collective-permute-done | bytes 32800 | tf_op jit(solution)/shard_map/exchange/ppermute | solution.py:318
  45.8 0.0 collective-permute-done.9.refs_2_
  45.8 0.0 collective-permute-done.11.refs_5_
  45.8 0.7 %spread.3 = bf16[4,16,2304]{2,1,0:T(8,128)(2,1)S(1)} custom-call(f32[64,2304]{1,0:T(8,128)S(1)} %get-tuple-element.30.begun, bf16[2,4,16,128]{3,2,1,0:T(8,128)(2,1)S(1)} %collective-permute-done.7.refs_0_, bf16[2,4,16,128]{3,2,1,0:T(8,128)(2,1)S(1)} %collective-permute-done.8.refs_1_, bf16[2,4,16,128]{3,2,1,0:T(8,128)(2,1)S(1)} %collective-permute-done.9.refs_2_, ...), custom_call_target="tpu_custom_call" | custom-call | flops 1000000000 | bytes 3690000 | tf_op jit(solution)/shard_map/spread/pallas_call | solution.py:422
  46.5 6.1 %collective-permute-start.12 = (bf16[16,2304]{1,0:T(8,128)(2,1)S(1)}, bf16[16,2304]{1,0:T(8,128)(2,1)S(1)}, u32[]{:S(2)}, u32[]{:S(2)}) collective-permute-start(bf16[16,2304]{1,0:T(8,128)(2,1)S(1)} %get-tuple-element.37), channel_id=1, source_target_pairs={{0,16},{1,17},{2,18},{3,19},{4,20},{5,21},{6,22},{7,23},{8,24},{9,... | collective-permute-start | bytes 221192 | tf_op jit(solution)/shard_map/reduce/ppermute | solution.py:318
  52.6 1.2 %collective-permute-start.13 = (bf16[16,2304]{1,0:T(8,128)(2,1)S(1)}, bf16[16,2304]{1,0:T(8,128)(2,1)S(1)}, u32[]{:S(2)}, u32[]{:S(2)}) collective-permute-start(bf16[16,2304]{1,0:T(8,128)(2,1)S(1)} %get-tuple-element.39), channel_id=1, source_target_pairs={{0,8},{1,9},{2,10},{3,11},{4,12},{5,13},{6,14},{7,15},{8,0},{9,1},... | collective-permute-start | bytes 221192 | tf_op jit(solution)/shard_map/reduce/ppermute | solution.py:318
  53.8 0.0 collective-permute-start.14
  53.8 0.6 collective-permute-done.12
  54.4 6.4 %collective-permute-done.13 = bf16[16,2304]{1,0:T(8,128)(2,1)S(1)} collective-permute-done((bf16[16,2304]{1,0:T(8,128)(2,1)S(1)}, bf16[16,2304]{1,0:T(8,128)(2,1)S(1)}, u32[]{:S(2)}, u32[]{:S(2)}) %collective-permute-start.13) | collective-permute-done | bytes 73760 | tf_op jit(solution)/shard_map/reduce/ppermute | solution.py:318
  60.8 0.0 collective-permute-done.14
  60.8 0.7 %fusion.2 = bf16[16,2304]{1,0:T(8,128)(2,1)} fusion(bf16[16,2304]{1,0:T(8,128)(2,1)S(1)} %collective-permute-done.14, bf16[16,2304]{1,0:T(8,128)(2,1)S(1)} %collective-permute-done.13, bf16[16,2304]{1,0:T(8,128)(2,1)S(1)} %collective-permute-done.12, bf16[4,16,2304]{2,1,0:T(8,128)(2,1)S(1)} %spread.3), kind=kLoop, calls=%fused_computation.3 | loop fusion | flops 294912 | bytes 368640 | tf_op jit(solution)/shard_map/reduce/convert_element_type | solution.py:435
  (2 shorter events, 0.0 us)
Async XLA Ops:
  0.9 7.1 %collective-permute-start = (bf16[16,2304]{1,0:T(8,128)(2,1)S(1)}, bf16[16,2304]{1,0:T(8,128)(2,1)S(1)}, u32[]{:S(2)}, u32[]{:S(2)}) collective-permute-start(bf16[16,2304]{1,0:T(8,128)(2,1)S(1)} %slice.15), channel_id=1, source_target_pairs={{0,32},{32,64},{64,96},{96,128},{128,160},{160,192},{192,224},{224... | collective-permute-start | bytes 221192 | tf_op jit(solution)/shard_map/rim/ppermute | solution.py:324
  2.9 19.6 %collective-permute-start.2 = (bf16[128,2304]{1,0:T(8,128)(2,1)}, bf16[128,2304]{1,0:T(8,128)(2,1)S(1)}, u32[]{:S(2)}, u32[]{:S(2)}) collective-permute-start(bf16[128,2304]{1,0:T(8,128)(2,1)} %w_one.1), channel_id=1, source_target_pairs={{0,130},{1,131},{2,128},{3,129},{4,134},{5,135},{6,132},{7,133},{8... | collective-permute-start | bytes 1769480 | tf_op jit(solution)/shard_map/weights/ppermute | solution.py:315
  5.7 18.7 %collective-permute-start.3 = (bf16[128,2304]{1,0:T(8,128)(2,1)}, bf16[128,2304]{1,0:T(8,128)(2,1)}, u32[]{:S(2)}, u32[]{:S(2)}) collective-permute-start(bf16[128,2304]{1,0:T(8,128)(2,1)} %w_one.1), channel_id=1, source_target_pairs={{0,4},{1,5},{2,6},{3,7},{4,0},{5,1},{6,2},{7,3},{8,12},{9,13},{10,... | collective-permute-start | bytes 1769480 | tf_op jit(solution)/shard_map/weights/ppermute | solution.py:318
  8.0 0.6 %copy-start.3 = (bf16[16,2304]{1,0:T(8,128)(2,1)}, bf16[16,2304]{1,0:T(8,128)(2,1)S(1)}, u32[]{:S(2)}) copy-start(bf16[16,2304]{1,0:T(8,128)(2,1)S(1)} %collective-permute-done.rim_hbm) | copy-start | bytes 221188
  8.6 14.5 %copy-start.1 = (f32[128]{0:T(128)S(1)}, f32[128]{0:T(128)}, u32[]{:S(2)}) copy-start(f32[128]{0:T(128)} %param.22) | copy-start | bytes 1540
  18.6 5.7 %copy-start.2 = (bf16[128,2304]{1,0:T(8,128)(2,1)S(1)}, bf16[128,2304]{1,0:T(8,128)(2,1)}, u32[]{:S(2)}) copy-start(bf16[128,2304]{1,0:T(8,128)(2,1)} %w_one.1) | copy-start | bytes 1769476
  18.7 11.9 %all-to-all-start = ((bf16[8,128,256]{2,1,0:T(8,128)(2,1)}), bf16[8,128,256]{2,1,0:T(8,128)(2,1)S(1)}, u32[]{:S(2)}, u32[]{:S(2)}) async-start(bf16[8,128,256]{2,1,0:T(8,128)(2,1)} %get-tuple-element.22), calls=%async_computation | async-start | bytes 1048576 | tf_op jit(solution)/shard_map/states/all_to_all | solution.py:373
  22.5 13.4 %collective-permute-start.10 = (bf16[128,2304]{1,0:T(8,128)(2,1)S(1)}, bf16[128,2304]{1,0:T(8,128)(2,1)S(1)}, u32[]{:S(2)}, u32[]{:S(2)}) collective-permute-start(bf16[128,2304]{1,0:T(8,128)(2,1)S(1)} %collective-permute-done.2.refs_0_), channel_id=1, source_target_pairs={{0,4},{1,5},{2,6},{3,7},{4,0},{5,1},{6,2},{7,3},{8,12},{9,13},{10,... | collective-permute-start | bytes 1769480 | tf_op jit(solution)/shard_map/weights/ppermute | solution.py:318
  23.1 1.2 %copy-start = (f32[640,384]{1,0:T(8,128)S(1)}, f32[640,384]{1,0:T(8,128)}, u32[]{:S(2)}) copy-start(f32[640,384]{1,0:T(8,128)} %get-tuple-element.21.pack) | copy-start | bytes 2949124
  24.4 17.1 %collective-permute-start.4 = (bf16[128,2304]{1,0:T(8,128)(2,1)S(1)}, bf16[128,2304]{1,0:T(8,128)(2,1)}, u32[]{:S(2)}, u32[]{:S(2)}) collective-permute-start(bf16[128,2304]{1,0:T(8,128)(2,1)S(1)} %copy-done.2), channel_id=1, source_target_pairs={{0,1},{1,0},{2,3},{3,2},{4,5},{5,4},{6,7},{7,6},{8,9},{9,8},{10,11... | collective-permute-start | bytes 1769480 | tf_op jit(solution)/shard_map/weights/ppermute | solution.py:318
  26.6 15.0 %collective-permute-start.5 = (bf16[128,2304]{1,0:T(8,128)(2,1)S(1)}, bf16[128,2304]{1,0:T(8,128)(2,1)}, u32[]{:S(2)}, u32[]{:S(2)}) collective-permute-start(bf16[128,2304]{1,0:T(8,128)(2,1)S(1)} %collective-permute-done.2.refs_0_), channel_id=1, source_target_pairs={{0,1},{1,0},{2,3},{3,2},{4,5},{5,4},{6,7},{7,6},{8,9},{9,8},{10,11... | collective-permute-start | bytes 1769480 | tf_op jit(solution)/shard_map/weights/ppermute | solution.py:318
  26.7 15.8 %collective-permute-start.6 = (bf16[128,2304]{1,0:T(8,128)(2,1)}, bf16[128,2304]{1,0:T(8,128)(2,1)}, u32[]{:S(2)}, u32[]{:S(2)}) collective-permute-start(bf16[128,2304]{1,0:T(8,128)(2,1)} %collective-permute-done.3.refs_2_), channel_id=1, source_target_pairs={{0,1},{1,0},{2,3},{3,2},{4,5},{5,4},{6,7},{7,6},{8,9},{9,8},{10,11... | collective-permute-start | bytes 1769480 | tf_op jit(solution)/shard_map/weights/ppermute | solution.py:318
  31.9 4.0 %collective-permute-start.1 = (bf16[4,4,16,128]{3,2,1,0:T(8,128)(2,1)S(1)}, bf16[4,4,16,128]{3,2,1,0:T(8,128)(2,1)S(1)}, u32[]{:S(2)}, u32[]{:S(2)}) collective-permute-start(bf16[4,4,16,128]{3,2,1,0:T(8,128)(2,1)S(1)} %get-tuple-element.24), channel_id=1, source_target_pairs={{0,1},{1,0},{2,3},{3,2},{4,5},{5,4},{6,7},{7,6},{8,9},{9,8},{10,11... | collective-permute-start | bytes 196616 | tf_op jit(solution)/shard_map/exchange/ppermute | solution.py:318
  35.9 9.8 %collective-permute-start.11 = (bf16[128,2304]{1,0:T(8,128)(2,1)S(1)}, bf16[128,2304]{1,0:T(8,128)(2,1)S(1)}, u32[]{:S(2)}, u32[]{:S(2)}) collective-permute-start(bf16[128,2304]{1,0:T(8,128)(2,1)S(1)} %collective-permute-done.10.refs_4_), channel_id=1, source_target_pairs={{0,1},{1,0},{2,3},{3,2},{4,5},{5,4},{6,7},{7,6},{8,9},{9,8},{10,11... | collective-permute-start | bytes 1769480 | tf_op jit(solution)/shard_map/spread/ppermute | solution.py:318
  38.4 6.3 %collective-permute-start.7 = (bf16[2,4,16,128]{3,2,1,0:T(8,128)(2,1)S(1)}, bf16[2,4,16,128]{3,2,1,0:T(8,128)(2,1)S(1)}, u32[]{:S(2)}, u32[]{:S(2)}) collective-permute-start(bf16[2,4,16,128]{3,2,1,0:T(8,128)(2,1)S(1)} %get-tuple-element.31), channel_id=1, source_target_pairs={{0,6},{1,7},{2,4},{3,5},{4,2},{5,3},{6,0},{7,1},{8,14},{9,15},{10,... | collective-permute-start | bytes 98312 | tf_op jit(solution)/shard_map/exchange/ppermute | solution.py:318
  41.5 4.3 %collective-permute-start.8 = (bf16[2,4,16,128]{3,2,1,0:T(8,128)(2,1)S(1)}, bf16[2,4,16,128]{3,2,1,0:T(8,128)(2,1)S(1)}, u32[]{:S(2)}, u32[]{:S(2)}) collective-permute-start(bf16[2,4,16,128]{3,2,1,0:T(8,128)(2,1)S(1)} %get-tuple-element.32), channel_id=1, source_target_pairs={{0,2},{1,3},{2,0},{3,1},{4,6},{5,7},{6,4},{7,5},{8,10},{9,11},{10,... | collective-permute-start | bytes 98312 | tf_op jit(solution)/shard_map/exchange/ppermute | solution.py:318
  41.5 4.2 %collective-permute-start.9 = (bf16[2,4,16,128]{3,2,1,0:T(8,128)(2,1)S(1)}, bf16[2,4,16,128]{3,2,1,0:T(8,128)(2,1)S(1)}, u32[]{:S(2)}, u32[]{:S(2)}) collective-permute-start(bf16[2,4,16,128]{3,2,1,0:T(8,128)(2,1)S(1)} %get-tuple-element.33), channel_id=1, source_target_pairs={{0,4},{1,5},{2,6},{3,7},{4,0},{5,1},{6,2},{7,3},{8,12},{9,13},{10,... | collective-permute-start | bytes 98312 | tf_op jit(solution)/shard_map/exchange/ppermute | solution.py:318
  46.5 7.9 %collective-permute-start.12 = (bf16[16,2304]{1,0:T(8,128)(2,1)S(1)}, bf16[16,2304]{1,0:T(8,128)(2,1)S(1)}, u32[]{:S(2)}, u32[]{:S(2)}) collective-permute-start(bf16[16,2304]{1,0:T(8,128)(2,1)S(1)} %get-tuple-element.37), channel_id=1, source_target_pairs={{0,16},{1,17},{2,18},{3,19},{4,20},{5,21},{6,22},{7,23},{8,24},{9,... | collective-permute-start | bytes 221192 | tf_op jit(solution)/shard_map/reduce/ppermute | solution.py:318
  52.6 8.2 %collective-permute-start.13 = (bf16[16,2304]{1,0:T(8,128)(2,1)S(1)}, bf16[16,2304]{1,0:T(8,128)(2,1)S(1)}, u32[]{:S(2)}, u32[]{:S(2)}) collective-permute-start(bf16[16,2304]{1,0:T(8,128)(2,1)S(1)} %get-tuple-element.39), channel_id=1, source_target_pairs={{0,8},{1,9},{2,10},{3,11},{4,12},{5,13},{6,14},{7,15},{8,0},{9,1},... | collective-permute-start | bytes 221192 | tf_op jit(solution)/shard_map/reduce/ppermute | solution.py:318
  53.8 7.0 %collective-permute-start.14 = (bf16[16,2304]{1,0:T(8,128)(2,1)S(1)}, bf16[16,2304]{1,0:T(8,128)(2,1)S(1)}, u32[]{:S(2)}, u32[]{:S(2)}) collective-permute-start(bf16[16,2304]{1,0:T(8,128)(2,1)S(1)} %get-tuple-element.38), channel_id=1, source_target_pairs={{0,24},{1,25},{2,26},{3,27},{4,28},{5,29},{6,30},{7,31},{8,16},{9,... | collective-permute-start | bytes 221192 | tf_op jit(solution)/shard_map/reduce/ppermute | solution.py:318

commit v5 on v4

--- a/solution.py
+++ b/solution.py
@@ -394,7 +394,7 @@
             out_shape=[shape((SUBS // 2, zs, 16, head), BF16)] * 2,
             scratch_shapes=[pltpu.VMEM((zs, SUBS // 2, 2, 16, head), BF16)],
             compiler_params=LIMIT,
-            cost_estimate=cost(2, 2),
+            cost_estimate=cost(2, 0),
         )(staged, states)
     with jax.named_scope("exchange"):
         sibling = flip(other, 1)

time: 61.9 us -> 61.9 us (level)
    ppermute x13, waiting for transfers between devices: 9.04 us -> 8.36 us  [flip(): lax.ppermute(value, 'head', [(h, h ^ mask) for h in range(head_count)])]
where the time goes in v5:
time: 61.9 us; the launch traced here: 61.5 us
  starting transfers between devices  30.9 us (50%)
  Pallas kernels  14.3 us (23%)
  waiting for transfers between devices  12.2 us (20%)
  local copies, waits for them, and re-layouts  2.74 us (4%)
  between operations  0.77 us (1%)
  other arithmetic  0.68 us (1%)
    ppermute x13, starting transfers between devices, flip(): lax.ppermute(value, 'head', [(h, h ^ mask) for h in range(head_count)])  22.4 us
    pallas_call x1, Pallas kernels, on_device(): pl.pallas_call(front, in_specs=[HBM] * 11, out_specs=[HBM] * 2, out_shape...  10 us
    ppermute x13, waiting for transfers between devices, flip(): lax.ppermute(value, 'head', [(h, h ^ mask) for h in range(head_count)])  8.36 us
    all_to_all x1, waiting for transfers between devices, on_device(): states = lax.all_to_all(sends, 'ctx', 0, 0, tiled=True)  3.8 us
    all_to_all x1, starting transfers between devices, on_device(): states = lax.all_to_all(sends, 'ctx', 0, 0, tiled=True)  3.73 us
    ppermute x1, starting transfers between devices, across(): return lax.ppermute(value, ('ctx', 'head'), pairs)  2.73 us
    pallas_call x1, Pallas kernels, on_device(): pl.pallas_call(spread, in_specs=[VMEM] * 7, out_specs=[VMEM] * 2, out_sha...  2.09 us
    ppermute x1, starting transfers between devices, on_device(): lax.ppermute(edge, 'ctx', [(i, (i + 1) % ctx_count) for i in range(ctx_co...  2.04 us
  transfers between devices with their start and end apart: 16, of which 5 were waited for; matrix products, arithmetic and copies ran while one was open for 0% of the time, Pallas kernels for 22%

profile of v5, /device:TPU:1, one launch (start us, length us, event | category | flops | bytes accessed | tf_op | source)
XLA Modules:
  0.0 61.5 jit_solution(15223043898059659762)
XLA Ops:
  0.0 0.9 %slice.15 = bf16[16,2304]{1,0:T(8,128)(2,1)S(1)} slice(bf16[512,2304]{1,0:T(8,128)(2,1)} %tokens_hbm.1), slice={[496:512], [0:2304]} | slice | bytes 147456 | tf_op jit(solution)/shard_map/slice | solution.py:322
  0.9 2.0 %collective-permute-start = (bf16[16,2304]{1,0:T(8,128)(2,1)S(1)}, bf16[16,2304]{1,0:T(8,128)(2,1)S(1)}, u32[]{:S(2)}, u32[]{:S(2)}) collective-permute-start(bf16[16,2304]{1,0:T(8,128)(2,1)S(1)} %slice.15), channel_id=1, source_target_pairs={{0,32},{32,64},{64,96},{96,128},{128,160},{160,192},{192,224},{224... | collective-permute-start | bytes 221192 | tf_op jit(solution)/shard_map/rim/ppermute | solution.py:324
  2.9 2.7 %collective-permute-start.2 = (bf16[128,2304]{1,0:T(8,128)(2,1)}, bf16[128,2304]{1,0:T(8,128)(2,1)S(1)}, u32[]{:S(2)}, u32[]{:S(2)}) collective-permute-start(bf16[128,2304]{1,0:T(8,128)(2,1)} %w_one.1), channel_id=1, source_target_pairs={{0,130},{1,131},{2,128},{3,129},{4,134},{5,135},{6,132},{7,133},{8... | collective-permute-start | bytes 1769480 | tf_op jit(solution)/shard_map/weights/ppermute | solution.py:315
  5.7 1.6 %collective-permute-start.3 = (bf16[128,2304]{1,0:T(8,128)(2,1)}, bf16[128,2304]{1,0:T(8,128)(2,1)}, u32[]{:S(2)}, u32[]{:S(2)}) collective-permute-start(bf16[128,2304]{1,0:T(8,128)(2,1)} %w_one.1), channel_id=1, source_target_pairs={{0,4},{1,5},{2,6},{3,7},{4,0},{5,1},{6,2},{7,3},{8,12},{9,13},{10,... | collective-permute-start | bytes 1769480 | tf_op jit(solution)/shard_map/weights/ppermute | solution.py:318
  8.0 0.0 collective-permute-done.rim_hbm
  8.0 0.0 copy-start.3
  8.0 0.6 %copy-done.3 = bf16[16,2304]{1,0:T(8,128)(2,1)} copy-done((bf16[16,2304]{1,0:T(8,128)(2,1)}, bf16[16,2304]{1,0:T(8,128)(2,1)S(1)}, u32[]{:S(2)}) %copy-start.3) | copy-done | bytes 73752
  8.6 0.0 copy-start.1
  8.6 10.0 %front.1 = (f32[640,384]{1,0:T(8,128)}, bf16[8,128,256]{2,1,0:T(8,128)(2,1)}) custom-call(bf16[512,2304]{1,0:T(8,128)(2,1)} %tokens_hbm.1, bf16[16,2304]{1,0:T(8,128)(2,1)} %copy-done.3, f32[1,1]{1,0:T(1,128)} %bitcast.17.alog_hbm, bf16[3,2304,128]{2,1,0:T(8,128)(2,1)} %bitcast.19, bf16[2304,128]{1,0:T(8,128)(2,1)} %f_down_hbm.1, ...), custom_call_target="tpu_custom_call" | custom-call | flops 40000000000 | bytes 33210000 | tf_op jit(solution)/shard_map/front/pallas_call | solution.py:329
  18.6 0.0 copy-start.2
  18.7 0.0 collective-permute-done.2.refs_0_
  18.7 1.3 %collective-permute-start.10 = (bf16[128,2304]{1,0:T(8,128)(2,1)S(1)}, bf16[128,2304]{1,0:T(8,128)(2,1)S(1)}, u32[]{:S(2)}, u32[]{:S(2)}) collective-permute-start(bf16[128,2304]{1,0:T(8,128)(2,1)S(1)} %collective-permute-done.2.refs_0_), channel_id=1, source_target_pairs={{0,4},{1,5},{2,6},{3,7},{4,0},{5,1},{6,2},{7,3},{8,12},{9,13},{10,... | collective-permute-start | bytes 1769480 | tf_op jit(solution)/shard_map/weights/ppermute | solution.py:318
  20.0 3.7 %all-to-all-start = ((bf16[8,128,256]{2,1,0:T(8,128)(2,1)}), bf16[8,128,256]{2,1,0:T(8,128)(2,1)S(1)}, u32[]{:S(2)}, u32[]{:S(2)}) async-start(bf16[8,128,256]{2,1,0:T(8,128)(2,1)} %get-tuple-element.22), calls=%async_computation | async-start | bytes 1048576 | tf_op jit(solution)/shard_map/states/all_to_all | solution.py:373
  23.7 0.0 copy-done.1
  23.7 0.0 copy-start
  23.7 1.2 %copy-done = f32[640,384]{1,0:T(8,128)S(1)} copy-done((f32[640,384]{1,0:T(8,128)S(1)}, f32[640,384]{1,0:T(8,128)}, u32[]{:S(2)}) %copy-start) | copy-done | bytes 983064
  24.9 0.1 stage.1.pack
  25.0 0.0 collective-permute-done.3.refs_2_
  25.0 0.0 copy-done.2
  25.0 2.4 %collective-permute-start.4 = (bf16[128,2304]{1,0:T(8,128)(2,1)S(1)}, bf16[128,2304]{1,0:T(8,128)(2,1)}, u32[]{:S(2)}, u32[]{:S(2)}) collective-permute-start(bf16[128,2304]{1,0:T(8,128)(2,1)S(1)} %copy-done.2), channel_id=1, source_target_pairs={{0,1},{1,0},{2,3},{3,2},{4,5},{5,4},{6,7},{7,6},{8,9},{9,8},{10,11... | collective-permute-start | bytes 1769480 | tf_op jit(solution)/shard_map/weights/ppermute | solution.py:318
  27.5 0.1 collective-permute-start.5
  27.6 0.4 collective-permute-start.6
  28.0 3.8 %all-to-all-done.states = bf16[8,128,256]{2,1,0:T(8,128)(2,1)S(1)} async-done(((bf16[8,128,256]{2,1,0:T(8,128)(2,1)}), bf16[8,128,256]{2,1,0:T(8,128)(2,1)S(1)}, u32[]{:S(2)}, u32[]{:S(2)}) %all-to-all-start) | async-done | bytes 524320 | tf_op jit(solution)/shard_map/states/all_to_all | solution.py:373
  31.8 1.3 %finish.1 = (bf16[4,4,16,128]{3,2,1,0:T(8,128)(2,1)S(1)}, bf16[4,4,16,128]{3,2,1,0:T(8,128)(2,1)S(1)}) custom-call(f32[640,384]{1,0:T(8,128)S(1)} %stage.1.pack, bf16[8,128,256]{2,1,0:T(8,128)(2,1)S(1)} %all-to-all-done.states), custom_call_target="tpu_custom_call" | custom-call | bytes 7380000 | tf_op jit(solution)/shard_map/finish/pallas_call | solution.py:390
  33.1 3.1 %collective-permute-start.1 = (bf16[4,4,16,128]{3,2,1,0:T(8,128)(2,1)S(1)}, bf16[4,4,16,128]{3,2,1,0:T(8,128)(2,1)S(1)}, u32[]{:S(2)}, u32[]{:S(2)}) collective-permute-start(bf16[4,4,16,128]{3,2,1,0:T(8,128)(2,1)S(1)} %get-tuple-element.24), channel_id=1, source_target_pairs={{0,1},{1,0},{2,3},{3,2},{4,5},{5,4},{6,7},{7,6},{8,9},{9,8},{10,11... | collective-permute-start | bytes 196616 | tf_op jit(solution)/shard_map/exchange/ppermute | solution.py:318
  36.2 0.9 %collective-permute-done.1.sibling = bf16[4,4,16,128]{3,2,1,0:T(8,128)(2,1)S(1)} collective-permute-done((bf16[4,4,16,128]{3,2,1,0:T(8,128)(2,1)S(1)}, bf16[4,4,16,128]{3,2,1,0:T(8,128)(2,1)S(1)}, u32[]{:S(2)}, u32[]{:S(2)}) %collective-permute-start.1) | collective-permute-done | bytes 65568 | tf_op jit(solution)/shard_map/exchange/ppermute | solution.py:318
  37.1 0.0 collective-permute-done.10.refs_4_
  37.1 0.4 collective-permute-start.11
  37.6 3.2 %collective-permute-start.7 = (bf16[2,4,16,128]{3,2,1,0:T(8,128)(2,1)S(1)}, bf16[2,4,16,128]{3,2,1,0:T(8,128)(2,1)S(1)}, u32[]{:S(2)}, u32[]{:S(2)}) collective-permute-start(bf16[2,4,16,128]{3,2,1,0:T(8,128)(2,1)S(1)} %get-tuple-element.31), channel_id=1, source_target_pairs={{0,6},{1,7},{2,4},{3,5},{4,2},{5,3},{6,0},{7,1},{8,14},{9,15},{10,... | collective-permute-start | bytes 98312 | tf_op jit(solution)/shard_map/exchange/ppermute | solution.py:318
  40.8 0.0 collective-permute-done.4.w_two
  40.8 0.4 collective-permute-start.8
  41.2 0.0 collective-permute-done.5.refs_1_
  41.2 1.2 %collective-permute-start.9 = (bf16[2,4,16,128]{3,2,1,0:T(8,128)(2,1)S(1)}, bf16[2,4,16,128]{3,2,1,0:T(8,128)(2,1)S(1)}, u32[]{:S(2)}, u32[]{:S(2)}) collective-permute-start(bf16[2,4,16,128]{3,2,1,0:T(8,128)(2,1)S(1)} %get-tuple-element.33), channel_id=1, source_target_pairs={{0,4},{1,5},{2,6},{3,7},{4,0},{5,1},{6,2},{7,3},{8,12},{9,13},{10,... | collective-permute-start | bytes 98312 | tf_op jit(solution)/shard_map/exchange/ppermute | solution.py:318
  42.4 0.0 collective-permute-done.6.refs_3_
  42.4 2.1 %spread.2 = (bf16[512,2304]{1,0:T(8,128)(2,1)S(1)}, f32[64,2304]{1,0:T(8,128)S(1)}) custom-call(bf16[2,4,16,128]{3,2,1,0:T(8,128)(2,1)S(1)} %get-tuple-element.25.part, bf16[128,2304]{1,0:T(8,128)(2,1)S(1)} %copy-done.2, bf16[128,2304]{1,0:T(8,128)(2,1)} %collective-permute-done.4.w_two, bf16[128,2304]{1,0:T(8,128)(2,1)S(1)} %collective-permute-done.2.refs_0_, ...), custom_call_target="tpu_custom_call" | custom-call | flops 2000000000 | bytes 7380000 | tf_op jit(solution)/shard_map/spread/pallas_call | solution.py:411
  44.5 0.0 collective-permute-done.7.refs_0_
  44.5 0.5 collective-permute-done.8.refs_1_
  45.1 0.0 collective-permute-done.9.refs_2_
  45.1 0.0 collective-permute-done.11.refs_5_
  45.1 0.7 %spread.3 = bf16[4,16,2304]{2,1,0:T(8,128)(2,1)S(1)} custom-call(f32[64,2304]{1,0:T(8,128)S(1)} %get-tuple-element.30.begun, bf16[2,4,16,128]{3,2,1,0:T(8,128)(2,1)S(1)} %collective-permute-done.7.refs_0_, bf16[2,4,16,128]{3,2,1,0:T(8,128)(2,1)S(1)} %collective-permute-done.8.refs_1_, bf16[2,4,16,128]{3,2,1,0:T(8,128)(2,1)S(1)} %collective-permute-done.9.refs_2_, ...), custom_call_target="tpu_custom_call" | custom-call | flops 1000000000 | bytes 3690000 | tf_op jit(solution)/shard_map/spread/pallas_call | solution.py:422
  45.8 6.9 %collective-permute-start.12 = (bf16[16,2304]{1,0:T(8,128)(2,1)S(1)}, bf16[16,2304]{1,0:T(8,128)(2,1)S(1)}, u32[]{:S(2)}, u32[]{:S(2)}) collective-permute-start(bf16[16,2304]{1,0:T(8,128)(2,1)S(1)} %get-tuple-element.37), channel_id=1, source_target_pairs={{0,16},{1,17},{2,18},{3,19},{4,20},{5,21},{6,22},{7,23},{8,24},{9,... | collective-permute-start | bytes 221192 | tf_op jit(solution)/shard_map/reduce/ppermute | solution.py:318
  52.7 1.2 %collective-permute-start.13 = (bf16[16,2304]{1,0:T(8,128)(2,1)S(1)}, bf16[16,2304]{1,0:T(8,128)(2,1)S(1)}, u32[]{:S(2)}, u32[]{:S(2)}) collective-permute-start(bf16[16,2304]{1,0:T(8,128)(2,1)S(1)} %get-tuple-element.39), channel_id=1, source_target_pairs={{0,8},{1,9},{2,10},{3,11},{4,12},{5,13},{6,14},{7,15},{8,0},{9,1},... | collective-permute-start | bytes 221192 | tf_op jit(solution)/shard_map/reduce/ppermute | solution.py:318
  53.9 0.0 collective-permute-start.14
  53.9 0.7 %collective-permute-done.12 = bf16[16,2304]{1,0:T(8,128)(2,1)S(1)} collective-permute-done((bf16[16,2304]{1,0:T(8,128)(2,1)S(1)}, bf16[16,2304]{1,0:T(8,128)(2,1)S(1)}, u32[]{:S(2)}, u32[]{:S(2)}) %collective-permute-start.12) | collective-permute-done | bytes 73760 | tf_op jit(solution)/shard_map/reduce/ppermute | solution.py:318
  54.6 6.2 %collective-permute-done.13 = bf16[16,2304]{1,0:T(8,128)(2,1)S(1)} collective-permute-done((bf16[16,2304]{1,0:T(8,128)(2,1)S(1)}, bf16[16,2304]{1,0:T(8,128)(2,1)S(1)}, u32[]{:S(2)}, u32[]{:S(2)}) %collective-permute-start.13) | collective-permute-done | bytes 73760 | tf_op jit(solution)/shard_map/reduce/ppermute | solution.py:318
  60.8 0.0 collective-permute-done.14
  60.8 0.7 %fusion.2 = bf16[16,2304]{1,0:T(8,128)(2,1)} fusion(bf16[16,2304]{1,0:T(8,128)(2,1)S(1)} %collective-permute-done.14, bf16[16,2304]{1,0:T(8,128)(2,1)S(1)} %collective-permute-done.13, bf16[16,2304]{1,0:T(8,128)(2,1)S(1)} %collective-permute-done.12, bf16[4,16,2304]{2,1,0:T(8,128)(2,1)S(1)} %spread.3), kind=kLoop, calls=%fused_computation.3 | loop fusion | flops 294912 | bytes 368640 | tf_op jit(solution)/shard_map/reduce/convert_element_type | solution.py:435
  (2 shorter events, 0.0 us)
Async XLA Ops:
  0.9 7.1 %collective-permute-start = (bf16[16,2304]{1,0:T(8,128)(2,1)S(1)}, bf16[16,2304]{1,0:T(8,128)(2,1)S(1)}, u32[]{:S(2)}, u32[]{:S(2)}) collective-permute-start(bf16[16,2304]{1,0:T(8,128)(2,1)S(1)} %slice.15), channel_id=1, source_target_pairs={{0,32},{32,64},{64,96},{96,128},{128,160},{160,192},{192,224},{224... | collective-permute-start | bytes 221192 | tf_op jit(solution)/shard_map/rim/ppermute | solution.py:324
  2.9 15.7 %collective-permute-start.2 = (bf16[128,2304]{1,0:T(8,128)(2,1)}, bf16[128,2304]{1,0:T(8,128)(2,1)S(1)}, u32[]{:S(2)}, u32[]{:S(2)}) collective-permute-start(bf16[128,2304]{1,0:T(8,128)(2,1)} %w_one.1), channel_id=1, source_target_pairs={{0,130},{1,131},{2,128},{3,129},{4,134},{5,135},{6,132},{7,133},{8... | collective-permute-start | bytes 1769480 | tf_op jit(solution)/shard_map/weights/ppermute | solution.py:315
  5.7 19.3 %collective-permute-start.3 = (bf16[128,2304]{1,0:T(8,128)(2,1)}, bf16[128,2304]{1,0:T(8,128)(2,1)}, u32[]{:S(2)}, u32[]{:S(2)}) collective-permute-start(bf16[128,2304]{1,0:T(8,128)(2,1)} %w_one.1), channel_id=1, source_target_pairs={{0,4},{1,5},{2,6},{3,7},{4,0},{5,1},{6,2},{7,3},{8,12},{9,13},{10,... | collective-permute-start | bytes 1769480 | tf_op jit(solution)/shard_map/weights/ppermute | solution.py:318
  8.0 0.6 %copy-start.3 = (bf16[16,2304]{1,0:T(8,128)(2,1)}, bf16[16,2304]{1,0:T(8,128)(2,1)S(1)}, u32[]{:S(2)}) copy-start(bf16[16,2304]{1,0:T(8,128)(2,1)S(1)} %collective-permute-done.rim_hbm) | copy-start | bytes 221188
  8.6 15.1 %copy-start.1 = (f32[128]{0:T(128)S(1)}, f32[128]{0:T(128)}, u32[]{:S(2)}) copy-start(f32[128]{0:T(128)} %param.22) | copy-start | bytes 1540
  18.6 6.4 %copy-start.2 = (bf16[128,2304]{1,0:T(8,128)(2,1)S(1)}, bf16[128,2304]{1,0:T(8,128)(2,1)}, u32[]{:S(2)}) copy-start(bf16[128,2304]{1,0:T(8,128)(2,1)} %w_one.1) | copy-start | bytes 1769476
  18.7 18.4 %collective-permute-start.10 = (bf16[128,2304]{1,0:T(8,128)(2,1)S(1)}, bf16[128,2304]{1,0:T(8,128)(2,1)S(1)}, u32[]{:S(2)}, u32[]{:S(2)}) collective-permute-start(bf16[128,2304]{1,0:T(8,128)(2,1)S(1)} %collective-permute-done.2.refs_0_), channel_id=1, source_target_pairs={{0,4},{1,5},{2,6},{3,7},{4,0},{5,1},{6,2},{7,3},{8,12},{9,13},{10,... | collective-permute-start | bytes 1769480 | tf_op jit(solution)/shard_map/weights/ppermute | solution.py:318
  20.0 11.8 %all-to-all-start = ((bf16[8,128,256]{2,1,0:T(8,128)(2,1)}), bf16[8,128,256]{2,1,0:T(8,128)(2,1)S(1)}, u32[]{:S(2)}, u32[]{:S(2)}) async-start(bf16[8,128,256]{2,1,0:T(8,128)(2,1)} %get-tuple-element.22), calls=%async_computation | async-start | bytes 1048576 | tf_op jit(solution)/shard_map/states/all_to_all | solution.py:373
  23.7 1.2 %copy-start = (f32[640,384]{1,0:T(8,128)S(1)}, f32[640,384]{1,0:T(8,128)}, u32[]{:S(2)}) copy-start(f32[640,384]{1,0:T(8,128)} %get-tuple-element.21.pack) | copy-start | bytes 2949124
  25.0 15.8 %collective-permute-start.4 = (bf16[128,2304]{1,0:T(8,128)(2,1)S(1)}, bf16[128,2304]{1,0:T(8,128)(2,1)}, u32[]{:S(2)}, u32[]{:S(2)}) collective-permute-start(bf16[128,2304]{1,0:T(8,128)(2,1)S(1)} %copy-done.2), channel_id=1, source_target_pairs={{0,1},{1,0},{2,3},{3,2},{4,5},{5,4},{6,7},{7,6},{8,9},{9,8},{10,11... | collective-permute-start | bytes 1769480 | tf_op jit(solution)/shard_map/weights/ppermute | solution.py:318
  27.5 13.8 %collective-permute-start.5 = (bf16[128,2304]{1,0:T(8,128)(2,1)S(1)}, bf16[128,2304]{1,0:T(8,128)(2,1)}, u32[]{:S(2)}, u32[]{:S(2)}) collective-permute-start(bf16[128,2304]{1,0:T(8,128)(2,1)S(1)} %collective-permute-done.2.refs_0_), channel_id=1, source_target_pairs={{0,1},{1,0},{2,3},{3,2},{4,5},{5,4},{6,7},{7,6},{8,9},{9,8},{10,11... | collective-permute-start | bytes 1769480 | tf_op jit(solution)/shard_map/weights/ppermute | solution.py:318
  27.6 14.9 %collective-permute-start.6 = (bf16[128,2304]{1,0:T(8,128)(2,1)}, bf16[128,2304]{1,0:T(8,128)(2,1)}, u32[]{:S(2)}, u32[]{:S(2)}) collective-permute-start(bf16[128,2304]{1,0:T(8,128)(2,1)} %collective-permute-done.3.refs_2_), channel_id=1, source_target_pairs={{0,1},{1,0},{2,3},{3,2},{4,5},{5,4},{6,7},{7,6},{8,9},{9,8},{10,11... | collective-permute-start | bytes 1769480 | tf_op jit(solution)/shard_map/weights/ppermute | solution.py:318
  33.1 4.0 %collective-permute-start.1 = (bf16[4,4,16,128]{3,2,1,0:T(8,128)(2,1)S(1)}, bf16[4,4,16,128]{3,2,1,0:T(8,128)(2,1)S(1)}, u32[]{:S(2)}, u32[]{:S(2)}) collective-permute-start(bf16[4,4,16,128]{3,2,1,0:T(8,128)(2,1)S(1)} %get-tuple-element.24), channel_id=1, source_target_pairs={{0,1},{1,0},{2,3},{3,2},{4,5},{5,4},{6,7},{7,6},{8,9},{9,8},{10,11... | collective-permute-start | bytes 196616 | tf_op jit(solution)/shard_map/exchange/ppermute | solution.py:318
  37.1 7.9 %collective-permute-start.11 = (bf16[128,2304]{1,0:T(8,128)(2,1)S(1)}, bf16[128,2304]{1,0:T(8,128)(2,1)S(1)}, u32[]{:S(2)}, u32[]{:S(2)}) collective-permute-start(bf16[128,2304]{1,0:T(8,128)(2,1)S(1)} %collective-permute-done.10.refs_4_), channel_id=1, source_target_pairs={{0,1},{1,0},{2,3},{3,2},{4,5},{5,4},{6,7},{7,6},{8,9},{9,8},{10,11... | collective-permute-start | bytes 1769480 | tf_op jit(solution)/shard_map/spread/ppermute | solution.py:318
  37.6 6.9 %collective-permute-start.7 = (bf16[2,4,16,128]{3,2,1,0:T(8,128)(2,1)S(1)}, bf16[2,4,16,128]{3,2,1,0:T(8,128)(2,1)S(1)}, u32[]{:S(2)}, u32[]{:S(2)}) collective-permute-start(bf16[2,4,16,128]{3,2,1,0:T(8,128)(2,1)S(1)} %get-tuple-element.31), channel_id=1, source_target_pairs={{0,6},{1,7},{2,4},{3,5},{4,2},{5,3},{6,0},{7,1},{8,14},{9,15},{10,... | collective-permute-start | bytes 98312 | tf_op jit(solution)/shard_map/exchange/ppermute | solution.py:318
  40.8 4.3 %collective-permute-start.8 = (bf16[2,4,16,128]{3,2,1,0:T(8,128)(2,1)S(1)}, bf16[2,4,16,128]{3,2,1,0:T(8,128)(2,1)S(1)}, u32[]{:S(2)}, u32[]{:S(2)}) collective-permute-start(bf16[2,4,16,128]{3,2,1,0:T(8,128)(2,1)S(1)} %get-tuple-element.32), channel_id=1, source_target_pairs={{0,2},{1,3},{2,0},{3,1},{4,6},{5,7},{6,4},{7,5},{8,10},{9,11},{10,... | collective-permute-start | bytes 98312 | tf_op jit(solution)/shard_map/exchange/ppermute | solution.py:318
  41.2 3.8 %collective-permute-start.9 = (bf16[2,4,16,128]{3,2,1,0:T(8,128)(2,1)S(1)}, bf16[2,4,16,128]{3,2,1,0:T(8,128)(2,1)S(1)}, u32[]{:S(2)}, u32[]{:S(2)}) collective-permute-start(bf16[2,4,16,128]{3,2,1,0:T(8,128)(2,1)S(1)} %get-tuple-element.33), channel_id=1, source_target_pairs={{0,4},{1,5},{2,6},{3,7},{4,0},{5,1},{6,2},{7,3},{8,12},{9,13},{10,... | collective-permute-start | bytes 98312 | tf_op jit(solution)/shard_map/exchange/ppermute | solution.py:318
  45.8 8.7 %collective-permute-start.12 = (bf16[16,2304]{1,0:T(8,128)(2,1)S(1)}, bf16[16,2304]{1,0:T(8,128)(2,1)S(1)}, u32[]{:S(2)}, u32[]{:S(2)}) collective-permute-start(bf16[16,2304]{1,0:T(8,128)(2,1)S(1)} %get-tuple-element.37), channel_id=1, source_target_pairs={{0,16},{1,17},{2,18},{3,19},{4,20},{5,21},{6,22},{7,23},{8,24},{9,... | collective-permute-start | bytes 221192 | tf_op jit(solution)/shard_map/reduce/ppermute | solution.py:318
  52.7 8.1 %collective-permute-start.13 = (bf16[16,2304]{1,0:T(8,128)(2,1)S(1)}, bf16[16,2304]{1,0:T(8,128)(2,1)S(1)}, u32[]{:S(2)}, u32[]{:S(2)}) collective-permute-start(bf16[16,2304]{1,0:T(8,128)(2,1)S(1)} %get-tuple-element.39), channel_id=1, source_target_pairs={{0,8},{1,9},{2,10},{3,11},{4,12},{5,13},{6,14},{7,15},{8,0},{9,1},... | collective-permute-start | bytes 221192 | tf_op jit(solution)/shard_map/reduce/ppermute | solution.py:318
  53.9 6.9 %collective-permute-start.14 = (bf16[16,2304]{1,0:T(8,128)(2,1)S(1)}, bf16[16,2304]{1,0:T(8,128)(2,1)S(1)}, u32[]{:S(2)}, u32[]{:S(2)}) collective-permute-start(bf16[16,2304]{1,0:T(8,128)(2,1)S(1)} %get-tuple-element.38), channel_id=1, source_target_pairs={{0,24},{1,25},{2,26},{3,27},{4,28},{5,29},{6,30},{7,31},{8,16},{9,... | collective-permute-start | bytes 221192 | tf_op jit(solution)/shard_map/reduce/ppermute | solution.py:318

commit v6 on v5

--- a/solution.py
+++ b/solution.py
@@ -203,7 +203,7 @@
     final[...] = jnp.concatenate(
         [whole[:, :head] + states[1][:, :head], whole[:, head:]], axis=1
     ).astype(BF16)
-    copies = load([(final, sends.at[i]) for i in range(sends.shape[0])], out_sems)
+    copies = load([(final, sends)], out_sems)
     queries = (unit_rows(query_raw) * (head ** (-0.5))).astype(BF16).astype(F32)
     query_rise = queries * rising
     for group, start in enumerate(range(0, rows, GROUP)):
@@ -224,6 +224,28 @@
         copy.wait()
 
 
+def fold(*refs):
+    found, (before, total, held) = refs[:-3], refs[-3:]
+    count = len(found)
+    mine = lax.rem(lax.axis_index("ctx"), count)
+    head = found[0].shape[0]
+    for back, ref in enumerate(found):
+        held[back] = ref[...]
+    row = lax.broadcasted_iota(jnp.int32, (head, 2 * head), 0)
+    col = lax.broadcasted_iota(jnp.int32, (head, 2 * head), 1)
+    state = jnp.where(row + head == col, 1.0, 0.0).astype(F32)
+    seen = state
+    for step in range(count):
+        seen = jnp.where(mine == step, state, seen)
+        item = held[lax.rem(mine - step + count, count)]
+        moved = jnp.dot(item[:, head:], state.astype(BF16), preferred_element_type=F32)
+        state = jnp.concatenate(
+            [moved[:, :head] + item[:, :head].astype(F32), moved[:, head:]], axis=1
+        )
+    before[...] = seen
+    total[...] = state[:, :head].astype(BF16)
+
+
 def stage(pack, gain, out):
     head = gain.shape[1]
     rows = pack.shape[0] - head
@@ -231,15 +253,13 @@
     out[:rows, 2 * head :] = pack[:rows, 2 * head :] * gain[...]
 
 
-def finish(pack, states, own, other, gated):
-    head = states.shape[1]
+def finish(pack, before, came, own, other, gated):
+    head = came.shape[0]
     rows = pack.shape[0] - head
-    ctx = lax.axis_index("ctx")
     core_at = lax.rem(lax.axis_index("head"), 2)
-    state = jnp.zeros((head, head), F32)
-    for step in range(states.shape[0] - 1):
-        moved = jnp.dot(states[step, :, head:], state.astype(BF16), preferred_element_type=F32)
-        state = jnp.where(step < ctx, moved + states[step, :, :head].astype(F32), state)
+    later = lax.axis_index("ctx") >= lax.axis_size("ctx") // 2
+    state = jnp.where(later, came[...].astype(F32), 0.0)
+    state = mm(before[:, head:], state) + before[:, :head]
     middle = mm(pack[rows:, head : 2 * head], state) + pack[rows:, :head]
     cores = []
     for group, start in enumerate((state, middle)):
@@ -332,7 +352,7 @@
             out_specs=[HBM] * 2,
             out_shape=[
                 shape((rows + head, 3 * head), F32),
-                shape((ctx_count, head, 2 * head), BF16),
+                shape((head, 2 * head), BF16),
             ],
             scratch_shapes=[
                 pltpu.VMEM((rows + 16, model), BF16),
@@ -351,7 +371,7 @@
                 pltpu.VMEM((head, 2 * head), BF16),
                 pltpu.VMEM((rows + head, 3 * head), F32),
                 dma((7 + 6 * CHUNKS,)),
-                dma((ctx_count,)),
+                dma((1,)),
                 dma((2 + rows // GROUP,)),
             ],
             compiler_params=FULL,
@@ -370,7 +390,23 @@
             taps,
         )
     with jax.named_scope("states"):
-        states = lax.all_to_all(sends, "ctx", 0, 0, tiled=True)
+        half = ctx_count // 2
+
+        def around(step):
+            pairs = [(c, c // half * half + (c + step) % half) for c in range(ctx_count)]
+            return lax.ppermute(sends, "ctx", pairs)
+
+        found = {step: around(step) for step in range(1, half)}
+        before, total = pl.pallas_call(
+            fold,
+            in_specs=[VMEM] * half,
+            out_specs=[VMEM] * 2,
+            out_shape=[shape((head, 2 * head), F32), shape((head, head), BF16)],
+            scratch_shapes=[pltpu.VMEM((half, head, 2 * head), BF16)],
+            compiler_params=LIMIT,
+            cost_estimate=cost(0.5, 0),
+        )(sends, *(found[step] for step in range(1, half)))
+        came = lax.ppermute(total, "ctx", [(c, (c + half) % ctx_count) for c in range(ctx_count)])
     (w_early,) = after((w_far,), pack)
     with jax.named_scope("weights"):
         w_both = flip(w_early, 4)
@@ -389,13 +425,13 @@
     with jax.named_scope("finish"):
         own, other = pl.pallas_call(
             finish,
-            in_specs=[VMEM] * 2,
+            in_specs=[VMEM] * 3,
             out_specs=[VMEM] * 2,
             out_shape=[shape((SUBS // 2, zs, 16, head), BF16)] * 2,
             scratch_shapes=[pltpu.VMEM((zs, SUBS // 2, 2, 16, head), BF16)],
             compiler_params=LIMIT,
             cost_estimate=cost(2, 0),
-        )(staged, states)
+        )(staged, before, came)
     with jax.named_scope("exchange"):
         sibling = flip(other, 1)
         kept, *sent = pl.pallas_call(

time: 61.9 us -> 61 us (0.985)
  Pallas kernels: 14.3 us -> 12.4 us
  local copies, waits for them, and re-layouts: 2.74 us -> 3.58 us
    ppermute x0 -> x4, starting transfers between devices: none -> 4.81 us  [the longest x3 4.52 us: around(): return lax.ppermute(sends, 'ctx', pairs)]
    all_to_all x1 -> x0, waiting for transfers between devices: 3.8 us -> none  [on_device(): states = lax.all_to_all(sends, 'ctx', 0, 0, tiled=True)]
    all_to_all x1 -> x0, starting transfers between devices: 3.73 us -> none  [on_device(): states = lax.all_to_all(sends, 'ctx', 0, 0, tiled=True)]
    ppermute x0 -> x4, waiting for transfers between devices: none -> 2.77 us  [the longest x1 2.76 us: on_device(): lax.ppermute(total, 'ctx', [(c, (c + half) % ctx_count) for c in range(ct...]
    pallas_call x1, Pallas kernels: 2.09 us -> 0.4 us  [on_device(): pl.pallas_call(spread, in_specs=[VMEM] * 7, out_specs=[VMEM] * 2, out_sha...]
    ppermute x13, starting transfers between devices: 22.4 us -> 21.3 us  [flip(): lax.ppermute(value, 'head', [(h, h ^ mask) for h in range(head_count)])]
    ppermute x13, waiting for transfers between devices: 8.36 us -> 9.48 us  [flip(): lax.ppermute(value, 'head', [(h, h ^ mask) for h in range(head_count)])]
    unnamed x8 -> x10, local copies, waits for them, and re-layouts: 1.83 us -> 2.68 us
  transfers between devices with their start and end apart: 16 -> 19, of which waited for: 5 -> 6; matrix products, arithmetic and copies ran while one was open for 0% -> 0% of each run, Pallas kernels for 22% -> 19%
where the time goes in v6:
time: 61 us; the launch traced here: 60.5 us
  starting transfers between devices  30.8 us (50%)
  Pallas kernels  12.4 us (20%)
  waiting for transfers between devices  12.3 us (20%)
  local copies, waits for them, and re-layouts  3.58 us (6%)
  between operations  0.75 us (1%)
  other arithmetic  0.68 us (1%)
    ppermute x13, starting transfers between devices, flip(): lax.ppermute(value, 'head', [(h, h ^ mask) for h in range(head_count)])  21.3 us
    pallas_call x1, Pallas kernels, on_device(): pl.pallas_call(front, in_specs=[HBM] * 11, out_specs=[HBM] * 2, out_shape...  10 us
    ppermute x13, waiting for transfers between devices, flip(): lax.ppermute(value, 'head', [(h, h ^ mask) for h in range(head_count)])  9.48 us
    ppermute x3, starting transfers between devices, around(): return lax.ppermute(sends, 'ctx', pairs)  4.52 us
    ppermute x1, waiting for transfers between devices, on_device(): lax.ppermute(total, 'ctx', [(c, (c + half) % ctx_count) for c in range(ct...  2.76 us
    ppermute x1, starting transfers between devices, across(): return lax.ppermute(value, ('ctx', 'head'), pairs)  2.73 us
    unnamed x10, local copies, waits for them, and re-layouts  2.68 us
    ppermute x1, starting transfers between devices, on_device(): lax.ppermute(edge, 'ctx', [(i, (i + 1) % ctx_count) for i in range(ctx_co...  2.04 us
  transfers between devices with their start and end apart: 19, of which 6 were waited for; matrix products, arithmetic and copies ran while one was open for 0% of the time, Pallas kernels for 19%

profile of v6, /device:TPU:1, one launch (start us, length us, event | category | flops | bytes accessed | tf_op | source)
XLA Modules:
  0.0 60.5 jit_solution(16801940608744076902)
XLA Ops:
  0.0 0.9 %slice.15 = bf16[16,2304]{1,0:T(8,128)(2,1)S(1)} slice(bf16[512,2304]{1,0:T(8,128)(2,1)} %tokens_hbm.1), slice={[496:512], [0:2304]} | slice | bytes 147456 | tf_op jit(solution)/shard_map/slice | solution.py:342
  0.9 2.0 %collective-permute-start = (bf16[16,2304]{1,0:T(8,128)(2,1)S(1)}, bf16[16,2304]{1,0:T(8,128)(2,1)S(1)}, u32[]{:S(2)}, u32[]{:S(2)}) collective-permute-start(bf16[16,2304]{1,0:T(8,128)(2,1)S(1)} %slice.15), channel_id=1, source_target_pairs={{0,32},{32,64},{64,96},{96,128},{128,160},{160,192},{192,224},{224... | collective-permute-start | bytes 221192 | tf_op jit(solution)/shard_map/rim/ppermute | solution.py:344
  2.9 2.7 %collective-permute-start.6 = (bf16[128,2304]{1,0:T(8,128)(2,1)}, bf16[128,2304]{1,0:T(8,128)(2,1)S(1)}, u32[]{:S(2)}, u32[]{:S(2)}) collective-permute-start(bf16[128,2304]{1,0:T(8,128)(2,1)} %w_one.1), channel_id=1, source_target_pairs={{0,130},{1,131},{2,128},{3,129},{4,134},{5,135},{6,132},{7,133},{8... | collective-permute-start | bytes 1769480 | tf_op jit(solution)/shard_map/weights/ppermute | solution.py:335
  5.7 1.6 %collective-permute-start.7 = (bf16[128,2304]{1,0:T(8,128)(2,1)}, bf16[128,2304]{1,0:T(8,128)(2,1)S(1)}, u32[]{:S(2)}, u32[]{:S(2)}) collective-permute-start(bf16[128,2304]{1,0:T(8,128)(2,1)} %w_one.1), channel_id=1, source_target_pairs={{0,4},{1,5},{2,6},{3,7},{4,0},{5,1},{6,2},{7,3},{8,12},{9,13},{10,... | collective-permute-start | bytes 1769480 | tf_op jit(solution)/shard_map/weights/ppermute | solution.py:338
  8.0 0.0 collective-permute-done.rim_hbm
  8.0 0.0 copy-start.4
  8.0 0.6 %copy-done.4 = bf16[16,2304]{1,0:T(8,128)(2,1)} copy-done((bf16[16,2304]{1,0:T(8,128)(2,1)}, bf16[16,2304]{1,0:T(8,128)(2,1)S(1)}, u32[]{:S(2)}) %copy-start.4) | copy-done | bytes 73752
  8.6 0.0 copy-start.2
  8.6 0.0 copy-start.3
  8.6 10.0 %front.1 = (f32[640,384]{1,0:T(8,128)}, bf16[128,256]{1,0:T(8,128)(2,1)}) custom-call(bf16[512,2304]{1,0:T(8,128)(2,1)} %tokens_hbm.1, bf16[16,2304]{1,0:T(8,128)(2,1)} %copy-done.4, f32[1,1]{1,0:T(1,128)} %bitcast.17.alog_hbm, bf16[3,2304,128]{2,1,0:T(8,128)(2,1)} %bitcast.19, bf16[2304,128]{1,0:T(8,128)(2,1)} %f_down_hbm.1, bf16[2304,128]{1,0:T(8,128)(2,1)} %o_down_hbm.1, ...), custom_call_target="tpu_custom_call" | custom-call | flops 40000000000 | bytes 33210000 | tf_op jit(solution)/shard_map/front/pallas_call | solution.py:349
  18.6 0.0 collective-permute-done.6.refs_0_
  18.6 1.4 %collective-permute-start.14 = (bf16[128,2304]{1,0:T(8,128)(2,1)S(1)}, bf16[128,2304]{1,0:T(8,128)(2,1)S(1)}, u32[]{:S(2)}, u32[]{:S(2)}) collective-permute-start(bf16[128,2304]{1,0:T(8,128)(2,1)S(1)} %collective-permute-done.6.refs_0_), channel_id=1, source_target_pairs={{0,4},{1,5},{2,6},{3,7},{4,0},{5,1},{6,2},{7,3},{8,12},{9,13},{10,... | collective-permute-start | bytes 1769480 | tf_op jit(solution)/shard_map/weights/ppermute | solution.py:338
  20.0 1.2 %collective-permute-start.1 = (bf16[128,256]{1,0:T(8,128)(2,1)}, bf16[128,256]{1,0:T(8,128)(2,1)S(1)}, u32[]{:S(2)}, u32[]{:S(2)}) collective-permute-start(bf16[128,256]{1,0:T(8,128)(2,1)} %get-tuple-element.24.refs_0_), channel_id=1, source_target_pairs={{0,32},{32,64},{64,96},{96,0},{128,160},{160,192},{192,224},{224,1... | collective-permute-start | bytes 196616 | tf_op jit(solution)/shard_map/states/ppermute | solution.py:397
  21.2 2.3 %collective-permute-start.2 = (bf16[128,256]{1,0:T(8,128)(2,1)}, bf16[128,256]{1,0:T(8,128)(2,1)S(1)}, u32[]{:S(2)}, u32[]{:S(2)}) collective-permute-start(bf16[128,256]{1,0:T(8,128)(2,1)} %get-tuple-element.24.refs_0_), channel_id=1, source_target_pairs={{0,64},{32,96},{64,0},{96,32},{128,192},{160,224},{192,128},{224,1... | collective-permute-start | bytes 196616 | tf_op jit(solution)/shard_map/states/ppermute | solution.py:397
  23.5 1.0 %collective-permute-start.3 = (bf16[128,256]{1,0:T(8,128)(2,1)}, bf16[128,256]{1,0:T(8,128)(2,1)S(1)}, u32[]{:S(2)}, u32[]{:S(2)}) collective-permute-start(bf16[128,256]{1,0:T(8,128)(2,1)} %get-tuple-element.24.refs_0_), channel_id=1, source_target_pairs={{0,96},{32,0},{64,32},{96,64},{128,224},{160,128},{192,160},{224,1... | collective-permute-start | bytes 196616 | tf_op jit(solution)/shard_map/states/ppermute | solution.py:397
  24.5 0.0 copy-done.2
  24.5 0.0 copy-start
  24.5 1.2 %copy-done = f32[640,384]{1,0:T(8,128)S(1)} copy-done((f32[640,384]{1,0:T(8,128)S(1)}, f32[640,384]{1,0:T(8,128)}, u32[]{:S(2)}) %copy-start) | copy-done | bytes 983064
  25.7 0.1 stage.1.pack
  25.8 0.0 collective-permute-done.7.refs_2_
  25.8 3.0 %collective-permute-start.10 = (bf16[128,2304]{1,0:T(8,128)(2,1)S(1)}, bf16[128,2304]{1,0:T(8,128)(2,1)S(1)}, u32[]{:S(2)}, u32[]{:S(2)}) collective-permute-start(bf16[128,2304]{1,0:T(8,128)(2,1)S(1)} %collective-permute-done.7.refs_2_), channel_id=1, source_target_pairs={{0,1},{1,0},{2,3},{3,2},{4,5},{5,4},{6,7},{7,6},{8,9},{9,8},{10,11... | collective-permute-start | bytes 1769480 | tf_op jit(solution)/shard_map/weights/ppermute | solution.py:338
  28.8 0.0 collective-permute-done.1.refs_1_
  28.8 0.0 copy-done.3
  28.8 0.1 collective-permute-start.8
  28.9 0.0 collective-permute-done.2.refs_2_
  28.9 0.6 %collective-permute-start.9 = (bf16[128,2304]{1,0:T(8,128)(2,1)S(1)}, bf16[128,2304]{1,0:T(8,128)(2,1)S(1)}, u32[]{:S(2)}, u32[]{:S(2)}) collective-permute-start(bf16[128,2304]{1,0:T(8,128)(2,1)S(1)} %collective-permute-done.6.refs_0_), channel_id=1, source_target_pairs={{0,1},{1,0},{2,3},{3,2},{4,5},{5,4},{6,7},{7,6},{8,9},{9,8},{10,11... | collective-permute-start | bytes 1769480 | tf_op jit(solution)/shard_map/weights/ppermute | solution.py:338
  29.5 0.0 collective-permute-done.3.refs_3_
  29.6 0.0 copy-start.1
  29.6 0.8 %copy-done.1 = bf16[128,256]{1,0:T(8,128)(2,1)S(1)} copy-done((bf16[128,256]{1,0:T(8,128)(2,1)S(1)}, bf16[128,256]{1,0:T(8,128)(2,1)}, u32[]{:S(2)}) %copy-start.1) | copy-done | bytes 65560
  30.4 0.6 %states.1 = (f32[128,256]{1,0:T(8,128)S(1)}, bf16[128,128]{1,0:T(8,128)(2,1)S(1)}) custom-call(bf16[128,256]{1,0:T(8,128)(2,1)S(1)} %copy-done.1, bf16[128,256]{1,0:T(8,128)(2,1)S(1)} %collective-permute-done.1.refs_1_, bf16[128,256]{1,0:T(8,128)(2,1)S(1)} %collective-permute-done.2.refs_2_, bf16[128,256]{1,0:T(8,128)(2,1)S(1)} %collective-permute-done.3.refs_3_), custom_call_target="tpu_custom_call" | custom-call | bytes 1845000 | tf_op jit(solution)/shard_map/states/pallas_call | solution.py:400
  31.0 0.3 collective-permute-start.4
  31.3 2.8 %collective-permute-done.4.came = bf16[128,128]{1,0:T(8,128)(2,1)S(1)} collective-permute-done((bf16[128,128]{1,0:T(8,128)(2,1)S(1)}, bf16[128,128]{1,0:T(8,128)(2,1)S(1)}, u32[]{:S(2)}, u32[]{:S(2)}) %collective-permute-start.4) | collective-permute-done | bytes 32800 | tf_op jit(solution)/shard_map/states/ppermute | solution.py:409
  34.1 0.5 finish.1
  34.6 2.4 %collective-permute-start.5 = (bf16[4,4,16,128]{3,2,1,0:T(8,128)(2,1)S(1)}, bf16[4,4,16,128]{3,2,1,0:T(8,128)(2,1)S(1)}, u32[]{:S(2)}, u32[]{:S(2)}) collective-permute-start(bf16[4,4,16,128]{3,2,1,0:T(8,128)(2,1)S(1)} %get-tuple-element.28), channel_id=1, source_target_pairs={{0,1},{1,0},{2,3},{3,2},{4,5},{5,4},{6,7},{7,6},{8,9},{9,8},{10,11... | collective-permute-start | bytes 196616 | tf_op jit(solution)/shard_map/exchange/ppermute | solution.py:338
  37.0 0.9 %collective-permute-done.5.sibling = bf16[4,4,16,128]{3,2,1,0:T(8,128)(2,1)S(1)} collective-permute-done((bf16[4,4,16,128]{3,2,1,0:T(8,128)(2,1)S(1)}, bf16[4,4,16,128]{3,2,1,0:T(8,128)(2,1)S(1)}, u32[]{:S(2)}, u32[]{:S(2)}) %collective-permute-start.5) | collective-permute-done | bytes 65568 | tf_op jit(solution)/shard_map/exchange/ppermute | solution.py:338
  37.9 0.0 collective-permute-done.14.refs_4_
  37.9 0.4 collective-permute-start.15
  38.4 1.0 %collective-permute-start.11 = (bf16[2,4,16,128]{3,2,1,0:T(8,128)(2,1)S(1)}, bf16[2,4,16,128]{3,2,1,0:T(8,128)(2,1)S(1)}, u32[]{:S(2)}, u32[]{:S(2)}) collective-permute-start(bf16[2,4,16,128]{3,2,1,0:T(8,128)(2,1)S(1)} %get-tuple-element.35), channel_id=1, source_target_pairs={{0,6},{1,7},{2,4},{3,5},{4,2},{5,3},{6,0},{7,1},{8,14},{9,15},{10,... | collective-permute-start | bytes 98312 | tf_op jit(solution)/shard_map/exchange/ppermute | solution.py:338
  39.3 0.0 collective-permute-done.10.refs_3_
  39.3 1.6 %collective-permute-start.12 = (bf16[2,4,16,128]{3,2,1,0:T(8,128)(2,1)S(1)}, bf16[2,4,16,128]{3,2,1,0:T(8,128)(2,1)S(1)}, u32[]{:S(2)}, u32[]{:S(2)}) collective-permute-start(bf16[2,4,16,128]{3,2,1,0:T(8,128)(2,1)S(1)} %get-tuple-element.36), channel_id=1, source_target_pairs={{0,2},{1,3},{2,0},{3,1},{4,6},{5,7},{6,4},{7,5},{8,10},{9,11},{10,... | collective-permute-start | bytes 98312 | tf_op jit(solution)/shard_map/exchange/ppermute | solution.py:338
  40.9 0.0 collective-permute-done.8.w_two
  40.9 1.6 %collective-permute-start.13 = (bf16[2,4,16,128]{3,2,1,0:T(8,128)(2,1)S(1)}, bf16[2,4,16,128]{3,2,1,0:T(8,128)(2,1)S(1)}, u32[]{:S(2)}, u32[]{:S(2)}) collective-permute-start(bf16[2,4,16,128]{3,2,1,0:T(8,128)(2,1)S(1)} %get-tuple-element.37), channel_id=1, source_target_pairs={{0,4},{1,5},{2,6},{3,7},{4,0},{5,1},{6,2},{7,3},{8,12},{9,13},{10,... | collective-permute-start | bytes 98312 | tf_op jit(solution)/shard_map/exchange/ppermute | solution.py:338
  42.5 0.0 collective-permute-done.9.refs_1_
  42.5 0.4 spread.2
  42.9 0.6 %collective-permute-done.11.refs_0_ = bf16[2,4,16,128]{3,2,1,0:T(8,128)(2,1)S(1)} collective-permute-done((bf16[2,4,16,128]{3,2,1,0:T(8,128)(2,1)S(1)}, bf16[2,4,16,128]{3,2,1,0:T(8,128)(2,1)S(1)}, u32[]{:S(2)}, u32[]{:S(2)}) %collective-permute-start.11) | collective-permute-done | bytes 32800 | tf_op jit(solution)/shard_map/exchange/ppermute | solution.py:338
  43.6 1.1 %collective-permute-done.12.refs_1_ = bf16[2,4,16,128]{3,2,1,0:T(8,128)(2,1)S(1)} collective-permute-done((bf16[2,4,16,128]{3,2,1,0:T(8,128)(2,1)S(1)}, bf16[2,4,16,128]{3,2,1,0:T(8,128)(2,1)S(1)}, u32[]{:S(2)}, u32[]{:S(2)}) %collective-permute-start.12) | collective-permute-done | bytes 32800 | tf_op jit(solution)/shard_map/exchange/ppermute | solution.py:338
  44.6 0.0 collective-permute-done.13.refs_2_
  44.6 0.0 collective-permute-done.15.refs_5_
  44.6 0.7 %spread.3 = bf16[4,16,2304]{2,1,0:T(8,128)(2,1)S(1)} custom-call(f32[64,2304]{1,0:T(8,128)S(1)} %get-tuple-element.34.begun, bf16[2,4,16,128]{3,2,1,0:T(8,128)(2,1)S(1)} %collective-permute-done.11.refs_0_, bf16[2,4,16,128]{3,2,1,0:T(8,128)(2,1)S(1)} %collective-permute-done.12.refs_1_, bf16[2,4,16,128]{3,2,1,0:T(8,128)(2,1)S(1)} %collective-permute-done.13.refs_2_, ...), custom_call_target="tpu_custom_call" | custom-call | flops 1000000000 | bytes 3690000 | tf_op jit(solution)/shard_map/spread/pallas_call | solution.py:458
  45.4 6.3 %collective-permute-start.16 = (bf16[16,2304]{1,0:T(8,128)(2,1)S(1)}, bf16[16,2304]{1,0:T(8,128)(2,1)S(1)}, u32[]{:S(2)}, u32[]{:S(2)}) collective-permute-start(bf16[16,2304]{1,0:T(8,128)(2,1)S(1)} %get-tuple-element.41), channel_id=1, source_target_pairs={{0,16},{1,17},{2,18},{3,19},{4,20},{5,21},{6,22},{7,23},{8,24},{9,... | collective-permute-start | bytes 221192 | tf_op jit(solution)/shard_map/reduce/ppermute | solution.py:338
  51.7 1.2 %collective-permute-start.17 = (bf16[16,2304]{1,0:T(8,128)(2,1)S(1)}, bf16[16,2304]{1,0:T(8,128)(2,1)S(1)}, u32[]{:S(2)}, u32[]{:S(2)}) collective-permute-start(bf16[16,2304]{1,0:T(8,128)(2,1)S(1)} %get-tuple-element.43), channel_id=1, source_target_pairs={{0,8},{1,9},{2,10},{3,11},{4,12},{5,13},{6,14},{7,15},{8,0},{9,1},... | collective-permute-start | bytes 221192 | tf_op jit(solution)/shard_map/reduce/ppermute | solution.py:338
  52.9 0.0 collective-permute-start.18
  52.9 0.6 %collective-permute-done.16 = bf16[16,2304]{1,0:T(8,128)(2,1)S(1)} collective-permute-done((bf16[16,2304]{1,0:T(8,128)(2,1)S(1)}, bf16[16,2304]{1,0:T(8,128)(2,1)S(1)}, u32[]{:S(2)}, u32[]{:S(2)}) %collective-permute-start.16) | collective-permute-done | bytes 73760 | tf_op jit(solution)/shard_map/reduce/ppermute | solution.py:338
  53.5 6.3 %collective-permute-done.17 = bf16[16,2304]{1,0:T(8,128)(2,1)S(1)} collective-permute-done((bf16[16,2304]{1,0:T(8,128)(2,1)S(1)}, bf16[16,2304]{1,0:T(8,128)(2,1)S(1)}, u32[]{:S(2)}, u32[]{:S(2)}) %collective-permute-start.17) | collective-permute-done | bytes 73760 | tf_op jit(solution)/shard_map/reduce/ppermute | solution.py:338
  59.8 0.0 collective-permute-done.18
  59.8 0.7 %fusion.2 = bf16[16,2304]{1,0:T(8,128)(2,1)} fusion(bf16[16,2304]{1,0:T(8,128)(2,1)S(1)} %collective-permute-done.18, bf16[16,2304]{1,0:T(8,128)(2,1)S(1)} %collective-permute-done.17, bf16[16,2304]{1,0:T(8,128)(2,1)S(1)} %collective-permute-done.16, bf16[4,16,2304]{2,1,0:T(8,128)(2,1)S(1)} %spread.3), kind=kLoop, calls=%fused_computation.3 | loop fusion | flops 294912 | bytes 368640 | tf_op jit(solution)/shard_map/reduce/convert_element_type | solution.py:471
  (2 shorter events, 0.0 us)
Async XLA Ops:
  0.9 7.1 %collective-permute-start = (bf16[16,2304]{1,0:T(8,128)(2,1)S(1)}, bf16[16,2304]{1,0:T(8,128)(2,1)S(1)}, u32[]{:S(2)}, u32[]{:S(2)}) collective-permute-start(bf16[16,2304]{1,0:T(8,128)(2,1)S(1)} %slice.15), channel_id=1, source_target_pairs={{0,32},{32,64},{64,96},{96,128},{128,160},{160,192},{192,224},{224... | collective-permute-start | bytes 221192 | tf_op jit(solution)/shard_map/rim/ppermute | solution.py:344
  2.9 15.7 %collective-permute-start.6 = (bf16[128,2304]{1,0:T(8,128)(2,1)}, bf16[128,2304]{1,0:T(8,128)(2,1)S(1)}, u32[]{:S(2)}, u32[]{:S(2)}) collective-permute-start(bf16[128,2304]{1,0:T(8,128)(2,1)} %w_one.1), channel_id=1, source_target_pairs={{0,130},{1,131},{2,128},{3,129},{4,134},{5,135},{6,132},{7,133},{8... | collective-permute-start | bytes 1769480 | tf_op jit(solution)/shard_map/weights/ppermute | solution.py:335
  5.7 20.1 %collective-permute-start.7 = (bf16[128,2304]{1,0:T(8,128)(2,1)}, bf16[128,2304]{1,0:T(8,128)(2,1)S(1)}, u32[]{:S(2)}, u32[]{:S(2)}) collective-permute-start(bf16[128,2304]{1,0:T(8,128)(2,1)} %w_one.1), channel_id=1, source_target_pairs={{0,4},{1,5},{2,6},{3,7},{4,0},{5,1},{6,2},{7,3},{8,12},{9,13},{10,... | collective-permute-start | bytes 1769480 | tf_op jit(solution)/shard_map/weights/ppermute | solution.py:338
  8.0 0.6 %copy-start.4 = (bf16[16,2304]{1,0:T(8,128)(2,1)}, bf16[16,2304]{1,0:T(8,128)(2,1)S(1)}, u32[]{:S(2)}) copy-start(bf16[16,2304]{1,0:T(8,128)(2,1)S(1)} %collective-permute-done.rim_hbm) | copy-start | bytes 221188
  8.6 15.9 %copy-start.2 = (f32[128]{0:T(128)S(1)}, f32[128]{0:T(128)}, u32[]{:S(2)}) copy-start(f32[128]{0:T(128)} %param.22) | copy-start | bytes 1540
  8.6 20.2 %copy-start.3 = (bf16[128,2304]{1,0:T(8,128)(2,1)S(1)}, bf16[128,2304]{1,0:T(8,128)(2,1)}, u32[]{:S(2)}) copy-start(bf16[128,2304]{1,0:T(8,128)(2,1)} %w_one.1) | copy-start | bytes 1769476
  18.6 19.3 %collective-permute-start.14 = (bf16[128,2304]{1,0:T(8,128)(2,1)S(1)}, bf16[128,2304]{1,0:T(8,128)(2,1)S(1)}, u32[]{:S(2)}, u32[]{:S(2)}) collective-permute-start(bf16[128,2304]{1,0:T(8,128)(2,1)S(1)} %collective-permute-done.6.refs_0_), channel_id=1, source_target_pairs={{0,4},{1,5},{2,6},{3,7},{4,0},{5,1},{6,2},{7,3},{8,12},{9,13},{10,... | collective-permute-start | bytes 1769480 | tf_op jit(solution)/shard_map/weights/ppermute | solution.py:338
  20.0 8.8 %collective-permute-start.1 = (bf16[128,256]{1,0:T(8,128)(2,1)}, bf16[128,256]{1,0:T(8,128)(2,1)S(1)}, u32[]{:S(2)}, u32[]{:S(2)}) collective-permute-start(bf16[128,256]{1,0:T(8,128)(2,1)} %get-tuple-element.24.refs_0_), channel_id=1, source_target_pairs={{0,32},{32,64},{64,96},{96,0},{128,160},{160,192},{192,224},{224,1... | collective-permute-start | bytes 196616 | tf_op jit(solution)/shard_map/states/ppermute | solution.py:397
  21.2 7.7 %collective-permute-start.2 = (bf16[128,256]{1,0:T(8,128)(2,1)}, bf16[128,256]{1,0:T(8,128)(2,1)S(1)}, u32[]{:S(2)}, u32[]{:S(2)}) collective-permute-start(bf16[128,256]{1,0:T(8,128)(2,1)} %get-tuple-element.24.refs_0_), channel_id=1, source_target_pairs={{0,64},{32,96},{64,0},{96,32},{128,192},{160,224},{192,128},{224,1... | collective-permute-start | bytes 196616 | tf_op jit(solution)/shard_map/states/ppermute | solution.py:397
  23.5 6.0 %collective-permute-start.3 = (bf16[128,256]{1,0:T(8,128)(2,1)}, bf16[128,256]{1,0:T(8,128)(2,1)S(1)}, u32[]{:S(2)}, u32[]{:S(2)}) collective-permute-start(bf16[128,256]{1,0:T(8,128)(2,1)} %get-tuple-element.24.refs_0_), channel_id=1, source_target_pairs={{0,96},{32,0},{64,32},{96,64},{128,224},{160,128},{192,160},{224,1... | collective-permute-start | bytes 196616 | tf_op jit(solution)/shard_map/states/ppermute | solution.py:397
  24.5 1.2 %copy-start = (f32[640,384]{1,0:T(8,128)S(1)}, f32[640,384]{1,0:T(8,128)}, u32[]{:S(2)}) copy-start(f32[640,384]{1,0:T(8,128)} %get-tuple-element.23.pack) | copy-start | bytes 2949124
  25.8 13.5 %collective-permute-start.10 = (bf16[128,2304]{1,0:T(8,128)(2,1)S(1)}, bf16[128,2304]{1,0:T(8,128)(2,1)S(1)}, u32[]{:S(2)}, u32[]{:S(2)}) collective-permute-start(bf16[128,2304]{1,0:T(8,128)(2,1)S(1)} %collective-permute-done.7.refs_2_), channel_id=1, source_target_pairs={{0,1},{1,0},{2,3},{3,2},{4,5},{5,4},{6,7},{7,6},{8,9},{9,8},{10,11... | collective-permute-start | bytes 1769480 | tf_op jit(solution)/shard_map/weights/ppermute | solution.py:338
  28.8 12.1 %collective-permute-start.8 = (bf16[128,2304]{1,0:T(8,128)(2,1)S(1)}, bf16[128,2304]{1,0:T(8,128)(2,1)S(1)}, u32[]{:S(2)}, u32[]{:S(2)}) collective-permute-start(bf16[128,2304]{1,0:T(8,128)(2,1)S(1)} %copy-done.3), channel_id=1, source_target_pairs={{0,1},{1,0},{2,3},{3,2},{4,5},{5,4},{6,7},{7,6},{8,9},{9,8},{10,11... | collective-permute-start | bytes 1769480 | tf_op jit(solution)/shard_map/weights/ppermute | solution.py:338
  28.9 13.6 %collective-permute-start.9 = (bf16[128,2304]{1,0:T(8,128)(2,1)S(1)}, bf16[128,2304]{1,0:T(8,128)(2,1)S(1)}, u32[]{:S(2)}, u32[]{:S(2)}) collective-permute-start(bf16[128,2304]{1,0:T(8,128)(2,1)S(1)} %collective-permute-done.6.refs_0_), channel_id=1, source_target_pairs={{0,1},{1,0},{2,3},{3,2},{4,5},{5,4},{6,7},{7,6},{8,9},{9,8},{10,11... | collective-permute-start | bytes 1769480 | tf_op jit(solution)/shard_map/weights/ppermute | solution.py:338
  29.6 0.8 %copy-start.1 = (bf16[128,256]{1,0:T(8,128)(2,1)S(1)}, bf16[128,256]{1,0:T(8,128)(2,1)}, u32[]{:S(2)}) copy-start(bf16[128,256]{1,0:T(8,128)(2,1)} %get-tuple-element.24.refs_0_) | copy-start | bytes 196612
  31.0 3.1 %collective-permute-start.4 = (bf16[128,128]{1,0:T(8,128)(2,1)S(1)}, bf16[128,128]{1,0:T(8,128)(2,1)S(1)}, u32[]{:S(2)}, u32[]{:S(2)}) collective-permute-start(bf16[128,128]{1,0:T(8,128)(2,1)S(1)} %get-tuple-element.26), channel_id=1, source_target_pairs={{0,128},{32,160},{64,192},{96,224},{128,0},{160,32},{192,64},{224,... | collective-permute-start | bytes 98312 | tf_op jit(solution)/shard_map/states/ppermute | solution.py:409
  34.6 3.3 %collective-permute-start.5 = (bf16[4,4,16,128]{3,2,1,0:T(8,128)(2,1)S(1)}, bf16[4,4,16,128]{3,2,1,0:T(8,128)(2,1)S(1)}, u32[]{:S(2)}, u32[]{:S(2)}) collective-permute-start(bf16[4,4,16,128]{3,2,1,0:T(8,128)(2,1)S(1)} %get-tuple-element.28), channel_id=1, source_target_pairs={{0,1},{1,0},{2,3},{3,2},{4,5},{5,4},{6,7},{7,6},{8,9},{9,8},{10,11... | collective-permute-start | bytes 196616 | tf_op jit(solution)/shard_map/exchange/ppermute | solution.py:338
  37.9 6.7 %collective-permute-start.15 = (bf16[128,2304]{1,0:T(8,128)(2,1)S(1)}, bf16[128,2304]{1,0:T(8,128)(2,1)S(1)}, u32[]{:S(2)}, u32[]{:S(2)}) collective-permute-start(bf16[128,2304]{1,0:T(8,128)(2,1)S(1)} %collective-permute-done.14.refs_4_), channel_id=1, source_target_pairs={{0,1},{1,0},{2,3},{3,2},{4,5},{5,4},{6,7},{7,6},{8,9},{9,8},{10,11... | collective-permute-start | bytes 1769480 | tf_op jit(solution)/shard_map/spread/ppermute | solution.py:338
  38.4 5.2 %collective-permute-start.11 = (bf16[2,4,16,128]{3,2,1,0:T(8,128)(2,1)S(1)}, bf16[2,4,16,128]{3,2,1,0:T(8,128)(2,1)S(1)}, u32[]{:S(2)}, u32[]{:S(2)}) collective-permute-start(bf16[2,4,16,128]{3,2,1,0:T(8,128)(2,1)S(1)} %get-tuple-element.35), channel_id=1, source_target_pairs={{0,6},{1,7},{2,4},{3,5},{4,2},{5,3},{6,0},{7,1},{8,14},{9,15},{10,... | collective-permute-start | bytes 98312 | tf_op jit(solution)/shard_map/exchange/ppermute | solution.py:338
  39.3 5.3 %collective-permute-start.12 = (bf16[2,4,16,128]{3,2,1,0:T(8,128)(2,1)S(1)}, bf16[2,4,16,128]{3,2,1,0:T(8,128)(2,1)S(1)}, u32[]{:S(2)}, u32[]{:S(2)}) collective-permute-start(bf16[2,4,16,128]{3,2,1,0:T(8,128)(2,1)S(1)} %get-tuple-element.36), channel_id=1, source_target_pairs={{0,2},{1,3},{2,0},{3,1},{4,6},{5,7},{6,4},{7,5},{8,10},{9,11},{10,... | collective-permute-start | bytes 98312 | tf_op jit(solution)/shard_map/exchange/ppermute | solution.py:338
  40.9 3.7 %collective-permute-start.13 = (bf16[2,4,16,128]{3,2,1,0:T(8,128)(2,1)S(1)}, bf16[2,4,16,128]{3,2,1,0:T(8,128)(2,1)S(1)}, u32[]{:S(2)}, u32[]{:S(2)}) collective-permute-start(bf16[2,4,16,128]{3,2,1,0:T(8,128)(2,1)S(1)} %get-tuple-element.37), channel_id=1, source_target_pairs={{0,4},{1,5},{2,6},{3,7},{4,0},{5,1},{6,2},{7,3},{8,12},{9,13},{10,... | collective-permute-start | bytes 98312 | tf_op jit(solution)/shard_map/exchange/ppermute | solution.py:338
  45.4 8.1 %collective-permute-start.16 = (bf16[16,2304]{1,0:T(8,128)(2,1)S(1)}, bf16[16,2304]{1,0:T(8,128)(2,1)S(1)}, u32[]{:S(2)}, u32[]{:S(2)}) collective-permute-start(bf16[16,2304]{1,0:T(8,128)(2,1)S(1)} %get-tuple-element.41), channel_id=1, source_target_pairs={{0,16},{1,17},{2,18},{3,19},{4,20},{5,21},{6,22},{7,23},{8,24},{9,... | collective-permute-start | bytes 221192 | tf_op jit(solution)/shard_map/reduce/ppermute | solution.py:338
  51.7 8.1 %collective-permute-start.17 = (bf16[16,2304]{1,0:T(8,128)(2,1)S(1)}, bf16[16,2304]{1,0:T(8,128)(2,1)S(1)}, u32[]{:S(2)}, u32[]{:S(2)}) collective-permute-start(bf16[16,2304]{1,0:T(8,128)(2,1)S(1)} %get-tuple-element.43), channel_id=1, source_target_pairs={{0,8},{1,9},{2,10},{3,11},{4,12},{5,13},{6,14},{7,15},{8,0},{9,1},... | collective-permute-start | bytes 221192 | tf_op jit(solution)/shard_map/reduce/ppermute | solution.py:338
  52.9 6.9 %collective-permute-start.18 = (bf16[16,2304]{1,0:T(8,128)(2,1)S(1)}, bf16[16,2304]{1,0:T(8,128)(2,1)S(1)}, u32[]{:S(2)}, u32[]{:S(2)}) collective-permute-start(bf16[16,2304]{1,0:T(8,128)(2,1)S(1)} %get-tuple-element.42), channel_id=1, source_target_pairs={{0,24},{1,25},{2,26},{3,27},{4,28},{5,29},{6,30},{7,31},{8,16},{9,... | collective-permute-start | bytes 221192 | tf_op jit(solution)/shard_map/reduce/ppermute | solution.py:338

commit v7 on v6

--- a/solution.py
+++ b/solution.py
@@ -410,6 +410,7 @@
     (w_early,) = after((w_far,), pack)
     with jax.named_scope("weights"):
         w_both = flip(w_early, 4)
+    (late_pack,) = after((pack,), total)
     with jax.named_scope("stage"):
         staged = pl.pallas_call(
             stage,
@@ -418,8 +419,8 @@
             out_shape=shape(pack.shape, F32),
             compiler_params=LIMIT,
             cost_estimate=cost(0.5, 0.5),
-        )(pack, norm_gain.reshape(1, head))
-    w_late, w_near, w_mine = after((w_far, w_next, w_out), staged)
+        )(late_pack, norm_gain.reshape(1, head))
+    w_late, w_near, w_mine = after((w_far, w_next, w_out), pack)
     with jax.named_scope("weights"):
         w_core, w_far_core, w_next_core = flip(w_mine, 1), flip(w_late, 1), flip(w_near, 1)
     with jax.named_scope("finish"):

time: 61 us -> 61.9 us (1.015)
    ppermute x13, starting transfers between devices: 21.3 us -> 22.9 us  [flip(): lax.ppermute(value, 'head', [(h, h ^ mask) for h in range(head_count)])]
    ppermute x1, waiting for transfers between devices: 2.76 us -> 1.47 us  [on_device(): lax.ppermute(total, 'ctx', [(c, (c + half) % ctx_count) for c in range(ct...]
    ppermute x1, waiting for transfers between devices: 0.01 us -> 1.14 us  [across(): return lax.ppermute(value, ('ctx', 'head'), pairs)]
    ppermute x3, starting transfers between devices: 4.52 us -> 3.49 us  [around(): return lax.ppermute(sends, 'ctx', pairs)]
    ppermute x13, waiting for transfers between devices: 9.48 us -> 10.2 us  [flip(): lax.ppermute(value, 'head', [(h, h ^ mask) for h in range(head_count)])]
  transfers between devices with their start and end apart: 19 -> 19, of which waited for: 6 -> 9; matrix products, arithmetic and copies ran while one was open for 0% -> 0% of each run, Pallas kernels for 19% -> 19%
where the time goes in v7:
time: 61.9 us; the launch traced here: 61.7 us
  starting transfers between devices  31.4 us (51%)
  waiting for transfers between devices  12.9 us (21%)
  Pallas kernels  12.4 us (20%)
  local copies, waits for them, and re-layouts  3.58 us (6%)
  between operations  0.76 us (1%)
  other arithmetic  0.68 us (1%)
    ppermute x13, starting transfers between devices, flip(): lax.ppermute(value, 'head', [(h, h ^ mask) for h in range(head_count)])  22.9 us
    ppermute x13, waiting for transfers between devices, flip(): lax.ppermute(value, 'head', [(h, h ^ mask) for h in range(head_count)])  10.2 us
    pallas_call x1, Pallas kernels, on_device(): pl.pallas_call(front, in_specs=[HBM] * 11, out_specs=[HBM] * 2, out_shape...  10 us
    ppermute x3, starting transfers between devices, around(): return lax.ppermute(sends, 'ctx', pairs)  3.49 us
    ppermute x1, starting transfers between devices, across(): return lax.ppermute(value, ('ctx', 'head'), pairs)  2.73 us
    unnamed x10, local copies, waits for them, and re-layouts  2.67 us
    ppermute x1, starting transfers between devices, on_device(): lax.ppermute(edge, 'ctx', [(i, (i + 1) % ctx_count) for i in range(ctx_co...  2.04 us
    ppermute x1, waiting for transfers between devices, on_device(): lax.ppermute(total, 'ctx', [(c, (c + half) % ctx_count) for c in range(ct...  1.47 us
  transfers between devices with their start and end apart: 19, of which 9 were waited for; matrix products, arithmetic and copies ran while one was open for 0% of the time, Pallas kernels for 19%

profile of v7, /device:TPU:1, one launch (start us, length us, event | category | flops | bytes accessed | tf_op | source)
XLA Modules:
  0.0 61.7 jit_solution(10934371565904872518)
XLA Ops:
  0.0 0.9 %slice.15 = bf16[16,2304]{1,0:T(8,128)(2,1)S(1)} slice(bf16[512,2304]{1,0:T(8,128)(2,1)} %tokens_hbm.1), slice={[496:512], [0:2304]} | slice | bytes 147456 | tf_op jit(solution)/shard_map/slice | solution.py:342
  0.9 2.0 %collective-permute-start = (bf16[16,2304]{1,0:T(8,128)(2,1)S(1)}, bf16[16,2304]{1,0:T(8,128)(2,1)S(1)}, u32[]{:S(2)}, u32[]{:S(2)}) collective-permute-start(bf16[16,2304]{1,0:T(8,128)(2,1)S(1)} %slice.15), channel_id=1, source_target_pairs={{0,32},{32,64},{64,96},{96,128},{128,160},{160,192},{192,224},{224... | collective-permute-start | bytes 221192 | tf_op jit(solution)/shard_map/rim/ppermute | solution.py:344
  2.9 1.6 %collective-permute-start.7 = (bf16[128,2304]{1,0:T(8,128)(2,1)}, bf16[128,2304]{1,0:T(8,128)(2,1)S(1)}, u32[]{:S(2)}, u32[]{:S(2)}) collective-permute-start(bf16[128,2304]{1,0:T(8,128)(2,1)} %w_one.1), channel_id=1, source_target_pairs={{0,4},{1,5},{2,6},{3,7},{4,0},{5,1},{6,2},{7,3},{8,12},{9,13},{10,... | collective-permute-start | bytes 1769480 | tf_op jit(solution)/shard_map/weights/ppermute | solution.py:338
  4.6 2.7 %collective-permute-start.6 = (bf16[128,2304]{1,0:T(8,128)(2,1)}, bf16[128,2304]{1,0:T(8,128)(2,1)S(1)}, u32[]{:S(2)}, u32[]{:S(2)}) collective-permute-start(bf16[128,2304]{1,0:T(8,128)(2,1)} %w_one.1), channel_id=1, source_target_pairs={{0,130},{1,131},{2,128},{3,129},{4,134},{5,135},{6,132},{7,133},{8... | collective-permute-start | bytes 1769480 | tf_op jit(solution)/shard_map/weights/ppermute | solution.py:335
  8.0 0.0 collective-permute-done.rim_hbm
  8.0 0.0 copy-start.4
  8.0 0.6 %copy-done.4 = bf16[16,2304]{1,0:T(8,128)(2,1)} copy-done((bf16[16,2304]{1,0:T(8,128)(2,1)}, bf16[16,2304]{1,0:T(8,128)(2,1)S(1)}, u32[]{:S(2)}) %copy-start.4) | copy-done | bytes 73752
  8.6 0.0 copy-start.3
  8.6 0.0 copy-start.2
  8.6 10.0 %front.1 = (f32[640,384]{1,0:T(8,128)}, bf16[128,256]{1,0:T(8,128)(2,1)}) custom-call(bf16[512,2304]{1,0:T(8,128)(2,1)} %tokens_hbm.1, bf16[16,2304]{1,0:T(8,128)(2,1)} %copy-done.4, f32[1,1]{1,0:T(1,128)} %bitcast.17.alog_hbm, bf16[3,2304,128]{2,1,0:T(8,128)(2,1)} %bitcast.19, bf16[2304,128]{1,0:T(8,128)(2,1)} %f_down_hbm.1, bf16[2304,128]{1,0:T(8,128)(2,1)} %o_down_hbm.1, ...), custom_call_target="tpu_custom_call" | custom-call | flops 40000000000 | bytes 33210000 | tf_op jit(solution)/shard_map/front/pallas_call | solution.py:349
  18.6 1.1 %collective-permute-done.6.refs_0_ = bf16[128,2304]{1,0:T(8,128)(2,1)S(1)} collective-permute-done((bf16[128,2304]{1,0:T(8,128)(2,1)}, bf16[128,2304]{1,0:T(8,128)(2,1)S(1)}, u32[]{:S(2)}, u32[]{:S(2)}) %collective-permute-start.6) | collective-permute-done | bytes 589856 | tf_op jit(solution)/shard_map/weights/ppermute | solution.py:335
  19.8 0.0 collective-permute-start.14
  19.8 2.5 %collective-permute-start.3 = (bf16[128,256]{1,0:T(8,128)(2,1)}, bf16[128,256]{1,0:T(8,128)(2,1)S(1)}, u32[]{:S(2)}, u32[]{:S(2)}) collective-permute-start(bf16[128,256]{1,0:T(8,128)(2,1)} %get-tuple-element.25.refs_0_), channel_id=1, source_target_pairs={{0,96},{32,0},{64,32},{96,64},{128,224},{160,128},{192,160},{224,1... | collective-permute-start | bytes 196616 | tf_op jit(solution)/shard_map/states/ppermute | solution.py:397
  22.2 0.7 %collective-permute-start.2 = (bf16[128,256]{1,0:T(8,128)(2,1)}, bf16[128,256]{1,0:T(8,128)(2,1)S(1)}, u32[]{:S(2)}, u32[]{:S(2)}) collective-permute-start(bf16[128,256]{1,0:T(8,128)(2,1)} %get-tuple-element.25.refs_0_), channel_id=1, source_target_pairs={{0,64},{32,96},{64,0},{96,32},{128,192},{160,224},{192,128},{224,1... | collective-permute-start | bytes 196616 | tf_op jit(solution)/shard_map/states/ppermute | solution.py:397
  22.9 0.3 collective-permute-start.1
  23.3 0.0 collective-permute-done.7.refs_2_
  23.3 0.0 copy-done.3
  23.3 3.0 %collective-permute-start.8 = (bf16[128,2304]{1,0:T(8,128)(2,1)S(1)}, bf16[128,2304]{1,0:T(8,128)(2,1)S(1)}, u32[]{:S(2)}, u32[]{:S(2)}) collective-permute-start(bf16[128,2304]{1,0:T(8,128)(2,1)S(1)} %copy-done.3), channel_id=1, source_target_pairs={{0,1},{1,0},{2,3},{3,2},{4,5},{5,4},{6,7},{7,6},{8,9},{9,8},{10,11... | collective-permute-start | bytes 1769480 | tf_op jit(solution)/shard_map/weights/ppermute | solution.py:338
  26.3 0.0 collective-permute-done.3.refs_3_
  26.3 0.7 %collective-permute-start.9 = (bf16[128,2304]{1,0:T(8,128)(2,1)S(1)}, bf16[128,2304]{1,0:T(8,128)(2,1)S(1)}, u32[]{:S(2)}, u32[]{:S(2)}) collective-permute-start(bf16[128,2304]{1,0:T(8,128)(2,1)S(1)} %collective-permute-done.6.refs_0_), channel_id=1, source_target_pairs={{0,1},{1,0},{2,3},{3,2},{4,5},{5,4},{6,7},{7,6},{8,9},{9,8},{10,11... | collective-permute-start | bytes 1769480 | tf_op jit(solution)/shard_map/weights/ppermute | solution.py:338
  27.0 0.1 collective-permute-done.2.refs_2_
  27.1 3.7 %collective-permute-start.10 = (bf16[128,2304]{1,0:T(8,128)(2,1)S(1)}, bf16[128,2304]{1,0:T(8,128)(2,1)S(1)}, u32[]{:S(2)}, u32[]{:S(2)}) collective-permute-start(bf16[128,2304]{1,0:T(8,128)(2,1)S(1)} %collective-permute-done.7.refs_2_), channel_id=1, source_target_pairs={{0,1},{1,0},{2,3},{3,2},{4,5},{5,4},{6,7},{7,6},{8,9},{9,8},{10,11... | collective-permute-start | bytes 1769480 | tf_op jit(solution)/shard_map/weights/ppermute | solution.py:338
  30.8 0.0 collective-permute-done.1.refs_1_
  30.8 0.0 copy-start.1
  30.8 0.8 %copy-done.1 = bf16[128,256]{1,0:T(8,128)(2,1)S(1)} copy-done((bf16[128,256]{1,0:T(8,128)(2,1)S(1)}, bf16[128,256]{1,0:T(8,128)(2,1)}, u32[]{:S(2)}) %copy-start.1) | copy-done | bytes 65560
  31.6 0.6 states.1
  32.2 0.3 collective-permute-start.4
  32.5 0.0 copy-done.2
  32.5 0.0 copy-start
  32.5 1.2 %copy-done = f32[640,384]{1,0:T(8,128)S(1)} copy-done((f32[640,384]{1,0:T(8,128)S(1)}, f32[640,384]{1,0:T(8,128)}, u32[]{:S(2)}) %copy-start) | copy-done | bytes 983064
  33.7 0.1 stage.1.pack
  33.8 1.5 %collective-permute-done.4.came = bf16[128,128]{1,0:T(8,128)(2,1)S(1)} collective-permute-done((bf16[128,128]{1,0:T(8,128)(2,1)S(1)}, bf16[128,128]{1,0:T(8,128)(2,1)S(1)}, u32[]{:S(2)}, u32[]{:S(2)}) %collective-permute-start.4) | collective-permute-done | bytes 32800 | tf_op jit(solution)/shard_map/states/ppermute | solution.py:409
  35.3 0.5 finish.1
  35.8 1.9 %collective-permute-start.5 = (bf16[4,4,16,128]{3,2,1,0:T(8,128)(2,1)S(1)}, bf16[4,4,16,128]{3,2,1,0:T(8,128)(2,1)S(1)}, u32[]{:S(2)}, u32[]{:S(2)}) collective-permute-start(bf16[4,4,16,128]{3,2,1,0:T(8,128)(2,1)S(1)} %get-tuple-element.30), channel_id=1, source_target_pairs={{0,1},{1,0},{2,3},{3,2},{4,5},{5,4},{6,7},{7,6},{8,9},{9,8},{10,11... | collective-permute-start | bytes 196616 | tf_op jit(solution)/shard_map/exchange/ppermute | solution.py:338
  37.7 0.9 %collective-permute-done.5.sibling = bf16[4,4,16,128]{3,2,1,0:T(8,128)(2,1)S(1)} collective-permute-done((bf16[4,4,16,128]{3,2,1,0:T(8,128)(2,1)S(1)}, bf16[4,4,16,128]{3,2,1,0:T(8,128)(2,1)S(1)}, u32[]{:S(2)}, u32[]{:S(2)}) %collective-permute-start.5) | collective-permute-done | bytes 65568 | tf_op jit(solution)/shard_map/exchange/ppermute | solution.py:338
  38.7 0.0 collective-permute-done.14.refs_4_
  38.7 0.4 collective-permute-start.15
  39.1 3.2 %collective-permute-start.11 = (bf16[2,4,16,128]{3,2,1,0:T(8,128)(2,1)S(1)}, bf16[2,4,16,128]{3,2,1,0:T(8,128)(2,1)S(1)}, u32[]{:S(2)}, u32[]{:S(2)}) collective-permute-start(bf16[2,4,16,128]{3,2,1,0:T(8,128)(2,1)S(1)} %get-tuple-element.37), channel_id=1, source_target_pairs={{0,6},{1,7},{2,4},{3,5},{4,2},{5,3},{6,0},{7,1},{8,14},{9,15},{10,... | collective-permute-start | bytes 98312 | tf_op jit(solution)/shard_map/exchange/ppermute | solution.py:338
  42.3 0.0 collective-permute-done.8.w_two
  42.3 1.0 %collective-permute-start.12 = (bf16[2,4,16,128]{3,2,1,0:T(8,128)(2,1)S(1)}, bf16[2,4,16,128]{3,2,1,0:T(8,128)(2,1)S(1)}, u32[]{:S(2)}, u32[]{:S(2)}) collective-permute-start(bf16[2,4,16,128]{3,2,1,0:T(8,128)(2,1)S(1)} %get-tuple-element.38), channel_id=1, source_target_pairs={{0,2},{1,3},{2,0},{3,1},{4,6},{5,7},{6,4},{7,5},{8,10},{9,11},{10,... | collective-permute-start | bytes 98312 | tf_op jit(solution)/shard_map/exchange/ppermute | solution.py:338
  43.3 0.0 collective-permute-done.9.refs_1_
  43.3 0.0 collective-permute-start.13
  43.3 0.0 collective-permute-done.10.refs_3_
  43.3 0.4 spread.2
  43.7 0.6 collective-permute-done.11.refs_0_
  44.3 2.3 %collective-permute-done.12.refs_1_ = bf16[2,4,16,128]{3,2,1,0:T(8,128)(2,1)S(1)} collective-permute-done((bf16[2,4,16,128]{3,2,1,0:T(8,128)(2,1)S(1)}, bf16[2,4,16,128]{3,2,1,0:T(8,128)(2,1)S(1)}, u32[]{:S(2)}, u32[]{:S(2)}) %collective-permute-start.12) | collective-permute-done | bytes 32800 | tf_op jit(solution)/shard_map/exchange/ppermute | solution.py:338
  46.6 0.0 collective-permute-done.13.refs_2_
  46.6 0.0 collective-permute-done.15.refs_5_
  46.6 0.7 %spread.3 = bf16[4,16,2304]{2,1,0:T(8,128)(2,1)S(1)} custom-call(f32[64,2304]{1,0:T(8,128)S(1)} %get-tuple-element.36.begun, bf16[2,4,16,128]{3,2,1,0:T(8,128)(2,1)S(1)} %collective-permute-done.11.refs_0_, bf16[2,4,16,128]{3,2,1,0:T(8,128)(2,1)S(1)} %collective-permute-done.12.refs_1_, bf16[2,4,16,128]{3,2,1,0:T(8,128)(2,1)S(1)} %collective-permute-done.13.refs_2_, ...), custom_call_target="tpu_custom_call" | custom-call | flops 1000000000 | bytes 3690000 | tf_op jit(solution)/shard_map/spread/pallas_call | solution.py:459
  47.3 6.1 %collective-permute-start.16 = (bf16[16,2304]{1,0:T(8,128)(2,1)S(1)}, bf16[16,2304]{1,0:T(8,128)(2,1)S(1)}, u32[]{:S(2)}, u32[]{:S(2)}) collective-permute-start(bf16[16,2304]{1,0:T(8,128)(2,1)S(1)} %get-tuple-element.43), channel_id=1, source_target_pairs={{0,16},{1,17},{2,18},{3,19},{4,20},{5,21},{6,22},{7,23},{8,24},{9,... | collective-permute-start | bytes 221192 | tf_op jit(solution)/shard_map/reduce/ppermute | solution.py:338
  53.4 0.3 collective-permute-start.18
  53.7 0.9 %collective-permute-start.17 = (bf16[16,2304]{1,0:T(8,128)(2,1)S(1)}, bf16[16,2304]{1,0:T(8,128)(2,1)S(1)}, u32[]{:S(2)}, u32[]{:S(2)}) collective-permute-start(bf16[16,2304]{1,0:T(8,128)(2,1)S(1)} %get-tuple-element.45), channel_id=1, source_target_pairs={{0,8},{1,9},{2,10},{3,11},{4,12},{5,13},{6,14},{7,15},{8,0},{9,1},... | collective-permute-start | bytes 221192 | tf_op jit(solution)/shard_map/reduce/ppermute | solution.py:338
  54.6 0.6 collective-permute-done.16
  55.2 4.5 %collective-permute-done.18 = bf16[16,2304]{1,0:T(8,128)(2,1)S(1)} collective-permute-done((bf16[16,2304]{1,0:T(8,128)(2,1)S(1)}, bf16[16,2304]{1,0:T(8,128)(2,1)S(1)}, u32[]{:S(2)}, u32[]{:S(2)}) %collective-permute-start.18) | collective-permute-done | bytes 73760 | tf_op jit(solution)/shard_map/reduce/ppermute | solution.py:338
  59.7 1.3 %collective-permute-done.17 = bf16[16,2304]{1,0:T(8,128)(2,1)S(1)} collective-permute-done((bf16[16,2304]{1,0:T(8,128)(2,1)S(1)}, bf16[16,2304]{1,0:T(8,128)(2,1)S(1)}, u32[]{:S(2)}, u32[]{:S(2)}) %collective-permute-start.17) | collective-permute-done | bytes 73760 | tf_op jit(solution)/shard_map/reduce/ppermute | solution.py:338
  61.1 0.7 %fusion.2 = bf16[16,2304]{1,0:T(8,128)(2,1)} fusion(bf16[16,2304]{1,0:T(8,128)(2,1)S(1)} %collective-permute-done.18, bf16[16,2304]{1,0:T(8,128)(2,1)S(1)} %collective-permute-done.17, bf16[16,2304]{1,0:T(8,128)(2,1)S(1)} %collective-permute-done.16, bf16[4,16,2304]{2,1,0:T(8,128)(2,1)S(1)} %spread.3), kind=kLoop, calls=%fused_computation.3 | loop fusion | flops 294912 | bytes 368640 | tf_op jit(solution)/shard_map/reduce/convert_element_type | solution.py:472
  (2 shorter events, 0.0 us)
Async XLA Ops:
  0.9 7.1 %collective-permute-start = (bf16[16,2304]{1,0:T(8,128)(2,1)S(1)}, bf16[16,2304]{1,0:T(8,128)(2,1)S(1)}, u32[]{:S(2)}, u32[]{:S(2)}) collective-permute-start(bf16[16,2304]{1,0:T(8,128)(2,1)S(1)} %slice.15), channel_id=1, source_target_pairs={{0,32},{32,64},{64,96},{96,128},{128,160},{160,192},{192,224},{224... | collective-permute-start | bytes 221192 | tf_op jit(solution)/shard_map/rim/ppermute | solution.py:344
  2.9 20.3 %collective-permute-start.7 = (bf16[128,2304]{1,0:T(8,128)(2,1)}, bf16[128,2304]{1,0:T(8,128)(2,1)S(1)}, u32[]{:S(2)}, u32[]{:S(2)}) collective-permute-start(bf16[128,2304]{1,0:T(8,128)(2,1)} %w_one.1), channel_id=1, source_target_pairs={{0,4},{1,5},{2,6},{3,7},{4,0},{5,1},{6,2},{7,3},{8,12},{9,13},{10,... | collective-permute-start | bytes 1769480 | tf_op jit(solution)/shard_map/weights/ppermute | solution.py:338
  4.6 15.2 %collective-permute-start.6 = (bf16[128,2304]{1,0:T(8,128)(2,1)}, bf16[128,2304]{1,0:T(8,128)(2,1)S(1)}, u32[]{:S(2)}, u32[]{:S(2)}) collective-permute-start(bf16[128,2304]{1,0:T(8,128)(2,1)} %w_one.1), channel_id=1, source_target_pairs={{0,130},{1,131},{2,128},{3,129},{4,134},{5,135},{6,132},{7,133},{8... | collective-permute-start | bytes 1769480 | tf_op jit(solution)/shard_map/weights/ppermute | solution.py:335
  8.0 0.6 %copy-start.4 = (bf16[16,2304]{1,0:T(8,128)(2,1)}, bf16[16,2304]{1,0:T(8,128)(2,1)S(1)}, u32[]{:S(2)}) copy-start(bf16[16,2304]{1,0:T(8,128)(2,1)S(1)} %collective-permute-done.rim_hbm) | copy-start | bytes 221188
  8.6 14.7 %copy-start.3 = (bf16[128,2304]{1,0:T(8,128)(2,1)S(1)}, bf16[128,2304]{1,0:T(8,128)(2,1)}, u32[]{:S(2)}) copy-start(bf16[128,2304]{1,0:T(8,128)(2,1)} %w_one.1) | copy-start | bytes 1769476
  8.6 23.9 %copy-start.2 = (f32[128]{0:T(128)S(1)}, f32[128]{0:T(128)}, u32[]{:S(2)}) copy-start(f32[128]{0:T(128)} %param.22) | copy-start | bytes 1540
  19.8 18.9 %collective-permute-start.14 = (bf16[128,2304]{1,0:T(8,128)(2,1)S(1)}, bf16[128,2304]{1,0:T(8,128)(2,1)S(1)}, u32[]{:S(2)}, u32[]{:S(2)}) collective-permute-start(bf16[128,2304]{1,0:T(8,128)(2,1)S(1)} %collective-permute-done.6.refs_0_), channel_id=1, source_target_pairs={{0,4},{1,5},{2,6},{3,7},{4,0},{5,1},{6,2},{7,3},{8,12},{9,13},{10,... | collective-permute-start | bytes 1769480 | tf_op jit(solution)/shard_map/weights/ppermute | solution.py:338
  19.8 6.5 %collective-permute-start.3 = (bf16[128,256]{1,0:T(8,128)(2,1)}, bf16[128,256]{1,0:T(8,128)(2,1)S(1)}, u32[]{:S(2)}, u32[]{:S(2)}) collective-permute-start(bf16[128,256]{1,0:T(8,128)(2,1)} %get-tuple-element.25.refs_0_), channel_id=1, source_target_pairs={{0,96},{32,0},{64,32},{96,64},{128,224},{160,128},{192,160},{224,1... | collective-permute-start | bytes 196616 | tf_op jit(solution)/shard_map/states/ppermute | solution.py:397
  22.2 4.9 %collective-permute-start.2 = (bf16[128,256]{1,0:T(8,128)(2,1)}, bf16[128,256]{1,0:T(8,128)(2,1)S(1)}, u32[]{:S(2)}, u32[]{:S(2)}) collective-permute-start(bf16[128,256]{1,0:T(8,128)(2,1)} %get-tuple-element.25.refs_0_), channel_id=1, source_target_pairs={{0,64},{32,96},{64,0},{96,32},{128,192},{160,224},{192,128},{224,1... | collective-permute-start | bytes 196616 | tf_op jit(solution)/shard_map/states/ppermute | solution.py:397
  22.9 7.8 %collective-permute-start.1 = (bf16[128,256]{1,0:T(8,128)(2,1)}, bf16[128,256]{1,0:T(8,128)(2,1)S(1)}, u32[]{:S(2)}, u32[]{:S(2)}) collective-permute-start(bf16[128,256]{1,0:T(8,128)(2,1)} %get-tuple-element.25.refs_0_), channel_id=1, source_target_pairs={{0,32},{32,64},{64,96},{96,0},{128,160},{160,192},{192,224},{224,1... | collective-permute-start | bytes 196616 | tf_op jit(solution)/shard_map/states/ppermute | solution.py:397
  23.3 19.0 %collective-permute-start.8 = (bf16[128,2304]{1,0:T(8,128)(2,1)S(1)}, bf16[128,2304]{1,0:T(8,128)(2,1)S(1)}, u32[]{:S(2)}, u32[]{:S(2)}) collective-permute-start(bf16[128,2304]{1,0:T(8,128)(2,1)S(1)} %copy-done.3), channel_id=1, source_target_pairs={{0,1},{1,0},{2,3},{3,2},{4,5},{5,4},{6,7},{7,6},{8,9},{9,8},{10,11... | collective-permute-start | bytes 1769480 | tf_op jit(solution)/shard_map/weights/ppermute | solution.py:338
  26.3 17.0 %collective-permute-start.9 = (bf16[128,2304]{1,0:T(8,128)(2,1)S(1)}, bf16[128,2304]{1,0:T(8,128)(2,1)S(1)}, u32[]{:S(2)}, u32[]{:S(2)}) collective-permute-start(bf16[128,2304]{1,0:T(8,128)(2,1)S(1)} %collective-permute-done.6.refs_0_), channel_id=1, source_target_pairs={{0,1},{1,0},{2,3},{3,2},{4,5},{5,4},{6,7},{7,6},{8,9},{9,8},{10,11... | collective-permute-start | bytes 1769480 | tf_op jit(solution)/shard_map/weights/ppermute | solution.py:338
  27.1 16.2 %collective-permute-start.10 = (bf16[128,2304]{1,0:T(8,128)(2,1)S(1)}, bf16[128,2304]{1,0:T(8,128)(2,1)S(1)}, u32[]{:S(2)}, u32[]{:S(2)}) collective-permute-start(bf16[128,2304]{1,0:T(8,128)(2,1)S(1)} %collective-permute-done.7.refs_2_), channel_id=1, source_target_pairs={{0,1},{1,0},{2,3},{3,2},{4,5},{5,4},{6,7},{7,6},{8,9},{9,8},{10,11... | collective-permute-start | bytes 1769480 | tf_op jit(solution)/shard_map/weights/ppermute | solution.py:338
  30.8 0.8 %copy-start.1 = (bf16[128,256]{1,0:T(8,128)(2,1)S(1)}, bf16[128,256]{1,0:T(8,128)(2,1)}, u32[]{:S(2)}) copy-start(bf16[128,256]{1,0:T(8,128)(2,1)} %get-tuple-element.25.refs_0_) | copy-start | bytes 196612
  32.2 3.0 %collective-permute-start.4 = (bf16[128,128]{1,0:T(8,128)(2,1)S(1)}, bf16[128,128]{1,0:T(8,128)(2,1)S(1)}, u32[]{:S(2)}, u32[]{:S(2)}) collective-permute-start(bf16[128,128]{1,0:T(8,128)(2,1)S(1)} %get-tuple-element.26), channel_id=1, source_target_pairs={{0,128},{32,160},{64,192},{96,224},{128,0},{160,32},{192,64},{224,... | collective-permute-start | bytes 98312 | tf_op jit(solution)/shard_map/states/ppermute | solution.py:409
  32.5 1.2 %copy-start = (f32[640,384]{1,0:T(8,128)S(1)}, f32[640,384]{1,0:T(8,128)}, u32[]{:S(2)}) copy-start(f32[640,384]{1,0:T(8,128)} %get-tuple-element.27.pack) | copy-start | bytes 2949124
  35.8 2.8 %collective-permute-start.5 = (bf16[4,4,16,128]{3,2,1,0:T(8,128)(2,1)S(1)}, bf16[4,4,16,128]{3,2,1,0:T(8,128)(2,1)S(1)}, u32[]{:S(2)}, u32[]{:S(2)}) collective-permute-start(bf16[4,4,16,128]{3,2,1,0:T(8,128)(2,1)S(1)} %get-tuple-element.30), channel_id=1, source_target_pairs={{0,1},{1,0},{2,3},{3,2},{4,5},{5,4},{6,7},{7,6},{8,9},{9,8},{10,11... | collective-permute-start | bytes 196616 | tf_op jit(solution)/shard_map/exchange/ppermute | solution.py:338
  38.7 7.9 %collective-permute-start.15 = (bf16[128,2304]{1,0:T(8,128)(2,1)S(1)}, bf16[128,2304]{1,0:T(8,128)(2,1)S(1)}, u32[]{:S(2)}, u32[]{:S(2)}) collective-permute-start(bf16[128,2304]{1,0:T(8,128)(2,1)S(1)} %collective-permute-done.14.refs_4_), channel_id=1, source_target_pairs={{0,1},{1,0},{2,3},{3,2},{4,5},{5,4},{6,7},{7,6},{8,9},{9,8},{10,11... | collective-permute-start | bytes 1769480 | tf_op jit(solution)/shard_map/spread/ppermute | solution.py:338
  39.1 5.2 %collective-permute-start.11 = (bf16[2,4,16,128]{3,2,1,0:T(8,128)(2,1)S(1)}, bf16[2,4,16,128]{3,2,1,0:T(8,128)(2,1)S(1)}, u32[]{:S(2)}, u32[]{:S(2)}) collective-permute-start(bf16[2,4,16,128]{3,2,1,0:T(8,128)(2,1)S(1)} %get-tuple-element.37), channel_id=1, source_target_pairs={{0,6},{1,7},{2,4},{3,5},{4,2},{5,3},{6,0},{7,1},{8,14},{9,15},{10,... | collective-permute-start | bytes 98312 | tf_op jit(solution)/shard_map/exchange/ppermute | solution.py:338
  42.3 4.3 %collective-permute-start.12 = (bf16[2,4,16,128]{3,2,1,0:T(8,128)(2,1)S(1)}, bf16[2,4,16,128]{3,2,1,0:T(8,128)(2,1)S(1)}, u32[]{:S(2)}, u32[]{:S(2)}) collective-permute-start(bf16[2,4,16,128]{3,2,1,0:T(8,128)(2,1)S(1)} %get-tuple-element.38), channel_id=1, source_target_pairs={{0,2},{1,3},{2,0},{3,1},{4,6},{5,7},{6,4},{7,5},{8,10},{9,11},{10,... | collective-permute-start | bytes 98312 | tf_op jit(solution)/shard_map/exchange/ppermute | solution.py:338
  43.3 3.3 %collective-permute-start.13 = (bf16[2,4,16,128]{3,2,1,0:T(8,128)(2,1)S(1)}, bf16[2,4,16,128]{3,2,1,0:T(8,128)(2,1)S(1)}, u32[]{:S(2)}, u32[]{:S(2)}) collective-permute-start(bf16[2,4,16,128]{3,2,1,0:T(8,128)(2,1)S(1)} %get-tuple-element.39), channel_id=1, source_target_pairs={{0,4},{1,5},{2,6},{3,7},{4,0},{5,1},{6,2},{7,3},{8,12},{9,13},{10,... | collective-permute-start | bytes 98312 | tf_op jit(solution)/shard_map/exchange/ppermute | solution.py:338
  47.3 7.9 %collective-permute-start.16 = (bf16[16,2304]{1,0:T(8,128)(2,1)S(1)}, bf16[16,2304]{1,0:T(8,128)(2,1)S(1)}, u32[]{:S(2)}, u32[]{:S(2)}) collective-permute-start(bf16[16,2304]{1,0:T(8,128)(2,1)S(1)} %get-tuple-element.43), channel_id=1, source_target_pairs={{0,16},{1,17},{2,18},{3,19},{4,20},{5,21},{6,22},{7,23},{8,24},{9,... | collective-permute-start | bytes 221192 | tf_op jit(solution)/shard_map/reduce/ppermute | solution.py:338
  53.4 6.3 %collective-permute-start.18 = (bf16[16,2304]{1,0:T(8,128)(2,1)S(1)}, bf16[16,2304]{1,0:T(8,128)(2,1)S(1)}, u32[]{:S(2)}, u32[]{:S(2)}) collective-permute-start(bf16[16,2304]{1,0:T(8,128)(2,1)S(1)} %get-tuple-element.44), channel_id=1, source_target_pairs={{0,24},{1,25},{2,26},{3,27},{4,28},{5,29},{6,30},{7,31},{8,16},{9,... | collective-permute-start | bytes 221192 | tf_op jit(solution)/shard_map/reduce/ppermute | solution.py:338
  53.7 7.4 %collective-permute-start.17 = (bf16[16,2304]{1,0:T(8,128)(2,1)S(1)}, bf16[16,2304]{1,0:T(8,128)(2,1)S(1)}, u32[]{:S(2)}, u32[]{:S(2)}) collective-permute-start(bf16[16,2304]{1,0:T(8,128)(2,1)S(1)} %get-tuple-element.45), channel_id=1, source_target_pairs={{0,8},{1,9},{2,10},{3,11},{4,12},{5,13},{6,14},{7,15},{8,0},{9,1},... | collective-permute-start | bytes 221192 | tf_op jit(solution)/shard_map/reduce/ppermute | solution.py:338

commit v8 on v6

--- a/solution.py
+++ b/solution.py
@@ -197,13 +197,15 @@
             states[group] = jnp.concatenate(
                 [state[:, :head] + pairs[at][:, :head], state[:, head:]], axis=1
             )
-    pack[rows:, : 2 * head] = states[0]
+    pack[rows : rows + head, : 2 * head] = states[0]
     store((pl.ds(rows, head), pl.ds(0, 2 * head)))
     whole = mm(states[1][:, head:], states[0])
     final[...] = jnp.concatenate(
         [whole[:, :head] + states[1][:, :head], whole[:, head:]], axis=1
     ).astype(BF16)
     copies = load([(final, sends)], out_sems)
+    pack[rows + head :, : 2 * head] = final[...].astype(F32)
+    store((pl.ds(rows + head, head), pl.ds(0, 2 * head)))
     queries = (unit_rows(query_raw) * (head ** (-0.5))).astype(BF16).astype(F32)
     query_rise = queries * rising
     for group, start in enumerate(range(0, rows, GROUP)):
@@ -224,13 +226,14 @@
         copy.wait()
 
 
-def fold(*refs):
+def fold(pack, *refs):
     found, (before, total, held) = refs[:-3], refs[-3:]
-    count = len(found)
+    count = len(found) + 1
     mine = lax.rem(lax.axis_index("ctx"), count)
     head = found[0].shape[0]
+    held[0] = pack[pack.shape[0] - head :, : 2 * head].astype(BF16)
     for back, ref in enumerate(found):
-        held[back] = ref[...]
+        held[back + 1] = ref[...]
     row = lax.broadcasted_iota(jnp.int32, (head, 2 * head), 0)
     col = lax.broadcasted_iota(jnp.int32, (head, 2 * head), 1)
     state = jnp.where(row + head == col, 1.0, 0.0).astype(F32)
@@ -248,19 +251,20 @@
 
 def stage(pack, gain, out):
     head = gain.shape[1]
-    rows = pack.shape[0] - head
+    rows = pack.shape[0] - 2 * head
     out[:, : 2 * head] = pack[:, : 2 * head]
     out[:rows, 2 * head :] = pack[:rows, 2 * head :] * gain[...]
 
 
 def finish(pack, before, came, own, other, gated):
     head = came.shape[0]
-    rows = pack.shape[0] - head
+    rows = pack.shape[0] - 2 * head
     core_at = lax.rem(lax.axis_index("head"), 2)
     later = lax.axis_index("ctx") >= lax.axis_size("ctx") // 2
     state = jnp.where(later, came[...].astype(F32), 0.0)
     state = mm(before[:, head:], state) + before[:, :head]
-    middle = mm(pack[rows:, head : 2 * head], state) + pack[rows:, :head]
+    middle = mm(pack[rows : rows + head, head : 2 * head], state)
+    middle = middle + pack[rows : rows + head, :head]
     cores = []
     for group, start in enumerate((state, middle)):
         rng = slice(group * SPAN, (group + 1) * SPAN)
@@ -351,7 +355,7 @@
             in_specs=[HBM] * 11,
             out_specs=[HBM] * 2,
             out_shape=[
-                shape((rows + head, 3 * head), F32),
+                shape((rows + 2 * head, 3 * head), F32),
                 shape((head, 2 * head), BF16),
             ],
             scratch_shapes=[
@@ -369,10 +373,10 @@
                 pltpu.VMEM((rows + 16, 6 * head), F32),
                 pltpu.VMEM((rows + 8, 3 * head), F32),
                 pltpu.VMEM((head, 2 * head), BF16),
-                pltpu.VMEM((rows + head, 3 * head), F32),
+                pltpu.VMEM((rows + 2 * head, 3 * head), F32),
                 dma((7 + 6 * CHUNKS,)),
                 dma((1,)),
-                dma((2 + rows // GROUP,)),
+                dma((3 + rows // GROUP,)),
             ],
             compiler_params=FULL,
             cost_estimate=cost(9, 40),
@@ -397,16 +401,6 @@
             return lax.ppermute(sends, "ctx", pairs)
 
         found = {step: around(step) for step in range(1, half)}
-        before, total = pl.pallas_call(
-            fold,
-            in_specs=[VMEM] * half,
-            out_specs=[VMEM] * 2,
-            out_shape=[shape((head, 2 * head), F32), shape((head, head), BF16)],
-            scratch_shapes=[pltpu.VMEM((half, head, 2 * head), BF16)],
-            compiler_params=LIMIT,
-            cost_estimate=cost(0.5, 0),
-        )(sends, *(found[step] for step in range(1, half)))
-        came = lax.ppermute(total, "ctx", [(c, (c + half) % ctx_count) for c in range(ctx_count)])
     (w_early,) = after((w_far,), pack)
     with jax.named_scope("weights"):
         w_both = flip(w_early, 4)
@@ -419,6 +413,17 @@
             compiler_params=LIMIT,
             cost_estimate=cost(0.5, 0.5),
         )(pack, norm_gain.reshape(1, head))
+    with jax.named_scope("states"):
+        before, total = pl.pallas_call(
+            fold,
+            in_specs=[VMEM] * half,
+            out_specs=[VMEM] * 2,
+            out_shape=[shape((head, 2 * head), F32), shape((head, head), BF16)],
+            scratch_shapes=[pltpu.VMEM((half, head, 2 * head), BF16)],
+            compiler_params=LIMIT,
+            cost_estimate=cost(0.5, 0),
+        )(staged, *(found[step] for step in range(1, half)))
+        came = lax.ppermute(total, "ctx", [(c, (c + half) % ctx_count) for c in range(ctx_count)])
     w_late, w_near, w_mine = after((w_far, w_next, w_out), staged)
     with jax.named_scope("weights"):
         w_core, w_far_core, w_next_core = flip(w_mine, 1), flip(w_late, 1), flip(w_near, 1)

time: 61 us -> 61 us (level)
  waiting for transfers between devices: 12.3 us -> 14.4 us
  starting transfers between devices: 30.8 us -> 29.8 us
  local copies, waits for them, and re-layouts: 3.58 us -> 2.81 us
    ppermute x1, waiting for transfers between devices: 0.01 us -> 1.12 us  [across(): return lax.ppermute(value, ('ctx', 'head'), pairs)]
    ppermute x3, starting transfers between devices: 4.52 us -> 3.49 us  [around(): return lax.ppermute(sends, 'ctx', pairs)]
    unnamed x10 -> x8, local copies, waits for them, and re-layouts: 2.68 us -> 1.91 us
    ppermute x13, waiting for transfers between devices: 9.48 us -> 10.2 us  [flip(): lax.ppermute(value, 'head', [(h, h ^ mask) for h in range(head_count)])]
  transfers between devices with their start and end apart: 19 -> 19, of which waited for: 6 -> 8; matrix products, arithmetic and copies ran while one was open for 0% -> 0% of each run, Pallas kernels for 19% -> 19%
where the time goes in v8:
time: 61 us; the launch traced here: 60.9 us
  starting transfers between devices  29.8 us (49%)
  waiting for transfers between devices  14.4 us (24%)
  Pallas kernels  12.4 us (20%)
  local copies, waits for them, and re-layouts  2.81 us (5%)
  between operations  0.76 us (1%)
  other arithmetic  0.68 us (1%)
    ppermute x13, starting transfers between devices, flip(): lax.ppermute(value, 'head', [(h, h ^ mask) for h in range(head_count)])  21.3 us
    ppermute x13, waiting for transfers between devices, flip(): lax.ppermute(value, 'head', [(h, h ^ mask) for h in range(head_count)])  10.2 us
    pallas_call x1, Pallas kernels, on_device(): pl.pallas_call(front, in_specs=[HBM] * 11, out_specs=[HBM] * 2, out_shape...  10 us
    ppermute x3, starting transfers between devices, around(): return lax.ppermute(sends, 'ctx', pairs)  3.49 us
    ppermute x1, waiting for transfers between devices, on_device(): lax.ppermute(total, 'ctx', [(c, (c + half) % ctx_count) for c in range(ct...  3.05 us
    ppermute x1, starting transfers between devices, across(): return lax.ppermute(value, ('ctx', 'head'), pairs)  2.73 us
    ppermute x1, starting transfers between devices, on_device(): lax.ppermute(edge, 'ctx', [(i, (i + 1) % ctx_count) for i in range(ctx_co...  2.04 us
    unnamed x8, local copies, waits for them, and re-layouts  1.91 us
  transfers between devices with their start and end apart: 19, of which 8 were waited for; matrix products, arithmetic and copies ran while one was open for 0% of the time, Pallas kernels for 19%

profile of v8, /device:TPU:1, one launch (start us, length us, event | category | flops | bytes accessed | tf_op | source)
XLA Modules:
  0.0 60.9 jit_solution(11136974209007749584)
XLA Ops:
  0.0 0.9 %slice.15 = bf16[16,2304]{1,0:T(8,128)(2,1)S(1)} slice(bf16[512,2304]{1,0:T(8,128)(2,1)} %tokens_hbm.1), slice={[496:512], [0:2304]} | slice | bytes 147456 | tf_op jit(solution)/shard_map/slice | solution.py:346
  0.9 2.0 %collective-permute-start = (bf16[16,2304]{1,0:T(8,128)(2,1)S(1)}, bf16[16,2304]{1,0:T(8,128)(2,1)S(1)}, u32[]{:S(2)}, u32[]{:S(2)}) collective-permute-start(bf16[16,2304]{1,0:T(8,128)(2,1)S(1)} %slice.15), channel_id=1, source_target_pairs={{0,32},{32,64},{64,96},{96,128},{128,160},{160,192},{192,224},{224... | collective-permute-start | bytes 221192 | tf_op jit(solution)/shard_map/rim/ppermute | solution.py:348
  2.9 1.6 %collective-permute-start.7 = (bf16[128,2304]{1,0:T(8,128)(2,1)}, bf16[128,2304]{1,0:T(8,128)(2,1)S(1)}, u32[]{:S(2)}, u32[]{:S(2)}) collective-permute-start(bf16[128,2304]{1,0:T(8,128)(2,1)} %w_one.1), channel_id=1, source_target_pairs={{0,4},{1,5},{2,6},{3,7},{4,0},{5,1},{6,2},{7,3},{8,12},{9,13},{10,... | collective-permute-start | bytes 1769480 | tf_op jit(solution)/shard_map/weights/ppermute | solution.py:342
  4.6 2.7 %collective-permute-start.6 = (bf16[128,2304]{1,0:T(8,128)(2,1)}, bf16[128,2304]{1,0:T(8,128)(2,1)S(1)}, u32[]{:S(2)}, u32[]{:S(2)}) collective-permute-start(bf16[128,2304]{1,0:T(8,128)(2,1)} %w_one.1), channel_id=1, source_target_pairs={{0,130},{1,131},{2,128},{3,129},{4,134},{5,135},{6,132},{7,133},{8... | collective-permute-start | bytes 1769480 | tf_op jit(solution)/shard_map/weights/ppermute | solution.py:339
  8.0 0.0 collective-permute-done.rim_hbm
  8.0 0.0 copy-start.3
  8.0 0.6 %copy-done.3 = bf16[16,2304]{1,0:T(8,128)(2,1)} copy-done((bf16[16,2304]{1,0:T(8,128)(2,1)}, bf16[16,2304]{1,0:T(8,128)(2,1)S(1)}, u32[]{:S(2)}) %copy-start.3) | copy-done | bytes 73752
  8.6 0.0 copy-start.1
  8.6 0.0 copy-start.2
  8.6 10.0 %front.1 = (f32[768,384]{1,0:T(8,128)}, bf16[128,256]{1,0:T(8,128)(2,1)}) custom-call(bf16[512,2304]{1,0:T(8,128)(2,1)} %tokens_hbm.1, bf16[16,2304]{1,0:T(8,128)(2,1)} %copy-done.3, f32[1,1]{1,0:T(1,128)} %bitcast.17.alog_hbm, bf16[3,2304,128]{2,1,0:T(8,128)(2,1)} %bitcast.19, bf16[2304,128]{1,0:T(8,128)(2,1)} %f_down_hbm.1, bf16[2304,128]{1,0:T(8,128)(2,1)} %o_down_hbm.1, ...), custom_call_target="tpu_custom_call" | custom-call | flops 40000000000 | bytes 33210000 | tf_op jit(solution)/shard_map/front/pallas_call | solution.py:353
  18.6 1.1 %collective-permute-done.6.refs_0_ = bf16[128,2304]{1,0:T(8,128)(2,1)S(1)} collective-permute-done((bf16[128,2304]{1,0:T(8,128)(2,1)}, bf16[128,2304]{1,0:T(8,128)(2,1)S(1)}, u32[]{:S(2)}, u32[]{:S(2)}) %collective-permute-start.6) | collective-permute-done | bytes 589856 | tf_op jit(solution)/shard_map/weights/ppermute | solution.py:339
  19.8 0.0 collective-permute-start.14
  19.8 2.5 %collective-permute-start.3 = (bf16[128,256]{1,0:T(8,128)(2,1)}, bf16[128,256]{1,0:T(8,128)(2,1)S(1)}, u32[]{:S(2)}, u32[]{:S(2)}) collective-permute-start(bf16[128,256]{1,0:T(8,128)(2,1)} %get-tuple-element.24), channel_id=1, source_target_pairs={{0,96},{32,0},{64,32},{96,64},{128,224},{160,128},{192,160},{224,1... | collective-permute-start | bytes 196616 | tf_op jit(solution)/shard_map/states/ppermute | solution.py:401
  22.2 0.7 %collective-permute-start.2 = (bf16[128,256]{1,0:T(8,128)(2,1)}, bf16[128,256]{1,0:T(8,128)(2,1)S(1)}, u32[]{:S(2)}, u32[]{:S(2)}) collective-permute-start(bf16[128,256]{1,0:T(8,128)(2,1)} %get-tuple-element.24), channel_id=1, source_target_pairs={{0,64},{32,96},{64,0},{96,32},{128,192},{160,224},{192,128},{224,1... | collective-permute-start | bytes 196616 | tf_op jit(solution)/shard_map/states/ppermute | solution.py:401
  22.9 0.3 collective-permute-start.1
  23.3 0.0 copy-done.1
  23.3 0.0 copy-start
  23.3 1.3 %copy-done = f32[768,384]{1,0:T(8,128)S(1)} copy-done((f32[768,384]{1,0:T(8,128)S(1)}, f32[768,384]{1,0:T(8,128)}, u32[]{:S(2)}) %copy-start) | copy-done | bytes 1179672
  24.5 0.1 stage.1.pack
  24.6 0.0 collective-permute-done.7.refs_2_
  24.6 0.0 copy-done.2
  24.6 3.1 %collective-permute-start.8 = (bf16[128,2304]{1,0:T(8,128)(2,1)S(1)}, bf16[128,2304]{1,0:T(8,128)(2,1)S(1)}, u32[]{:S(2)}, u32[]{:S(2)}) collective-permute-start(bf16[128,2304]{1,0:T(8,128)(2,1)S(1)} %copy-done.2), channel_id=1, source_target_pairs={{0,1},{1,0},{2,3},{3,2},{4,5},{5,4},{6,7},{7,6},{8,9},{9,8},{10,11... | collective-permute-start | bytes 1769480 | tf_op jit(solution)/shard_map/weights/ppermute | solution.py:342
  27.7 0.0 collective-permute-done.3.refs_2_
  27.7 0.1 collective-permute-start.9
  27.8 0.0 collective-permute-done.2.refs_1_
  27.8 2.9 %collective-permute-start.10 = (bf16[128,2304]{1,0:T(8,128)(2,1)S(1)}, bf16[128,2304]{1,0:T(8,128)(2,1)S(1)}, u32[]{:S(2)}, u32[]{:S(2)}) collective-permute-start(bf16[128,2304]{1,0:T(8,128)(2,1)S(1)} %collective-permute-done.7.refs_2_), channel_id=1, source_target_pairs={{0,1},{1,0},{2,3},{3,2},{4,5},{5,4},{6,7},{7,6},{8,9},{9,8},{10,11... | collective-permute-start | bytes 1769480 | tf_op jit(solution)/shard_map/weights/ppermute | solution.py:342
  30.8 0.0 collective-permute-done.1.refs_0_
  30.8 0.6 %states.1 = (f32[128,256]{1,0:T(8,128)S(1)}, bf16[128,128]{1,0:T(8,128)(2,1)S(1)}) custom-call(f32[768,384]{1,0:T(8,128)S(1)} %stage.1.pack, bf16[128,256]{1,0:T(8,128)(2,1)S(1)} %collective-permute-done.1.refs_0_, bf16[128,256]{1,0:T(8,128)(2,1)S(1)} %collective-permute-done.2.refs_1_, bf16[128,256]{1,0:T(8,128)(2,1)S(1)} %collective-permute-done.3.refs_2_), custom_call_target="tpu_custom_call" | custom-call | bytes 1845000 | tf_op jit(solution)/shard_map/states/pallas_call | solution.py:417
  31.4 0.3 collective-permute-start.4
  31.7 3.0 %collective-permute-done.4.came = bf16[128,128]{1,0:T(8,128)(2,1)S(1)} collective-permute-done((bf16[128,128]{1,0:T(8,128)(2,1)S(1)}, bf16[128,128]{1,0:T(8,128)(2,1)S(1)}, u32[]{:S(2)}, u32[]{:S(2)}) %collective-permute-start.4) | collective-permute-done | bytes 32800 | tf_op jit(solution)/shard_map/states/ppermute | solution.py:426
  34.7 0.5 finish.1
  35.3 1.6 %collective-permute-start.5 = (bf16[4,4,16,128]{3,2,1,0:T(8,128)(2,1)S(1)}, bf16[4,4,16,128]{3,2,1,0:T(8,128)(2,1)S(1)}, u32[]{:S(2)}, u32[]{:S(2)}) collective-permute-start(bf16[4,4,16,128]{3,2,1,0:T(8,128)(2,1)S(1)} %get-tuple-element.28), channel_id=1, source_target_pairs={{0,1},{1,0},{2,3},{3,2},{4,5},{5,4},{6,7},{7,6},{8,9},{9,8},{10,11... | collective-permute-start | bytes 196616 | tf_op jit(solution)/shard_map/exchange/ppermute | solution.py:342
  36.9 0.9 %collective-permute-done.5.sibling = bf16[4,4,16,128]{3,2,1,0:T(8,128)(2,1)S(1)} collective-permute-done((bf16[4,4,16,128]{3,2,1,0:T(8,128)(2,1)S(1)}, bf16[4,4,16,128]{3,2,1,0:T(8,128)(2,1)S(1)}, u32[]{:S(2)}, u32[]{:S(2)}) %collective-permute-start.5) | collective-permute-done | bytes 65568 | tf_op jit(solution)/shard_map/exchange/ppermute | solution.py:342
  37.8 0.0 collective-permute-done.14.refs_4_
  37.8 0.4 collective-permute-start.15
  38.3 3.2 %collective-permute-start.11 = (bf16[2,4,16,128]{3,2,1,0:T(8,128)(2,1)S(1)}, bf16[2,4,16,128]{3,2,1,0:T(8,128)(2,1)S(1)}, u32[]{:S(2)}, u32[]{:S(2)}) collective-permute-start(bf16[2,4,16,128]{3,2,1,0:T(8,128)(2,1)S(1)} %get-tuple-element.35), channel_id=1, source_target_pairs={{0,6},{1,7},{2,4},{3,5},{4,2},{5,3},{6,0},{7,1},{8,14},{9,15},{10,... | collective-permute-start | bytes 98312 | tf_op jit(solution)/shard_map/exchange/ppermute | solution.py:342
  41.4 0.0 collective-permute-done.8.w_two
  41.4 1.0 %collective-permute-start.12 = (bf16[2,4,16,128]{3,2,1,0:T(8,128)(2,1)S(1)}, bf16[2,4,16,128]{3,2,1,0:T(8,128)(2,1)S(1)}, u32[]{:S(2)}, u32[]{:S(2)}) collective-permute-start(bf16[2,4,16,128]{3,2,1,0:T(8,128)(2,1)S(1)} %get-tuple-element.36), channel_id=1, source_target_pairs={{0,2},{1,3},{2,0},{3,1},{4,6},{5,7},{6,4},{7,5},{8,10},{9,11},{10,... | collective-permute-start | bytes 98312 | tf_op jit(solution)/shard_map/exchange/ppermute | solution.py:342
  42.4 0.0 collective-permute-done.9.refs_1_
  42.4 0.0 collective-permute-start.13
  42.4 0.0 collective-permute-done.10.refs_3_
  42.4 0.4 spread.2
  42.9 0.6 collective-permute-done.11.refs_0_
  43.4 2.3 %collective-permute-done.12.refs_1_ = bf16[2,4,16,128]{3,2,1,0:T(8,128)(2,1)S(1)} collective-permute-done((bf16[2,4,16,128]{3,2,1,0:T(8,128)(2,1)S(1)}, bf16[2,4,16,128]{3,2,1,0:T(8,128)(2,1)S(1)}, u32[]{:S(2)}, u32[]{:S(2)}) %collective-permute-start.12) | collective-permute-done | bytes 32800 | tf_op jit(solution)/shard_map/exchange/ppermute | solution.py:342
  45.7 0.0 collective-permute-done.13.refs_2_
  45.7 0.0 collective-permute-done.15.refs_5_
  45.7 0.7 %spread.3 = bf16[4,16,2304]{2,1,0:T(8,128)(2,1)S(1)} custom-call(f32[64,2304]{1,0:T(8,128)S(1)} %get-tuple-element.34.begun, bf16[2,4,16,128]{3,2,1,0:T(8,128)(2,1)S(1)} %collective-permute-done.11.refs_0_, bf16[2,4,16,128]{3,2,1,0:T(8,128)(2,1)S(1)} %collective-permute-done.12.refs_1_, bf16[2,4,16,128]{3,2,1,0:T(8,128)(2,1)S(1)} %collective-permute-done.13.refs_2_, ...), custom_call_target="tpu_custom_call" | custom-call | flops 1000000000 | bytes 3690000 | tf_op jit(solution)/shard_map/spread/pallas_call | solution.py:463
  46.5 6.1 %collective-permute-start.16 = (bf16[16,2304]{1,0:T(8,128)(2,1)S(1)}, bf16[16,2304]{1,0:T(8,128)(2,1)S(1)}, u32[]{:S(2)}, u32[]{:S(2)}) collective-permute-start(bf16[16,2304]{1,0:T(8,128)(2,1)S(1)} %get-tuple-element.41), channel_id=1, source_target_pairs={{0,16},{1,17},{2,18},{3,19},{4,20},{5,21},{6,22},{7,23},{8,24},{9,... | collective-permute-start | bytes 221192 | tf_op jit(solution)/shard_map/reduce/ppermute | solution.py:342
  52.6 0.3 collective-permute-start.18
  52.9 0.9 %collective-permute-start.17 = (bf16[16,2304]{1,0:T(8,128)(2,1)S(1)}, bf16[16,2304]{1,0:T(8,128)(2,1)S(1)}, u32[]{:S(2)}, u32[]{:S(2)}) collective-permute-start(bf16[16,2304]{1,0:T(8,128)(2,1)S(1)} %get-tuple-element.43), channel_id=1, source_target_pairs={{0,8},{1,9},{2,10},{3,11},{4,12},{5,13},{6,14},{7,15},{8,0},{9,1},... | collective-permute-start | bytes 221192 | tf_op jit(solution)/shard_map/reduce/ppermute | solution.py:342
  53.8 0.6 collective-permute-done.16
  54.4 4.5 %collective-permute-done.18 = bf16[16,2304]{1,0:T(8,128)(2,1)S(1)} collective-permute-done((bf16[16,2304]{1,0:T(8,128)(2,1)S(1)}, bf16[16,2304]{1,0:T(8,128)(2,1)S(1)}, u32[]{:S(2)}, u32[]{:S(2)}) %collective-permute-start.18) | collective-permute-done | bytes 73760 | tf_op jit(solution)/shard_map/reduce/ppermute | solution.py:342
  58.9 1.3 %collective-permute-done.17 = bf16[16,2304]{1,0:T(8,128)(2,1)S(1)} collective-permute-done((bf16[16,2304]{1,0:T(8,128)(2,1)S(1)}, bf16[16,2304]{1,0:T(8,128)(2,1)S(1)}, u32[]{:S(2)}, u32[]{:S(2)}) %collective-permute-start.17) | collective-permute-done | bytes 73760 | tf_op jit(solution)/shard_map/reduce/ppermute | solution.py:342
  60.2 0.7 %fusion.2 = bf16[16,2304]{1,0:T(8,128)(2,1)} fusion(bf16[16,2304]{1,0:T(8,128)(2,1)S(1)} %collective-permute-done.18, bf16[16,2304]{1,0:T(8,128)(2,1)S(1)} %collective-permute-done.17, bf16[16,2304]{1,0:T(8,128)(2,1)S(1)} %collective-permute-done.16, bf16[4,16,2304]{2,1,0:T(8,128)(2,1)S(1)} %spread.3), kind=kLoop, calls=%fused_computation.3 | loop fusion | flops 294912 | bytes 368640 | tf_op jit(solution)/shard_map/reduce/convert_element_type | solution.py:476
  (2 shorter events, 0.0 us)
Async XLA Ops:
  0.9 7.1 %collective-permute-start = (bf16[16,2304]{1,0:T(8,128)(2,1)S(1)}, bf16[16,2304]{1,0:T(8,128)(2,1)S(1)}, u32[]{:S(2)}, u32[]{:S(2)}) collective-permute-start(bf16[16,2304]{1,0:T(8,128)(2,1)S(1)} %slice.15), channel_id=1, source_target_pairs={{0,32},{32,64},{64,96},{96,128},{128,160},{160,192},{192,224},{224... | collective-permute-start | bytes 221192 | tf_op jit(solution)/shard_map/rim/ppermute | solution.py:348
  2.9 21.7 %collective-permute-start.7 = (bf16[128,2304]{1,0:T(8,128)(2,1)}, bf16[128,2304]{1,0:T(8,128)(2,1)S(1)}, u32[]{:S(2)}, u32[]{:S(2)}) collective-permute-start(bf16[128,2304]{1,0:T(8,128)(2,1)} %w_one.1), channel_id=1, source_target_pairs={{0,4},{1,5},{2,6},{3,7},{4,0},{5,1},{6,2},{7,3},{8,12},{9,13},{10,... | collective-permute-start | bytes 1769480 | tf_op jit(solution)/shard_map/weights/ppermute | solution.py:342
  4.6 15.2 %collective-permute-start.6 = (bf16[128,2304]{1,0:T(8,128)(2,1)}, bf16[128,2304]{1,0:T(8,128)(2,1)S(1)}, u32[]{:S(2)}, u32[]{:S(2)}) collective-permute-start(bf16[128,2304]{1,0:T(8,128)(2,1)} %w_one.1), channel_id=1, source_target_pairs={{0,130},{1,131},{2,128},{3,129},{4,134},{5,135},{6,132},{7,133},{8... | collective-permute-start | bytes 1769480 | tf_op jit(solution)/shard_map/weights/ppermute | solution.py:339
  8.0 0.6 %copy-start.3 = (bf16[16,2304]{1,0:T(8,128)(2,1)}, bf16[16,2304]{1,0:T(8,128)(2,1)S(1)}, u32[]{:S(2)}) copy-start(bf16[16,2304]{1,0:T(8,128)(2,1)S(1)} %collective-permute-done.rim_hbm) | copy-start | bytes 221188
  8.6 14.7 %copy-start.1 = (f32[128]{0:T(128)S(1)}, f32[128]{0:T(128)}, u32[]{:S(2)}) copy-start(f32[128]{0:T(128)} %param.22) | copy-start | bytes 1540
  8.6 16.0 %copy-start.2 = (bf16[128,2304]{1,0:T(8,128)(2,1)S(1)}, bf16[128,2304]{1,0:T(8,128)(2,1)}, u32[]{:S(2)}) copy-start(bf16[128,2304]{1,0:T(8,128)(2,1)} %w_one.1) | copy-start | bytes 1769476
  19.8 18.1 %collective-permute-start.14 = (bf16[128,2304]{1,0:T(8,128)(2,1)S(1)}, bf16[128,2304]{1,0:T(8,128)(2,1)S(1)}, u32[]{:S(2)}, u32[]{:S(2)}) collective-permute-start(bf16[128,2304]{1,0:T(8,128)(2,1)S(1)} %collective-permute-done.6.refs_0_), channel_id=1, source_target_pairs={{0,4},{1,5},{2,6},{3,7},{4,0},{5,1},{6,2},{7,3},{8,12},{9,13},{10,... | collective-permute-start | bytes 1769480 | tf_op jit(solution)/shard_map/weights/ppermute | solution.py:342
  19.8 8.0 %collective-permute-start.3 = (bf16[128,256]{1,0:T(8,128)(2,1)}, bf16[128,256]{1,0:T(8,128)(2,1)S(1)}, u32[]{:S(2)}, u32[]{:S(2)}) collective-permute-start(bf16[128,256]{1,0:T(8,128)(2,1)} %get-tuple-element.24), channel_id=1, source_target_pairs={{0,96},{32,0},{64,32},{96,64},{128,224},{160,128},{192,160},{224,1... | collective-permute-start | bytes 196616 | tf_op jit(solution)/shard_map/states/ppermute | solution.py:401
  22.2 5.6 %collective-permute-start.2 = (bf16[128,256]{1,0:T(8,128)(2,1)}, bf16[128,256]{1,0:T(8,128)(2,1)S(1)}, u32[]{:S(2)}, u32[]{:S(2)}) collective-permute-start(bf16[128,256]{1,0:T(8,128)(2,1)} %get-tuple-element.24), channel_id=1, source_target_pairs={{0,64},{32,96},{64,0},{96,32},{128,192},{160,224},{192,128},{224,1... | collective-permute-start | bytes 196616 | tf_op jit(solution)/shard_map/states/ppermute | solution.py:401
  22.9 7.8 %collective-permute-start.1 = (bf16[128,256]{1,0:T(8,128)(2,1)}, bf16[128,256]{1,0:T(8,128)(2,1)S(1)}, u32[]{:S(2)}, u32[]{:S(2)}) collective-permute-start(bf16[128,256]{1,0:T(8,128)(2,1)} %get-tuple-element.24), channel_id=1, source_target_pairs={{0,32},{32,64},{64,96},{96,0},{128,160},{160,192},{192,224},{224,1... | collective-permute-start | bytes 196616 | tf_op jit(solution)/shard_map/states/ppermute | solution.py:401
  23.3 1.3 %copy-start = (f32[768,384]{1,0:T(8,128)S(1)}, f32[768,384]{1,0:T(8,128)}, u32[]{:S(2)}) copy-start(f32[768,384]{1,0:T(8,128)} %get-tuple-element.23.pack) | copy-start | bytes 3538948
  24.6 16.8 %collective-permute-start.8 = (bf16[128,2304]{1,0:T(8,128)(2,1)S(1)}, bf16[128,2304]{1,0:T(8,128)(2,1)S(1)}, u32[]{:S(2)}, u32[]{:S(2)}) collective-permute-start(bf16[128,2304]{1,0:T(8,128)(2,1)S(1)} %copy-done.2), channel_id=1, source_target_pairs={{0,1},{1,0},{2,3},{3,2},{4,5},{5,4},{6,7},{7,6},{8,9},{9,8},{10,11... | collective-permute-start | bytes 1769480 | tf_op jit(solution)/shard_map/weights/ppermute | solution.py:342
  27.7 14.7 %collective-permute-start.9 = (bf16[128,2304]{1,0:T(8,128)(2,1)S(1)}, bf16[128,2304]{1,0:T(8,128)(2,1)S(1)}, u32[]{:S(2)}, u32[]{:S(2)}) collective-permute-start(bf16[128,2304]{1,0:T(8,128)(2,1)S(1)} %collective-permute-done.6.refs_0_), channel_id=1, source_target_pairs={{0,1},{1,0},{2,3},{3,2},{4,5},{5,4},{6,7},{7,6},{8,9},{9,8},{10,11... | collective-permute-start | bytes 1769480 | tf_op jit(solution)/shard_map/weights/ppermute | solution.py:342
  27.8 14.6 %collective-permute-start.10 = (bf16[128,2304]{1,0:T(8,128)(2,1)S(1)}, bf16[128,2304]{1,0:T(8,128)(2,1)S(1)}, u32[]{:S(2)}, u32[]{:S(2)}) collective-permute-start(bf16[128,2304]{1,0:T(8,128)(2,1)S(1)} %collective-permute-done.7.refs_2_), channel_id=1, source_target_pairs={{0,1},{1,0},{2,3},{3,2},{4,5},{5,4},{6,7},{7,6},{8,9},{9,8},{10,11... | collective-permute-start | bytes 1769480 | tf_op jit(solution)/shard_map/weights/ppermute | solution.py:342
  31.4 3.3 %collective-permute-start.4 = (bf16[128,128]{1,0:T(8,128)(2,1)S(1)}, bf16[128,128]{1,0:T(8,128)(2,1)S(1)}, u32[]{:S(2)}, u32[]{:S(2)}) collective-permute-start(bf16[128,128]{1,0:T(8,128)(2,1)S(1)} %get-tuple-element.26), channel_id=1, source_target_pairs={{0,128},{32,160},{64,192},{96,224},{128,0},{160,32},{192,64},{224,... | collective-permute-start | bytes 98312 | tf_op jit(solution)/shard_map/states/ppermute | solution.py:426
  35.3 2.5 %collective-permute-start.5 = (bf16[4,4,16,128]{3,2,1,0:T(8,128)(2,1)S(1)}, bf16[4,4,16,128]{3,2,1,0:T(8,128)(2,1)S(1)}, u32[]{:S(2)}, u32[]{:S(2)}) collective-permute-start(bf16[4,4,16,128]{3,2,1,0:T(8,128)(2,1)S(1)} %get-tuple-element.28), channel_id=1, source_target_pairs={{0,1},{1,0},{2,3},{3,2},{4,5},{5,4},{6,7},{7,6},{8,9},{9,8},{10,11... | collective-permute-start | bytes 196616 | tf_op jit(solution)/shard_map/exchange/ppermute | solution.py:342
  37.8 7.9 %collective-permute-start.15 = (bf16[128,2304]{1,0:T(8,128)(2,1)S(1)}, bf16[128,2304]{1,0:T(8,128)(2,1)S(1)}, u32[]{:S(2)}, u32[]{:S(2)}) collective-permute-start(bf16[128,2304]{1,0:T(8,128)(2,1)S(1)} %collective-permute-done.14.refs_4_), channel_id=1, source_target_pairs={{0,1},{1,0},{2,3},{3,2},{4,5},{5,4},{6,7},{7,6},{8,9},{9,8},{10,11... | collective-permute-start | bytes 1769480 | tf_op jit(solution)/shard_map/spread/ppermute | solution.py:342
  38.3 5.2 %collective-permute-start.11 = (bf16[2,4,16,128]{3,2,1,0:T(8,128)(2,1)S(1)}, bf16[2,4,16,128]{3,2,1,0:T(8,128)(2,1)S(1)}, u32[]{:S(2)}, u32[]{:S(2)}) collective-permute-start(bf16[2,4,16,128]{3,2,1,0:T(8,128)(2,1)S(1)} %get-tuple-element.35), channel_id=1, source_target_pairs={{0,6},{1,7},{2,4},{3,5},{4,2},{5,3},{6,0},{7,1},{8,14},{9,15},{10,... | collective-permute-start | bytes 98312 | tf_op jit(solution)/shard_map/exchange/ppermute | solution.py:342
  41.4 4.3 %collective-permute-start.12 = (bf16[2,4,16,128]{3,2,1,0:T(8,128)(2,1)S(1)}, bf16[2,4,16,128]{3,2,1,0:T(8,128)(2,1)S(1)}, u32[]{:S(2)}, u32[]{:S(2)}) collective-permute-start(bf16[2,4,16,128]{3,2,1,0:T(8,128)(2,1)S(1)} %get-tuple-element.36), channel_id=1, source_target_pairs={{0,2},{1,3},{2,0},{3,1},{4,6},{5,7},{6,4},{7,5},{8,10},{9,11},{10,... | collective-permute-start | bytes 98312 | tf_op jit(solution)/shard_map/exchange/ppermute | solution.py:342
  42.4 3.3 %collective-permute-start.13 = (bf16[2,4,16,128]{3,2,1,0:T(8,128)(2,1)S(1)}, bf16[2,4,16,128]{3,2,1,0:T(8,128)(2,1)S(1)}, u32[]{:S(2)}, u32[]{:S(2)}) collective-permute-start(bf16[2,4,16,128]{3,2,1,0:T(8,128)(2,1)S(1)} %get-tuple-element.37), channel_id=1, source_target_pairs={{0,4},{1,5},{2,6},{3,7},{4,0},{5,1},{6,2},{7,3},{8,12},{9,13},{10,... | collective-permute-start | bytes 98312 | tf_op jit(solution)/shard_map/exchange/ppermute | solution.py:342
  46.5 7.9 %collective-permute-start.16 = (bf16[16,2304]{1,0:T(8,128)(2,1)S(1)}, bf16[16,2304]{1,0:T(8,128)(2,1)S(1)}, u32[]{:S(2)}, u32[]{:S(2)}) collective-permute-start(bf16[16,2304]{1,0:T(8,128)(2,1)S(1)} %get-tuple-element.41), channel_id=1, source_target_pairs={{0,16},{1,17},{2,18},{3,19},{4,20},{5,21},{6,22},{7,23},{8,24},{9,... | collective-permute-start | bytes 221192 | tf_op jit(solution)/shard_map/reduce/ppermute | solution.py:342
  52.6 6.3 %collective-permute-start.18 = (bf16[16,2304]{1,0:T(8,128)(2,1)S(1)}, bf16[16,2304]{1,0:T(8,128)(2,1)S(1)}, u32[]{:S(2)}, u32[]{:S(2)}) collective-permute-start(bf16[16,2304]{1,0:T(8,128)(2,1)S(1)} %get-tuple-element.42), channel_id=1, source_target_pairs={{0,24},{1,25},{2,26},{3,27},{4,28},{5,29},{6,30},{7,31},{8,16},{9,... | collective-permute-start | bytes 221192 | tf_op jit(solution)/shard_map/reduce/ppermute | solution.py:342
  52.9 7.3 %collective-permute-start.17 = (bf16[16,2304]{1,0:T(8,128)(2,1)S(1)}, bf16[16,2304]{1,0:T(8,128)(2,1)S(1)}, u32[]{:S(2)}, u32[]{:S(2)}) collective-permute-start(bf16[16,2304]{1,0:T(8,128)(2,1)S(1)} %get-tuple-element.43), channel_id=1, source_target_pairs={{0,8},{1,9},{2,10},{3,11},{4,12},{5,13},{6,14},{7,15},{8,0},{9,1},... | collective-permute-start | bytes 221192 | tf_op jit(solution)/shard_map/reduce/ppermute | solution.py:342

commit v9 on v8

--- a/solution.py
+++ b/solution.py
@@ -401,9 +401,6 @@
             return lax.ppermute(sends, "ctx", pairs)
 
         found = {step: around(step) for step in range(1, half)}
-    (w_early,) = after((w_far,), pack)
-    with jax.named_scope("weights"):
-        w_both = flip(w_early, 4)
     with jax.named_scope("stage"):
         staged = pl.pallas_call(
             stage,
@@ -413,6 +410,9 @@
             compiler_params=LIMIT,
             cost_estimate=cost(0.5, 0.5),
         )(pack, norm_gain.reshape(1, head))
+    (w_early,) = after((w_far,), staged)
+    with jax.named_scope("weights"):
+        w_both = flip(w_early, 4)
     with jax.named_scope("states"):
         before, total = pl.pallas_call(
             fold,

time: 61 us -> 60.9 us (level)
  waiting for transfers between devices: 14.4 us -> 13.2 us
  starting transfers between devices: 29.8 us -> 30.9 us
    ppermute x13, starting transfers between devices: 21.3 us -> 22.5 us  [flip(): lax.ppermute(value, 'head', [(h, h ^ mask) for h in range(head_count)])]
    ppermute x1, waiting for transfers between devices: 1.12 us -> 0.01 us  [across(): return lax.ppermute(value, ('ctx', 'head'), pairs)]
    unnamed x8 -> x10, local copies, waits for them, and re-layouts: 1.91 us -> 1.9 us
  transfers between devices with their start and end apart: 19 -> 19, of which waited for: 8 -> 7; matrix products, arithmetic and copies ran while one was open for 0% -> 0% of each run, Pallas kernels for 19% -> 19%
where the time goes in v9:
time: 60.9 us; the launch traced here: 60.7 us
  starting transfers between devices  30.9 us (51%)
  waiting for transfers between devices  13.2 us (22%)
  Pallas kernels  12.4 us (20%)
  local copies, waits for them, and re-layouts  2.81 us (5%)
  between operations  0.76 us (1%)
  other arithmetic  0.68 us (1%)
    ppermute x13, starting transfers between devices, flip(): lax.ppermute(value, 'head', [(h, h ^ mask) for h in range(head_count)])  22.5 us
    ppermute x13, waiting for transfers between devices, flip(): lax.ppermute(value, 'head', [(h, h ^ mask) for h in range(head_count)])  10.1 us
    pallas_call x1, Pallas kernels, on_device(): pl.pallas_call(front, in_specs=[HBM] * 11, out_specs=[HBM] * 2, out_shape...  10 us
    ppermute x3, starting transfers between devices, around(): return lax.ppermute(sends, 'ctx', pairs)  3.27 us
    ppermute x1, waiting for transfers between devices, on_device(): lax.ppermute(total, 'ctx', [(c, (c + half) % ctx_count) for c in range(ct...  2.99 us
    ppermute x1, starting transfers between devices, across(): return lax.ppermute(value, ('ctx', 'head'), pairs)  2.73 us
    ppermute x1, starting transfers between devices, on_device(): lax.ppermute(edge, 'ctx', [(i, (i + 1) % ctx_count) for i in range(ctx_co...  2.04 us
    unnamed x10, local copies, waits for them, and re-layouts  1.9 us
  transfers between devices with their start and end apart: 19, of which 7 were waited for; matrix products, arithmetic and copies ran while one was open for 0% of the time, Pallas kernels for 19%

profile of v9, /device:TPU:1, one launch (start us, length us, event | category | flops | bytes accessed | tf_op | source)
XLA Modules:
  0.0 60.7 jit_solution(4598769555125718797)
XLA Ops:
  0.0 0.9 %slice.15 = bf16[16,2304]{1,0:T(8,128)(2,1)S(1)} slice(bf16[512,2304]{1,0:T(8,128)(2,1)} %tokens_hbm.1), slice={[496:512], [0:2304]} | slice | bytes 147456 | tf_op jit(solution)/shard_map/slice | solution.py:346
  0.9 2.0 %collective-permute-start = (bf16[16,2304]{1,0:T(8,128)(2,1)S(1)}, bf16[16,2304]{1,0:T(8,128)(2,1)S(1)}, u32[]{:S(2)}, u32[]{:S(2)}) collective-permute-start(bf16[16,2304]{1,0:T(8,128)(2,1)S(1)} %slice.15), channel_id=1, source_target_pairs={{0,32},{32,64},{64,96},{96,128},{128,160},{160,192},{192,224},{224... | collective-permute-start | bytes 221192 | tf_op jit(solution)/shard_map/rim/ppermute | solution.py:348
  2.9 1.6 %collective-permute-start.7 = (bf16[128,2304]{1,0:T(8,128)(2,1)}, bf16[128,2304]{1,0:T(8,128)(2,1)S(1)}, u32[]{:S(2)}, u32[]{:S(2)}) collective-permute-start(bf16[128,2304]{1,0:T(8,128)(2,1)} %w_one.1), channel_id=1, source_target_pairs={{0,4},{1,5},{2,6},{3,7},{4,0},{5,1},{6,2},{7,3},{8,12},{9,13},{10,... | collective-permute-start | bytes 1769480 | tf_op jit(solution)/shard_map/weights/ppermute | solution.py:342
  4.6 2.7 %collective-permute-start.6 = (bf16[128,2304]{1,0:T(8,128)(2,1)}, bf16[128,2304]{1,0:T(8,128)(2,1)S(1)}, u32[]{:S(2)}, u32[]{:S(2)}) collective-permute-start(bf16[128,2304]{1,0:T(8,128)(2,1)} %w_one.1), channel_id=1, source_target_pairs={{0,130},{1,131},{2,128},{3,129},{4,134},{5,135},{6,132},{7,133},{8... | collective-permute-start | bytes 1769480 | tf_op jit(solution)/shard_map/weights/ppermute | solution.py:339
  8.0 0.0 collective-permute-done.rim_hbm
  8.0 0.0 copy-start.3
  8.0 0.6 %copy-done.3 = bf16[16,2304]{1,0:T(8,128)(2,1)} copy-done((bf16[16,2304]{1,0:T(8,128)(2,1)}, bf16[16,2304]{1,0:T(8,128)(2,1)S(1)}, u32[]{:S(2)}) %copy-start.3) | copy-done | bytes 73752
  8.6 0.0 copy-start.1
  8.6 0.0 copy-start.2
  8.6 10.0 %front.1 = (f32[768,384]{1,0:T(8,128)}, bf16[128,256]{1,0:T(8,128)(2,1)}) custom-call(bf16[512,2304]{1,0:T(8,128)(2,1)} %tokens_hbm.1, bf16[16,2304]{1,0:T(8,128)(2,1)} %copy-done.3, f32[1,1]{1,0:T(1,128)} %bitcast.17.alog_hbm, bf16[3,2304,128]{2,1,0:T(8,128)(2,1)} %bitcast.19, bf16[2304,128]{1,0:T(8,128)(2,1)} %f_down_hbm.1, bf16[2304,128]{1,0:T(8,128)(2,1)} %o_down_hbm.1, ...), custom_call_target="tpu_custom_call" | custom-call | flops 40000000000 | bytes 33210000 | tf_op jit(solution)/shard_map/front/pallas_call | solution.py:353
  18.6 0.0 copy-done.1
  18.6 0.0 copy-start
  18.6 1.3 %copy-done = f32[768,384]{1,0:T(8,128)S(1)} copy-done((f32[768,384]{1,0:T(8,128)S(1)}, f32[768,384]{1,0:T(8,128)}, u32[]{:S(2)}) %copy-start) | copy-done | bytes 1179672
  19.9 0.0 copy-start.4
  19.9 0.1 stage.1.pack
  20.0 0.0 collective-permute-done.6.refs_0_
  20.0 0.8 %collective-permute-start.14 = (bf16[128,2304]{1,0:T(8,128)(2,1)S(1)}, bf16[128,2304]{1,0:T(8,128)(2,1)S(1)}, u32[]{:S(2)}, u32[]{:S(2)}) collective-permute-start(bf16[128,2304]{1,0:T(8,128)(2,1)S(1)} %collective-permute-done.6.refs_0_), channel_id=1, source_target_pairs={{0,4},{1,5},{2,6},{3,7},{4,0},{5,1},{6,2},{7,3},{8,12},{9,13},{10,... | collective-permute-start | bytes 1769480 | tf_op jit(solution)/shard_map/weights/ppermute | solution.py:342
  20.8 0.0 copy-done.4
  20.8 1.6 %collective-permute-start.3 = (bf16[128,256]{1,0:T(8,128)(2,1)S(1)}, bf16[128,256]{1,0:T(8,128)(2,1)S(1)}, u32[]{:S(2)}, u32[]{:S(2)}) collective-permute-start(bf16[128,256]{1,0:T(8,128)(2,1)S(1)} %copy-done.4), channel_id=1, source_target_pairs={{0,96},{32,0},{64,32},{96,64},{128,224},{160,128},{192,160},{224,1... | collective-permute-start | bytes 196616 | tf_op jit(solution)/shard_map/states/ppermute | solution.py:401
  22.4 1.4 %collective-permute-start.2 = (bf16[128,256]{1,0:T(8,128)(2,1)S(1)}, bf16[128,256]{1,0:T(8,128)(2,1)S(1)}, u32[]{:S(2)}, u32[]{:S(2)}) collective-permute-start(bf16[128,256]{1,0:T(8,128)(2,1)S(1)} %copy-done.4), channel_id=1, source_target_pairs={{0,64},{32,96},{64,0},{96,32},{128,192},{160,224},{192,128},{224,1... | collective-permute-start | bytes 196616 | tf_op jit(solution)/shard_map/states/ppermute | solution.py:401
  23.7 0.3 collective-permute-start.1
  24.1 0.0 collective-permute-done.7.refs_2_
  24.1 0.0 copy-done.2
  24.1 2.4 %collective-permute-start.8 = (bf16[128,2304]{1,0:T(8,128)(2,1)S(1)}, bf16[128,2304]{1,0:T(8,128)(2,1)S(1)}, u32[]{:S(2)}, u32[]{:S(2)}) collective-permute-start(bf16[128,2304]{1,0:T(8,128)(2,1)S(1)} %copy-done.2), channel_id=1, source_target_pairs={{0,1},{1,0},{2,3},{3,2},{4,5},{5,4},{6,7},{7,6},{8,9},{9,8},{10,11... | collective-permute-start | bytes 1769480 | tf_op jit(solution)/shard_map/weights/ppermute | solution.py:342
  26.4 0.0 collective-permute-done.3.refs_2_
  26.4 1.2 %collective-permute-start.9 = (bf16[128,2304]{1,0:T(8,128)(2,1)S(1)}, bf16[128,2304]{1,0:T(8,128)(2,1)S(1)}, u32[]{:S(2)}, u32[]{:S(2)}) collective-permute-start(bf16[128,2304]{1,0:T(8,128)(2,1)S(1)} %collective-permute-done.6.refs_0_), channel_id=1, source_target_pairs={{0,1},{1,0},{2,3},{3,2},{4,5},{5,4},{6,7},{7,6},{8,9},{9,8},{10,11... | collective-permute-start | bytes 1769480 | tf_op jit(solution)/shard_map/weights/ppermute | solution.py:342
  27.6 0.0 collective-permute-done.2.refs_1_
  27.6 2.9 %collective-permute-start.10 = (bf16[128,2304]{1,0:T(8,128)(2,1)S(1)}, bf16[128,2304]{1,0:T(8,128)(2,1)S(1)}, u32[]{:S(2)}, u32[]{:S(2)}) collective-permute-start(bf16[128,2304]{1,0:T(8,128)(2,1)S(1)} %collective-permute-done.7.refs_2_), channel_id=1, source_target_pairs={{0,1},{1,0},{2,3},{3,2},{4,5},{5,4},{6,7},{7,6},{8,9},{9,8},{10,11... | collective-permute-start | bytes 1769480 | tf_op jit(solution)/shard_map/weights/ppermute | solution.py:342
  30.5 0.0 collective-permute-done.1.refs_0_
  30.6 0.6 %states.1 = (f32[128,256]{1,0:T(8,128)S(1)}, bf16[128,128]{1,0:T(8,128)(2,1)S(1)}) custom-call(f32[768,384]{1,0:T(8,128)S(1)} %stage.1.pack, bf16[128,256]{1,0:T(8,128)(2,1)S(1)} %collective-permute-done.1.refs_0_, bf16[128,256]{1,0:T(8,128)(2,1)S(1)} %collective-permute-done.2.refs_1_, bf16[128,256]{1,0:T(8,128)(2,1)S(1)} %collective-permute-done.3.refs_2_), custom_call_target="tpu_custom_call" | custom-call | bytes 1845000 | tf_op jit(solution)/shard_map/states/pallas_call | solution.py:417
  31.2 0.3 collective-permute-start.4
  31.5 3.0 %collective-permute-done.4.came = bf16[128,128]{1,0:T(8,128)(2,1)S(1)} collective-permute-done((bf16[128,128]{1,0:T(8,128)(2,1)S(1)}, bf16[128,128]{1,0:T(8,128)(2,1)S(1)}, u32[]{:S(2)}, u32[]{:S(2)}) %collective-permute-start.4) | collective-permute-done | bytes 32800 | tf_op jit(solution)/shard_map/states/ppermute | solution.py:426
  34.5 0.5 finish.1
  35.1 1.7 %collective-permute-start.5 = (bf16[4,4,16,128]{3,2,1,0:T(8,128)(2,1)S(1)}, bf16[4,4,16,128]{3,2,1,0:T(8,128)(2,1)S(1)}, u32[]{:S(2)}, u32[]{:S(2)}) collective-permute-start(bf16[4,4,16,128]{3,2,1,0:T(8,128)(2,1)S(1)} %get-tuple-element.28), channel_id=1, source_target_pairs={{0,1},{1,0},{2,3},{3,2},{4,5},{5,4},{6,7},{7,6},{8,9},{9,8},{10,11... | collective-permute-start | bytes 196616 | tf_op jit(solution)/shard_map/exchange/ppermute | solution.py:342
  36.7 0.9 %collective-permute-done.5.sibling = bf16[4,4,16,128]{3,2,1,0:T(8,128)(2,1)S(1)} collective-permute-done((bf16[4,4,16,128]{3,2,1,0:T(8,128)(2,1)S(1)}, bf16[4,4,16,128]{3,2,1,0:T(8,128)(2,1)S(1)}, u32[]{:S(2)}, u32[]{:S(2)}) %collective-permute-start.5) | collective-permute-done | bytes 65568 | tf_op jit(solution)/shard_map/exchange/ppermute | solution.py:342
  37.7 0.0 collective-permute-done.14.refs_4_
  37.7 0.4 collective-permute-start.15
  38.1 3.1 %collective-permute-start.11 = (bf16[2,4,16,128]{3,2,1,0:T(8,128)(2,1)S(1)}, bf16[2,4,16,128]{3,2,1,0:T(8,128)(2,1)S(1)}, u32[]{:S(2)}, u32[]{:S(2)}) collective-permute-start(bf16[2,4,16,128]{3,2,1,0:T(8,128)(2,1)S(1)} %get-tuple-element.35), channel_id=1, source_target_pairs={{0,6},{1,7},{2,4},{3,5},{4,2},{5,3},{6,0},{7,1},{8,14},{9,15},{10,... | collective-permute-start | bytes 98312 | tf_op jit(solution)/shard_map/exchange/ppermute | solution.py:342
  41.2 0.0 collective-permute-done.8.w_two
  41.2 1.0 %collective-permute-start.12 = (bf16[2,4,16,128]{3,2,1,0:T(8,128)(2,1)S(1)}, bf16[2,4,16,128]{3,2,1,0:T(8,128)(2,1)S(1)}, u32[]{:S(2)}, u32[]{:S(2)}) collective-permute-start(bf16[2,4,16,128]{3,2,1,0:T(8,128)(2,1)S(1)} %get-tuple-element.36), channel_id=1, source_target_pairs={{0,2},{1,3},{2,0},{3,1},{4,6},{5,7},{6,4},{7,5},{8,10},{9,11},{10,... | collective-permute-start | bytes 98312 | tf_op jit(solution)/shard_map/exchange/ppermute | solution.py:342
  42.2 0.0 collective-permute-done.9.refs_1_
  42.2 0.1 collective-permute-start.13
  42.3 0.0 collective-permute-done.10.refs_3_
  42.3 0.4 spread.2
  42.7 0.6 collective-permute-done.11.refs_0_
  43.3 2.2 %collective-permute-done.12.refs_1_ = bf16[2,4,16,128]{3,2,1,0:T(8,128)(2,1)S(1)} collective-permute-done((bf16[2,4,16,128]{3,2,1,0:T(8,128)(2,1)S(1)}, bf16[2,4,16,128]{3,2,1,0:T(8,128)(2,1)S(1)}, u32[]{:S(2)}, u32[]{:S(2)}) %collective-permute-start.12) | collective-permute-done | bytes 32800 | tf_op jit(solution)/shard_map/exchange/ppermute | solution.py:342
  45.5 0.0 collective-permute-done.13.refs_2_
  45.5 0.0 collective-permute-done.15.refs_5_
  45.5 0.7 %spread.3 = bf16[4,16,2304]{2,1,0:T(8,128)(2,1)S(1)} custom-call(f32[64,2304]{1,0:T(8,128)S(1)} %get-tuple-element.34.begun, bf16[2,4,16,128]{3,2,1,0:T(8,128)(2,1)S(1)} %collective-permute-done.11.refs_0_, bf16[2,4,16,128]{3,2,1,0:T(8,128)(2,1)S(1)} %collective-permute-done.12.refs_1_, bf16[2,4,16,128]{3,2,1,0:T(8,128)(2,1)S(1)} %collective-permute-done.13.refs_2_, ...), custom_call_target="tpu_custom_call" | custom-call | flops 1000000000 | bytes 3690000 | tf_op jit(solution)/shard_map/spread/pallas_call | solution.py:463
  46.3 6.1 %collective-permute-start.16 = (bf16[16,2304]{1,0:T(8,128)(2,1)S(1)}, bf16[16,2304]{1,0:T(8,128)(2,1)S(1)}, u32[]{:S(2)}, u32[]{:S(2)}) collective-permute-start(bf16[16,2304]{1,0:T(8,128)(2,1)S(1)} %get-tuple-element.41), channel_id=1, source_target_pairs={{0,16},{1,17},{2,18},{3,19},{4,20},{5,21},{6,22},{7,23},{8,24},{9,... | collective-permute-start | bytes 221192 | tf_op jit(solution)/shard_map/reduce/ppermute | solution.py:342
  52.4 0.3 collective-permute-start.18
  52.7 0.9 %collective-permute-start.17 = (bf16[16,2304]{1,0:T(8,128)(2,1)S(1)}, bf16[16,2304]{1,0:T(8,128)(2,1)S(1)}, u32[]{:S(2)}, u32[]{:S(2)}) collective-permute-start(bf16[16,2304]{1,0:T(8,128)(2,1)S(1)} %get-tuple-element.43), channel_id=1, source_target_pairs={{0,8},{1,9},{2,10},{3,11},{4,12},{5,13},{6,14},{7,15},{8,0},{9,1},... | collective-permute-start | bytes 221192 | tf_op jit(solution)/shard_map/reduce/ppermute | solution.py:342
  53.6 0.6 collective-permute-done.16
  54.2 4.5 %collective-permute-done.18 = bf16[16,2304]{1,0:T(8,128)(2,1)S(1)} collective-permute-done((bf16[16,2304]{1,0:T(8,128)(2,1)S(1)}, bf16[16,2304]{1,0:T(8,128)(2,1)S(1)}, u32[]{:S(2)}, u32[]{:S(2)}) %collective-permute-start.18) | collective-permute-done | bytes 73760 | tf_op jit(solution)/shard_map/reduce/ppermute | solution.py:342
  58.7 1.3 %collective-permute-done.17 = bf16[16,2304]{1,0:T(8,128)(2,1)S(1)} collective-permute-done((bf16[16,2304]{1,0:T(8,128)(2,1)S(1)}, bf16[16,2304]{1,0:T(8,128)(2,1)S(1)}, u32[]{:S(2)}, u32[]{:S(2)}) %collective-permute-start.17) | collective-permute-done | bytes 73760 | tf_op jit(solution)/shard_map/reduce/ppermute | solution.py:342
  60.0 0.7 %fusion.2 = bf16[16,2304]{1,0:T(8,128)(2,1)} fusion(bf16[16,2304]{1,0:T(8,128)(2,1)S(1)} %collective-permute-done.18, bf16[16,2304]{1,0:T(8,128)(2,1)S(1)} %collective-permute-done.17, bf16[16,2304]{1,0:T(8,128)(2,1)S(1)} %collective-permute-done.16, bf16[4,16,2304]{2,1,0:T(8,128)(2,1)S(1)} %spread.3), kind=kLoop, calls=%fused_computation.3 | loop fusion | flops 294912 | bytes 368640 | tf_op jit(solution)/shard_map/reduce/convert_element_type | solution.py:476
  (2 shorter events, 0.0 us)
Async XLA Ops:
  0.9 7.1 %collective-permute-start = (bf16[16,2304]{1,0:T(8,128)(2,1)S(1)}, bf16[16,2304]{1,0:T(8,128)(2,1)S(1)}, u32[]{:S(2)}, u32[]{:S(2)}) collective-permute-start(bf16[16,2304]{1,0:T(8,128)(2,1)S(1)} %slice.15), channel_id=1, source_target_pairs={{0,32},{32,64},{64,96},{96,128},{128,160},{160,192},{192,224},{224... | collective-permute-start | bytes 221192 | tf_op jit(solution)/shard_map/rim/ppermute | solution.py:348
  2.9 21.1 %collective-permute-start.7 = (bf16[128,2304]{1,0:T(8,128)(2,1)}, bf16[128,2304]{1,0:T(8,128)(2,1)S(1)}, u32[]{:S(2)}, u32[]{:S(2)}) collective-permute-start(bf16[128,2304]{1,0:T(8,128)(2,1)} %w_one.1), channel_id=1, source_target_pairs={{0,4},{1,5},{2,6},{3,7},{4,0},{5,1},{6,2},{7,3},{8,12},{9,13},{10,... | collective-permute-start | bytes 1769480 | tf_op jit(solution)/shard_map/weights/ppermute | solution.py:342
  4.6 15.4 %collective-permute-start.6 = (bf16[128,2304]{1,0:T(8,128)(2,1)}, bf16[128,2304]{1,0:T(8,128)(2,1)S(1)}, u32[]{:S(2)}, u32[]{:S(2)}) collective-permute-start(bf16[128,2304]{1,0:T(8,128)(2,1)} %w_one.1), channel_id=1, source_target_pairs={{0,130},{1,131},{2,128},{3,129},{4,134},{5,135},{6,132},{7,133},{8... | collective-permute-start | bytes 1769480 | tf_op jit(solution)/shard_map/weights/ppermute | solution.py:339
  8.0 0.6 %copy-start.3 = (bf16[16,2304]{1,0:T(8,128)(2,1)}, bf16[16,2304]{1,0:T(8,128)(2,1)S(1)}, u32[]{:S(2)}) copy-start(bf16[16,2304]{1,0:T(8,128)(2,1)S(1)} %collective-permute-done.rim_hbm) | copy-start | bytes 221188
  8.6 10.0 %copy-start.1 = (f32[128]{0:T(128)S(1)}, f32[128]{0:T(128)}, u32[]{:S(2)}) copy-start(f32[128]{0:T(128)} %param.22) | copy-start | bytes 1540
  8.6 15.5 %copy-start.2 = (bf16[128,2304]{1,0:T(8,128)(2,1)S(1)}, bf16[128,2304]{1,0:T(8,128)(2,1)}, u32[]{:S(2)}) copy-start(bf16[128,2304]{1,0:T(8,128)(2,1)} %w_one.1) | copy-start | bytes 1769476
  18.6 1.3 %copy-start = (f32[768,384]{1,0:T(8,128)S(1)}, f32[768,384]{1,0:T(8,128)}, u32[]{:S(2)}) copy-start(f32[768,384]{1,0:T(8,128)} %get-tuple-element.23.pack) | copy-start | bytes 3538948
  19.9 0.9 %copy-start.4 = (bf16[128,256]{1,0:T(8,128)(2,1)S(1)}, bf16[128,256]{1,0:T(8,128)(2,1)}, u32[]{:S(2)}) copy-start(bf16[128,256]{1,0:T(8,128)(2,1)} %get-tuple-element.24) | copy-start | bytes 196612
  20.0 17.7 %collective-permute-start.14 = (bf16[128,2304]{1,0:T(8,128)(2,1)S(1)}, bf16[128,2304]{1,0:T(8,128)(2,1)S(1)}, u32[]{:S(2)}, u32[]{:S(2)}) collective-permute-start(bf16[128,2304]{1,0:T(8,128)(2,1)S(1)} %collective-permute-done.6.refs_0_), channel_id=1, source_target_pairs={{0,4},{1,5},{2,6},{3,7},{4,0},{5,1},{6,2},{7,3},{8,12},{9,13},{10,... | collective-permute-start | bytes 1769480 | tf_op jit(solution)/shard_map/weights/ppermute | solution.py:342
  20.8 5.6 %collective-permute-start.3 = (bf16[128,256]{1,0:T(8,128)(2,1)S(1)}, bf16[128,256]{1,0:T(8,128)(2,1)S(1)}, u32[]{:S(2)}, u32[]{:S(2)}) collective-permute-start(bf16[128,256]{1,0:T(8,128)(2,1)S(1)} %copy-done.4), channel_id=1, source_target_pairs={{0,96},{32,0},{64,32},{96,64},{128,224},{160,128},{192,160},{224,1... | collective-permute-start | bytes 196616 | tf_op jit(solution)/shard_map/states/ppermute | solution.py:401
  22.4 5.3 %collective-permute-start.2 = (bf16[128,256]{1,0:T(8,128)(2,1)S(1)}, bf16[128,256]{1,0:T(8,128)(2,1)S(1)}, u32[]{:S(2)}, u32[]{:S(2)}) collective-permute-start(bf16[128,256]{1,0:T(8,128)(2,1)S(1)} %copy-done.4), channel_id=1, source_target_pairs={{0,64},{32,96},{64,0},{96,32},{128,192},{160,224},{192,128},{224,1... | collective-permute-start | bytes 196616 | tf_op jit(solution)/shard_map/states/ppermute | solution.py:401
  23.7 6.8 %collective-permute-start.1 = (bf16[128,256]{1,0:T(8,128)(2,1)S(1)}, bf16[128,256]{1,0:T(8,128)(2,1)S(1)}, u32[]{:S(2)}, u32[]{:S(2)}) collective-permute-start(bf16[128,256]{1,0:T(8,128)(2,1)S(1)} %copy-done.4), channel_id=1, source_target_pairs={{0,32},{32,64},{64,96},{96,0},{128,160},{160,192},{192,224},{224,1... | collective-permute-start | bytes 196616 | tf_op jit(solution)/shard_map/states/ppermute | solution.py:401
  24.1 17.2 %collective-permute-start.8 = (bf16[128,2304]{1,0:T(8,128)(2,1)S(1)}, bf16[128,2304]{1,0:T(8,128)(2,1)S(1)}, u32[]{:S(2)}, u32[]{:S(2)}) collective-permute-start(bf16[128,2304]{1,0:T(8,128)(2,1)S(1)} %copy-done.2), channel_id=1, source_target_pairs={{0,1},{1,0},{2,3},{3,2},{4,5},{5,4},{6,7},{7,6},{8,9},{9,8},{10,11... | collective-permute-start | bytes 1769480 | tf_op jit(solution)/shard_map/weights/ppermute | solution.py:342
  26.4 15.8 %collective-permute-start.9 = (bf16[128,2304]{1,0:T(8,128)(2,1)S(1)}, bf16[128,2304]{1,0:T(8,128)(2,1)S(1)}, u32[]{:S(2)}, u32[]{:S(2)}) collective-permute-start(bf16[128,2304]{1,0:T(8,128)(2,1)S(1)} %collective-permute-done.6.refs_0_), channel_id=1, source_target_pairs={{0,1},{1,0},{2,3},{3,2},{4,5},{5,4},{6,7},{7,6},{8,9},{9,8},{10,11... | collective-permute-start | bytes 1769480 | tf_op jit(solution)/shard_map/weights/ppermute | solution.py:342
  27.6 14.6 %collective-permute-start.10 = (bf16[128,2304]{1,0:T(8,128)(2,1)S(1)}, bf16[128,2304]{1,0:T(8,128)(2,1)S(1)}, u32[]{:S(2)}, u32[]{:S(2)}) collective-permute-start(bf16[128,2304]{1,0:T(8,128)(2,1)S(1)} %collective-permute-done.7.refs_2_), channel_id=1, source_target_pairs={{0,1},{1,0},{2,3},{3,2},{4,5},{5,4},{6,7},{7,6},{8,9},{9,8},{10,11... | collective-permute-start | bytes 1769480 | tf_op jit(solution)/shard_map/weights/ppermute | solution.py:342
  31.2 3.3 %collective-permute-start.4 = (bf16[128,128]{1,0:T(8,128)(2,1)S(1)}, bf16[128,128]{1,0:T(8,128)(2,1)S(1)}, u32[]{:S(2)}, u32[]{:S(2)}) collective-permute-start(bf16[128,128]{1,0:T(8,128)(2,1)S(1)} %get-tuple-element.26), channel_id=1, source_target_pairs={{0,128},{32,160},{64,192},{96,224},{128,0},{160,32},{192,64},{224,... | collective-permute-start | bytes 98312 | tf_op jit(solution)/shard_map/states/ppermute | solution.py:426
  35.1 2.6 %collective-permute-start.5 = (bf16[4,4,16,128]{3,2,1,0:T(8,128)(2,1)S(1)}, bf16[4,4,16,128]{3,2,1,0:T(8,128)(2,1)S(1)}, u32[]{:S(2)}, u32[]{:S(2)}) collective-permute-start(bf16[4,4,16,128]{3,2,1,0:T(8,128)(2,1)S(1)} %get-tuple-element.28), channel_id=1, source_target_pairs={{0,1},{1,0},{2,3},{3,2},{4,5},{5,4},{6,7},{7,6},{8,9},{9,8},{10,11... | collective-permute-start | bytes 196616 | tf_op jit(solution)/shard_map/exchange/ppermute | solution.py:342
  37.7 7.8 %collective-permute-start.15 = (bf16[128,2304]{1,0:T(8,128)(2,1)S(1)}, bf16[128,2304]{1,0:T(8,128)(2,1)S(1)}, u32[]{:S(2)}, u32[]{:S(2)}) collective-permute-start(bf16[128,2304]{1,0:T(8,128)(2,1)S(1)} %collective-permute-done.14.refs_4_), channel_id=1, source_target_pairs={{0,1},{1,0},{2,3},{3,2},{4,5},{5,4},{6,7},{7,6},{8,9},{9,8},{10,11... | collective-permute-start | bytes 1769480 | tf_op jit(solution)/shard_map/spread/ppermute | solution.py:342
  38.1 5.2 %collective-permute-start.11 = (bf16[2,4,16,128]{3,2,1,0:T(8,128)(2,1)S(1)}, bf16[2,4,16,128]{3,2,1,0:T(8,128)(2,1)S(1)}, u32[]{:S(2)}, u32[]{:S(2)}) collective-permute-start(bf16[2,4,16,128]{3,2,1,0:T(8,128)(2,1)S(1)} %get-tuple-element.35), channel_id=1, source_target_pairs={{0,6},{1,7},{2,4},{3,5},{4,2},{5,3},{6,0},{7,1},{8,14},{9,15},{10,... | collective-permute-start | bytes 98312 | tf_op jit(solution)/shard_map/exchange/ppermute | solution.py:342
  41.2 4.3 %collective-permute-start.12 = (bf16[2,4,16,128]{3,2,1,0:T(8,128)(2,1)S(1)}, bf16[2,4,16,128]{3,2,1,0:T(8,128)(2,1)S(1)}, u32[]{:S(2)}, u32[]{:S(2)}) collective-permute-start(bf16[2,4,16,128]{3,2,1,0:T(8,128)(2,1)S(1)} %get-tuple-element.36), channel_id=1, source_target_pairs={{0,2},{1,3},{2,0},{3,1},{4,6},{5,7},{6,4},{7,5},{8,10},{9,11},{10,... | collective-permute-start | bytes 98312 | tf_op jit(solution)/shard_map/exchange/ppermute | solution.py:342
  42.2 3.3 %collective-permute-start.13 = (bf16[2,4,16,128]{3,2,1,0:T(8,128)(2,1)S(1)}, bf16[2,4,16,128]{3,2,1,0:T(8,128)(2,1)S(1)}, u32[]{:S(2)}, u32[]{:S(2)}) collective-permute-start(bf16[2,4,16,128]{3,2,1,0:T(8,128)(2,1)S(1)} %get-tuple-element.37), channel_id=1, source_target_pairs={{0,4},{1,5},{2,6},{3,7},{4,0},{5,1},{6,2},{7,3},{8,12},{9,13},{10,... | collective-permute-start | bytes 98312 | tf_op jit(solution)/shard_map/exchange/ppermute | solution.py:342
  46.3 7.9 %collective-permute-start.16 = (bf16[16,2304]{1,0:T(8,128)(2,1)S(1)}, bf16[16,2304]{1,0:T(8,128)(2,1)S(1)}, u32[]{:S(2)}, u32[]{:S(2)}) collective-permute-start(bf16[16,2304]{1,0:T(8,128)(2,1)S(1)} %get-tuple-element.41), channel_id=1, source_target_pairs={{0,16},{1,17},{2,18},{3,19},{4,20},{5,21},{6,22},{7,23},{8,24},{9,... | collective-permute-start | bytes 221192 | tf_op jit(solution)/shard_map/reduce/ppermute | solution.py:342
  52.4 6.3 %collective-permute-start.18 = (bf16[16,2304]{1,0:T(8,128)(2,1)S(1)}, bf16[16,2304]{1,0:T(8,128)(2,1)S(1)}, u32[]{:S(2)}, u32[]{:S(2)}) collective-permute-start(bf16[16,2304]{1,0:T(8,128)(2,1)S(1)} %get-tuple-element.42), channel_id=1, source_target_pairs={{0,24},{1,25},{2,26},{3,27},{4,28},{5,29},{6,30},{7,31},{8,16},{9,... | collective-permute-start | bytes 221192 | tf_op jit(solution)/shard_map/reduce/ppermute | solution.py:342
  52.7 7.3 %collective-permute-start.17 = (bf16[16,2304]{1,0:T(8,128)(2,1)S(1)}, bf16[16,2304]{1,0:T(8,128)(2,1)S(1)}, u32[]{:S(2)}, u32[]{:S(2)}) collective-permute-start(bf16[16,2304]{1,0:T(8,128)(2,1)S(1)} %get-tuple-element.43), channel_id=1, source_target_pairs={{0,8},{1,9},{2,10},{3,11},{4,12},{5,13},{6,14},{7,15},{8,0},{9,1},... | collective-permute-start | bytes 221192 | tf_op jit(solution)/shard_map/reduce/ppermute | solution.py:342

commit v10 on v9

--- a/solution.py
+++ b/solution.py
@@ -421,7 +421,7 @@
             out_shape=[shape((head, 2 * head), F32), shape((head, head), BF16)],
             scratch_shapes=[pltpu.VMEM((half, head, 2 * head), BF16)],
             compiler_params=LIMIT,
-            cost_estimate=cost(0.5, 0),
+            cost_estimate=cost(0.5, 2),
         )(staged, *(found[step] for step in range(1, half)))
         came = lax.ppermute(total, "ctx", [(c, (c + half) % ctx_count) for c in range(ctx_count)])
     w_late, w_near, w_mine = after((w_far, w_next, w_out), staged)
@@ -435,7 +435,7 @@
             out_shape=[shape((SUBS // 2, zs, 16, head), BF16)] * 2,
             scratch_shapes=[pltpu.VMEM((zs, SUBS // 2, 2, 16, head), BF16)],
             compiler_params=LIMIT,
-            cost_estimate=cost(2, 0),
+            cost_estimate=cost(2, 4),
         )(staged, before, came)
     with jax.named_scope("exchange"):
         sibling = flip(other, 1)

time: 60.9 us -> 61.5 us (level)
  starting transfers between devices: 30.9 us -> 32.4 us
  waiting for transfers between devices: 13.2 us -> 12.3 us
    ppermute x1, waiting for transfers between devices: 2.99 us -> 0.01 us  [on_device(): lax.ppermute(total, 'ctx', [(c, (c + half) % ctx_count) for c in range(ct...]
    ppermute x3, waiting for transfers between devices: 0.01 us -> 2.75 us  [around(): return lax.ppermute(sends, 'ctx', pairs)]
    ppermute x13, starting transfers between devices: 22.5 us -> 24.1 us  [flip(): lax.ppermute(value, 'head', [(h, h ^ mask) for h in range(head_count)])]
    unnamed x10 -> x8, local copies, waits for them, and re-layouts: 1.9 us -> 1.91 us
  transfers between devices with their start and end apart: 19 -> 19, of which waited for: 7 -> 9; matrix products, arithmetic and copies ran while one was open for 0% -> 0% of each run, Pallas kernels for 19% -> 19%
where the time goes in v10:
time: 61.5 us; the launch traced here: 61.4 us
  starting transfers between devices  32.4 us (53%)
  Pallas kernels  12.4 us (20%)
  waiting for transfers between devices  12.3 us (20%)
  local copies, waits for them, and re-layouts  2.82 us (5%)
  between operations  0.76 us (1%)
  other arithmetic  0.68 us (1%)
    ppermute x13, starting transfers between devices, flip(): lax.ppermute(value, 'head', [(h, h ^ mask) for h in range(head_count)])  24.1 us
    pallas_call x1, Pallas kernels, on_device(): pl.pallas_call(front, in_specs=[HBM] * 11, out_specs=[HBM] * 2, out_shape...  9.98 us
    ppermute x13, waiting for transfers between devices, flip(): lax.ppermute(value, 'head', [(h, h ^ mask) for h in range(head_count)])  9.58 us
    ppermute x3, starting transfers between devices, around(): return lax.ppermute(sends, 'ctx', pairs)  3.39 us
    ppermute x3, waiting for transfers between devices, around(): return lax.ppermute(sends, 'ctx', pairs)  2.75 us
    ppermute x1, starting transfers between devices, across(): return lax.ppermute(value, ('ctx', 'head'), pairs)  2.73 us
    ppermute x1, starting transfers between devices, on_device(): lax.ppermute(edge, 'ctx', [(i, (i + 1) % ctx_count) for i in range(ctx_co...  2.04 us
    unnamed x8, local copies, waits for them, and re-layouts  1.91 us
  transfers between devices with their start and end apart: 19, of which 9 were waited for; matrix products, arithmetic and copies ran while one was open for 0% of the time, Pallas kernels for 19%

profile of v10, /device:TPU:1, one launch (start us, length us, event | category | flops | bytes accessed | tf_op | source)
XLA Modules:
  0.0 61.4 jit_solution(16419993457349416026)
XLA Ops:
  0.0 0.9 %slice.15 = bf16[16,2304]{1,0:T(8,128)(2,1)S(1)} slice(bf16[512,2304]{1,0:T(8,128)(2,1)} %tokens_hbm.1), slice={[496:512], [0:2304]} | slice | bytes 147456 | tf_op jit(solution)/shard_map/slice | solution.py:346
  0.9 2.0 %collective-permute-start = (bf16[16,2304]{1,0:T(8,128)(2,1)S(1)}, bf16[16,2304]{1,0:T(8,128)(2,1)S(1)}, u32[]{:S(2)}, u32[]{:S(2)}) collective-permute-start(bf16[16,2304]{1,0:T(8,128)(2,1)S(1)} %slice.15), channel_id=1, source_target_pairs={{0,32},{32,64},{64,96},{96,128},{128,160},{160,192},{192,224},{224... | collective-permute-start | bytes 221192 | tf_op jit(solution)/shard_map/rim/ppermute | solution.py:348
  2.9 1.6 %collective-permute-start.7 = (bf16[128,2304]{1,0:T(8,128)(2,1)}, bf16[128,2304]{1,0:T(8,128)(2,1)S(1)}, u32[]{:S(2)}, u32[]{:S(2)}) collective-permute-start(bf16[128,2304]{1,0:T(8,128)(2,1)} %w_one.1), channel_id=1, source_target_pairs={{0,4},{1,5},{2,6},{3,7},{4,0},{5,1},{6,2},{7,3},{8,12},{9,13},{10,... | collective-permute-start | bytes 1769480 | tf_op jit(solution)/shard_map/weights/ppermute | solution.py:342
  4.6 2.7 %collective-permute-start.6 = (bf16[128,2304]{1,0:T(8,128)(2,1)}, bf16[128,2304]{1,0:T(8,128)(2,1)S(1)}, u32[]{:S(2)}, u32[]{:S(2)}) collective-permute-start(bf16[128,2304]{1,0:T(8,128)(2,1)} %w_one.1), channel_id=1, source_target_pairs={{0,130},{1,131},{2,128},{3,129},{4,134},{5,135},{6,132},{7,133},{8... | collective-permute-start | bytes 1769480 | tf_op jit(solution)/shard_map/weights/ppermute | solution.py:339
  8.0 0.0 collective-permute-done.rim_hbm
  8.0 0.0 copy-start.3
  8.0 0.6 %copy-done.3 = bf16[16,2304]{1,0:T(8,128)(2,1)} copy-done((bf16[16,2304]{1,0:T(8,128)(2,1)}, bf16[16,2304]{1,0:T(8,128)(2,1)S(1)}, u32[]{:S(2)}) %copy-start.3) | copy-done | bytes 73752
  8.6 0.0 copy-start.1
  8.6 10.0 %front.1 = (f32[768,384]{1,0:T(8,128)}, bf16[128,256]{1,0:T(8,128)(2,1)}) custom-call(bf16[512,2304]{1,0:T(8,128)(2,1)} %tokens_hbm.1, bf16[16,2304]{1,0:T(8,128)(2,1)} %copy-done.3, f32[1,1]{1,0:T(1,128)} %bitcast.17.alog_hbm, bf16[3,2304,128]{2,1,0:T(8,128)(2,1)} %bitcast.19, bf16[2304,128]{1,0:T(8,128)(2,1)} %f_down_hbm.1, bf16[2304,128]{1,0:T(8,128)(2,1)} %o_down_hbm.1, ...), custom_call_target="tpu_custom_call" | custom-call | flops 40000000000 | bytes 33210000 | tf_op jit(solution)/shard_map/front/pallas_call | solution.py:353
  18.6 1.7 %collective-permute-start.3 = (bf16[128,256]{1,0:T(8,128)(2,1)}, bf16[128,256]{1,0:T(8,128)(2,1)S(1)}, u32[]{:S(2)}, u32[]{:S(2)}) collective-permute-start(bf16[128,256]{1,0:T(8,128)(2,1)} %get-tuple-element.24), channel_id=1, source_target_pairs={{0,96},{32,0},{64,32},{96,64},{128,224},{160,128},{192,160},{224,1... | collective-permute-start | bytes 196616 | tf_op jit(solution)/shard_map/states/ppermute | solution.py:401
  20.3 1.4 %collective-permute-start.2 = (bf16[128,256]{1,0:T(8,128)(2,1)}, bf16[128,256]{1,0:T(8,128)(2,1)S(1)}, u32[]{:S(2)}, u32[]{:S(2)}) collective-permute-start(bf16[128,256]{1,0:T(8,128)(2,1)} %get-tuple-element.24), channel_id=1, source_target_pairs={{0,64},{32,96},{64,0},{96,32},{128,192},{160,224},{192,128},{224,1... | collective-permute-start | bytes 196616 | tf_op jit(solution)/shard_map/states/ppermute | solution.py:401
  21.7 0.3 collective-permute-start.1
  22.0 0.0 copy-done.1
  22.0 0.0 copy-start
  22.0 1.3 %copy-done = f32[768,384]{1,0:T(8,128)S(1)} copy-done((f32[768,384]{1,0:T(8,128)S(1)}, f32[768,384]{1,0:T(8,128)}, u32[]{:S(2)}) %copy-start) | copy-done | bytes 1179672
  23.3 0.1 stage.1.pack
  23.3 0.0 copy-start.2
  23.3 0.0 collective-permute-done.6.refs_0_
  23.4 0.1 collective-permute-start.14
  23.5 0.0 collective-permute-done.3.refs_2_
  23.5 1.7 %collective-permute-done.2.refs_1_ = bf16[128,256]{1,0:T(8,128)(2,1)S(1)} collective-permute-done((bf16[128,256]{1,0:T(8,128)(2,1)}, bf16[128,256]{1,0:T(8,128)(2,1)S(1)}, u32[]{:S(2)}, u32[]{:S(2)}) %collective-permute-start.2) | collective-permute-done | bytes 65568 | tf_op jit(solution)/shard_map/states/ppermute | solution.py:401
  25.1 1.1 %collective-permute-done.1.refs_0_ = bf16[128,256]{1,0:T(8,128)(2,1)S(1)} collective-permute-done((bf16[128,256]{1,0:T(8,128)(2,1)}, bf16[128,256]{1,0:T(8,128)(2,1)S(1)}, u32[]{:S(2)}, u32[]{:S(2)}) %collective-permute-start.1) | collective-permute-done | bytes 65568 | tf_op jit(solution)/shard_map/states/ppermute | solution.py:401
  26.2 0.6 %states.1 = (f32[128,256]{1,0:T(8,128)S(1)}, bf16[128,128]{1,0:T(8,128)(2,1)S(1)}) custom-call(f32[768,384]{1,0:T(8,128)S(1)} %stage.1.pack, bf16[128,256]{1,0:T(8,128)(2,1)S(1)} %collective-permute-done.1.refs_0_, bf16[128,256]{1,0:T(8,128)(2,1)S(1)} %collective-permute-done.2.refs_1_, bf16[128,256]{1,0:T(8,128)(2,1)S(1)} %collective-permute-done.3.refs_2_), custom_call_target="tpu_custom_call" | custom-call | flops 2000000000 | bytes 1845000 | tf_op jit(solution)/shard_map/states/pallas_call | solution.py:417
  26.8 0.1 collective-permute-start.4
  27.0 0.0 collective-permute-done.7.refs_2_
  27.0 0.0 copy-done.2
  27.0 3.3 %collective-permute-start.8 = (bf16[128,2304]{1,0:T(8,128)(2,1)S(1)}, bf16[128,2304]{1,0:T(8,128)(2,1)S(1)}, u32[]{:S(2)}, u32[]{:S(2)}) collective-permute-start(bf16[128,2304]{1,0:T(8,128)(2,1)S(1)} %copy-done.2), channel_id=1, source_target_pairs={{0,1},{1,0},{2,3},{3,2},{4,5},{5,4},{6,7},{7,6},{8,9},{9,8},{10,11... | collective-permute-start | bytes 1769480 | tf_op jit(solution)/shard_map/weights/ppermute | solution.py:342
  30.3 0.1 collective-permute-start.9
  30.4 0.4 collective-permute-start.10
  30.8 0.0 collective-permute-done.4.came
  30.8 0.5 finish.1
  31.3 3.4 %collective-permute-start.5 = (bf16[4,4,16,128]{3,2,1,0:T(8,128)(2,1)S(1)}, bf16[4,4,16,128]{3,2,1,0:T(8,128)(2,1)S(1)}, u32[]{:S(2)}, u32[]{:S(2)}) collective-permute-start(bf16[4,4,16,128]{3,2,1,0:T(8,128)(2,1)S(1)} %get-tuple-element.28), channel_id=1, source_target_pairs={{0,1},{1,0},{2,3},{3,2},{4,5},{5,4},{6,7},{7,6},{8,9},{9,8},{10,11... | collective-permute-start | bytes 196616 | tf_op jit(solution)/shard_map/exchange/ppermute | solution.py:342
  34.7 0.9 %collective-permute-done.5.sibling = bf16[4,4,16,128]{3,2,1,0:T(8,128)(2,1)S(1)} collective-permute-done((bf16[4,4,16,128]{3,2,1,0:T(8,128)(2,1)S(1)}, bf16[4,4,16,128]{3,2,1,0:T(8,128)(2,1)S(1)}, u32[]{:S(2)}, u32[]{:S(2)}) %collective-permute-start.5) | collective-permute-done | bytes 65568 | tf_op jit(solution)/shard_map/exchange/ppermute | solution.py:342
  35.6 0.3 collective-permute-done.14.refs_4_
  35.9 3.3 %collective-permute-start.15 = (bf16[128,2304]{1,0:T(8,128)(2,1)S(1)}, bf16[128,2304]{1,0:T(8,128)(2,1)S(1)}, u32[]{:S(2)}, u32[]{:S(2)}) collective-permute-start(bf16[128,2304]{1,0:T(8,128)(2,1)S(1)} %collective-permute-done.14.refs_4_), channel_id=1, source_target_pairs={{0,1},{1,0},{2,3},{3,2},{4,5},{5,4},{6,7},{7,6},{8,9},{9,8},{10,11... | collective-permute-start | bytes 1769480 | tf_op jit(solution)/shard_map/spread/ppermute | solution.py:342
  39.2 1.5 %collective-permute-start.11 = (bf16[2,4,16,128]{3,2,1,0:T(8,128)(2,1)S(1)}, bf16[2,4,16,128]{3,2,1,0:T(8,128)(2,1)S(1)}, u32[]{:S(2)}, u32[]{:S(2)}) collective-permute-start(bf16[2,4,16,128]{3,2,1,0:T(8,128)(2,1)S(1)} %get-tuple-element.35), channel_id=1, source_target_pairs={{0,6},{1,7},{2,4},{3,5},{4,2},{5,3},{6,0},{7,1},{8,14},{9,15},{10,... | collective-permute-start | bytes 98312 | tf_op jit(solution)/shard_map/exchange/ppermute | solution.py:342
  40.7 0.0 collective-permute-done.8.w_two
  40.7 1.2 %collective-permute-start.12 = (bf16[2,4,16,128]{3,2,1,0:T(8,128)(2,1)S(1)}, bf16[2,4,16,128]{3,2,1,0:T(8,128)(2,1)S(1)}, u32[]{:S(2)}, u32[]{:S(2)}) collective-permute-start(bf16[2,4,16,128]{3,2,1,0:T(8,128)(2,1)S(1)} %get-tuple-element.36), channel_id=1, source_target_pairs={{0,2},{1,3},{2,0},{3,1},{4,6},{5,7},{6,4},{7,5},{8,10},{9,11},{10,... | collective-permute-start | bytes 98312 | tf_op jit(solution)/shard_map/exchange/ppermute | solution.py:342
  41.9 0.0 collective-permute-done.9.refs_1_
  41.9 1.5 %collective-permute-start.13 = (bf16[2,4,16,128]{3,2,1,0:T(8,128)(2,1)S(1)}, bf16[2,4,16,128]{3,2,1,0:T(8,128)(2,1)S(1)}, u32[]{:S(2)}, u32[]{:S(2)}) collective-permute-start(bf16[2,4,16,128]{3,2,1,0:T(8,128)(2,1)S(1)} %get-tuple-element.37), channel_id=1, source_target_pairs={{0,4},{1,5},{2,6},{3,7},{4,0},{5,1},{6,2},{7,3},{8,12},{9,13},{10,... | collective-permute-start | bytes 98312 | tf_op jit(solution)/shard_map/exchange/ppermute | solution.py:342
  43.3 0.0 collective-permute-done.10.refs_3_
  43.3 0.4 spread.2
  43.8 0.6 collective-permute-done.11.refs_0_
  44.4 0.8 %collective-permute-done.12.refs_1_ = bf16[2,4,16,128]{3,2,1,0:T(8,128)(2,1)S(1)} collective-permute-done((bf16[2,4,16,128]{3,2,1,0:T(8,128)(2,1)S(1)}, bf16[2,4,16,128]{3,2,1,0:T(8,128)(2,1)S(1)}, u32[]{:S(2)}, u32[]{:S(2)}) %collective-permute-start.12) | collective-permute-done | bytes 32800 | tf_op jit(solution)/shard_map/exchange/ppermute | solution.py:342
  45.2 0.0 collective-permute-done.13.refs_2_
  45.2 0.0 collective-permute-done.15.refs_5_
  45.2 0.7 %spread.3 = bf16[4,16,2304]{2,1,0:T(8,128)(2,1)S(1)} custom-call(f32[64,2304]{1,0:T(8,128)S(1)} %get-tuple-element.34.begun, bf16[2,4,16,128]{3,2,1,0:T(8,128)(2,1)S(1)} %collective-permute-done.11.refs_0_, bf16[2,4,16,128]{3,2,1,0:T(8,128)(2,1)S(1)} %collective-permute-done.12.refs_1_, bf16[2,4,16,128]{3,2,1,0:T(8,128)(2,1)S(1)} %collective-permute-done.13.refs_2_, ...), custom_call_target="tpu_custom_call" | custom-call | flops 1000000000 | bytes 3690000 | tf_op jit(solution)/shard_map/spread/pallas_call | solution.py:463
  45.9 6.6 %collective-permute-start.16 = (bf16[16,2304]{1,0:T(8,128)(2,1)S(1)}, bf16[16,2304]{1,0:T(8,128)(2,1)S(1)}, u32[]{:S(2)}, u32[]{:S(2)}) collective-permute-start(bf16[16,2304]{1,0:T(8,128)(2,1)S(1)} %get-tuple-element.41), channel_id=1, source_target_pairs={{0,16},{1,17},{2,18},{3,19},{4,20},{5,21},{6,22},{7,23},{8,24},{9,... | collective-permute-start | bytes 221192 | tf_op jit(solution)/shard_map/reduce/ppermute | solution.py:342
  52.5 0.0 collective-permute-start.18
  52.5 1.2 %collective-permute-start.17 = (bf16[16,2304]{1,0:T(8,128)(2,1)S(1)}, bf16[16,2304]{1,0:T(8,128)(2,1)S(1)}, u32[]{:S(2)}, u32[]{:S(2)}) collective-permute-start(bf16[16,2304]{1,0:T(8,128)(2,1)S(1)} %get-tuple-element.43), channel_id=1, source_target_pairs={{0,8},{1,9},{2,10},{3,11},{4,12},{5,13},{6,14},{7,15},{8,0},{9,1},... | collective-permute-start | bytes 221192 | tf_op jit(solution)/shard_map/reduce/ppermute | solution.py:342
  53.7 0.7 %collective-permute-done.16 = bf16[16,2304]{1,0:T(8,128)(2,1)S(1)} collective-permute-done((bf16[16,2304]{1,0:T(8,128)(2,1)S(1)}, bf16[16,2304]{1,0:T(8,128)(2,1)S(1)}, u32[]{:S(2)}, u32[]{:S(2)}) %collective-permute-start.16) | collective-permute-done | bytes 73760 | tf_op jit(solution)/shard_map/reduce/ppermute | solution.py:342
  54.4 3.6 %collective-permute-done.18 = bf16[16,2304]{1,0:T(8,128)(2,1)S(1)} collective-permute-done((bf16[16,2304]{1,0:T(8,128)(2,1)S(1)}, bf16[16,2304]{1,0:T(8,128)(2,1)S(1)}, u32[]{:S(2)}, u32[]{:S(2)}) %collective-permute-start.18) | collective-permute-done | bytes 73760 | tf_op jit(solution)/shard_map/reduce/ppermute | solution.py:342
  57.9 2.8 %collective-permute-done.17 = bf16[16,2304]{1,0:T(8,128)(2,1)S(1)} collective-permute-done((bf16[16,2304]{1,0:T(8,128)(2,1)S(1)}, bf16[16,2304]{1,0:T(8,128)(2,1)S(1)}, u32[]{:S(2)}, u32[]{:S(2)}) %collective-permute-start.17) | collective-permute-done | bytes 73760 | tf_op jit(solution)/shard_map/reduce/ppermute | solution.py:342
  60.7 0.7 %fusion.2 = bf16[16,2304]{1,0:T(8,128)(2,1)} fusion(bf16[16,2304]{1,0:T(8,128)(2,1)S(1)} %collective-permute-done.18, bf16[16,2304]{1,0:T(8,128)(2,1)S(1)} %collective-permute-done.17, bf16[16,2304]{1,0:T(8,128)(2,1)S(1)} %collective-permute-done.16, bf16[4,16,2304]{2,1,0:T(8,128)(2,1)S(1)} %spread.3), kind=kLoop, calls=%fused_computation.3 | loop fusion | flops 294912 | bytes 368640 | tf_op jit(solution)/shard_map/reduce/convert_element_type | solution.py:476
  (2 shorter events, 0.0 us)
Async XLA Ops:
  0.9 7.1 %collective-permute-start = (bf16[16,2304]{1,0:T(8,128)(2,1)S(1)}, bf16[16,2304]{1,0:T(8,128)(2,1)S(1)}, u32[]{:S(2)}, u32[]{:S(2)}) collective-permute-start(bf16[16,2304]{1,0:T(8,128)(2,1)S(1)} %slice.15), channel_id=1, source_target_pairs={{0,32},{32,64},{64,96},{96,128},{128,160},{160,192},{192,224},{224... | collective-permute-start | bytes 221192 | tf_op jit(solution)/shard_map/rim/ppermute | solution.py:348
  2.9 24.0 %collective-permute-start.7 = (bf16[128,2304]{1,0:T(8,128)(2,1)}, bf16[128,2304]{1,0:T(8,128)(2,1)S(1)}, u32[]{:S(2)}, u32[]{:S(2)}) collective-permute-start(bf16[128,2304]{1,0:T(8,128)(2,1)} %w_one.1), channel_id=1, source_target_pairs={{0,4},{1,5},{2,6},{3,7},{4,0},{5,1},{6,2},{7,3},{8,12},{9,13},{10,... | collective-permute-start | bytes 1769480 | tf_op jit(solution)/shard_map/weights/ppermute | solution.py:342
  4.6 18.8 %collective-permute-start.6 = (bf16[128,2304]{1,0:T(8,128)(2,1)}, bf16[128,2304]{1,0:T(8,128)(2,1)S(1)}, u32[]{:S(2)}, u32[]{:S(2)}) collective-permute-start(bf16[128,2304]{1,0:T(8,128)(2,1)} %w_one.1), channel_id=1, source_target_pairs={{0,130},{1,131},{2,128},{3,129},{4,134},{5,135},{6,132},{7,133},{8... | collective-permute-start | bytes 1769480 | tf_op jit(solution)/shard_map/weights/ppermute | solution.py:339
  8.0 0.6 %copy-start.3 = (bf16[16,2304]{1,0:T(8,128)(2,1)}, bf16[16,2304]{1,0:T(8,128)(2,1)S(1)}, u32[]{:S(2)}) copy-start(bf16[16,2304]{1,0:T(8,128)(2,1)S(1)} %collective-permute-done.rim_hbm) | copy-start | bytes 221188
  8.6 13.4 %copy-start.1 = (f32[128]{0:T(128)S(1)}, f32[128]{0:T(128)}, u32[]{:S(2)}) copy-start(f32[128]{0:T(128)} %param.22) | copy-start | bytes 1540
  18.6 4.9 %collective-permute-start.3 = (bf16[128,256]{1,0:T(8,128)(2,1)}, bf16[128,256]{1,0:T(8,128)(2,1)S(1)}, u32[]{:S(2)}, u32[]{:S(2)}) collective-permute-start(bf16[128,256]{1,0:T(8,128)(2,1)} %get-tuple-element.24), channel_id=1, source_target_pairs={{0,96},{32,0},{64,32},{96,64},{128,224},{160,128},{192,160},{224,1... | collective-permute-start | bytes 196616 | tf_op jit(solution)/shard_map/states/ppermute | solution.py:401
  20.3 4.8 %collective-permute-start.2 = (bf16[128,256]{1,0:T(8,128)(2,1)}, bf16[128,256]{1,0:T(8,128)(2,1)S(1)}, u32[]{:S(2)}, u32[]{:S(2)}) collective-permute-start(bf16[128,256]{1,0:T(8,128)(2,1)} %get-tuple-element.24), channel_id=1, source_target_pairs={{0,64},{32,96},{64,0},{96,32},{128,192},{160,224},{192,128},{224,1... | collective-permute-start | bytes 196616 | tf_op jit(solution)/shard_map/states/ppermute | solution.py:401
  21.7 4.5 %collective-permute-start.1 = (bf16[128,256]{1,0:T(8,128)(2,1)}, bf16[128,256]{1,0:T(8,128)(2,1)S(1)}, u32[]{:S(2)}, u32[]{:S(2)}) collective-permute-start(bf16[128,256]{1,0:T(8,128)(2,1)} %get-tuple-element.24), channel_id=1, source_target_pairs={{0,32},{32,64},{64,96},{96,0},{128,160},{160,192},{192,224},{224,1... | collective-permute-start | bytes 196616 | tf_op jit(solution)/shard_map/states/ppermute | solution.py:401
  22.0 1.3 %copy-start = (f32[768,384]{1,0:T(8,128)S(1)}, f32[768,384]{1,0:T(8,128)}, u32[]{:S(2)}) copy-start(f32[768,384]{1,0:T(8,128)} %get-tuple-element.23.pack) | copy-start | bytes 3538948
  23.3 3.6 %copy-start.2 = (bf16[128,2304]{1,0:T(8,128)(2,1)S(1)}, bf16[128,2304]{1,0:T(8,128)(2,1)}, u32[]{:S(2)}) copy-start(bf16[128,2304]{1,0:T(8,128)(2,1)} %w_one.1) | copy-start | bytes 1769476
  23.4 12.6 %collective-permute-start.14 = (bf16[128,2304]{1,0:T(8,128)(2,1)S(1)}, bf16[128,2304]{1,0:T(8,128)(2,1)S(1)}, u32[]{:S(2)}, u32[]{:S(2)}) collective-permute-start(bf16[128,2304]{1,0:T(8,128)(2,1)S(1)} %collective-permute-done.6.refs_0_), channel_id=1, source_target_pairs={{0,4},{1,5},{2,6},{3,7},{4,0},{5,1},{6,2},{7,3},{8,12},{9,13},{10,... | collective-permute-start | bytes 1769480 | tf_op jit(solution)/shard_map/weights/ppermute | solution.py:342
  26.8 4.0 %collective-permute-start.4 = (bf16[128,128]{1,0:T(8,128)(2,1)S(1)}, bf16[128,128]{1,0:T(8,128)(2,1)S(1)}, u32[]{:S(2)}, u32[]{:S(2)}) collective-permute-start(bf16[128,128]{1,0:T(8,128)(2,1)S(1)} %get-tuple-element.26), channel_id=1, source_target_pairs={{0,128},{32,160},{64,192},{96,224},{128,0},{160,32},{192,64},{224,... | collective-permute-start | bytes 98312 | tf_op jit(solution)/shard_map/states/ppermute | solution.py:426
  27.0 13.7 %collective-permute-start.8 = (bf16[128,2304]{1,0:T(8,128)(2,1)S(1)}, bf16[128,2304]{1,0:T(8,128)(2,1)S(1)}, u32[]{:S(2)}, u32[]{:S(2)}) collective-permute-start(bf16[128,2304]{1,0:T(8,128)(2,1)S(1)} %copy-done.2), channel_id=1, source_target_pairs={{0,1},{1,0},{2,3},{3,2},{4,5},{5,4},{6,7},{7,6},{8,9},{9,8},{10,11... | collective-permute-start | bytes 1769480 | tf_op jit(solution)/shard_map/weights/ppermute | solution.py:342
  30.3 11.6 %collective-permute-start.9 = (bf16[128,2304]{1,0:T(8,128)(2,1)S(1)}, bf16[128,2304]{1,0:T(8,128)(2,1)S(1)}, u32[]{:S(2)}, u32[]{:S(2)}) collective-permute-start(bf16[128,2304]{1,0:T(8,128)(2,1)S(1)} %collective-permute-done.6.refs_0_), channel_id=1, source_target_pairs={{0,1},{1,0},{2,3},{3,2},{4,5},{5,4},{6,7},{7,6},{8,9},{9,8},{10,11... | collective-permute-start | bytes 1769480 | tf_op jit(solution)/shard_map/weights/ppermute | solution.py:342
  30.4 13.0 %collective-permute-start.10 = (bf16[128,2304]{1,0:T(8,128)(2,1)S(1)}, bf16[128,2304]{1,0:T(8,128)(2,1)S(1)}, u32[]{:S(2)}, u32[]{:S(2)}) collective-permute-start(bf16[128,2304]{1,0:T(8,128)(2,1)S(1)} %collective-permute-done.7.refs_2_), channel_id=1, source_target_pairs={{0,1},{1,0},{2,3},{3,2},{4,5},{5,4},{6,7},{7,6},{8,9},{9,8},{10,11... | collective-permute-start | bytes 1769480 | tf_op jit(solution)/shard_map/weights/ppermute | solution.py:342
  31.3 4.3 %collective-permute-start.5 = (bf16[4,4,16,128]{3,2,1,0:T(8,128)(2,1)S(1)}, bf16[4,4,16,128]{3,2,1,0:T(8,128)(2,1)S(1)}, u32[]{:S(2)}, u32[]{:S(2)}) collective-permute-start(bf16[4,4,16,128]{3,2,1,0:T(8,128)(2,1)S(1)} %get-tuple-element.28), channel_id=1, source_target_pairs={{0,1},{1,0},{2,3},{3,2},{4,5},{5,4},{6,7},{7,6},{8,9},{9,8},{10,11... | collective-permute-start | bytes 196616 | tf_op jit(solution)/shard_map/exchange/ppermute | solution.py:342
  35.9 9.3 %collective-permute-start.15 = (bf16[128,2304]{1,0:T(8,128)(2,1)S(1)}, bf16[128,2304]{1,0:T(8,128)(2,1)S(1)}, u32[]{:S(2)}, u32[]{:S(2)}) collective-permute-start(bf16[128,2304]{1,0:T(8,128)(2,1)S(1)} %collective-permute-done.14.refs_4_), channel_id=1, source_target_pairs={{0,1},{1,0},{2,3},{3,2},{4,5},{5,4},{6,7},{7,6},{8,9},{9,8},{10,11... | collective-permute-start | bytes 1769480 | tf_op jit(solution)/shard_map/spread/ppermute | solution.py:342
  39.2 5.2 %collective-permute-start.11 = (bf16[2,4,16,128]{3,2,1,0:T(8,128)(2,1)S(1)}, bf16[2,4,16,128]{3,2,1,0:T(8,128)(2,1)S(1)}, u32[]{:S(2)}, u32[]{:S(2)}) collective-permute-start(bf16[2,4,16,128]{3,2,1,0:T(8,128)(2,1)S(1)} %get-tuple-element.35), channel_id=1, source_target_pairs={{0,6},{1,7},{2,4},{3,5},{4,2},{5,3},{6,0},{7,1},{8,14},{9,15},{10,... | collective-permute-start | bytes 98312 | tf_op jit(solution)/shard_map/exchange/ppermute | solution.py:342
  40.7 4.5 %collective-permute-start.12 = (bf16[2,4,16,128]{3,2,1,0:T(8,128)(2,1)S(1)}, bf16[2,4,16,128]{3,2,1,0:T(8,128)(2,1)S(1)}, u32[]{:S(2)}, u32[]{:S(2)}) collective-permute-start(bf16[2,4,16,128]{3,2,1,0:T(8,128)(2,1)S(1)} %get-tuple-element.36), channel_id=1, source_target_pairs={{0,2},{1,3},{2,0},{3,1},{4,6},{5,7},{6,4},{7,5},{8,10},{9,11},{10,... | collective-permute-start | bytes 98312 | tf_op jit(solution)/shard_map/exchange/ppermute | solution.py:342
  41.9 3.3 %collective-permute-start.13 = (bf16[2,4,16,128]{3,2,1,0:T(8,128)(2,1)S(1)}, bf16[2,4,16,128]{3,2,1,0:T(8,128)(2,1)S(1)}, u32[]{:S(2)}, u32[]{:S(2)}) collective-permute-start(bf16[2,4,16,128]{3,2,1,0:T(8,128)(2,1)S(1)} %get-tuple-element.37), channel_id=1, source_target_pairs={{0,4},{1,5},{2,6},{3,7},{4,0},{5,1},{6,2},{7,3},{8,12},{9,13},{10,... | collective-permute-start | bytes 98312 | tf_op jit(solution)/shard_map/exchange/ppermute | solution.py:342
  45.9 8.4 %collective-permute-start.16 = (bf16[16,2304]{1,0:T(8,128)(2,1)S(1)}, bf16[16,2304]{1,0:T(8,128)(2,1)S(1)}, u32[]{:S(2)}, u32[]{:S(2)}) collective-permute-start(bf16[16,2304]{1,0:T(8,128)(2,1)S(1)} %get-tuple-element.41), channel_id=1, source_target_pairs={{0,16},{1,17},{2,18},{3,19},{4,20},{5,21},{6,22},{7,23},{8,24},{9,... | collective-permute-start | bytes 221192 | tf_op jit(solution)/shard_map/reduce/ppermute | solution.py:342
  52.5 5.4 %collective-permute-start.18 = (bf16[16,2304]{1,0:T(8,128)(2,1)S(1)}, bf16[16,2304]{1,0:T(8,128)(2,1)S(1)}, u32[]{:S(2)}, u32[]{:S(2)}) collective-permute-start(bf16[16,2304]{1,0:T(8,128)(2,1)S(1)} %get-tuple-element.42), channel_id=1, source_target_pairs={{0,24},{1,25},{2,26},{3,27},{4,28},{5,29},{6,30},{7,31},{8,16},{9,... | collective-permute-start | bytes 221192 | tf_op jit(solution)/shard_map/reduce/ppermute | solution.py:342
  52.5 8.2 %collective-permute-start.17 = (bf16[16,2304]{1,0:T(8,128)(2,1)S(1)}, bf16[16,2304]{1,0:T(8,128)(2,1)S(1)}, u32[]{:S(2)}, u32[]{:S(2)}) collective-permute-start(bf16[16,2304]{1,0:T(8,128)(2,1)S(1)} %get-tuple-element.43), channel_id=1, source_target_pairs={{0,8},{1,9},{2,10},{3,11},{4,12},{5,13},{6,14},{7,15},{8,0},{9,1},... | collective-permute-start | bytes 221192 | tf_op jit(solution)/shard_map/reduce/ppermute | solution.py:342
